TPU v7x, 32 devices: a whole 2x2x4 slice. The times are simulated.
32 devices in a mesh: groups: 2 (over y), orb: 4 (over z), fit: 2 (over x), rep: 2 (over core).
Axes of the slice: x: 2, y: 2, z: 4, core: 2. Of those that a mesh axis runs over, the one named last changes fastest.
Arguments:
- blocks: bfloat16 [64, 2048, 256], P(('groups', 'orb'), 'fit'), parts along dimension 0, may hold values from -0.8984375 to 0.8984375
- occ_energy: bfloat16 [64], P(('groups', 'orb')), parts along dimension 0, may hold values from -2 to -0.5
- pair_list: int32 [128, 2], P(('groups', 'orb', 'rep')), parts along dimension 0, may hold values from 0 to 31, as said below
- pno_sizes: int32 [128], P(('groups', 'orb', 'rep')), parts along dimension 0, may hold values from 64 to 256
- fock_virt: float32 [128, 256, 256], P(('groups', 'orb', 'rep')), parts along dimension 0, as said below
Outputs:
- amplitudes: bfloat16 [128, 256, 256], P(('groups', 'orb', 'rep')), parts along dimension 0
- grads: float32 [64, 2048, 256], P(('groups', 'orb'), 'fit'), parts along dimension 0
There are 2 independent parts, one for each index of `groups`. A program takes and returns all parts, laid end to end along the dimension named above; each array names one. Nothing has to cross between parts.
Inputs may be any that keep to these rules, and one draw needn't show every extreme that they name: `pair_list`: each row names two different orbitals; orbital g lies on orb index g // 8. Among the orbitals named by one device's 8 rows (aligned blocks of 8 rows), at most 2 distinct ones lie on any one orb index, and for every device exactly 2 lie on some orb index. `fock_virt`: symmetric with a positive diagonal.
All inputs are finite; a program needn't handle non-finite values.
Results may differ from a plain program's by a relative error of at most 0.014.
Values may be sent and summed in bfloat16 or wider, within the bound.
No kernel may reach another device: no remote copies, remote signals or barrier semaphores. Data moves between devices by JAX's collectives and lax.ppermute only.
A program may use at most 128 MiB of HBM per device.

v0:
```python
import jax
import jax.numpy as jnp
from jax import lax
from jax.sharding import PartitionSpec as P

CAP = 2
ITERS = 2


def iterate_pairs(exchange_ints, fock_here, occ_sums, pno_mask):
    diagonal = jnp.diagonal(fock_here, axis1=1, axis2=2)
    denominator = diagonal[:, :, None] + diagonal[:, None, :] - occ_sums[:, None, None]
    current = jnp.zeros_like(exchange_ints)
    for iteration in range(ITERS):
        left_term = jnp.einsum("pab,pbc->pac", fock_here, current, precision=lax.Precision.HIGHEST)
        right_term = jnp.einsum("pab,pbc->pac", current, fock_here, precision=lax.Precision.HIGHEST)
        residual = (
            exchange_ints + left_term + right_term - occ_sums[:, None, None] * current
        ) * pno_mask
        current = current - residual / denominator
    return current.astype(jnp.bfloat16)


def per_device(blocks, occ_energy, pair_list, pno_sizes, fock_virt):
    orb_count = lax.axis_size("orb")
    local_orbs, fit_rows, virt = blocks.shape
    pair_count = pair_list.shape[0]
    total_orbs = local_orbs * orb_count
    slot_total = orb_count * CAP
    endpoints = pair_list.reshape(-1)
    source = endpoints // local_orbs
    within = endpoints % local_orbs
    named = endpoints[:, None] == jnp.arange(total_orbs, dtype=jnp.int32)[None, :]
    wanted_table = jnp.any(named, axis=0).reshape(orb_count, local_orbs).astype(jnp.int32)
    position = jnp.cumsum(wanted_table, axis=1) - 1
    columns = jnp.arange(CAP, dtype=jnp.int32)
    matches = wanted_table[:, :, None] * (position[:, :, None] == columns[None, None, :]).astype(
        jnp.int32
    )
    wanted = jnp.sum(matches * jnp.arange(local_orbs, dtype=jnp.int32)[None, :, None], axis=1)
    slot_index = source * CAP + position[source, within]
    requested = lax.all_to_all(wanted, "orb", split_axis=0, concat_axis=0, tiled=True)
    flat_requested = requested.reshape(-1)
    picked = jnp.take(blocks, flat_requested, axis=0).reshape(orb_count, CAP, fit_rows, virt)
    picked_energy = jnp.take(occ_energy, flat_requested).reshape(orb_count, CAP)
    arrived, arrived_energy = (
        lax.all_to_all(picked, "orb", split_axis=0, concat_axis=0, tiled=True),
        lax.all_to_all(picked_energy, "orb", split_axis=0, concat_axis=0, tiled=True),
    )
    arrived = arrived.reshape(slot_total, fit_rows, virt)
    end_blocks = jnp.take(arrived, slot_index, axis=0)
    end_energy = jnp.take(arrived_energy.reshape(-1), slot_index).astype(jnp.float32)
    shaped_blocks = end_blocks.reshape(pair_count, 2, fit_rows, virt)
    left_blocks = shaped_blocks[:, 0]
    right_blocks = shaped_blocks[:, 1]
    energies = end_energy.reshape(pair_count, 2)
    occ_sums = energies[:, 0] + energies[:, 1]
    pno_rows = (jnp.arange(virt, dtype=jnp.int32)[None, :] < pno_sizes[:, None]).astype(jnp.float32)
    pno_mask = pno_rows[:, :, None] * pno_rows[:, None, :]
    partial_ints = jnp.einsum(
        "pfa,pfb->pab", left_blocks, right_blocks, preferred_element_type=jnp.float32
    )
    exchange_ints = (
        lax.psum(partial_ints.astype(jnp.bfloat16), "fit").astype(jnp.float32) * pno_mask
    )
    amplitudes = iterate_pairs(exchange_ints, fock_virt, occ_sums, pno_mask)
    amp_float = amplitudes.astype(jnp.float32)
    weighted = (2.0 * amp_float - jnp.swapaxes(amp_float, 1, 2)).astype(jnp.bfloat16)
    left_grad = jnp.einsum(
        "pfb,pab->pfa", right_blocks, weighted, preferred_element_type=jnp.float32
    )
    right_grad = jnp.einsum(
        "pfa,pab->pfb", left_blocks, weighted, preferred_element_type=jnp.float32
    )
    contributions = jnp.stack([left_grad, right_grad], axis=1).reshape(
        2 * pair_count, fit_rows, virt
    )
    slot_pick = (slot_index[:, None] == jnp.arange(slot_total, dtype=jnp.int32)[None, :]).astype(
        jnp.float32
    )
    slot_sums = jnp.einsum("es,efv->sfv", slot_pick, contributions, precision=lax.Precision.HIGHEST)
    slot_sums = slot_sums.astype(jnp.bfloat16).reshape(orb_count, CAP, fit_rows, virt)
    returned = lax.all_to_all(slot_sums, "orb", split_axis=0, concat_axis=0, tiled=True).reshape(
        slot_total, fit_rows, virt
    )
    owner_pick = (
        jnp.arange(local_orbs, dtype=jnp.int32)[:, None] == flat_requested[None, :]
    ).astype(jnp.bfloat16)
    local_grads = jnp.einsum(
        "kn,nfv->kfv", owner_pick, returned, preferred_element_type=jnp.float32
    )
    grads = lax.psum(local_grads.astype(jnp.bfloat16), "rep").astype(jnp.float32)
    return (amplitudes, grads)


def solution(mesh):
    placed = (
        P(("groups", "orb"), "fit", None),
        P(("groups", "orb")),
        P(("groups", "orb", "rep"), None),
        P(("groups", "orb", "rep")),
        P(("groups", "orb", "rep"), None, None),
    )
    return jax.shard_map(
        per_device,
        mesh=mesh,
        in_specs=placed,
        out_specs=(P(("groups", "orb", "rep"), None, None), P(("groups", "orb"), "fit", None)),
        check_vma=False,
    )
```

profile of v0, /device:TPU:9, one launch (start us, length us, event | category | flops | bytes accessed | tf_op | source)
XLA Modules:
  0.0 399.6 jit_solution(4939889804425606416)
XLA Ops:
  7.2 0.0 copy-start
  7.2 0.8 copy.89
  7.9 0.1 reshape.320
  8.0 0.1 fusion.42
  8.1 0.1 reshape.330
  8.2 0.2 reduce_window_sum.11
  8.4 0.1 multiply_reduce_fusion
  8.5 0.1 copy.96
  8.6 7.8 %all_to_all.25 = s32[4,1,2]{2,1,0:T(1,128)S(1)} all-to-all(s32[4,1,2]{2,1,0:T(1,128)S(1)} %copy.96), channel_id=1, replica_groups=mesh['groups'=2,'orb'=4,'fit'=2,'rep'=2] {'orb'}, dimensions={0} | all-to-all | bytes 64 | tf_op jit(solution)/shard_map/all_to_all | solution.py:42
  16.4 0.5 broadcast.459
  16.9 0.7 reduce.8
  17.6 0.1 reshape.323
  17.7 0.6 gather_fusion.3
  18.4 0.1 gather.43
  18.5 0.6 copy.106
  19.0 4.4 %all-to-all-start.2 = ((bf16[4,1,2]{2,1,0:T(2,128)(2,1)}), bf16[4,1,2]{2,1,0:T(2,128)(2,1)S(1)}, u32[]{:S(2)}, u32[]{:S(2)}) async-start(bf16[4,1,2]{2,1,0:T(2,128)(2,1)} %copy.106), calls=%async_computation.2 | async-start | bytes 4096 | tf_op jit(solution)/shard_map/all_to_all | solution.py:48
  23.4 5.0 %gather_fusion.1 = bf16[8,1024,256]{2,1,0:T(8,128)(2,1)} fusion(bf16[8,1024,256]{2,1,0:T(8,128)(2,1)} %param.5, s32[1024]{0:T(1024)S(1)} %pad_clamp_fusion.1), kind=kCustom, calls=%fused_computation.1 | custom fusion | bytes 8388640 | tf_op jit(solution)/shard_map/jit(_take)/gather | solution.py:44
  28.4 0.1 copy.97
  28.5 0.1 copy.98
  28.6 4.7 %broadcast_select_fusion = bf16[4,2,1024,256]{3,2,1,0:T(8,128)(2,1)} fusion(bf16[4,2,1024,256]{3,2,1,0:T(8,128)(2,1)} %bitcast.89, pred[4,2]{1,0:T(4,128)(4,1)S(1)} %copy.98), kind=kLoop, calls=%fused_computation.12 | loop fusion | flops 2097152 | bytes 8388616 | tf_op jit(solution)/shard_map/jit(_take)/select_n | solution.py:44
  33.3 0.0 all-to-all-done.2
  33.3 5.0 %all-to-all-start.1 = ((bf16[4,2,1024,256]{3,2,1,0:T(8,128)(2,1)}), bf16[4,2,1024,256]{3,2,1,0:T(8,128)(2,1)}, u32[]{:S(2)}, u32[]{:S(2)}) async-start(bf16[4,2,1024,256]{3,2,1,0:T(8,128)(2,1)} %broadcast_select_fusion), calls=%async_computation.1 | async-start | bytes 8388608 | tf_op jit(solution)/shard_map/all_to_all | solution.py:47
  38.3 0.0 all-reduce.3.cloned.1.call-start
  38.4 0.1 reshape.321
  38.5 0.7 gather_fusion
  39.2 0.1 gather.36
  39.3 0.1 fusion.43
  39.4 0.1 reshape.325
  39.5 0.7 gather_fusion.4
  40.2 0.1 gather.45
  40.3 0.1 copy.95
  40.4 85.8 %all-to-all-done.1 = bf16[4,2,1024,256]{3,2,1,0:T(8,128)(2,1)} async-done(((bf16[4,2,1024,256]{3,2,1,0:T(8,128)(2,1)}), bf16[4,2,1024,256]{3,2,1,0:T(8,128)(2,1)}, u32[]{:S(2)}, u32[]{:S(2)}) %all-to-all-start.1) | async-done | bytes 4194336 | tf_op jit(solution)/shard_map/all_to_all | solution.py:47
  126.2 7.1 %gather_fusion.2 = bf16[16,1024,256]{2,1,0:T(8,128)(2,1)} fusion(bf16[8,1024,256]{2,1,0:T(8,128)(2,1)} %bitcast.5, s32[1024]{0:T(1024)S(1)} %pad_clamp_fusion), kind=kCustom, calls=%fused_computation.2 | custom fusion | bytes 16777280 | tf_op jit(solution)/shard_map/jit(_take)/gather | solution.py:51
  133.2 7.4 %copy_select_fusion = bf16[8,2,1024,256]{3,2,0,1:T(8,128)(2,1)} fusion(bf16[8,2,1024,256]{3,2,1,0:T(8,128)(2,1)} %bitcast.88, pred[8,2]{0,1:T(4,128)(4,1)S(1)} %copy.95), kind=kLoop, calls=%fused_computation.9 | loop fusion | flops 4194304 | bytes 16777232 | tf_op jit(solution)/shard_map/jit(_take)/select_n | solution.py:51
  140.7 6.0 %fusion.23 = bf16[8,256,256]{2,1,0:T(8,128)(2,1)} fusion(bf16[8,2,1024,256]{3,2,0,1:T(8,128)(2,1)} %copy_select_fusion), kind=kOutput, calls=%fused_computation.38 | convolution fusion | flops 1074266112 | bytes 9437184 | tf_op jit(solution)/shard_map/pfa,pfb->pab/dot_general | solution.py:60
  146.7 0.0 all-reduce.3.cloned.1.call-update
  146.7 16.4 %copy.107 = f32[8,256,256]{0,2,1:T(8,128)} copy(f32[8,256,256]{2,1,0:T(8,128)S(1)} %copy-done.2) | data formatting | bytes 4194304 | tf_op args[4]
  163.1 2.3 gather_fusion.5
  165.4 0.1 copy.108
  165.5 3.2 fusion.38
  168.6 3.2 fusion.40
  171.8 0.2 add_reduce_fusion
  172.0 19.4 %all-reduce.3.cloned.1.call-done = bf16[8,256,256]{2,1,0:T(8,128)(2,1)} async-done(((bf16[8,256,256]{2,1,0:T(8,128)(2,1)}), bf16[8,256,256]{2,1,0:T(8,128)(2,1)}) %all-reduce.3.cloned.1.call-update) | async-done | bytes 1048592 | tf_op jit(solution)/shard_map/psum | solution.py:64
  191.5 5.3 %fusion.21 = f32[8,256,256]{1,2,0:T(8,128)S(1)} fusion(f32[8,256,256]{2,1,0:T(8,128)S(1)} %copy-done.2, f32[8,256,256]{2,1,0:T(8,128)} %fusion.38, f32[8,256,256]{1,2,0:T(8,128)} %fusion.40, bf16[8,256,256]{2,1,0:T(8,128)(2,1)} %all-reduce.3.cloned.1.call-done, f32[8]{0:T(128)S(1)} %add_reduce_fusion, f32[8,256]{1,0:T(8,128)S(1)} %copy.108, ...), kind=kOutput, calls=%fused_computation.37 | convolution fusion | flops 1616379904 | bytes 9453632 | tf_op jit(solution)/shard_map/pab,pbc->pac/dot_general | solution.py:15
  196.8 4.8 %fusion.19 = bf16[8,256,256]{2,1,0:T(8,128)(2,1)S(1)} fusion(f32[8,256,256]{1,2,0:T(8,128)S(1)} %fusion.21, bf16[8,256,256]{2,1,0:T(8,128)(2,1)S(1)} %copy-done.7, f32[8,256,256]{2,1,0:T(8,128)S(1)} %copy-done.2, f32[8,256,256]{2,1,0:T(8,128)S(1)} %copy-done.4, f32[8,256,256]{1,2,0:T(8,128)S(1)} %copy-done.5, f32[8]{0:T(128)S(1)} %add_reduce_fusion, ...), kind=kOutput, calls=%fused_computation.36 | convolution fusion | flops 1626341376 | bytes 10502208 | tf_op jit(solution)/shard_map/pab,pbc->pac/dot_general | solution.py:16
  201.6 0.0 copy-start.3
  201.6 0.7 copy.112
  202.3 3.5 fusion.5
  205.8 3.5 fusion.6
  209.3 1.5 pad_maximum_fusion
  210.8 1.9 copy.115
  212.8 13.8 %fusion.7 = bf16[8,1024,256]{2,0,1:T(8,128)(2,1)} fusion(f32[16,1024,256]{2,1,0:T(8,128)S(1)} %bitcast.87, s32[16]{0:T(128)S(1)} %multiply_add_fusion), kind=kOutput, calls=%fused_computation.21 | convolution fusion | flops 404750464 | bytes 20971584 | tf_op jit(solution)/shard_map/es,efv->sfv/dot_general | solution.py:81
  226.5 7.2 %reshape.328 = bf16[4,2,1024,256]{3,1,0,2:T(2,128)(2,1)} reshape(bf16[8,1024,256]{2,0,1:T(8,128)(2,1)} %fusion.7) | data formatting | bytes 8388608 | tf_op jit(solution)/shard_map/reshape | solution.py:82
  233.8 7.1 %copy.117 = bf16[4,2,1024,256]{3,1,2,0:T(2,128)(2,1)} copy(bf16[4,2,1024,256]{3,1,0,2:T(2,128)(2,1)} %reshape.328) | data formatting | bytes 8388608 | tf_op jit(solution)/shard_map/reshape | solution.py:82
  240.8 5.1 %all-to-all-start.3 = ((bf16[4,2,1024,256]{3,1,2,0:T(2,128)(2,1)}), bf16[4,2,1024,256]{3,1,2,0:T(2,128)(2,1)}, u32[]{:S(2)}, u32[]{:S(2)}) async-start(bf16[4,2,1024,256]{3,1,2,0:T(2,128)(2,1)} %copy.117), calls=%async_computation.3 | async-start | bytes 8388608 | tf_op jit(solution)/shard_map/all_to_all | solution.py:83
  245.9 0.1 all-reduce.5.cloned.1.call-start
  246.0 0.1 reshape.326
  246.1 89.3 %all-to-all-done.3 = bf16[4,2,1024,256]{3,1,2,0:T(2,128)(2,1)} async-done(((bf16[4,2,1024,256]{3,1,2,0:T(2,128)(2,1)}), bf16[4,2,1024,256]{3,1,2,0:T(2,128)(2,1)}, u32[]{:S(2)}, u32[]{:S(2)}) %all-to-all-start.3) | async-done | bytes 4194336 | tf_op jit(solution)/shard_map/all_to_all | solution.py:83
  335.4 7.1 %copy.118 = bf16[4,2,1024,256]{3,1,0,2:T(2,128)(2,1)} copy(bf16[4,2,1024,256]{3,1,2,0:T(2,128)(2,1)} %all-to-all-done.3) | data formatting | bytes 8388608 | tf_op jit(solution)/shard_map/all_to_all | solution.py:83
  342.5 7.2 %reshape.329 = bf16[8,1024,256]{2,0,1:T(8,128)(2,1)} reshape(bf16[4,2,1024,256]{3,1,0,2:T(2,128)(2,1)} %copy.118) | data formatting | bytes 8388608 | tf_op jit(solution)/shard_map/reshape | solution.py:83
  349.7 5.4 %convolution_convert_fusion = bf16[8,1024,256]{2,0,1:T(8,128)(2,1)} fusion(bf16[8,1024,256]{2,0,1:T(8,128)(2,1)} %reshape.329, s32[8]{0:T(128)S(1)} %reshape.326), kind=kOutput, calls=%fused_computation.22 | convolution fusion | flops 35651648 | bytes 8388640 | tf_op jit(solution)/shard_map/kn,nfv->kfv/dot_general | solution.py:89
  355.1 0.0 all-reduce.5.cloned.1.call-update
  355.1 31.2 %all-reduce.5.cloned.1.call-done = bf16[8,1024,256]{2,0,1:T(8,128)(2,1)} async-done(((bf16[8,1024,256]{2,0,1:T(8,128)(2,1)}), bf16[8,1024,256]{2,0,1:T(8,128)(2,1)}) %all-reduce.5.cloned.1.call-update) | async-done | bytes 4194320 | tf_op jit(solution)/shard_map/psum | solution.py:92
  386.3 6.5 %copy.119 = f32[8,1024,256]{2,1,0:T(8,128)} copy(bf16[8,1024,256]{2,0,1:T(8,128)(2,1)} %all-reduce.5.cloned.1.call-done) | data formatting | bytes 12582912
  (28 shorter events, 0.2 us)
Async XLA Ops:
  7.2 10.5 %copy-start = (bf16[8]{0:T(256)(128)(2,1)S(1)}, bf16[8]{0:T(256)(128)(2,1)}, u32[]{:S(2)}) copy-start(bf16[8]{0:T(256)(128)(2,1)} %param.6) | copy-start | bytes 52
  19.0 14.3 %all-to-all-start.2 = ((bf16[4,1,2]{2,1,0:T(2,128)(2,1)}), bf16[4,1,2]{2,1,0:T(2,128)(2,1)S(1)}, u32[]{:S(2)}, u32[]{:S(2)}) async-start(bf16[4,1,2]{2,1,0:T(2,128)(2,1)} %copy.106), calls=%async_computation.2 | async-start | bytes 4096 | tf_op jit(solution)/shard_map/all_to_all | solution.py:48
  33.3 6.0 %copy-start.6 = (s32[8]{0:T(128)S(1)}, s32[8]{0:T(128)}, u32[]{:S(2)}) copy-start(s32[8]{0:T(128)} %param.8) | copy-start | bytes 100
  33.3 92.9 %all-to-all-start.1 = ((bf16[4,2,1024,256]{3,2,1,0:T(8,128)(2,1)}), bf16[4,2,1024,256]{3,2,1,0:T(8,128)(2,1)}, u32[]{:S(2)}, u32[]{:S(2)}) async-start(bf16[4,2,1024,256]{3,2,1,0:T(8,128)(2,1)} %broadcast_select_fusion), calls=%async_computation.1 | async-start | bytes 8388608 | tf_op jit(solution)/shard_map/all_to_all | solution.py:47
  38.3 153.1 %all-reduce.3.cloned.1.call-start = ((), (), s32[]{:S(2)}) async-start(), calls=%async_computation.4 | async-start | bytes 2097152 | tf_op jit(solution)/shard_map/psum | solution.py:64
  140.7 6.0 %copy-start.2 = (f32[8,256,256]{2,1,0:T(8,128)S(1)}, f32[8,256,256]{2,1,0:T(8,128)}, u32[]{:S(2)}) copy-start(f32[8,256,256]{2,1,0:T(8,128)} %param.9) | copy-start | bytes 6291460
  191.5 5.3 %copy-start.4 = (f32[8,256,256]{2,1,0:T(8,128)S(1)}, f32[8,256,256]{2,1,0:T(8,128)}, u32[]{:S(2)}) copy-start(f32[8,256,256]{2,1,0:T(8,128)} %fusion.38) | copy-start | bytes 6291460
  191.5 5.3 %copy-start.5 = (f32[8,256,256]{1,2,0:T(8,128)S(1)}, f32[8,256,256]{1,2,0:T(8,128)}, u32[]{:S(2)}) copy-start(f32[8,256,256]{1,2,0:T(8,128)} %fusion.40) | copy-start | bytes 6291460
  191.5 5.3 %copy-start.7 = (bf16[8,256,256]{2,1,0:T(8,128)(2,1)S(1)}, bf16[8,256,256]{2,1,0:T(8,128)(2,1)}, u32[]{:S(2)}) copy-start(bf16[8,256,256]{2,1,0:T(8,128)(2,1)} %all-reduce.3.cloned.1.call-done) | copy-start | bytes 3145732
  201.6 4.2 %copy-start.3 = (bf16[8,256,256]{2,1,0:T(8,128)(2,1)}, bf16[8,256,256]{2,1,0:T(8,128)(2,1)S(1)}, u32[]{:S(2)}) copy-start(bf16[8,256,256]{2,1,0:T(8,128)(2,1)S(1)} %fusion.19) | copy-start | bytes 3145732
  240.8 94.6 %all-to-all-start.3 = ((bf16[4,2,1024,256]{3,1,2,0:T(2,128)(2,1)}), bf16[4,2,1024,256]{3,1,2,0:T(2,128)(2,1)}, u32[]{:S(2)}, u32[]{:S(2)}) async-start(bf16[4,2,1024,256]{3,1,2,0:T(2,128)(2,1)} %copy.117), calls=%async_computation.3 | async-start | bytes 8388608 | tf_op jit(solution)/shard_map/all_to_all | solution.py:83
  245.9 140.5 %all-reduce.5.cloned.1.call-start = ((), (), s32[]{:S(2)}) async-start(), calls=%async_computation.5 | async-start | bytes 8388608 | tf_op jit(solution)/shard_map/psum | solution.py:92
  386.3 6.5 %copy-start.1 = (bf16[8]{0:T(256)(128)(2,1)S(1)}, bf16[8]{0:T(256)(128)(2,1)}, u32[]{:S(2)}) copy-start(bf16[8]{0:T(256)(128)(2,1)} %param.6) | copy-start | bytes 52
Sparse Core Ops, SparseCore 0:
  146.8 44.5 all-reduce.2
  355.3 31.0 all-reduce.4
where the time goes:
time: 402 us; the launch traced here: 400 us
  waiting for transfers between devices  226 us (56%)
  local copies, waits for them, and re-layouts  73.6 us (18%)
  matrix products  48.6 us (12%)
  other arithmetic  15.1 us (4%)
  starting transfers between devices  14.6 us (4%)
  between operations  14.2 us (4%)
  blocking collectives  7.78 us (2%)
    all_to_all x1, waiting for transfers between devices, per_device(): lax.all_to_all(slot_sums, 'orb', split_axis=0, concat_axis=0, tiled=True)  89.3 us
    all_to_all x1, waiting for transfers between devices, per_device(): lax.all_to_all(picked, 'orb', split_axis=0, concat_axis=0, tiled=True)  85.8 us
    psum x1, waiting for transfers between devices, per_device(): lax.psum(local_grads.astype(jnp.bfloat16), 'rep').astype(jnp.float32)  31.2 us
    unnamed x19, local copies, waits for them, and re-layouts  23.6 us
    psum x1, waiting for transfers between devices, per_device(): lax.psum(partial_ints.astype(jnp.bfloat16), 'fit').astype(jnp.float32)  19.4 us
    reshape x2, local copies, waits for them, and re-layouts, per_device(): slot_sums.astype(jnp.bfloat16).reshape(orb_count, CAP, fit_rows, virt)  14.3 us
    dot_general x1, matrix products, per_device(): jnp.einsum('es,efv->sfv', slot_pick, contributions, precision=lax.Precisi...  13.8 us
    dot_general x2, matrix products, iterate_pairs(): jnp.einsum('pab,pbc->pac', fock_here, current, precision=lax.Precision.HI...  8.47 us
  transfers between devices with their start and end apart: 5, of which 4 were waited for; matrix products, arithmetic and copies ran while one was open for 9% of the time, Pallas kernels for 0%

commit v1 on v0

v1 whole, which is shorter than its diff:
```python
import functools

import jax
import jax.numpy as jnp
from jax import lax
from jax.experimental import pallas as pl
from jax.experimental.pallas import tpu as pltpu
from jax.sharding import PartitionSpec as P

CAP = 2
FORWARD_CHUNKS = 2
BACK_CHUNKS = 4
VMEM_LIMIT = 40 * 1024 * 1024

F32 = jnp.float32
BF16 = jnp.bfloat16

ANY = pl.BlockSpec(memory_space=pl.ANY)
SMEM = pl.BlockSpec(memory_space=pltpu.SMEM)
VMEM = pl.BlockSpec(memory_space=pltpu.VMEM)


def params():
    return pltpu.CompilerParams(vmem_limit_bytes=VMEM_LIMIT)


def cost(flops, nbytes):
    return pl.CostEstimate(flops=int(flops), bytes_accessed=int(nbytes), transcendentals=0)


def shifted(n, d):
    return [(s, (s + d) % n) for s in range(n)]


def pick_kernel(start, rows, index_ref, blocks_ref, *rest):
    outs, sems = rest[:-1], rest[-1]
    copies = []
    for d, out in enumerate(outs):
        for k in range(CAP):
            copies.append(
                pltpu.make_async_copy(
                    blocks_ref.at[index_ref[d, k], pl.ds(start, rows)],
                    out.at[k],
                    sems.at[d * CAP + k],
                )
            )
    for c in copies:
        c.start()
    for c in copies:
        c.wait()


def pick_blocks(index, blocks, start, rows):
    count = index.shape[0]
    virt = blocks.shape[2]
    shape = jax.ShapeDtypeStruct((CAP, rows, virt), BF16)
    return pl.pallas_call(
        functools.partial(pick_kernel, start, rows),
        out_shape=[shape] * count,
        in_specs=[SMEM, ANY],
        out_specs=[ANY] * count,
        scratch_shapes=[pltpu.SemaphoreType.DMA((count * CAP,))],
        compiler_params=params(),
        cost_estimate=cost(0, 2 * count * CAP * rows * virt * 2),
        name="pick_blocks",
    )(index, blocks)


def load_slots(own_ref, blocks_ref, arrived, held, sems, start, offset, rows):
    copies = []
    for k in range(CAP):
        copies.append(
            pltpu.make_async_copy(
                blocks_ref.at[own_ref[k], pl.ds(start, rows)], held.at[k], sems.at[k]
            )
        )
    for d, ref in enumerate(arrived):
        for k in range(CAP):
            s = (d + 1) * CAP + k
            copies.append(
                pltpu.make_async_copy(ref.at[k, pl.ds(offset, rows)], held.at[s], sems.at[s])
            )
    for c in copies:
        c.start()
    return copies


def exchange_kernel(start, rows, first, n, slot_ref, own_ref, blocks_ref, *rest):
    arrived = rest[: n - 1]
    rest = rest[n - 1 :]
    if not first:
        before_ref, rest = rest[0], rest[1:]
    out_ref, held, sems = rest
    for c in load_slots(own_ref, blocks_ref, arrived, held, sems, start, 0, rows):
        c.wait()

    def step(p, carry):
        product = lax.dot_general(
            held[slot_ref[2 * p]],
            held[slot_ref[2 * p + 1]],
            (((0,), (0,)), ((), ())),
            preferred_element_type=F32,
        )
        if not first:
            product = product + before_ref[p]
        out_ref[p] = product.astype(out_ref.dtype)
        return carry

    lax.fori_loop(0, out_ref.shape[0], step, 0)


def exchange_chunk(slots, own, blocks, arrived, before, start, rows, last):
    n = len(arrived) + 1
    pairs = slots.shape[0] // 2
    virt = blocks.shape[2]
    first = before is None
    return pl.pallas_call(
        functools.partial(exchange_kernel, start, rows, first, n),
        out_shape=jax.ShapeDtypeStruct((pairs, virt, virt), BF16 if last else F32),
        in_specs=[SMEM, SMEM, ANY] + [ANY] * (n - 1) + ([] if first else [VMEM]),
        out_specs=VMEM,
        scratch_shapes=[
            pltpu.VMEM((n * CAP, rows, virt), BF16),
            pltpu.SemaphoreType.DMA((n * CAP,)),
        ],
        compiler_params=params(),
        cost_estimate=cost(
            2 * pairs * rows * virt * virt, n * CAP * rows * virt * 2 + pairs * virt * virt * 6
        ),
        name="exchange_chunk",
    )(slots, own, blocks, *arrived, *([] if first else [before]))


def amplitude_kernel(parts, energy_ref, ends_ref, size_ref, fock_ref, *rest):
    ints = rest[:parts]
    amp_ref, weight_ref = rest[parts:]
    p = pl.program_id(0)
    virt = fock_ref.shape[-1]
    occ = energy_ref[ends_ref[2 * p]] + energy_ref[ends_ref[2 * p + 1]]
    size = size_ref[p]
    fock = fock_ref[0]
    row = lax.broadcasted_iota(jnp.int32, (virt, virt), 0)
    col = lax.broadcasted_iota(jnp.int32, (virt, virt), 1)
    on_diagonal = row == col
    diagonal = jnp.where(on_diagonal, fock, 0.0)
    denominator = (
        jnp.sum(diagonal, axis=1, keepdims=True) + jnp.sum(diagonal, axis=0, keepdims=True) - occ
    )
    inverse = jnp.where((row < size) & (col < size), 1.0 / denominator, 0.0)
    total = ints[0][0].astype(F32)
    for ref in ints[1:]:
        total = total + ref[0].astype(F32)
    current = -total * inverse
    off = jnp.where(on_diagonal, 0.0, fock)
    off_high = off.astype(BF16)
    cur_high = current.astype(BF16)
    change = jnp.dot(off_high, cur_high, preferred_element_type=F32) + jnp.dot(
        cur_high, off_high, preferred_element_type=F32
    )
    amp = (current - change * inverse).astype(BF16)
    amp_ref[0] = amp
    wide = amp.astype(F32)
    flipped = wide.T
    weight_ref[0] = (2.0 * flipped - wide).astype(BF16)
    weight_ref[1] = (2.0 * wide - flipped).astype(BF16)


def amplitude_step(energies, ends, sizes, fock, ints):
    pairs, virt, _ = fock.shape
    block = pl.BlockSpec((1, virt, virt), lambda p: (p, 0, 0))
    return pl.pallas_call(
        functools.partial(amplitude_kernel, len(ints)),
        grid=(pairs,),
        out_shape=[
            jax.ShapeDtypeStruct((pairs, virt, virt), BF16),
            jax.ShapeDtypeStruct((2 * pairs, virt, virt), BF16),
        ],
        in_specs=[SMEM, SMEM, SMEM, block] + [block] * len(ints),
        out_specs=[block, pl.BlockSpec((2, virt, virt), lambda p: (p, 0, 0))],
        compiler_params=params(),
        cost_estimate=cost(4 * pairs * virt**3, pairs * virt * virt * 14),
        name="amplitude_step",
    )(energies, ends, sizes, fock, *ints)


def gradient_kernel(start, offset, rows, n, slot_ref, own_ref, weight_ref, blocks_ref, *rest):
    arrived = rest[: n - 1]
    outs = rest[n - 1 : 2 * n - 1]
    held, sums, sems = rest[2 * n - 1 :]
    copies = load_slots(own_ref, blocks_ref, arrived, held, sems, start, offset, rows)
    sums[...] = jnp.zeros_like(sums)
    for c in copies:
        c.wait()

    def step(p, carry):
        left = slot_ref[2 * p]
        right = slot_ref[2 * p + 1]
        sums[left] += jnp.dot(held[right], weight_ref[2 * p], preferred_element_type=F32)
        sums[right] += jnp.dot(held[left], weight_ref[2 * p + 1], preferred_element_type=F32)
        return carry

    lax.fori_loop(0, weight_ref.shape[0] // 2, step, 0)
    for d, out in enumerate(outs):
        for k in range(CAP):
            out[k] = sums[d * CAP + k].astype(BF16)


def gradient_chunk(slots, own, weights, blocks, arrived, start, offset, rows):
    n = len(arrived) + 1
    ends = slots.shape[0]
    virt = blocks.shape[2]
    return pl.pallas_call(
        functools.partial(gradient_kernel, start, offset, rows, n),
        out_shape=[jax.ShapeDtypeStruct((CAP, rows, virt), BF16)] * n,
        in_specs=[SMEM, SMEM, VMEM, ANY] + [ANY] * (n - 1),
        out_specs=[VMEM] * n,
        scratch_shapes=[
            pltpu.VMEM((n * CAP, rows, virt), BF16),
            pltpu.VMEM((n * CAP, rows, virt), F32),
            pltpu.SemaphoreType.DMA((n * CAP,)),
        ],
        compiler_params=params(),
        cost_estimate=cost(
            2 * ends * rows * virt * virt, 4 * n * CAP * rows * virt + ends * virt * virt * 2
        ),
        name="gradient_chunk",
    )(slots, own, weights, blocks, *arrived)


def collect_kernel(count, index_ref, *rest):
    terms = rest[:count]
    out_ref = rest[-1]
    out_ref[...] = jnp.zeros_like(out_ref)
    for d, ref in enumerate(terms):
        for k in range(CAP):
            g = index_ref[d, k]
            out_ref[g] += ref[k].astype(F32)


def collect_chunk(index, terms, before, local_orbs, fit_rows, start, rows):
    virt = terms[0].shape[2]
    count = len(terms)
    more = [] if before is None else [before]
    at = start // rows
    return pl.pallas_call(
        functools.partial(collect_kernel, count),
        grid=(1,),
        out_shape=jax.ShapeDtypeStruct((local_orbs, fit_rows, virt), F32),
        in_specs=[SMEM]
        + [pl.BlockSpec((CAP, rows, virt), lambda i: (0, 0, 0))] * count
        + [ANY] * len(more),
        out_specs=pl.BlockSpec((local_orbs, rows, virt), lambda i: (0, at, 0)),
        input_output_aliases={} if before is None else {1 + count: 0},
        compiler_params=params(),
        cost_estimate=cost(0, (count * CAP * 2 + local_orbs * 4) * rows * virt),
        name="collect_chunk",
    )(index, *terms, *more)


def per_device(blocks, occ_energy, pair_list, pno_sizes, fock_virt):
    n = lax.axis_size("orb")
    n_fit = lax.axis_size("fit")
    n_rep = lax.axis_size("rep")
    local_orbs, fit_rows, virt = blocks.shape
    total_orbs = local_orbs * n
    me = lax.axis_index("orb")

    endpoints = pair_list.reshape(-1)
    relative = (endpoints - me * local_orbs) % total_orbs
    named = jnp.any(
        relative[:, None] == jnp.arange(total_orbs, dtype=jnp.int32)[None, :], axis=0
    ).reshape(n, local_orbs)
    table = named.astype(jnp.int32)
    position = jnp.cumsum(table, axis=1) - 1
    columns = jnp.arange(CAP, dtype=jnp.int32)
    locals_ = jnp.arange(local_orbs, dtype=jnp.int32)
    matches = table[:, :, None] * (position[:, :, None] == columns[None, None, :])
    wanted = jnp.sum(matches * locals_[None, :, None], axis=1)
    end_hot = relative[:, None] == jnp.arange(total_orbs, dtype=jnp.int32)[None, :]
    slots = (relative // local_orbs) * CAP + jnp.sum(
        jnp.where(end_hot, position.reshape(1, -1), 0), axis=1
    )
    slots = slots.astype(jnp.int32)

    energies_here = occ_energy.astype(F32)
    got = {}
    for d in range(1, n):
        note = jnp.concatenate([wanted[d].astype(F32), energies_here])
        got[d] = lax.ppermute(note, "orb", shifted(n, d))
    asked = jnp.stack(
        [wanted[0]] + [got[d][:CAP].astype(jnp.int32) for d in range(1, n)]
    )
    energies = jnp.concatenate([energies_here] + [got[n - d][CAP:] for d in range(1, n)])

    forward_chunks = FORWARD_CHUNKS
    rows = fit_rows // forward_chunks
    own = wanted[0]
    arrived = []
    for c in range(forward_chunks):
        picked = pick_blocks(asked[1:], blocks, c * rows, rows)
        arrived.append(
            [lax.ppermute(picked[d - 1], "orb", shifted(n, n - d)) for d in range(1, n)]
        )
    ints = None
    for c in range(forward_chunks):
        ints = exchange_chunk(
            slots, own, blocks, arrived[c], ints, c * rows, rows, c == forward_chunks - 1
        )
    if n_fit == 2:
        parts = [ints, lax.ppermute(ints, "fit", shifted(2, 1))]
    elif n_fit > 1:
        every = lax.all_gather(ints, "fit")
        parts = [every[i] for i in range(n_fit)]
    else:
        parts = [ints]
    amplitudes, weights = amplitude_step(energies, relative, pno_sizes, fock_virt, parts)

    swap = shifted(n_rep, 1)
    both = [asked, lax.ppermute(asked.astype(F32), "rep", swap).astype(jnp.int32)]
    index = jnp.concatenate(both)
    back_rows = fit_rows // BACK_CHUNKS
    returned = []
    for c in range(BACK_CHUNKS):
        start = c * back_rows
        sums = gradient_chunk(
            slots, own, weights, blocks, arrived[start // rows], start, start % rows, back_rows
        )
        returned.append(
            [sums[0]] + [lax.ppermute(sums[d], "orb", shifted(n, d)) for d in range(1, n)]
        )
    grads = None
    for c in range(BACK_CHUNKS):
        other = [lax.ppermute(x, "rep", swap) for x in returned[c]]
        grads = collect_chunk(
            index, returned[c] + other, grads, local_orbs, fit_rows, c * back_rows, back_rows
        )
    return amplitudes, grads


def solution(mesh):
    placed = (
        P(("groups", "orb"), "fit", None),
        P(("groups", "orb")),
        P(("groups", "orb", "rep"), None),
        P(("groups", "orb", "rep")),
        P(("groups", "orb", "rep"), None, None),
    )
    return jax.shard_map(
        per_device,
        mesh=mesh,
        in_specs=placed,
        out_specs=(P(("groups", "orb", "rep"), None, None), P(("groups", "orb"), "fit", None)),
        check_vma=False,
    )
```

time: 402 us -> 266 us (0.66)
  waiting for transfers between devices: 226 us -> 161 us
  local copies, waits for them, and re-layouts: 73.6 us -> 19 us
  matrix products: 48.6 us -> 0 us
  Pallas kernels: 0 us -> 42.1 us
  starting transfers between devices: 14.6 us -> 40.3 us
  between operations: 14.2 us -> 0.91 us
  other arithmetic: 15.1 us -> 2.42 us
  blocking collectives: 7.78 us -> 0 us
    all_to_all x3 -> x0, waiting for transfers between devices: 175 us -> none  [the longest x1 89.3 us: per_device(): lax.all_to_all(slot_sums, 'orb', split_axis=0, concat_axis=0, tiled=True)]
    ppermute x0 -> x39, waiting for transfers between devices: none -> 161 us  [the longest x6 78.3 us: per_device(): lax.ppermute(picked[d - 1], 'orb', shifted(n, n - d))]
    psum x2 -> x0, waiting for transfers between devices: 50.6 us -> none  [the longest x1 31.2 us: per_device(): lax.psum(local_grads.astype(jnp.bfloat16), 'rep').astype(jnp.float32)]
    dot_general x9 -> x0, matrix products: 48.6 us -> none  [the longest x1 13.8 us: per_device(): jnp.einsum('es,efv->sfv', slot_pick, contributions, precision=lax.Precisi...]
    pallas_call x0 -> x13, Pallas kernels: none -> 42.1 us  [the longest x4 17 us: gradient_chunk(): pl.pallas_call(functools.partial(gradient_kernel, start, offset, rows, n)...]
    ppermute x0 -> x39, starting transfers between devices: none -> 40.3 us  [the longest x12 17.6 us: per_device(): lax.ppermute(sums[d], 'orb', shifted(n, d))]
    reshape x8 -> x0, local copies, waits for them, and re-layouts: 21.9 us -> none  [the longest x2 14.3 us: per_device(): slot_sums.astype(jnp.bfloat16).reshape(orb_count, CAP, fit_rows, virt)]
    gather x10 -> x0, local copies, waits for them, and re-layouts: 16.7 us -> none  [the longest x1 7.09 us: per_device(): end_blocks = jnp.take(arrived, slot_index, axis=0)]
  transfers between devices with their start and end apart: 5 -> 39, of which waited for: 4 -> 16; matrix products, arithmetic and copies ran while one was open for 9% -> 0% of each run, Pallas kernels for 0% -> 9%
where the time goes in v1:
time: 266 us; the launch traced here: 265 us
  waiting for transfers between devices  161 us (61%)
  Pallas kernels  42.1 us (16%)
  starting transfers between devices  40.3 us (15%)
  local copies, waits for them, and re-layouts  19 us (7%)
    ppermute x6, waiting for transfers between devices, per_device(): lax.ppermute(picked[d - 1], 'orb', shifted(n, n - d))  78.3 us
    ppermute x12, waiting for transfers between devices, per_device(): lax.ppermute(sums[d], 'orb', shifted(n, d))  58.9 us
    ppermute x1, waiting for transfers between devices, per_device(): parts = [ints, lax.ppermute(ints, 'fit', shifted(2, 1))]  22.7 us
    unnamed x63, local copies, waits for them, and re-layouts  18.4 us
    ppermute x12, starting transfers between devices, per_device(): lax.ppermute(sums[d], 'orb', shifted(n, d))  17.6 us
    pallas_call x4, Pallas kernels, gradient_chunk(): pl.pallas_call(functools.partial(gradient_kernel, start, offset, rows, n)...  17 us
    pallas_call x4, Pallas kernels, collect_chunk(): pl.pallas_call(functools.partial(collect_kernel, count), grid=(1,), out_s...  10.8 us
    ppermute x16, starting transfers between devices, per_device(): other = [lax.ppermute(x, 'rep', swap) for x in returned[c]]  7.57 us
  transfers between devices with their start and end apart: 39, of which 16 were waited for; matrix products, arithmetic and copies ran while one was open for 0% of the time, Pallas kernels for 9%

profile of v1, /device:TPU:9, one launch (start us, length us, event | category | flops | bytes accessed | tf_op | source)
XLA Modules:
  0.0 265.4 jit_solution(14848760457838039195)
XLA Ops:
  3.0 2.5 collective-permute-start.1
  5.5 2.2 collective-permute-start.2
  7.7 0.7 collective-permute-done.2
  8.4 2.2 copy-done
  10.6 1.6 pick_blocks.3
  12.2 2.3 collective-permute-start.6
  15.1 0.9 collective-permute-start.8
  16.0 1.8 pick_blocks.2
  18.4 1.8 collective-permute-start.4
  20.2 3.8 %collective-permute-done.6.rest_0_ = bf16[2,512,256]{2,1,0:T(8,128)(2,1)S(1)} collective-permute-done((bf16[2,512,256]{2,1,0:T(8,128)(2,1)S(1)}, bf16[2,512,256]{2,1,0:T(8,128)(2,1)S(1)}, u32[]{:S(2)}, u32[]{:S(2)}) %collective-permute-start.6) | collective-permute-done | bytes 524320 | tf_op jit(solution)/shard_map/ppermute | solution.py:302
  24.0 1.0 collective-permute-start.5
  25.4 25.5 %collective-permute-done.7.rest_1_ = bf16[2,512,256]{2,1,0:T(8,128)(2,1)S(1)} collective-permute-done((bf16[2,512,256]{2,1,0:T(8,128)(2,1)}, bf16[2,512,256]{2,1,0:T(8,128)(2,1)S(1)}, u32[]{:S(2)}, u32[]{:S(2)}) %collective-permute-start.7) | collective-permute-done | bytes 524320 | tf_op jit(solution)/shard_map/ppermute | solution.py:302
  50.9 31.7 %collective-permute-done.8.rest_2_ = bf16[2,512,256]{2,1,0:T(8,128)(2,1)S(1)} collective-permute-done((bf16[2,512,256]{2,1,0:T(8,128)(2,1)}, bf16[2,512,256]{2,1,0:T(8,128)(2,1)S(1)}, u32[]{:S(2)}, u32[]{:S(2)}) %collective-permute-start.8) | collective-permute-done | bytes 524320 | tf_op jit(solution)/shard_map/ppermute | solution.py:302
  82.6 2.2 copy-done.1
  84.8 3.0 %exchange_chunk.2.rest_3_ = f32[8,256,256]{2,1,0:T(8,128)S(1)} custom-call(s32[16]{0:T(128)S(1)} %multiply_add_fusion.slot_ref, s32[2]{0:T(128)S(1)} %bitcast.8, bf16[8,1024,256]{2,1,0:T(8,128)(2,1)S(1)} %copy-done.1, bf16[2,512,256]{2,1,0:T(8,128)(2,1)S(1)} %collective-permute-done.6.rest_0_, bf16[2,512,256]{2,1,0:T(8,128)(2,1)S(1)} %collective-permute-done.7.rest_1_, ...), custom_call_target="tpu_custom_call" | custom-call | flops 536870912 | bytes 5242880 | tf_op jit(solution)/shard_map/exchange_chunk/pallas_call | solution.py:117
  87.8 3.5 %collective-permute-done.3.rest_0_ = bf16[2,512,256]{2,1,0:T(8,128)(2,1)S(1)} collective-permute-done((bf16[2,512,256]{2,1,0:T(8,128)(2,1)}, bf16[2,512,256]{2,1,0:T(8,128)(2,1)S(1)}, u32[]{:S(2)}, u32[]{:S(2)}) %collective-permute-start.3) | collective-permute-done | bytes 524320 | tf_op jit(solution)/shard_map/ppermute | solution.py:302
  91.3 2.6 collective-permute-done.4.rest_1_
  93.8 11.2 %collective-permute-done.5.rest_2_ = bf16[2,512,256]{2,1,0:T(8,128)(2,1)S(1)} collective-permute-done((bf16[2,512,256]{2,1,0:T(8,128)(2,1)}, bf16[2,512,256]{2,1,0:T(8,128)(2,1)S(1)}, u32[]{:S(2)}, u32[]{:S(2)}) %collective-permute-start.5) | collective-permute-done | bytes 524320 | tf_op jit(solution)/shard_map/ppermute | solution.py:302
  105.1 2.9 %exchange_chunk.3.rest_0_ = bf16[8,256,256]{2,1,0:T(8,128)(2,1)S(1)} custom-call(s32[16]{0:T(128)S(1)} %multiply_add_fusion.slot_ref, s32[2]{0:T(128)S(1)} %bitcast.9, bf16[8,1024,256]{2,1,0:T(8,128)(2,1)S(1)} %copy-done.1, bf16[2,512,256]{2,1,0:T(8,128)(2,1)S(1)} %collective-permute-done.3.rest_0_, bf16[2,512,256]{2,1,0:T(8,128)(2,1)S(1)} %collective-permute-done.4.rest_1_, ...), custom_call_target="tpu_custom_call" | custom-call | flops 536870912 | bytes 5242880 | tf_op jit(solution)/shard_map/exchange_chunk/pallas_call | solution.py:117
  108.0 1.3 collective-permute-start.9
  109.6 22.7 %collective-permute-done.9.rest_1_ = bf16[8,256,256]{2,1,0:T(8,128)(2,1)S(1)} collective-permute-done((bf16[8,256,256]{2,1,0:T(8,128)(2,1)S(1)}, bf16[8,256,256]{2,1,0:T(8,128)(2,1)S(1)}, u32[]{:S(2)}, u32[]{:S(2)}) %collective-permute-start.9) | collective-permute-done | bytes 1048608 | tf_op jit(solution)/shard_map/ppermute | solution.py:310
  132.3 5.0 %amplitude_step.1 = (bf16[8,256,256]{2,1,0:T(8,128)(2,1)}, bf16[16,256,256]{2,1,0:T(8,128)(2,1)S(1)}) custom-call(f32[32]{0:T(128)S(1)} %pad_maximum_fusion.3.energy_ref, s32[16]{0:T(128)S(1)} %and_select_fusion.1.ends_ref, s32[8]{0:T(128)S(1)} %copy-done.30, f32[8,256,256]{2,1,0:T(8,128)S(1)} %copy-done.3, bf16[8,256,256]{2,1,0:T(8,128)(2,1)S(1)} %exchange_chunk.3.rest_0_, ...), custom_call_target="tpu_custom_call" | custom-call | flops 536870912 | bytes 7340032 | tf_op jit(solution)/shard_map/amplitude_step/pallas_call | solution.py:171
  137.3 4.2 %gradient_chunk.7 = (bf16[2,256,256]{2,1,0:T(8,128)(2,1)S(1)}, bf16[2,256,256]{2,1,0:T(8,128)(2,1)S(1)}, bf16[2,256,256]{2,1,0:T(8,128)(2,1)S(1)}, bf16[2,256,256]{2,1,0:T(8,128)(2,1)S(1)}) custom-call(s32[16]{0:T(128)S(1)} %multiply_add_fusion.slot_ref, s32[2]{0:T(128)S(1)} %bitcast.10, bf16[16,256,256]{2,1,0:T(8,128)(2,1)S(1)} %get-tuple-element.33.weight_ref, ...), custom_call_target="tpu_custom_call" | custom-call | flops 536870912 | bytes 4194304 | tf_op jit(solution)/shard_map/gradient_chunk/pallas_call | solution.py:212
  141.6 2.1 collective-permute-start.32
  143.7 1.3 collective-permute-start.34
  145.0 2.0 collective-permute-start.10
  147.1 4.2 %gradient_chunk.6 = (bf16[2,256,256]{2,1,0:T(8,128)(2,1)S(1)}, bf16[2,256,256]{2,1,0:T(8,128)(2,1)S(1)}, bf16[2,256,256]{2,1,0:T(8,128)(2,1)S(1)}, bf16[2,256,256]{2,1,0:T(8,128)(2,1)S(1)}) custom-call(s32[16]{0:T(128)S(1)} %multiply_add_fusion.slot_ref, s32[2]{0:T(128)S(1)} %bitcast.11, bf16[16,256,256]{2,1,0:T(8,128)(2,1)S(1)} %get-tuple-element.33.weight_ref, ...), custom_call_target="tpu_custom_call" | custom-call | flops 536870912 | bytes 4194304 | tf_op jit(solution)/shard_map/gradient_chunk/pallas_call | solution.py:212
  151.6 4.4 %collective-permute-start.26 = (bf16[2,256,256]{2,1,0:T(8,128)(2,1)S(1)}, bf16[2,256,256]{2,1,0:T(8,128)(2,1)S(1)}, u32[]{:S(2)}, u32[]{:S(2)}) collective-permute-start(bf16[2,256,256]{2,1,0:T(8,128)(2,1)S(1)} %get-tuple-element.44), channel_id=1, source_target_pairs={{0,8},{4,12},{8,0},{12,4},{1,9},{5,13},{9,1},{13,5},{2,10},{6,14},... | collective-permute-start | bytes 786440 | tf_op jit(solution)/shard_map/ppermute | solution.py:329
  156.0 9.3 %collective-permute-done.33.rest_2_ = bf16[2,256,256]{2,1,0:T(8,128)(2,1)S(1)} collective-permute-done((bf16[2,256,256]{2,1,0:T(8,128)(2,1)S(1)}, bf16[2,256,256]{2,1,0:T(8,128)(2,1)S(1)}, u32[]{:S(2)}, u32[]{:S(2)}) %collective-permute-start.33) | collective-permute-done | bytes 262176 | tf_op jit(solution)/shard_map/ppermute | solution.py:329
  165.3 10.9 %collective-permute-done.34.rest_3_ = bf16[2,256,256]{2,1,0:T(8,128)(2,1)S(1)} collective-permute-done((bf16[2,256,256]{2,1,0:T(8,128)(2,1)S(1)}, bf16[2,256,256]{2,1,0:T(8,128)(2,1)S(1)}, u32[]{:S(2)}, u32[]{:S(2)}) %collective-permute-start.34) | collective-permute-done | bytes 262176 | tf_op jit(solution)/shard_map/ppermute | solution.py:329
  176.2 1.3 collective-permute-start.28
  177.5 4.2 %gradient_chunk.5 = (bf16[2,256,256]{2,1,0:T(8,128)(2,1)S(1)}, bf16[2,256,256]{2,1,0:T(8,128)(2,1)S(1)}, bf16[2,256,256]{2,1,0:T(8,128)(2,1)S(1)}, bf16[2,256,256]{2,1,0:T(8,128)(2,1)S(1)}) custom-call(s32[16]{0:T(128)S(1)} %multiply_add_fusion.slot_ref, s32[2]{0:T(128)S(1)} %bitcast.12, bf16[16,256,256]{2,1,0:T(8,128)(2,1)S(1)} %get-tuple-element.33.weight_ref, ...), custom_call_target="tpu_custom_call" | custom-call | flops 536870912 | bytes 4194304 | tf_op jit(solution)/shard_map/gradient_chunk/pallas_call | solution.py:212
  181.8 4.2 %gradient_chunk.4 = (bf16[2,256,256]{2,1,0:T(8,128)(2,1)S(1)}, bf16[2,256,256]{2,1,0:T(8,128)(2,1)S(1)}, bf16[2,256,256]{2,1,0:T(8,128)(2,1)S(1)}, bf16[2,256,256]{2,1,0:T(8,128)(2,1)S(1)}) custom-call(s32[16]{0:T(128)S(1)} %multiply_add_fusion.slot_ref, s32[2]{0:T(128)S(1)} %bitcast.13, bf16[16,256,256]{2,1,0:T(8,128)(2,1)S(1)} %get-tuple-element.33.weight_ref, ...), custom_call_target="tpu_custom_call" | custom-call | flops 536870912 | bytes 4194304 | tf_op jit(solution)/shard_map/gradient_chunk/pallas_call | solution.py:212
  186.7 1.7 collective-permute-start.18
  188.4 4.9 %collective-permute-start.19 = (bf16[2,256,256]{2,1,0:T(8,128)(2,1)S(1)}, bf16[2,256,256]{2,1,0:T(8,128)(2,1)S(1)}, u32[]{:S(2)}, u32[]{:S(2)}) collective-permute-start(bf16[2,256,256]{2,1,0:T(8,128)(2,1)S(1)} %get-tuple-element.40), channel_id=1, source_target_pairs={{0,8},{4,12},{8,0},{12,4},{1,9},{5,13},{9,1},{13,5},{2,10},{6,14},... | collective-permute-start | bytes 786440 | tf_op jit(solution)/shard_map/ppermute | solution.py:329
  194.0 1.7 collective-permute-start.11
  195.7 2.3 collective-permute-done.18.rest_1_
  197.9 1.2 collective-permute-start.12
  199.1 12.4 %collective-permute-done.19.rest_2_ = bf16[2,256,256]{2,1,0:T(8,128)(2,1)S(1)} collective-permute-done((bf16[2,256,256]{2,1,0:T(8,128)(2,1)S(1)}, bf16[2,256,256]{2,1,0:T(8,128)(2,1)S(1)}, u32[]{:S(2)}, u32[]{:S(2)}) %collective-permute-start.19) | collective-permute-done | bytes 262176 | tf_op jit(solution)/shard_map/ppermute | solution.py:329
  211.6 15.5 %collective-permute-done.20.rest_3_ = bf16[2,256,256]{2,1,0:T(8,128)(2,1)S(1)} collective-permute-done((bf16[2,256,256]{2,1,0:T(8,128)(2,1)S(1)}, bf16[2,256,256]{2,1,0:T(8,128)(2,1)S(1)}, u32[]{:S(2)}, u32[]{:S(2)}) %collective-permute-start.20) | collective-permute-done | bytes 262176 | tf_op jit(solution)/shard_map/ppermute | solution.py:329
  227.0 1.2 collective-permute-start.36
  228.4 0.9 collective-permute-start.38
  229.3 4.7 %collective-permute-done.12.rest_2_ = bf16[2,256,256]{2,1,0:T(8,128)(2,1)S(1)} collective-permute-done((bf16[2,256,256]{2,1,0:T(8,128)(2,1)S(1)}, bf16[2,256,256]{2,1,0:T(8,128)(2,1)S(1)}, u32[]{:S(2)}, u32[]{:S(2)}) %collective-permute-start.12) | collective-permute-done | bytes 262176 | tf_op jit(solution)/shard_map/ppermute | solution.py:329
  234.7 3.7 %collective-permute-done.13.rest_3_ = bf16[2,256,256]{2,1,0:T(8,128)(2,1)} collective-permute-done((bf16[2,256,256]{2,1,0:T(8,128)(2,1)S(1)}, bf16[2,256,256]{2,1,0:T(8,128)(2,1)}, u32[]{:S(2)}, u32[]{:S(2)}) %collective-permute-start.13) | collective-permute-done | bytes 262176 | tf_op jit(solution)/shard_map/ppermute | solution.py:329
  238.4 0.8 collective-permute-start.30
  239.2 0.7 copy-done.24
  241.1 0.7 copy-done.28
  241.8 0.7 copy-done.4
  243.0 0.7 copy-done.6
  243.7 0.7 copy-done.10
  245.0 0.7 copy-done.8
  245.7 0.7 copy-done.12
  246.9 0.9 copy-done.15
  247.9 0.9 copy-done.17
  248.8 0.9 copy-done.19
  249.8 0.9 copy-done.21
  250.7 0.9 copy-done.23
  251.7 0.9 copy-done.25
  252.6 0.9 copy-done.27
  253.6 0.9 copy-done.29
  254.5 2.4 collect_chunk.4.rest_8_
  257.0 2.4 collect_chunk.5.rest_8_
  259.5 2.8 %collect_chunk.6.rest_8_ = f32[8,1024,256]{2,1,0:T(8,128)} custom-call(s32[8,2]{1,0:T(8,128)S(1)} %concatenate.21.index_ref, bf16[2,256,256]{2,1,0:T(8,128)(2,1)S(1)} %get-tuple-element.38.rest_0_, bf16[2,256,256]{2,1,0:T(8,128)(2,1)S(1)} %collective-permute-done.18.rest_1_, ...), custom_call_target="tpu_custom_call", output_to_operand_aliasing={{}: (9, {})} | custom-call | bytes 4194304 | tf_op jit(solution)/shard_map/collect_chunk/pallas_call | solution.py:245
  262.3 3.1 %collect_chunk.7 = f32[8,1024,256]{2,1,0:T(8,128)} custom-call(s32[8,2]{1,0:T(8,128)S(1)} %concatenate.21.index_ref, bf16[2,256,256]{2,1,0:T(8,128)(2,1)S(1)} %get-tuple-element.34.rest_0_, bf16[2,256,256]{2,1,0:T(8,128)(2,1)S(1)} %collective-permute-done.11.rest_1_, ...), custom_call_target="tpu_custom_call", output_to_operand_aliasing={{}: (9, {})} | custom-call | bytes 4194304 | tf_op jit(solution)/shard_map/collect_chunk/pallas_call | solution.py:245
  (117 shorter events, 9.6 us)
Async XLA Ops:
  3.0 4.7 %collective-permute-start = (f32[10]{0:T(128)S(1)}, f32[10]{0:T(128)S(1)}, u32[]{:S(2)}, u32[]{:S(2)}) collective-permute-start(f32[10]{0:T(128)S(1)} %get-tuple-element.53), channel_id=1, source_target_pairs={{0,12},{4,0},{8,4},{12,8},{1,13},{5,1},{9,5},{13,9},{2,14},{6,2},{... | collective-permute-start | bytes 128 | tf_op jit(solution)/shard_map/ppermute | solution.py:289
  3.0 4.7 %collective-permute-start.1 = (f32[10]{0:T(128)S(1)}, f32[10]{0:T(128)S(1)}, u32[]{:S(2)}, u32[]{:S(2)}) collective-permute-start(f32[10]{0:T(128)S(1)} %get-tuple-element.54), channel_id=1, source_target_pairs={{0,8},{4,12},{8,0},{12,4},{1,9},{5,13},{9,1},{13,5},{2,10},{6,14},... | collective-permute-start | bytes 128 | tf_op jit(solution)/shard_map/ppermute | solution.py:289
  5.5 2.9 %collective-permute-start.2 = (f32[10]{0:T(128)S(1)}, f32[10]{0:T(128)S(1)}, u32[]{:S(2)}, u32[]{:S(2)}) collective-permute-start(f32[10]{0:T(128)S(1)} %get-tuple-element.55), channel_id=1, source_target_pairs={{0,4},{4,8},{8,12},{12,0},{1,5},{5,9},{9,13},{13,1},{2,6},{6,10},{... | collective-permute-start | bytes 128 | tf_op jit(solution)/shard_map/ppermute | solution.py:289
  8.4 2.2 copy-start
  12.2 11.8 %collective-permute-start.6 = (bf16[2,512,256]{2,1,0:T(8,128)(2,1)S(1)}, bf16[2,512,256]{2,1,0:T(8,128)(2,1)S(1)}, u32[]{:S(2)}, u32[]{:S(2)}) collective-permute-start(bf16[2,512,256]{2,1,0:T(8,128)(2,1)S(1)} %get-tuple-element.29), channel_id=1, source_target_pairs={{0,12},{4,0},{8,4},{12,8},{1,13},{5,1},{9,5},{13,9},{2,14},{6,2},{... | collective-permute-start | bytes 1572872 | tf_op jit(solution)/shard_map/ppermute | solution.py:302
  14.6 36.3 %collective-permute-start.7 = (bf16[2,512,256]{2,1,0:T(8,128)(2,1)}, bf16[2,512,256]{2,1,0:T(8,128)(2,1)S(1)}, u32[]{:S(2)}, u32[]{:S(2)}) collective-permute-start(bf16[2,512,256]{2,1,0:T(8,128)(2,1)} %get-tuple-element.30), channel_id=1, source_target_pairs={{0,8},{4,12},{8,0},{12,4},{1,9},{5,13},{9,1},{13,5},{2,10},{6,14},... | collective-permute-start | bytes 1572872 | tf_op jit(solution)/shard_map/ppermute | solution.py:302
  15.1 67.4 %collective-permute-start.8 = (bf16[2,512,256]{2,1,0:T(8,128)(2,1)}, bf16[2,512,256]{2,1,0:T(8,128)(2,1)S(1)}, u32[]{:S(2)}, u32[]{:S(2)}) collective-permute-start(bf16[2,512,256]{2,1,0:T(8,128)(2,1)} %get-tuple-element.31), channel_id=1, source_target_pairs={{0,4},{4,8},{8,12},{12,0},{1,5},{5,9},{9,13},{13,1},{2,6},{6,10},{... | collective-permute-start | bytes 1572872 | tf_op jit(solution)/shard_map/ppermute | solution.py:302
  17.8 73.5 %collective-permute-start.3 = (bf16[2,512,256]{2,1,0:T(8,128)(2,1)}, bf16[2,512,256]{2,1,0:T(8,128)(2,1)S(1)}, u32[]{:S(2)}, u32[]{:S(2)}) collective-permute-start(bf16[2,512,256]{2,1,0:T(8,128)(2,1)} %get-tuple-element.26), channel_id=1, source_target_pairs={{0,12},{4,0},{8,4},{12,8},{1,13},{5,1},{9,5},{13,9},{2,14},{6,2},{... | collective-permute-start | bytes 1572872 | tf_op jit(solution)/shard_map/ppermute | solution.py:302
  18.4 75.4 %collective-permute-start.4 = (bf16[2,512,256]{2,1,0:T(8,128)(2,1)}, bf16[2,512,256]{2,1,0:T(8,128)(2,1)S(1)}, u32[]{:S(2)}, u32[]{:S(2)}) collective-permute-start(bf16[2,512,256]{2,1,0:T(8,128)(2,1)} %get-tuple-element.27), channel_id=1, source_target_pairs={{0,8},{4,12},{8,0},{12,4},{1,9},{5,13},{9,1},{13,5},{2,10},{6,14},... | collective-permute-start | bytes 1572872 | tf_op jit(solution)/shard_map/ppermute | solution.py:302
  24.0 81.0 %collective-permute-start.5 = (bf16[2,512,256]{2,1,0:T(8,128)(2,1)}, bf16[2,512,256]{2,1,0:T(8,128)(2,1)S(1)}, u32[]{:S(2)}, u32[]{:S(2)}) collective-permute-start(bf16[2,512,256]{2,1,0:T(8,128)(2,1)} %get-tuple-element.28), channel_id=1, source_target_pairs={{0,4},{4,8},{8,12},{12,0},{1,5},{5,9},{9,13},{13,1},{2,6},{6,10},{... | collective-permute-start | bytes 1572872 | tf_op jit(solution)/shard_map/ppermute | solution.py:302
  82.6 2.2 copy-start.1
  84.8 47.5 %copy-start.3 = (f32[8,256,256]{2,1,0:T(8,128)S(1)}, f32[8,256,256]{2,1,0:T(8,128)}, u32[]{:S(2)}) copy-start(f32[8,256,256]{2,1,0:T(8,128)} %fock_ref.1) | copy-start | bytes 6291460
  84.8 47.5 %copy-start.30 = (s32[8]{0:T(128)S(1)}, s32[8]{0:T(128)}, u32[]{:S(2)}) copy-start(s32[8]{0:T(128)} %size_ref.1) | copy-start | bytes 100
  87.8 49.6 %copy-start.2 = (bf16[8,1024,256]{2,1,0:T(8,128)(2,1)S(1)}, bf16[8,1024,256]{2,1,0:T(8,128)(2,1)}, u32[]{:S(2)}) copy-start(bf16[8,1024,256]{2,1,0:T(8,128)(2,1)} %blocks_ref.15) | copy-start | bytes 12582916
  108.0 24.3 %collective-permute-start.9 = (bf16[8,256,256]{2,1,0:T(8,128)(2,1)S(1)}, bf16[8,256,256]{2,1,0:T(8,128)(2,1)S(1)}, u32[]{:S(2)}, u32[]{:S(2)}) collective-permute-start(bf16[8,256,256]{2,1,0:T(8,128)(2,1)S(1)} %exchange_chunk.3.rest_0_), channel_id=1, source_target_pairs={{0,2},{2,0},{1,3},{3,1},{4,6},{6,4},{5,7},{7,5},{8,10},{10,8},{9,1... | collective-permute-start | bytes 3145736 | tf_op jit(solution)/shard_map/ppermute | solution.py:310
  141.6 44.4 %copy-start.14 = (bf16[2,256,256]{2,1,0:T(8,128)(2,1)}, bf16[2,256,256]{2,1,0:T(8,128)(2,1)S(1)}, u32[]{:S(2)}) copy-start(bf16[2,256,256]{2,1,0:T(8,128)(2,1)S(1)} %get-tuple-element.46.rest_0_) | copy-start | bytes 786436
  141.6 10.0 %collective-permute-start.32 = (bf16[2,256,256]{2,1,0:T(8,128)(2,1)S(1)}, bf16[2,256,256]{2,1,0:T(8,128)(2,1)S(1)}, u32[]{:S(2)}, u32[]{:S(2)}) collective-permute-start(bf16[2,256,256]{2,1,0:T(8,128)(2,1)S(1)} %get-tuple-element.47), channel_id=1, source_target_pairs={{0,4},{4,8},{8,12},{12,0},{1,5},{5,9},{9,13},{13,1},{2,6},{6,10},{... | collective-permute-start | bytes 786440 | tf_op jit(solution)/shard_map/ppermute | solution.py:329
  143.7 21.5 %collective-permute-start.33 = (bf16[2,256,256]{2,1,0:T(8,128)(2,1)S(1)}, bf16[2,256,256]{2,1,0:T(8,128)(2,1)S(1)}, u32[]{:S(2)}, u32[]{:S(2)}) collective-permute-start(bf16[2,256,256]{2,1,0:T(8,128)(2,1)S(1)} %get-tuple-element.48), channel_id=1, source_target_pairs={{0,8},{4,12},{8,0},{12,4},{1,9},{5,13},{9,1},{13,5},{2,10},{6,14},... | collective-permute-start | bytes 786440 | tf_op jit(solution)/shard_map/ppermute | solution.py:329
  143.7 32.4 %collective-permute-start.34 = (bf16[2,256,256]{2,1,0:T(8,128)(2,1)S(1)}, bf16[2,256,256]{2,1,0:T(8,128)(2,1)S(1)}, u32[]{:S(2)}, u32[]{:S(2)}) collective-permute-start(bf16[2,256,256]{2,1,0:T(8,128)(2,1)S(1)} %get-tuple-element.49), channel_id=1, source_target_pairs={{0,12},{4,0},{8,4},{12,8},{1,13},{5,1},{9,5},{13,9},{2,14},{6,2},{... | collective-permute-start | bytes 786440 | tf_op jit(solution)/shard_map/ppermute | solution.py:329
  145.0 6.3 %collective-permute-start.10 = (f32[4,2]{1,0:T(4,128)S(1)}, f32[4,2]{1,0:T(4,128)S(1)}, u32[]{:S(2)}, u32[]{:S(2)}) collective-permute-start(f32[4,2]{1,0:T(4,128)S(1)} %add_convert_fusion), channel_id=1, source_target_pairs={{0,1},{1,0},{2,3},{3,2},{4,5},{5,4},{6,7},{7,6},{8,9},{9,8},{10,11... | collective-permute-start | bytes 104 | tf_op jit(solution)/shard_map/ppermute | solution.py:319
  147.0 39.0 %collective-permute-start.35 = (bf16[2,256,256]{2,1,0:T(8,128)(2,1)S(1)}, bf16[2,256,256]{2,1,0:T(8,128)(2,1)S(1)}, u32[]{:S(2)}, u32[]{:S(2)}) collective-permute-start(bf16[2,256,256]{2,1,0:T(8,128)(2,1)S(1)} %get-tuple-element.46.rest_0_), channel_id=1, source_target_pairs={{0,1},{1,0},{2,3},{3,2},{4,5},{5,4},{6,7},{7,6},{8,9},{9,8},{10,11... | collective-permute-start | bytes 786440 | tf_op jit(solution)/shard_map/ppermute | solution.py:333
  151.3 37.1 %collective-permute-start.25 = (bf16[2,256,256]{2,1,0:T(8,128)(2,1)S(1)}, bf16[2,256,256]{2,1,0:T(8,128)(2,1)S(1)}, u32[]{:S(2)}, u32[]{:S(2)}) collective-permute-start(bf16[2,256,256]{2,1,0:T(8,128)(2,1)S(1)} %get-tuple-element.43), channel_id=1, source_target_pairs={{0,4},{4,8},{8,12},{12,0},{1,5},{5,9},{9,13},{13,1},{2,6},{6,10},{... | collective-permute-start | bytes 786440 | tf_op jit(solution)/shard_map/ppermute | solution.py:329
  151.6 94.1 %copy-start.16 = (bf16[2,256,256]{2,1,0:T(8,128)(2,1)}, bf16[2,256,256]{2,1,0:T(8,128)(2,1)S(1)}, u32[]{:S(2)}) copy-start(bf16[2,256,256]{2,1,0:T(8,128)(2,1)S(1)} %collective-permute-done.32.rest_1_) | copy-start | bytes 786436
  151.6 41.7 %collective-permute-start.26 = (bf16[2,256,256]{2,1,0:T(8,128)(2,1)S(1)}, bf16[2,256,256]{2,1,0:T(8,128)(2,1)S(1)}, u32[]{:S(2)}, u32[]{:S(2)}) collective-permute-start(bf16[2,256,256]{2,1,0:T(8,128)(2,1)S(1)} %get-tuple-element.44), channel_id=1, source_target_pairs={{0,8},{4,12},{8,0},{12,4},{1,9},{5,13},{9,1},{13,5},{2,10},{6,14},... | collective-permute-start | bytes 786440 | tf_op jit(solution)/shard_map/ppermute | solution.py:329
  165.3 81.6 %copy-start.18 = (bf16[2,256,256]{2,1,0:T(8,128)(2,1)}, bf16[2,256,256]{2,1,0:T(8,128)(2,1)S(1)}, u32[]{:S(2)}) copy-start(bf16[2,256,256]{2,1,0:T(8,128)(2,1)S(1)} %collective-permute-done.33.rest_2_) | copy-start | bytes 786436
  165.3 28.0 %collective-permute-start.27 = (bf16[2,256,256]{2,1,0:T(8,128)(2,1)S(1)}, bf16[2,256,256]{2,1,0:T(8,128)(2,1)S(1)}, u32[]{:S(2)}, u32[]{:S(2)}) collective-permute-start(bf16[2,256,256]{2,1,0:T(8,128)(2,1)S(1)} %get-tuple-element.45), channel_id=1, source_target_pairs={{0,12},{4,0},{8,4},{12,8},{1,13},{5,1},{9,5},{13,9},{2,14},{6,2},{... | collective-permute-start | bytes 786440 | tf_op jit(solution)/shard_map/ppermute | solution.py:329
  176.2 70.7 %copy-start.20 = (bf16[2,256,256]{2,1,0:T(8,128)(2,1)}, bf16[2,256,256]{2,1,0:T(8,128)(2,1)S(1)}, u32[]{:S(2)}) copy-start(bf16[2,256,256]{2,1,0:T(8,128)(2,1)S(1)} %collective-permute-done.34.rest_3_) | copy-start | bytes 786436
  176.2 17.8 %collective-permute-start.28 = (bf16[2,256,256]{2,1,0:T(8,128)(2,1)S(1)}, bf16[2,256,256]{2,1,0:T(8,128)(2,1)S(1)}, u32[]{:S(2)}, u32[]{:S(2)}) collective-permute-start(bf16[2,256,256]{2,1,0:T(8,128)(2,1)S(1)} %get-tuple-element.42.rest_0_), channel_id=1, source_target_pairs={{0,1},{1,0},{2,3},{3,2},{4,5},{5,4},{6,7},{7,6},{8,9},{9,8},{10,11... | collective-permute-start | bytes 786440 | tf_op jit(solution)/shard_map/ppermute | solution.py:333
  186.7 11.2 %collective-permute-start.18 = (bf16[2,256,256]{2,1,0:T(8,128)(2,1)S(1)}, bf16[2,256,256]{2,1,0:T(8,128)(2,1)S(1)}, u32[]{:S(2)}, u32[]{:S(2)}) collective-permute-start(bf16[2,256,256]{2,1,0:T(8,128)(2,1)S(1)} %get-tuple-element.39), channel_id=1, source_target_pairs={{0,4},{4,8},{8,12},{12,0},{1,5},{5,9},{9,13},{13,1},{2,6},{6,10},{... | collective-permute-start | bytes 786440 | tf_op jit(solution)/shard_map/ppermute | solution.py:329
  188.4 23.1 %collective-permute-start.19 = (bf16[2,256,256]{2,1,0:T(8,128)(2,1)S(1)}, bf16[2,256,256]{2,1,0:T(8,128)(2,1)S(1)}, u32[]{:S(2)}, u32[]{:S(2)}) collective-permute-start(bf16[2,256,256]{2,1,0:T(8,128)(2,1)S(1)} %get-tuple-element.40), channel_id=1, source_target_pairs={{0,8},{4,12},{8,0},{12,4},{1,9},{5,13},{9,1},{13,5},{2,10},{6,14},... | collective-permute-start | bytes 786440 | tf_op jit(solution)/shard_map/ppermute | solution.py:329
  193.3 33.7 %collective-permute-start.20 = (bf16[2,256,256]{2,1,0:T(8,128)(2,1)S(1)}, bf16[2,256,256]{2,1,0:T(8,128)(2,1)S(1)}, u32[]{:S(2)}, u32[]{:S(2)}) collective-permute-start(bf16[2,256,256]{2,1,0:T(8,128)(2,1)S(1)} %get-tuple-element.41), channel_id=1, source_target_pairs={{0,12},{4,0},{8,4},{12,8},{1,13},{5,1},{9,5},{13,9},{2,14},{6,2},{... | collective-permute-start | bytes 786440 | tf_op jit(solution)/shard_map/ppermute | solution.py:329
  193.3 34.9 %collective-permute-start.21 = (bf16[2,256,256]{2,1,0:T(8,128)(2,1)S(1)}, bf16[2,256,256]{2,1,0:T(8,128)(2,1)S(1)}, u32[]{:S(2)}, u32[]{:S(2)}) collective-permute-start(bf16[2,256,256]{2,1,0:T(8,128)(2,1)S(1)} %get-tuple-element.38.rest_0_), channel_id=1, source_target_pairs={{0,1},{1,0},{2,3},{3,2},{4,5},{5,4},{6,7},{7,6},{8,9},{9,8},{10,11... | collective-permute-start | bytes 786440 | tf_op jit(solution)/shard_map/ppermute | solution.py:333
  194.0 34.4 %collective-permute-start.11 = (bf16[2,256,256]{2,1,0:T(8,128)(2,1)S(1)}, bf16[2,256,256]{2,1,0:T(8,128)(2,1)S(1)}, u32[]{:S(2)}, u32[]{:S(2)}) collective-permute-start(bf16[2,256,256]{2,1,0:T(8,128)(2,1)S(1)} %get-tuple-element.35), channel_id=1, source_target_pairs={{0,4},{4,8},{8,12},{12,0},{1,5},{5,9},{9,13},{13,1},{2,6},{6,10},{... | collective-permute-start | bytes 786440 | tf_op jit(solution)/shard_map/ppermute | solution.py:329
  197.9 36.1 %collective-permute-start.12 = (bf16[2,256,256]{2,1,0:T(8,128)(2,1)S(1)}, bf16[2,256,256]{2,1,0:T(8,128)(2,1)S(1)}, u32[]{:S(2)}, u32[]{:S(2)}) collective-permute-start(bf16[2,256,256]{2,1,0:T(8,128)(2,1)S(1)} %get-tuple-element.36), channel_id=1, source_target_pairs={{0,8},{4,12},{8,0},{12,4},{1,9},{5,13},{9,1},{13,5},{2,10},{6,14},... | collective-permute-start | bytes 786440 | tf_op jit(solution)/shard_map/ppermute | solution.py:329
  211.5 26.8 %collective-permute-start.13 = (bf16[2,256,256]{2,1,0:T(8,128)(2,1)S(1)}, bf16[2,256,256]{2,1,0:T(8,128)(2,1)}, u32[]{:S(2)}, u32[]{:S(2)}) collective-permute-start(bf16[2,256,256]{2,1,0:T(8,128)(2,1)S(1)} %get-tuple-element.37), channel_id=1, source_target_pairs={{0,12},{4,0},{8,4},{12,8},{1,13},{5,1},{9,5},{13,9},{2,14},{6,2},{... | collective-permute-start | bytes 786440 | tf_op jit(solution)/shard_map/ppermute | solution.py:329
  227.0 12.1 %collective-permute-start.36 = (bf16[2,256,256]{2,1,0:T(8,128)(2,1)S(1)}, bf16[2,256,256]{2,1,0:T(8,128)(2,1)S(1)}, u32[]{:S(2)}, u32[]{:S(2)}) collective-permute-start(bf16[2,256,256]{2,1,0:T(8,128)(2,1)S(1)} %collective-permute-done.32.rest_1_), channel_id=1, source_target_pairs={{0,1},{1,0},{2,3},{3,2},{4,5},{5,4},{6,7},{7,6},{8,9},{9,8},{10,11... | collective-permute-start | bytes 786440 | tf_op jit(solution)/shard_map/ppermute | solution.py:333
  228.2 11.7 %collective-permute-start.37 = (bf16[2,256,256]{2,1,0:T(8,128)(2,1)S(1)}, bf16[2,256,256]{2,1,0:T(8,128)(2,1)S(1)}, u32[]{:S(2)}, u32[]{:S(2)}) collective-permute-start(bf16[2,256,256]{2,1,0:T(8,128)(2,1)S(1)} %collective-permute-done.33.rest_2_), channel_id=1, source_target_pairs={{0,1},{1,0},{2,3},{3,2},{4,5},{5,4},{6,7},{7,6},{8,9},{9,8},{10,11... | collective-permute-start | bytes 786440 | tf_op jit(solution)/shard_map/ppermute | solution.py:333
  228.4 12.7 %collective-permute-start.38 = (bf16[2,256,256]{2,1,0:T(8,128)(2,1)S(1)}, bf16[2,256,256]{2,1,0:T(8,128)(2,1)S(1)}, u32[]{:S(2)}, u32[]{:S(2)}) collective-permute-start(bf16[2,256,256]{2,1,0:T(8,128)(2,1)S(1)} %collective-permute-done.34.rest_3_), channel_id=1, source_target_pairs={{0,1},{1,0},{2,3},{3,2},{4,5},{5,4},{6,7},{7,6},{8,9},{9,8},{10,11... | collective-permute-start | bytes 786440 | tf_op jit(solution)/shard_map/ppermute | solution.py:333
  234.0 7.8 %collective-permute-start.29 = (bf16[2,256,256]{2,1,0:T(8,128)(2,1)S(1)}, bf16[2,256,256]{2,1,0:T(8,128)(2,1)S(1)}, u32[]{:S(2)}, u32[]{:S(2)}) collective-permute-start(bf16[2,256,256]{2,1,0:T(8,128)(2,1)S(1)} %collective-permute-done.25.rest_1_), channel_id=1, source_target_pairs={{0,1},{1,0},{2,3},{3,2},{4,5},{5,4},{6,7},{7,6},{8,9},{9,8},{10,11... | collective-permute-start | bytes 786440 | tf_op jit(solution)/shard_map/ppermute | solution.py:333
  238.4 4.6 %collective-permute-start.30 = (bf16[2,256,256]{2,1,0:T(8,128)(2,1)S(1)}, bf16[2,256,256]{2,1,0:T(8,128)(2,1)S(1)}, u32[]{:S(2)}, u32[]{:S(2)}) collective-permute-start(bf16[2,256,256]{2,1,0:T(8,128)(2,1)S(1)} %collective-permute-done.26.rest_2_), channel_id=1, source_target_pairs={{0,1},{1,0},{2,3},{3,2},{4,5},{5,4},{6,7},{7,6},{8,9},{9,8},{10,11... | collective-permute-start | bytes 786440 | tf_op jit(solution)/shard_map/ppermute | solution.py:333
  239.2 0.7 copy-start.24
  239.9 3.9 %collective-permute-start.31 = (bf16[2,256,256]{2,1,0:T(8,128)(2,1)S(1)}, bf16[2,256,256]{2,1,0:T(8,128)(2,1)S(1)}, u32[]{:S(2)}, u32[]{:S(2)}) collective-permute-start(bf16[2,256,256]{2,1,0:T(8,128)(2,1)S(1)} %collective-permute-done.27.rest_3_), channel_id=1, source_target_pairs={{0,1},{1,0},{2,3},{3,2},{4,5},{5,4},{6,7},{7,6},{8,9},{9,8},{10,11... | collective-permute-start | bytes 786440 | tf_op jit(solution)/shard_map/ppermute | solution.py:333
  240.6 4.4 %collective-permute-start.22 = (bf16[2,256,256]{2,1,0:T(8,128)(2,1)S(1)}, bf16[2,256,256]{2,1,0:T(8,128)(2,1)S(1)}, u32[]{:S(2)}, u32[]{:S(2)}) collective-permute-start(bf16[2,256,256]{2,1,0:T(8,128)(2,1)S(1)} %collective-permute-done.18.rest_1_), channel_id=1, source_target_pairs={{0,1},{1,0},{2,3},{3,2},{4,5},{5,4},{6,7},{7,6},{8,9},{9,8},{10,11... | collective-permute-start | bytes 786440 | tf_op jit(solution)/shard_map/ppermute | solution.py:333
  241.8 3.9 %collective-permute-start.23 = (bf16[2,256,256]{2,1,0:T(8,128)(2,1)S(1)}, bf16[2,256,256]{2,1,0:T(8,128)(2,1)S(1)}, u32[]{:S(2)}, u32[]{:S(2)}) collective-permute-start(bf16[2,256,256]{2,1,0:T(8,128)(2,1)S(1)} %collective-permute-done.19.rest_2_), channel_id=1, source_target_pairs={{0,1},{1,0},{2,3},{3,2},{4,5},{5,4},{6,7},{7,6},{8,9},{9,8},{10,11... | collective-permute-start | bytes 786440 | tf_op jit(solution)/shard_map/ppermute | solution.py:333
  242.5 19.8 %collective-permute-start.14 = (bf16[2,256,256]{2,1,0:T(8,128)(2,1)S(1)}, bf16[2,256,256]{2,1,0:T(8,128)(2,1)}, u32[]{:S(2)}, u32[]{:S(2)}) collective-permute-start(bf16[2,256,256]{2,1,0:T(8,128)(2,1)S(1)} %get-tuple-element.34.rest_0_), channel_id=1, source_target_pairs={{0,1},{1,0},{2,3},{3,2},{4,5},{5,4},{6,7},{7,6},{8,9},{9,8},{10,11... | collective-permute-start | bytes 786440 | tf_op jit(solution)/shard_map/ppermute | solution.py:333
  243.0 0.7 copy-start.6
  243.7 15.7 %collective-permute-start.24 = (bf16[2,256,256]{2,1,0:T(8,128)(2,1)S(1)}, bf16[2,256,256]{2,1,0:T(8,128)(2,1)}, u32[]{:S(2)}, u32[]{:S(2)}) collective-permute-start(bf16[2,256,256]{2,1,0:T(8,128)(2,1)S(1)} %collective-permute-done.20.rest_3_), channel_id=1, source_target_pairs={{0,1},{1,0},{2,3},{3,2},{4,5},{5,4},{6,7},{7,6},{8,9},{9,8},{10,11... | collective-permute-start | bytes 786440 | tf_op jit(solution)/shard_map/ppermute | solution.py:333
  244.4 17.8 %collective-permute-start.15 = (bf16[2,256,256]{2,1,0:T(8,128)(2,1)S(1)}, bf16[2,256,256]{2,1,0:T(8,128)(2,1)}, u32[]{:S(2)}, u32[]{:S(2)}) collective-permute-start(bf16[2,256,256]{2,1,0:T(8,128)(2,1)S(1)} %collective-permute-done.11.rest_1_), channel_id=1, source_target_pairs={{0,1},{1,0},{2,3},{3,2},{4,5},{5,4},{6,7},{7,6},{8,9},{9,8},{10,11... | collective-permute-start | bytes 786440 | tf_op jit(solution)/shard_map/ppermute | solution.py:333
  245.7 16.6 %collective-permute-start.16 = (bf16[2,256,256]{2,1,0:T(8,128)(2,1)S(1)}, bf16[2,256,256]{2,1,0:T(8,128)(2,1)}, u32[]{:S(2)}, u32[]{:S(2)}) collective-permute-start(bf16[2,256,256]{2,1,0:T(8,128)(2,1)S(1)} %collective-permute-done.12.rest_2_), channel_id=1, source_target_pairs={{0,1},{1,0},{2,3},{3,2},{4,5},{5,4},{6,7},{7,6},{8,9},{9,8},{10,11... | collective-permute-start | bytes 786440 | tf_op jit(solution)/shard_map/ppermute | solution.py:333
  245.7 0.7 copy-start.12
  246.4 15.9 %collective-permute-start.17 = (bf16[2,256,256]{2,1,0:T(8,128)(2,1)}, bf16[2,256,256]{2,1,0:T(8,128)(2,1)}, u32[]{:S(2)}, u32[]{:S(2)}) collective-permute-start(bf16[2,256,256]{2,1,0:T(8,128)(2,1)} %collective-permute-done.13.rest_3_), channel_id=1, source_target_pairs={{0,1},{1,0},{2,3},{3,2},{4,5},{5,4},{6,7},{7,6},{8,9},{9,8},{10,11... | collective-permute-start | bytes 786440 | tf_op jit(solution)/shard_map/ppermute | solution.py:333
  246.9 1.0 copy-start.15
  247.9 0.9 copy-start.17
  248.8 0.9 copy-start.19
  249.8 0.9 copy-start.21
  250.7 0.9 copy-start.23
  251.7 0.9 copy-start.25
  252.6 0.9 copy-start.27
  253.6 0.9 copy-start.29
  254.5 2.4 copy-start.5
  254.5 2.4 copy-start.7
  254.5 2.5 copy-start.11
  257.0 2.5 copy-start.9
  257.0 2.5 copy-start.13
  (6 other events, 4.2 us)

commit v2 on v1

--- a/solution.py
+++ b/solution.py
@@ -8,7 +8,7 @@
 from jax.sharding import PartitionSpec as P
 
 CAP = 2
-FORWARD_CHUNKS = 2
+FORWARD_CHUNKS = 4
 BACK_CHUNKS = 4
 VMEM_LIMIT = 40 * 1024 * 1024
 
@@ -229,32 +229,51 @@
 
 def collect_kernel(count, index_ref, *rest):
     terms = rest[:count]
-    out_ref = rest[-1]
-    out_ref[...] = jnp.zeros_like(out_ref)
+    out_ref, sums = rest[count:]
+    sums[...] = jnp.zeros_like(sums)
     for d, ref in enumerate(terms):
         for k in range(CAP):
             g = index_ref[d, k]
-            out_ref[g] += ref[k].astype(F32)
-
-
-def collect_chunk(index, terms, before, local_orbs, fit_rows, start, rows):
-    virt = terms[0].shape[2]
+            sums[g] += ref[k].astype(F32)
+    out_ref[...] = sums[...].astype(BF16)
+
+
+def collect_chunk(index, terms, local_orbs):
+    _, rows, virt = terms[0].shape
     count = len(terms)
+    return pl.pallas_call(
+        functools.partial(collect_kernel, count),
+        out_shape=jax.ShapeDtypeStruct((local_orbs, rows, virt), BF16),
+        in_specs=[SMEM] + [VMEM] * count,
+        out_specs=VMEM,
+        scratch_shapes=[pltpu.VMEM((local_orbs, rows, virt), F32)],
+        compiler_params=params(),
+        cost_estimate=cost(0, (count * CAP + local_orbs) * 2 * rows * virt),
+        name="collect_chunk",
+    )(index, *terms)
+
+
+def add_kernel(mine_ref, other_ref, *rest):
+    rest[-1][...] = mine_ref[...].astype(F32) + other_ref[...].astype(F32)
+
+
+def add_chunk(mine, other, before, fit_rows, start):
+    local_orbs, rows, virt = mine.shape
+    step = min(rows, 64)
+    at = start // step
     more = [] if before is None else [before]
-    at = start // rows
-    return pl.pallas_call(
-        functools.partial(collect_kernel, count),
-        grid=(1,),
+    source = pl.BlockSpec((local_orbs, step, virt), lambda i: (0, i, 0))
+    return pl.pallas_call(
+        add_kernel,
+        grid=(rows // step,),
         out_shape=jax.ShapeDtypeStruct((local_orbs, fit_rows, virt), F32),
-        in_specs=[SMEM]
-        + [pl.BlockSpec((CAP, rows, virt), lambda i: (0, 0, 0))] * count
-        + [ANY] * len(more),
-        out_specs=pl.BlockSpec((local_orbs, rows, virt), lambda i: (0, at, 0)),
-        input_output_aliases={} if before is None else {1 + count: 0},
-        compiler_params=params(),
-        cost_estimate=cost(0, (count * CAP * 2 + local_orbs * 4) * rows * virt),
-        name="collect_chunk",
-    )(index, *terms, *more)
+        in_specs=[source, source] + [ANY] * len(more),
+        out_specs=pl.BlockSpec((local_orbs, step, virt), lambda i: (0, at + i, 0)),
+        input_output_aliases={} if before is None else {2: 0},
+        compiler_params=params(),
+        cost_estimate=cost(0, 8 * local_orbs * rows * virt),
+        name="add_chunk",
+    )(mine, other, *more)
 
 
 def per_device(blocks, occ_energy, pair_list, pno_sizes, fock_virt):
@@ -316,8 +335,6 @@
     amplitudes, weights = amplitude_step(energies, relative, pno_sizes, fock_virt, parts)
 
     swap = shifted(n_rep, 1)
-    both = [asked, lax.ppermute(asked.astype(F32), "rep", swap).astype(jnp.int32)]
-    index = jnp.concatenate(both)
     back_rows = fit_rows // BACK_CHUNKS
     returned = []
     for c in range(BACK_CHUNKS):
@@ -330,10 +347,9 @@
         )
     grads = None
     for c in range(BACK_CHUNKS):
-        other = [lax.ppermute(x, "rep", swap) for x in returned[c]]
-        grads = collect_chunk(
-            index, returned[c] + other, grads, local_orbs, fit_rows, c * back_rows, back_rows
-        )
+        mine = collect_chunk(asked, returned[c], local_orbs)
+        other = lax.ppermute(mine, "rep", swap)
+        grads = add_chunk(mine, other, grads, fit_rows, c * back_rows)
     return amplitudes, grads
 
 

time: 266 us -> 246 us (0.925)
  waiting for transfers between devices: 161 us -> 130 us
  local copies, waits for them, and re-layouts: 19 us -> 5.02 us
  Pallas kernels: 42.1 us -> 55.8 us
  starting transfers between devices: 40.3 us -> 50.1 us
    ppermute x6 -> x12, waiting for transfers between devices: 78.3 us -> 51 us  [per_device(): lax.ppermute(picked[d - 1], 'orb', shifted(n, n - d))]
    ppermute x6 -> x12, starting transfers between devices: 7.19 us -> 22.7 us  [per_device(): lax.ppermute(picked[d - 1], 'orb', shifted(n, n - d))]
    unnamed x63 -> x11, local copies, waits for them, and re-layouts: 18.4 us -> 4.48 us
    pallas_call x2 -> x4, Pallas kernels: 5.93 us -> 15.2 us  [exchange_chunk(): pl.pallas_call(functools.partial(exchange_kernel, start, rows, first, n),...]
    ppermute x12, starting transfers between devices: 17.6 us -> 11 us  [per_device(): lax.ppermute(sums[d], 'orb', shifted(n, d))]
    pallas_call x2 -> x4, Pallas kernels: 3.38 us -> 6.6 us  [pick_blocks(): pl.pallas_call(functools.partial(pick_kernel, start, rows), out_shape=[sh...]
    ppermute x12, waiting for transfers between devices: 58.9 us -> 55.9 us  [per_device(): lax.ppermute(sums[d], 'orb', shifted(n, d))]
    pallas_call x4 -> x8, Pallas kernels: 10.8 us -> 12 us  [the longest x4 8.01 us: add_chunk(): pl.pallas_call(add_kernel, grid=(rows // step,), out_shape=jax.ShapeDtype...]
  transfers between devices with their start and end apart: 39 -> 32, of which waited for: 16 -> 19; matrix products, arithmetic and copies ran while one was open for 0% -> 0% of each run, Pallas kernels for 9% -> 16%
where the time goes in v2:
time: 246 us; the launch traced here: 245 us
  waiting for transfers between devices  130 us (53%)
  Pallas kernels  55.8 us (23%)
  starting transfers between devices  50.1 us (20%)
  local copies, waits for them, and re-layouts  5.02 us (2%)
    ppermute x12, waiting for transfers between devices, per_device(): lax.ppermute(sums[d], 'orb', shifted(n, d))  55.9 us
    ppermute x12, waiting for transfers between devices, per_device(): lax.ppermute(picked[d - 1], 'orb', shifted(n, n - d))  51 us
    ppermute x1, waiting for transfers between devices, per_device(): parts = [ints, lax.ppermute(ints, 'fit', shifted(2, 1))]  22.7 us
    ppermute x12, starting transfers between devices, per_device(): lax.ppermute(picked[d - 1], 'orb', shifted(n, n - d))  22.7 us
    pallas_call x4, Pallas kernels, gradient_chunk(): pl.pallas_call(functools.partial(gradient_kernel, start, offset, rows, n)...  16.9 us
    pallas_call x4, Pallas kernels, exchange_chunk(): pl.pallas_call(functools.partial(exchange_kernel, start, rows, first, n),...  15.2 us
    ppermute x12, starting transfers between devices, per_device(): lax.ppermute(sums[d], 'orb', shifted(n, d))  11 us
    ppermute x4, starting transfers between devices, per_device(): other = lax.ppermute(mine, 'rep', swap)  10.4 us
  transfers between devices with their start and end apart: 32, of which 19 were waited for; matrix products, arithmetic and copies ran while one was open for 0% of the time, Pallas kernels for 16%

profile of v2, /device:TPU:9, one launch (start us, length us, event | category | flops | bytes accessed | tf_op | source)
XLA Modules:
  0.0 244.6 jit_solution(14284628284566098122)
XLA Ops:
  0.6 0.7 broadcast_subtract_fusion
  1.7 0.2 reduce_window_sum.11
  2.0 0.2 convert_reduce_fusion.2
  2.3 0.7 convert_element_type.41
  3.0 2.5 %collective-permute-start.1 = (f32[10]{0:T(128)S(1)}, f32[10]{0:T(128)S(1)}, u32[]{:S(2)}, u32[]{:S(2)}) collective-permute-start(f32[10]{0:T(128)S(1)} %get-tuple-element.66), channel_id=1, source_target_pairs={{0,8},{4,12},{8,0},{12,4},{1,9},{5,13},{9,1},{13,5},{2,10},{6,14},... | collective-permute-start | bytes 128 | tf_op jit(solution)/shard_map/ppermute | solution.py:308
  5.5 2.2 collective-permute-start.2
  7.7 0.7 collective-permute-done.2
  8.4 2.2 copy-done
  10.6 1.6 pick_blocks.7
  12.3 2.3 collective-permute-start.12
  14.6 0.6 collective-permute-start.13
  15.2 0.9 collective-permute-start.14
  16.1 1.7 pick_blocks.6
  17.7 1.3 collective-permute-start.10
  19.1 1.6 pick_blocks.5
  20.7 0.5 collective-permute-start.11
  21.3 1.0 collective-permute-start.9
  22.2 11.6 %collective-permute-done.13.rest_1_ = bf16[2,256,256]{2,1,0:T(8,128)(2,1)S(1)} collective-permute-done((bf16[2,256,256]{2,1,0:T(8,128)(2,1)S(1)}, bf16[2,256,256]{2,1,0:T(8,128)(2,1)S(1)}, u32[]{:S(2)}, u32[]{:S(2)}) %collective-permute-start.13) | collective-permute-done | bytes 262176 | tf_op jit(solution)/shard_map/ppermute | solution.py:321
  33.8 12.5 %collective-permute-start.6 = (bf16[2,256,256]{2,1,0:T(8,128)(2,1)S(1)}, bf16[2,256,256]{2,1,0:T(8,128)(2,1)S(1)}, u32[]{:S(2)}, u32[]{:S(2)}) collective-permute-start(bf16[2,256,256]{2,1,0:T(8,128)(2,1)S(1)} %get-tuple-element.35), channel_id=1, source_target_pairs={{0,12},{4,0},{8,4},{12,8},{1,13},{5,1},{9,5},{13,9},{2,14},{6,2},{... | collective-permute-start | bytes 786440 | tf_op jit(solution)/shard_map/ppermute | solution.py:321
  46.5 0.2 select_reduce_fusion
  46.7 2.2 copy-done.1
  48.9 1.6 pick_blocks.4
  50.7 15.0 %collective-permute-done.10.rest_1_ = bf16[2,256,256]{2,1,0:T(8,128)(2,1)S(1)} collective-permute-done((bf16[2,256,256]{2,1,0:T(8,128)(2,1)}, bf16[2,256,256]{2,1,0:T(8,128)(2,1)S(1)}, u32[]{:S(2)}, u32[]{:S(2)}) %collective-permute-start.10) | collective-permute-done | bytes 262176 | tf_op jit(solution)/shard_map/ppermute | solution.py:321
  65.7 5.5 %collective-permute-done.11.rest_2_ = bf16[2,256,256]{2,1,0:T(8,128)(2,1)S(1)} collective-permute-done((bf16[2,256,256]{2,1,0:T(8,128)(2,1)S(1)}, bf16[2,256,256]{2,1,0:T(8,128)(2,1)S(1)}, u32[]{:S(2)}, u32[]{:S(2)}) %collective-permute-start.11) | collective-permute-done | bytes 262176 | tf_op jit(solution)/shard_map/ppermute | solution.py:321
  71.2 3.4 %collective-permute-start.4 = (bf16[2,256,256]{2,1,0:T(8,128)(2,1)S(1)}, bf16[2,256,256]{2,1,0:T(8,128)(2,1)S(1)}, u32[]{:S(2)}, u32[]{:S(2)}) collective-permute-start(bf16[2,256,256]{2,1,0:T(8,128)(2,1)S(1)} %get-tuple-element.33), channel_id=1, source_target_pairs={{0,8},{4,12},{8,0},{12,4},{1,9},{5,13},{9,1},{13,5},{2,10},{6,14},... | collective-permute-start | bytes 786440 | tf_op jit(solution)/shard_map/ppermute | solution.py:321
  74.6 3.8 %exchange_chunk.4.rest_3_ = f32[8,256,256]{2,1,0:T(8,128)S(1)} custom-call(s32[16]{0:T(128)S(1)} %multiply_add_fusion.slot_ref, s32[2]{0:T(128)S(1)} %bitcast.8, bf16[8,1024,256]{2,1,0:T(8,128)(2,1)S(1)} %copy-done.2, bf16[2,256,256]{2,1,0:T(8,128)(2,1)S(1)} %collective-permute-done.12.rest_0_, bf16[2,256,256]{2,1,0:T(8,128)(2,1)S(1)} %collective-permute-done.13.rest_1_, ...), custom_call_target="tpu_custom_call" | custom-call | flops 268435456 | bytes 4194304 | tf_op jit(solution)/shard_map/exchange_chunk/pallas_call | solution.py:117
  78.4 3.8 %exchange_chunk.5.rest_3_ = f32[8,256,256]{2,1,0:T(8,128)S(1)} custom-call(s32[16]{0:T(128)S(1)} %multiply_add_fusion.slot_ref, s32[2]{0:T(128)S(1)} %bitcast.9, bf16[8,1024,256]{2,1,0:T(8,128)(2,1)S(1)} %copy-done.2, bf16[2,256,256]{2,1,0:T(8,128)(2,1)S(1)} %collective-permute-done.9.rest_0_, bf16[2,256,256]{2,1,0:T(8,128)(2,1)S(1)} %collective-permute-done.10.rest_1_, ...), custom_call_target="tpu_custom_call" | custom-call | flops 268435456 | bytes 4194304 | tf_op jit(solution)/shard_map/exchange_chunk/pallas_call | solution.py:117
  82.2 5.9 %collective-permute-done.7.rest_1_ = bf16[2,256,256]{2,1,0:T(8,128)(2,1)S(1)} collective-permute-done((bf16[2,256,256]{2,1,0:T(8,128)(2,1)S(1)}, bf16[2,256,256]{2,1,0:T(8,128)(2,1)S(1)}, u32[]{:S(2)}, u32[]{:S(2)}) %collective-permute-start.7) | collective-permute-done | bytes 262176 | tf_op jit(solution)/shard_map/ppermute | solution.py:321
  88.1 5.6 %collective-permute-done.8.rest_2_ = bf16[2,256,256]{2,1,0:T(8,128)(2,1)S(1)} collective-permute-done((bf16[2,256,256]{2,1,0:T(8,128)(2,1)S(1)}, bf16[2,256,256]{2,1,0:T(8,128)(2,1)S(1)}, u32[]{:S(2)}, u32[]{:S(2)}) %collective-permute-start.8) | collective-permute-done | bytes 262176 | tf_op jit(solution)/shard_map/ppermute | solution.py:321
  93.8 3.8 %exchange_chunk.6.rest_3_ = f32[8,256,256]{2,1,0:T(8,128)S(1)} custom-call(s32[16]{0:T(128)S(1)} %multiply_add_fusion.slot_ref, s32[2]{0:T(128)S(1)} %bitcast.10, bf16[8,1024,256]{2,1,0:T(8,128)(2,1)S(1)} %copy-done.2, bf16[2,256,256]{2,1,0:T(8,128)(2,1)S(1)} %collective-permute-done.6.rest_0_, bf16[2,256,256]{2,1,0:T(8,128)(2,1)S(1)} %collective-permute-done.7.rest_1_, ...), custom_call_target="tpu_custom_call" | custom-call | flops 268435456 | bytes 4194304 | tf_op jit(solution)/shard_map/exchange_chunk/pallas_call | solution.py:117
  97.6 1.8 collective-permute-done.4.rest_1_
  99.4 5.6 %collective-permute-done.5.rest_2_ = bf16[2,256,256]{2,1,0:T(8,128)(2,1)S(1)} collective-permute-done((bf16[2,256,256]{2,1,0:T(8,128)(2,1)S(1)}, bf16[2,256,256]{2,1,0:T(8,128)(2,1)S(1)}, u32[]{:S(2)}, u32[]{:S(2)}) %collective-permute-start.5) | collective-permute-done | bytes 262176 | tf_op jit(solution)/shard_map/ppermute | solution.py:321
  105.0 3.8 %exchange_chunk.7.rest_0_ = bf16[8,256,256]{2,1,0:T(8,128)(2,1)S(1)} custom-call(s32[16]{0:T(128)S(1)} %multiply_add_fusion.slot_ref, s32[2]{0:T(128)S(1)} %bitcast.11, bf16[8,1024,256]{2,1,0:T(8,128)(2,1)S(1)} %copy-done.2, bf16[2,256,256]{2,1,0:T(8,128)(2,1)S(1)} %collective-permute-done.3.rest_0_, ...), custom_call_target="tpu_custom_call" | custom-call | flops 268435456 | bytes 4194304 | tf_op jit(solution)/shard_map/exchange_chunk/pallas_call | solution.py:117
  108.8 1.3 collective-permute-start.15
  110.4 22.7 %collective-permute-done.15.rest_1_ = bf16[8,256,256]{2,1,0:T(8,128)(2,1)S(1)} collective-permute-done((bf16[8,256,256]{2,1,0:T(8,128)(2,1)S(1)}, bf16[8,256,256]{2,1,0:T(8,128)(2,1)S(1)}, u32[]{:S(2)}, u32[]{:S(2)}) %collective-permute-start.15) | collective-permute-done | bytes 1048608 | tf_op jit(solution)/shard_map/ppermute | solution.py:329
  133.1 5.0 %amplitude_step.1 = (bf16[8,256,256]{2,1,0:T(8,128)(2,1)}, bf16[16,256,256]{2,1,0:T(8,128)(2,1)S(1)}) custom-call(f32[32]{0:T(128)S(1)} %pad_maximum_fusion.3.energy_ref, s32[16]{0:T(128)S(1)} %and_select_fusion.1.ends_ref, s32[8]{0:T(128)S(1)} %copy-done.4, f32[8,256,256]{2,1,0:T(8,128)S(1)} %copy-done.3, bf16[8,256,256]{2,1,0:T(8,128)(2,1)S(1)} %exchange_chunk.7.rest_0_, ...), custom_call_target="tpu_custom_call" | custom-call | flops 536870912 | bytes 7340032 | tf_op jit(solution)/shard_map/amplitude_step/pallas_call | solution.py:171
  138.2 4.2 %gradient_chunk.7 = (bf16[2,256,256]{2,1,0:T(8,128)(2,1)S(1)}, bf16[2,256,256]{2,1,0:T(8,128)(2,1)S(1)}, bf16[2,256,256]{2,1,0:T(8,128)(2,1)S(1)}, bf16[2,256,256]{2,1,0:T(8,128)(2,1)S(1)}) custom-call(s32[16]{0:T(128)S(1)} %multiply_add_fusion.slot_ref, s32[2]{0:T(128)S(1)} %bitcast.12, bf16[16,256,256]{2,1,0:T(8,128)(2,1)S(1)} %get-tuple-element.45.weight_ref, ...), custom_call_target="tpu_custom_call" | custom-call | flops 536870912 | bytes 4194304 | tf_op jit(solution)/shard_map/gradient_chunk/pallas_call | solution.py:212
  142.4 2.2 collective-permute-start.28
  144.6 1.3 collective-permute-start.30
  145.9 4.2 %gradient_chunk.6 = (bf16[2,256,256]{2,1,0:T(8,128)(2,1)S(1)}, bf16[2,256,256]{2,1,0:T(8,128)(2,1)S(1)}, bf16[2,256,256]{2,1,0:T(8,128)(2,1)S(1)}, bf16[2,256,256]{2,1,0:T(8,128)(2,1)S(1)}) custom-call(s32[16]{0:T(128)S(1)} %multiply_add_fusion.slot_ref, s32[2]{0:T(128)S(1)} %bitcast.13, bf16[16,256,256]{2,1,0:T(8,128)(2,1)S(1)} %get-tuple-element.45.weight_ref, ...), custom_call_target="tpu_custom_call" | custom-call | flops 536870912 | bytes 4194304 | tf_op jit(solution)/shard_map/gradient_chunk/pallas_call | solution.py:212
  150.1 0.3 collective-permute-start.24
  150.4 4.2 %collective-permute-start.25 = (bf16[2,256,256]{2,1,0:T(8,128)(2,1)S(1)}, bf16[2,256,256]{2,1,0:T(8,128)(2,1)S(1)}, u32[]{:S(2)}, u32[]{:S(2)}) collective-permute-start(bf16[2,256,256]{2,1,0:T(8,128)(2,1)S(1)} %get-tuple-element.56), channel_id=1, source_target_pairs={{0,8},{4,12},{8,0},{12,4},{1,9},{5,13},{9,1},{13,5},{2,10},{6,14},... | collective-permute-start | bytes 786440 | tf_op jit(solution)/shard_map/ppermute | solution.py:346
  154.6 4.2 %gradient_chunk.5 = (bf16[2,256,256]{2,1,0:T(8,128)(2,1)S(1)}, bf16[2,256,256]{2,1,0:T(8,128)(2,1)S(1)}, bf16[2,256,256]{2,1,0:T(8,128)(2,1)S(1)}, bf16[2,256,256]{2,1,0:T(8,128)(2,1)S(1)}) custom-call(s32[16]{0:T(128)S(1)} %multiply_add_fusion.slot_ref, s32[2]{0:T(128)S(1)} %bitcast.14, bf16[16,256,256]{2,1,0:T(8,128)(2,1)S(1)} %get-tuple-element.45.weight_ref, ...), custom_call_target="tpu_custom_call" | custom-call | flops 536870912 | bytes 4194304 | tf_op jit(solution)/shard_map/gradient_chunk/pallas_call | solution.py:212
  158.9 7.3 %collective-permute-done.29.rest_2_ = bf16[2,256,256]{2,1,0:T(8,128)(2,1)S(1)} collective-permute-done((bf16[2,256,256]{2,1,0:T(8,128)(2,1)S(1)}, bf16[2,256,256]{2,1,0:T(8,128)(2,1)S(1)}, u32[]{:S(2)}, u32[]{:S(2)}) %collective-permute-start.29) | collective-permute-done | bytes 262176 | tf_op jit(solution)/shard_map/ppermute | solution.py:346
  166.2 4.2 %gradient_chunk.4 = (bf16[2,256,256]{2,1,0:T(8,128)(2,1)S(1)}, bf16[2,256,256]{2,1,0:T(8,128)(2,1)S(1)}, bf16[2,256,256]{2,1,0:T(8,128)(2,1)S(1)}, bf16[2,256,256]{2,1,0:T(8,128)(2,1)S(1)}) custom-call(s32[16]{0:T(128)S(1)} %multiply_add_fusion.slot_ref, s32[2]{0:T(128)S(1)} %bitcast.15, bf16[16,256,256]{2,1,0:T(8,128)(2,1)S(1)} %get-tuple-element.45.weight_ref, ...), custom_call_target="tpu_custom_call" | custom-call | flops 536870912 | bytes 4194304 | tf_op jit(solution)/shard_map/gradient_chunk/pallas_call | solution.py:212
  170.5 7.7 %collective-permute-done.30.rest_3_ = bf16[2,256,256]{2,1,0:T(8,128)(2,1)S(1)} collective-permute-done((bf16[2,256,256]{2,1,0:T(8,128)(2,1)S(1)}, bf16[2,256,256]{2,1,0:T(8,128)(2,1)S(1)}, u32[]{:S(2)}, u32[]{:S(2)}) %collective-permute-start.30) | collective-permute-done | bytes 262176 | tf_op jit(solution)/shard_map/ppermute | solution.py:346
  178.2 8.3 %collective-permute-done.24.rest_1_ = bf16[2,256,256]{2,1,0:T(8,128)(2,1)S(1)} collective-permute-done((bf16[2,256,256]{2,1,0:T(8,128)(2,1)S(1)}, bf16[2,256,256]{2,1,0:T(8,128)(2,1)S(1)}, u32[]{:S(2)}, u32[]{:S(2)}) %collective-permute-start.24) | collective-permute-done | bytes 262176 | tf_op jit(solution)/shard_map/ppermute | solution.py:346
  186.5 13.0 %collective-permute-done.25.rest_2_ = bf16[2,256,256]{2,1,0:T(8,128)(2,1)S(1)} collective-permute-done((bf16[2,256,256]{2,1,0:T(8,128)(2,1)S(1)}, bf16[2,256,256]{2,1,0:T(8,128)(2,1)S(1)}, u32[]{:S(2)}, u32[]{:S(2)}) %collective-permute-start.25) | collective-permute-done | bytes 262176 | tf_op jit(solution)/shard_map/ppermute | solution.py:346
  199.6 3.0 %collective-permute-start.17 = (bf16[2,256,256]{2,1,0:T(8,128)(2,1)S(1)}, bf16[2,256,256]{2,1,0:T(8,128)(2,1)S(1)}, u32[]{:S(2)}, u32[]{:S(2)}) collective-permute-start(bf16[2,256,256]{2,1,0:T(8,128)(2,1)S(1)} %get-tuple-element.48), channel_id=1, source_target_pairs={{0,8},{4,12},{8,0},{12,4},{1,9},{5,13},{9,1},{13,5},{2,10},{6,14},... | collective-permute-start | bytes 786440 | tf_op jit(solution)/shard_map/ppermute | solution.py:346
  202.6 4.3 %collective-permute-done.20.rest_1_ = bf16[2,256,256]{2,1,0:T(8,128)(2,1)S(1)} collective-permute-done((bf16[2,256,256]{2,1,0:T(8,128)(2,1)S(1)}, bf16[2,256,256]{2,1,0:T(8,128)(2,1)S(1)}, u32[]{:S(2)}, u32[]{:S(2)}) %collective-permute-start.20) | collective-permute-done | bytes 262176 | tf_op jit(solution)/shard_map/ppermute | solution.py:346
  206.9 1.0 collect_chunk.7.mine_ref
  207.9 1.0 collect_chunk.6.mine_ref
  208.9 13.0 %collective-permute-done.21.rest_2_ = bf16[2,256,256]{2,1,0:T(8,128)(2,1)S(1)} collective-permute-done((bf16[2,256,256]{2,1,0:T(8,128)(2,1)S(1)}, bf16[2,256,256]{2,1,0:T(8,128)(2,1)S(1)}, u32[]{:S(2)}, u32[]{:S(2)}) %collective-permute-start.21) | collective-permute-done | bytes 262176 | tf_op jit(solution)/shard_map/ppermute | solution.py:346
  222.0 4.1 %collective-permute-start.31 = (bf16[8,256,256]{2,1,0:T(8,128)(2,1)S(1)}, bf16[8,256,256]{2,1,0:T(8,128)(2,1)S(1)}, u32[]{:S(2)}, u32[]{:S(2)}) collective-permute-start(bf16[8,256,256]{2,1,0:T(8,128)(2,1)S(1)} %collect_chunk.7.mine_ref), channel_id=1, source_target_pairs={{0,1},{1,0},{2,3},{3,2},{4,5},{5,4},{6,7},{7,6},{8,9},{9,8},{10,11... | collective-permute-start | bytes 3145736 | tf_op jit(solution)/shard_map/ppermute | solution.py:351
  226.1 1.0 collect_chunk.5.mine_ref
  227.1 0.5 collective-permute-done.16.rest_1_
  227.6 4.1 %collective-permute-start.23 = (bf16[8,256,256]{2,1,0:T(8,128)(2,1)S(1)}, bf16[8,256,256]{2,1,0:T(8,128)(2,1)S(1)}, u32[]{:S(2)}, u32[]{:S(2)}) collective-permute-start(bf16[8,256,256]{2,1,0:T(8,128)(2,1)S(1)} %collect_chunk.5.mine_ref), channel_id=1, source_target_pairs={{0,1},{1,0},{2,3},{3,2},{4,5},{5,4},{6,7},{7,6},{8,9},{9,8},{10,11... | collective-permute-start | bytes 3145736 | tf_op jit(solution)/shard_map/ppermute | solution.py:351
  231.7 1.5 collective-permute-done.17.rest_2_
  233.4 1.0 collect_chunk.4.mine_ref
  234.4 2.2 collective-permute-start.19
  236.5 2.0 add_chunk.4.rest_0_
  238.5 2.0 add_chunk.5.rest_0_
  240.5 2.0 add_chunk.6.rest_0_
  242.6 2.0 add_chunk.7
  (57 shorter events, 1.6 us)
Async XLA Ops:
  3.0 4.7 %collective-permute-start = (f32[10]{0:T(128)S(1)}, f32[10]{0:T(128)S(1)}, u32[]{:S(2)}, u32[]{:S(2)}) collective-permute-start(f32[10]{0:T(128)S(1)} %get-tuple-element.65), channel_id=1, source_target_pairs={{0,12},{4,0},{8,4},{12,8},{1,13},{5,1},{9,5},{13,9},{2,14},{6,2},{... | collective-permute-start | bytes 128 | tf_op jit(solution)/shard_map/ppermute | solution.py:308
  3.0 4.7 %collective-permute-start.1 = (f32[10]{0:T(128)S(1)}, f32[10]{0:T(128)S(1)}, u32[]{:S(2)}, u32[]{:S(2)}) collective-permute-start(f32[10]{0:T(128)S(1)} %get-tuple-element.66), channel_id=1, source_target_pairs={{0,8},{4,12},{8,0},{12,4},{1,9},{5,13},{9,1},{13,5},{2,10},{6,14},... | collective-permute-start | bytes 128 | tf_op jit(solution)/shard_map/ppermute | solution.py:308
  5.5 2.9 %collective-permute-start.2 = (f32[10]{0:T(128)S(1)}, f32[10]{0:T(128)S(1)}, u32[]{:S(2)}, u32[]{:S(2)}) collective-permute-start(f32[10]{0:T(128)S(1)} %get-tuple-element.67), channel_id=1, source_target_pairs={{0,4},{4,8},{8,12},{12,0},{1,5},{5,9},{9,13},{13,1},{2,6},{6,10},{... | collective-permute-start | bytes 128 | tf_op jit(solution)/shard_map/ppermute | solution.py:308
  8.4 2.2 copy-start
  12.3 9.0 %collective-permute-start.12 = (bf16[2,256,256]{2,1,0:T(8,128)(2,1)S(1)}, bf16[2,256,256]{2,1,0:T(8,128)(2,1)S(1)}, u32[]{:S(2)}, u32[]{:S(2)}) collective-permute-start(bf16[2,256,256]{2,1,0:T(8,128)(2,1)S(1)} %get-tuple-element.41), channel_id=1, source_target_pairs={{0,12},{4,0},{8,4},{12,8},{1,13},{5,1},{9,5},{13,9},{2,14},{6,2},{... | collective-permute-start | bytes 786440 | tf_op jit(solution)/shard_map/ppermute | solution.py:321
  14.6 19.2 %collective-permute-start.13 = (bf16[2,256,256]{2,1,0:T(8,128)(2,1)S(1)}, bf16[2,256,256]{2,1,0:T(8,128)(2,1)S(1)}, u32[]{:S(2)}, u32[]{:S(2)}) collective-permute-start(bf16[2,256,256]{2,1,0:T(8,128)(2,1)S(1)} %get-tuple-element.42), channel_id=1, source_target_pairs={{0,8},{4,12},{8,0},{12,4},{1,9},{5,13},{9,1},{13,5},{2,10},{6,14},... | collective-permute-start | bytes 786440 | tf_op jit(solution)/shard_map/ppermute | solution.py:321
  15.2 35.4 %collective-permute-start.14 = (bf16[2,256,256]{2,1,0:T(8,128)(2,1)S(1)}, bf16[2,256,256]{2,1,0:T(8,128)(2,1)S(1)}, u32[]{:S(2)}, u32[]{:S(2)}) collective-permute-start(bf16[2,256,256]{2,1,0:T(8,128)(2,1)S(1)} %get-tuple-element.43), channel_id=1, source_target_pairs={{0,4},{4,8},{8,12},{12,0},{1,5},{5,9},{9,13},{13,1},{2,6},{6,10},{... | collective-permute-start | bytes 786440 | tf_op jit(solution)/shard_map/ppermute | solution.py:321
  17.7 48.0 %collective-permute-start.10 = (bf16[2,256,256]{2,1,0:T(8,128)(2,1)}, bf16[2,256,256]{2,1,0:T(8,128)(2,1)S(1)}, u32[]{:S(2)}, u32[]{:S(2)}) collective-permute-start(bf16[2,256,256]{2,1,0:T(8,128)(2,1)} %get-tuple-element.39), channel_id=1, source_target_pairs={{0,8},{4,12},{8,0},{12,4},{1,9},{5,13},{9,1},{13,5},{2,10},{6,14},... | collective-permute-start | bytes 786440 | tf_op jit(solution)/shard_map/ppermute | solution.py:321
  20.7 50.5 %collective-permute-start.11 = (bf16[2,256,256]{2,1,0:T(8,128)(2,1)S(1)}, bf16[2,256,256]{2,1,0:T(8,128)(2,1)S(1)}, u32[]{:S(2)}, u32[]{:S(2)}) collective-permute-start(bf16[2,256,256]{2,1,0:T(8,128)(2,1)S(1)} %get-tuple-element.40), channel_id=1, source_target_pairs={{0,4},{4,8},{8,12},{12,0},{1,5},{5,9},{9,13},{13,1},{2,6},{6,10},{... | collective-permute-start | bytes 786440 | tf_op jit(solution)/shard_map/ppermute | solution.py:321
  21.3 50.0 %collective-permute-start.9 = (bf16[2,256,256]{2,1,0:T(8,128)(2,1)S(1)}, bf16[2,256,256]{2,1,0:T(8,128)(2,1)S(1)}, u32[]{:S(2)}, u32[]{:S(2)}) collective-permute-start(bf16[2,256,256]{2,1,0:T(8,128)(2,1)S(1)} %get-tuple-element.38), channel_id=1, source_target_pairs={{0,12},{4,0},{8,4},{12,8},{1,13},{5,1},{9,5},{13,9},{2,14},{6,2},{... | collective-permute-start | bytes 786440 | tf_op jit(solution)/shard_map/ppermute | solution.py:321
  33.8 40.8 %collective-permute-start.6 = (bf16[2,256,256]{2,1,0:T(8,128)(2,1)S(1)}, bf16[2,256,256]{2,1,0:T(8,128)(2,1)S(1)}, u32[]{:S(2)}, u32[]{:S(2)}) collective-permute-start(bf16[2,256,256]{2,1,0:T(8,128)(2,1)S(1)} %get-tuple-element.35), channel_id=1, source_target_pairs={{0,12},{4,0},{8,4},{12,8},{1,13},{5,1},{9,5},{13,9},{2,14},{6,2},{... | collective-permute-start | bytes 786440 | tf_op jit(solution)/shard_map/ppermute | solution.py:321
  46.7 2.2 copy-start.1
  48.9 25.7 %copy-start.2 = (bf16[8,1024,256]{2,1,0:T(8,128)(2,1)S(1)}, bf16[8,1024,256]{2,1,0:T(8,128)(2,1)}, u32[]{:S(2)}) copy-start(bf16[8,1024,256]{2,1,0:T(8,128)(2,1)} %blocks_ref.23) | copy-start | bytes 12582916
  50.6 37.6 %collective-permute-start.7 = (bf16[2,256,256]{2,1,0:T(8,128)(2,1)S(1)}, bf16[2,256,256]{2,1,0:T(8,128)(2,1)S(1)}, u32[]{:S(2)}, u32[]{:S(2)}) collective-permute-start(bf16[2,256,256]{2,1,0:T(8,128)(2,1)S(1)} %get-tuple-element.36), channel_id=1, source_target_pairs={{0,8},{4,12},{8,0},{12,4},{1,9},{5,13},{9,1},{13,5},{2,10},{6,14},... | collective-permute-start | bytes 786440 | tf_op jit(solution)/shard_map/ppermute | solution.py:321
  65.7 28.1 %collective-permute-start.8 = (bf16[2,256,256]{2,1,0:T(8,128)(2,1)S(1)}, bf16[2,256,256]{2,1,0:T(8,128)(2,1)S(1)}, u32[]{:S(2)}, u32[]{:S(2)}) collective-permute-start(bf16[2,256,256]{2,1,0:T(8,128)(2,1)S(1)} %get-tuple-element.37), channel_id=1, source_target_pairs={{0,4},{4,8},{8,12},{12,0},{1,5},{5,9},{9,13},{13,1},{2,6},{6,10},{... | collective-permute-start | bytes 786440 | tf_op jit(solution)/shard_map/ppermute | solution.py:321
  71.2 26.4 %collective-permute-start.3 = (bf16[2,256,256]{2,1,0:T(8,128)(2,1)S(1)}, bf16[2,256,256]{2,1,0:T(8,128)(2,1)S(1)}, u32[]{:S(2)}, u32[]{:S(2)}) collective-permute-start(bf16[2,256,256]{2,1,0:T(8,128)(2,1)S(1)} %get-tuple-element.32), channel_id=1, source_target_pairs={{0,12},{4,0},{8,4},{12,8},{1,13},{5,1},{9,5},{13,9},{2,14},{6,2},{... | collective-permute-start | bytes 786440 | tf_op jit(solution)/shard_map/ppermute | solution.py:321
  71.2 28.2 %collective-permute-start.4 = (bf16[2,256,256]{2,1,0:T(8,128)(2,1)S(1)}, bf16[2,256,256]{2,1,0:T(8,128)(2,1)S(1)}, u32[]{:S(2)}, u32[]{:S(2)}) collective-permute-start(bf16[2,256,256]{2,1,0:T(8,128)(2,1)S(1)} %get-tuple-element.33), channel_id=1, source_target_pairs={{0,8},{4,12},{8,0},{12,4},{1,9},{5,13},{9,1},{13,5},{2,10},{6,14},... | collective-permute-start | bytes 786440 | tf_op jit(solution)/shard_map/ppermute | solution.py:321
  74.6 30.4 %collective-permute-start.5 = (bf16[2,256,256]{2,1,0:T(8,128)(2,1)S(1)}, bf16[2,256,256]{2,1,0:T(8,128)(2,1)S(1)}, u32[]{:S(2)}, u32[]{:S(2)}) collective-permute-start(bf16[2,256,256]{2,1,0:T(8,128)(2,1)S(1)} %get-tuple-element.34), channel_id=1, source_target_pairs={{0,4},{4,8},{8,12},{12,0},{1,5},{5,9},{9,13},{13,1},{2,6},{6,10},{... | collective-permute-start | bytes 786440 | tf_op jit(solution)/shard_map/ppermute | solution.py:321
  97.6 35.5 %copy-start.3 = (f32[8,256,256]{2,1,0:T(8,128)S(1)}, f32[8,256,256]{2,1,0:T(8,128)}, u32[]{:S(2)}) copy-start(f32[8,256,256]{2,1,0:T(8,128)} %fock_ref.1) | copy-start | bytes 6291460
  97.6 35.5 %copy-start.4 = (s32[8]{0:T(128)S(1)}, s32[8]{0:T(128)}, u32[]{:S(2)}) copy-start(s32[8]{0:T(128)} %size_ref.1) | copy-start | bytes 100
  108.8 24.3 %collective-permute-start.15 = (bf16[8,256,256]{2,1,0:T(8,128)(2,1)S(1)}, bf16[8,256,256]{2,1,0:T(8,128)(2,1)S(1)}, u32[]{:S(2)}, u32[]{:S(2)}) collective-permute-start(bf16[8,256,256]{2,1,0:T(8,128)(2,1)S(1)} %exchange_chunk.7.rest_0_), channel_id=1, source_target_pairs={{0,2},{2,0},{1,3},{3,1},{4,6},{6,4},{5,7},{7,5},{8,10},{10,8},{9,1... | collective-permute-start | bytes 3145736 | tf_op jit(solution)/shard_map/ppermute | solution.py:329
  142.4 16.4 %collective-permute-start.28 = (bf16[2,256,256]{2,1,0:T(8,128)(2,1)S(1)}, bf16[2,256,256]{2,1,0:T(8,128)(2,1)S(1)}, u32[]{:S(2)}, u32[]{:S(2)}) collective-permute-start(bf16[2,256,256]{2,1,0:T(8,128)(2,1)S(1)} %get-tuple-element.59), channel_id=1, source_target_pairs={{0,4},{4,8},{8,12},{12,0},{1,5},{5,9},{9,13},{13,1},{2,6},{6,10},{... | collective-permute-start | bytes 786440 | tf_op jit(solution)/shard_map/ppermute | solution.py:346
  144.6 21.6 %collective-permute-start.29 = (bf16[2,256,256]{2,1,0:T(8,128)(2,1)S(1)}, bf16[2,256,256]{2,1,0:T(8,128)(2,1)S(1)}, u32[]{:S(2)}, u32[]{:S(2)}) collective-permute-start(bf16[2,256,256]{2,1,0:T(8,128)(2,1)S(1)} %get-tuple-element.60), channel_id=1, source_target_pairs={{0,8},{4,12},{8,0},{12,4},{1,9},{5,13},{9,1},{13,5},{2,10},{6,14},... | collective-permute-start | bytes 786440 | tf_op jit(solution)/shard_map/ppermute | solution.py:346
  144.6 33.5 %collective-permute-start.30 = (bf16[2,256,256]{2,1,0:T(8,128)(2,1)S(1)}, bf16[2,256,256]{2,1,0:T(8,128)(2,1)S(1)}, u32[]{:S(2)}, u32[]{:S(2)}) collective-permute-start(bf16[2,256,256]{2,1,0:T(8,128)(2,1)S(1)} %get-tuple-element.61), channel_id=1, source_target_pairs={{0,12},{4,0},{8,4},{12,8},{1,13},{5,1},{9,5},{13,9},{2,14},{6,2},{... | collective-permute-start | bytes 786440 | tf_op jit(solution)/shard_map/ppermute | solution.py:346
  150.1 36.4 %collective-permute-start.24 = (bf16[2,256,256]{2,1,0:T(8,128)(2,1)S(1)}, bf16[2,256,256]{2,1,0:T(8,128)(2,1)S(1)}, u32[]{:S(2)}, u32[]{:S(2)}) collective-permute-start(bf16[2,256,256]{2,1,0:T(8,128)(2,1)S(1)} %get-tuple-element.55), channel_id=1, source_target_pairs={{0,4},{4,8},{8,12},{12,0},{1,5},{5,9},{9,13},{13,1},{2,6},{6,10},{... | collective-permute-start | bytes 786440 | tf_op jit(solution)/shard_map/ppermute | solution.py:346
  150.4 49.1 %collective-permute-start.25 = (bf16[2,256,256]{2,1,0:T(8,128)(2,1)S(1)}, bf16[2,256,256]{2,1,0:T(8,128)(2,1)S(1)}, u32[]{:S(2)}, u32[]{:S(2)}) collective-permute-start(bf16[2,256,256]{2,1,0:T(8,128)(2,1)S(1)} %get-tuple-element.56), channel_id=1, source_target_pairs={{0,8},{4,12},{8,0},{12,4},{1,9},{5,13},{9,1},{13,5},{2,10},{6,14},... | collective-permute-start | bytes 786440 | tf_op jit(solution)/shard_map/ppermute | solution.py:346
  158.8 40.8 %collective-permute-start.26 = (bf16[2,256,256]{2,1,0:T(8,128)(2,1)S(1)}, bf16[2,256,256]{2,1,0:T(8,128)(2,1)S(1)}, u32[]{:S(2)}, u32[]{:S(2)}) collective-permute-start(bf16[2,256,256]{2,1,0:T(8,128)(2,1)S(1)} %get-tuple-element.57), channel_id=1, source_target_pairs={{0,12},{4,0},{8,4},{12,8},{1,13},{5,1},{9,5},{13,9},{2,14},{6,2},{... | collective-permute-start | bytes 786440 | tf_op jit(solution)/shard_map/ppermute | solution.py:346
  166.2 40.7 %collective-permute-start.20 = (bf16[2,256,256]{2,1,0:T(8,128)(2,1)S(1)}, bf16[2,256,256]{2,1,0:T(8,128)(2,1)S(1)}, u32[]{:S(2)}, u32[]{:S(2)}) collective-permute-start(bf16[2,256,256]{2,1,0:T(8,128)(2,1)S(1)} %get-tuple-element.51), channel_id=1, source_target_pairs={{0,4},{4,8},{8,12},{12,0},{1,5},{5,9},{9,13},{13,1},{2,6},{6,10},{... | collective-permute-start | bytes 786440 | tf_op jit(solution)/shard_map/ppermute | solution.py:346
  178.2 43.8 %collective-permute-start.21 = (bf16[2,256,256]{2,1,0:T(8,128)(2,1)S(1)}, bf16[2,256,256]{2,1,0:T(8,128)(2,1)S(1)}, u32[]{:S(2)}, u32[]{:S(2)}) collective-permute-start(bf16[2,256,256]{2,1,0:T(8,128)(2,1)S(1)} %get-tuple-element.52), channel_id=1, source_target_pairs={{0,8},{4,12},{8,0},{12,4},{1,9},{5,13},{9,1},{13,5},{2,10},{6,14},... | collective-permute-start | bytes 786440 | tf_op jit(solution)/shard_map/ppermute | solution.py:346
  186.5 39.6 %collective-permute-start.22 = (bf16[2,256,256]{2,1,0:T(8,128)(2,1)S(1)}, bf16[2,256,256]{2,1,0:T(8,128)(2,1)S(1)}, u32[]{:S(2)}, u32[]{:S(2)}) collective-permute-start(bf16[2,256,256]{2,1,0:T(8,128)(2,1)S(1)} %get-tuple-element.53), channel_id=1, source_target_pairs={{0,12},{4,0},{8,4},{12,8},{1,13},{5,1},{9,5},{13,9},{2,14},{6,2},{... | collective-permute-start | bytes 786440 | tf_op jit(solution)/shard_map/ppermute | solution.py:346
  199.5 28.1 %collective-permute-start.16 = (bf16[2,256,256]{2,1,0:T(8,128)(2,1)S(1)}, bf16[2,256,256]{2,1,0:T(8,128)(2,1)S(1)}, u32[]{:S(2)}, u32[]{:S(2)}) collective-permute-start(bf16[2,256,256]{2,1,0:T(8,128)(2,1)S(1)} %get-tuple-element.47), channel_id=1, source_target_pairs={{0,4},{4,8},{8,12},{12,0},{1,5},{5,9},{9,13},{13,1},{2,6},{6,10},{... | collective-permute-start | bytes 786440 | tf_op jit(solution)/shard_map/ppermute | solution.py:346
  199.6 33.6 %collective-permute-start.17 = (bf16[2,256,256]{2,1,0:T(8,128)(2,1)S(1)}, bf16[2,256,256]{2,1,0:T(8,128)(2,1)S(1)}, u32[]{:S(2)}, u32[]{:S(2)}) collective-permute-start(bf16[2,256,256]{2,1,0:T(8,128)(2,1)S(1)} %get-tuple-element.48), channel_id=1, source_target_pairs={{0,8},{4,12},{8,0},{12,4},{1,9},{5,13},{9,1},{13,5},{2,10},{6,14},... | collective-permute-start | bytes 786440 | tf_op jit(solution)/shard_map/ppermute | solution.py:346
  206.9 26.5 %collective-permute-start.18 = (bf16[2,256,256]{2,1,0:T(8,128)(2,1)S(1)}, bf16[2,256,256]{2,1,0:T(8,128)(2,1)S(1)}, u32[]{:S(2)}, u32[]{:S(2)}) collective-permute-start(bf16[2,256,256]{2,1,0:T(8,128)(2,1)S(1)} %get-tuple-element.49), channel_id=1, source_target_pairs={{0,12},{4,0},{8,4},{12,8},{1,13},{5,1},{9,5},{13,9},{2,14},{6,2},{... | collective-permute-start | bytes 786440 | tf_op jit(solution)/shard_map/ppermute | solution.py:346
  222.0 14.6 %collective-permute-start.31 = (bf16[8,256,256]{2,1,0:T(8,128)(2,1)S(1)}, bf16[8,256,256]{2,1,0:T(8,128)(2,1)S(1)}, u32[]{:S(2)}, u32[]{:S(2)}) collective-permute-start(bf16[8,256,256]{2,1,0:T(8,128)(2,1)S(1)} %collect_chunk.7.mine_ref), channel_id=1, source_target_pairs={{0,1},{1,0},{2,3},{3,2},{4,5},{5,4},{6,7},{7,6},{8,9},{9,8},{10,11... | collective-permute-start | bytes 3145736 | tf_op jit(solution)/shard_map/ppermute | solution.py:351
  226.1 12.4 %collective-permute-start.27 = (bf16[8,256,256]{2,1,0:T(8,128)(2,1)S(1)}, bf16[8,256,256]{2,1,0:T(8,128)(2,1)S(1)}, u32[]{:S(2)}, u32[]{:S(2)}) collective-permute-start(bf16[8,256,256]{2,1,0:T(8,128)(2,1)S(1)} %collect_chunk.6.mine_ref), channel_id=1, source_target_pairs={{0,1},{1,0},{2,3},{3,2},{4,5},{5,4},{6,7},{7,6},{8,9},{9,8},{10,11... | collective-permute-start | bytes 3145736 | tf_op jit(solution)/shard_map/ppermute | solution.py:351
  227.6 13.0 %collective-permute-start.23 = (bf16[8,256,256]{2,1,0:T(8,128)(2,1)S(1)}, bf16[8,256,256]{2,1,0:T(8,128)(2,1)S(1)}, u32[]{:S(2)}, u32[]{:S(2)}) collective-permute-start(bf16[8,256,256]{2,1,0:T(8,128)(2,1)S(1)} %collect_chunk.5.mine_ref), channel_id=1, source_target_pairs={{0,1},{1,0},{2,3},{3,2},{4,5},{5,4},{6,7},{7,6},{8,9},{9,8},{10,11... | collective-permute-start | bytes 3145736 | tf_op jit(solution)/shard_map/ppermute | solution.py:351
  234.4 8.2 %collective-permute-start.19 = (bf16[8,256,256]{2,1,0:T(8,128)(2,1)S(1)}, bf16[8,256,256]{2,1,0:T(8,128)(2,1)S(1)}, u32[]{:S(2)}, u32[]{:S(2)}) collective-permute-start(bf16[8,256,256]{2,1,0:T(8,128)(2,1)S(1)} %collect_chunk.4.mine_ref), channel_id=1, source_target_pairs={{0,1},{1,0},{2,3},{3,2},{4,5},{5,4},{6,7},{7,6},{8,9},{9,8},{10,11... | collective-permute-start | bytes 3145736 | tf_op jit(solution)/shard_map/ppermute | solution.py:351

commit v3 on v2

v3 whole, which is shorter than its diff:
```python
import functools
from typing import NamedTuple

import jax
import jax.numpy as jnp
from jax import lax
from jax.experimental import pallas as pl
from jax.experimental.pallas import tpu as pltpu
from jax.sharding import PartitionSpec as P

CAP = 2
FORWARD_ROWS = (21, 16, 12, 9, 6)
BACK_ROWS = (14, 14, 15, 15)
BACK_GROUPS = (2, 3, 4, 5)
SETTLE_WEIGHT = 50
MERGE_WEIGHT = 50
EXCHANGE_WEIGHT = 50
VMEM_LIMIT = 40 * 1024 * 1024

F32 = jnp.float32
BF16 = jnp.bfloat16

ANY = pl.BlockSpec(memory_space=pl.ANY)
SMEM = pl.BlockSpec(memory_space=pltpu.SMEM)
VMEM = pl.BlockSpec(memory_space=pltpu.VMEM)


def params():
    return pltpu.CompilerParams(vmem_limit_bytes=VMEM_LIMIT)


def cost(flops, nbytes):
    return pl.CostEstimate(flops=int(flops), bytes_accessed=int(nbytes), transcendentals=0)


def weighed(times, flops, nbytes):
    return cost(times * flops, times * nbytes)


def shifted(n, d):
    return [(s, (s + d) % n) for s in range(n)]


def pick_kernel(start, rows, waits, index_ref, blocks_ref, *rest):
    outs, sems = rest[waits:-1], rest[-1]
    copies = []
    for d, out in enumerate(outs):
        for k in range(CAP):
            copies.append(
                pltpu.make_async_copy(
                    blocks_ref.at[index_ref[d, k], pl.ds(start, rows)],
                    out.at[k],
                    sems.at[d * CAP + k],
                )
            )
    for c in copies:
        c.start()
    for c in copies:
        c.wait()


def pick_blocks(index, blocks, start, rows, after=()):
    count = index.shape[0]
    virt = blocks.shape[2]
    shape = jax.ShapeDtypeStruct((CAP, rows, virt), BF16)
    return pl.pallas_call(
        functools.partial(pick_kernel, start, rows, len(after)),
        out_shape=[shape] * count,
        in_specs=[SMEM, ANY] + [ANY] * len(after),
        out_specs=[ANY] * count,
        scratch_shapes=[pltpu.SemaphoreType.DMA((count * CAP,))],
        compiler_params=params(),
        cost_estimate=cost(0, 2 * count * CAP * rows * virt * 2),
        name="pick_blocks",
    )(index, blocks, *after)


def merge_kernel(count, *refs):
    sources, out, sems = refs[:count], refs[-2], refs[-1]
    copies = [
        pltpu.make_async_copy(ref, out.at[pl.ds(d * CAP, CAP)], sems.at[d])
        for d, ref in enumerate(sources)
    ]
    for c in copies:
        c.start()
    for c in copies:
        c.wait()


def merge_chunk(arrived, after=()):
    count = len(arrived)
    _, rows, virt = arrived[0].shape
    return pl.pallas_call(
        functools.partial(merge_kernel, count),
        out_shape=jax.ShapeDtypeStruct((count * CAP, rows, virt), BF16),
        in_specs=[ANY] * (count + len(after)),
        out_specs=ANY,
        scratch_shapes=[pltpu.SemaphoreType.DMA((count,))],
        compiler_params=params(),
        cost_estimate=weighed(MERGE_WEIGHT, 0, 4 * count * CAP * rows * virt),
        name="merge_chunk",
    )(*arrived, *after)


class Rows(NamedTuple):
    start: int
    count: int


def load_all(fit_ref, chunks, mine, merged, held, sems):
    n_fit = len(mine)
    total = sum(c.count for c in chunks)
    copies = []
    for f in range(n_fit):
        place = lax.rem(fit_ref[0] + (n_fit - f), n_fit)
        at = 0
        for i, c in enumerate(chunks):
            rows = pl.ds(pl.multiple_of(place * total + at, 16), c.count)
            copies.append(
                pltpu.make_async_copy(
                    mine[f].at[:, pl.ds(c.start, c.count)],
                    held.at[pl.ds(0, CAP), rows],
                    sems.at[len(copies)],
                )
            )
            copies.append(
                pltpu.make_async_copy(
                    merged[i][f],
                    held.at[pl.ds(CAP, held.shape[0] - CAP), rows],
                    sems.at[len(copies)],
                )
            )
            at += c.count
    for c in copies:
        c.start()
    return copies


def cross(left, right):
    return lax.dot_general(left, right, (((0,), (0,)), ((), ())), preferred_element_type=F32)


def split_refs(rest, n_fit, chunks):
    mine, rest = rest[:n_fit], rest[n_fit:]
    merged = []
    for _ in chunks:
        merged.append(rest[:n_fit])
        rest = rest[n_fit:]
    return mine, merged, rest


def exchange_kernel(chunks, n_fit, first, waits, slot_ref, fit_ref, *rest):
    mine, merged, rest = split_refs(rest[waits:], n_fit, chunks)
    if not first:
        before_ref, rest = rest[0], rest[1:]
    out_ref, held, sems = rest
    for c in load_all(fit_ref, chunks, mine, merged, held, sems):
        c.wait()

    def step(p, carry):
        product = cross(held[slot_ref[2 * p]], held[slot_ref[2 * p + 1]])
        if not first:
            product = before_ref[p] + product
        out_ref[p] = product
        return carry

    lax.fori_loop(0, out_ref.shape[0], step, 0)


def exchange_chunks(slots, fit, chunks, mine, merged, before, after=()):
    n_fit = len(mine)
    pairs = slots.shape[0] // 2
    virt = mine[0].shape[2]
    all_slots = CAP + merged[0][0].shape[0]
    rows = sum(c.count for c in chunks) * n_fit
    first = before is None
    return pl.pallas_call(
        functools.partial(exchange_kernel, chunks, n_fit, first, len(after)),
        out_shape=jax.ShapeDtypeStruct((pairs, virt, virt), F32),
        in_specs=[SMEM, SMEM]
        + [ANY] * (len(after) + n_fit * (1 + len(chunks)))
        + ([] if first else [VMEM]),
        out_specs=VMEM,
        scratch_shapes=[
            pltpu.VMEM((all_slots, rows, virt), BF16),
            pltpu.SemaphoreType.DMA((2 * n_fit * len(chunks),)),
        ],
        compiler_params=params(),
        cost_estimate=weighed(EXCHANGE_WEIGHT,
            2 * pairs * rows * virt * virt, all_slots * rows * virt * 2 + pairs * virt * virt * 8
        ),
        name="exchange_chunks",
    )(slots, fit, *after, *mine, *[x for m in merged for x in m], *([] if first else [before]))


def prepare_kernel(energy_ref, ends_ref, size_ref, fock_ref, inverse_ref, off_ref):
    p = pl.program_id(0)
    virt = fock_ref.shape[-1]
    occ = energy_ref[ends_ref[2 * p]] + energy_ref[ends_ref[2 * p + 1]]
    size = size_ref[p]
    fock = fock_ref[0]
    row = lax.broadcasted_iota(jnp.int32, (virt, virt), 0)
    col = lax.broadcasted_iota(jnp.int32, (virt, virt), 1)
    on_diagonal = row == col
    diagonal = jnp.where(on_diagonal, fock, 0.0)
    denominator = (
        jnp.sum(diagonal, axis=1, keepdims=True) + jnp.sum(diagonal, axis=0, keepdims=True) - occ
    )
    inverse_ref[0] = jnp.where((row < size) & (col < size), 1.0 / denominator, 0.0)
    off_ref[0] = jnp.where(on_diagonal, 0.0, fock).astype(BF16)


def prepare_pairs(energies, ends, sizes, fock):
    pairs, virt, _ = fock.shape
    block = pl.BlockSpec((1, virt, virt), lambda p: (p, 0, 0))
    return pl.pallas_call(
        prepare_kernel,
        grid=(pairs,),
        out_shape=[
            jax.ShapeDtypeStruct((pairs, virt, virt), F32),
            jax.ShapeDtypeStruct((pairs, virt, virt), BF16),
        ],
        in_specs=[SMEM, SMEM, SMEM, block],
        out_specs=[block, block],
        compiler_params=params(),
        cost_estimate=cost(10 * pairs * virt * virt, pairs * virt * virt * 10),
        name="prepare_pairs",
    )(energies, ends, sizes, fock)


def add_gradients(slot_ref, weight_ref, block_of, sums, outs):
    sums[...] = jnp.zeros_like(sums)

    def step(p, carry):
        left = slot_ref[2 * p]
        right = slot_ref[2 * p + 1]
        sums[left] += jnp.dot(block_of(right), weight_ref[2 * p], preferred_element_type=F32)
        sums[right] += jnp.dot(block_of(left), weight_ref[2 * p + 1], preferred_element_type=F32)
        return carry

    lax.fori_loop(0, weight_ref.shape[0] // 2, step, 0)
    for d, out in enumerate(outs):
        for k in range(CAP):
            out[k] = sums[d * CAP + k].astype(BF16)


def middle_kernel(chunk, n, n_fit, slot_ref, fit_ref, *rest):
    mine, merged, rest = split_refs(rest, n_fit, [chunk])
    before_ref, inverse_ref, off_ref, amp_ref, weight_ref = rest[:5]
    outs = rest[5 : 5 + n]
    held, sums, sems = rest[5 + n :]
    for c in load_all(fit_ref, [chunk], mine, merged, held, sems):
        c.wait()

    def step(p, carry):
        total = before_ref[p] + cross(held[slot_ref[2 * p]], held[slot_ref[2 * p + 1]])
        inverse = inverse_ref[p]
        off = off_ref[p]
        current = -total * inverse
        rounded = current.astype(BF16)
        change = jnp.dot(off, rounded, preferred_element_type=F32) + jnp.dot(
            rounded, off, preferred_element_type=F32
        )
        amp = (current - change * inverse).astype(BF16)
        amp_ref[p] = amp
        wide = amp.astype(F32)
        flipped = wide.T
        weight_ref[2 * p] = (2.0 * flipped - wide).astype(BF16)
        weight_ref[2 * p + 1] = (2.0 * wide - flipped).astype(BF16)
        return carry

    lax.fori_loop(0, amp_ref.shape[0], step, 0, unroll=2)
    here = pl.ds(pl.multiple_of(fit_ref[0] * chunk.count, 16), chunk.count)
    add_gradients(slot_ref, weight_ref, lambda s: held[s, here], sums, outs)


def middle_step(slots, fit, chunk, mine, merged, before, inverse, off):
    n_fit = len(mine)
    pairs, virt, _ = before.shape
    all_slots = CAP + merged[0].shape[0]
    n = all_slots // CAP
    return pl.pallas_call(
        functools.partial(middle_kernel, chunk, n, n_fit),
        out_shape=[
            jax.ShapeDtypeStruct((pairs, virt, virt), BF16),
            jax.ShapeDtypeStruct((2 * pairs, virt, virt), BF16),
        ]
        + [jax.ShapeDtypeStruct((CAP, chunk.count, virt), BF16)] * n,
        in_specs=[SMEM, SMEM] + [ANY] * (2 * n_fit) + [VMEM] * 3,
        out_specs=[VMEM] * (2 + n),
        scratch_shapes=[
            pltpu.VMEM((all_slots, n_fit * chunk.count, virt), BF16),
            pltpu.VMEM((all_slots, chunk.count, virt), F32),
            pltpu.SemaphoreType.DMA((2 * n_fit,)),
        ],
        compiler_params=params(),
        cost_estimate=cost(
            pairs * (4 * virt**3 + 6 * chunk.count * n_fit * virt * virt),
            pairs * virt * virt * 16,
        ),
        name="middle_step",
    )(slots, fit, *mine, *merged, before, inverse, off)


def gradient_kernel(parts, n, slot_ref, weight_ref, mine_ref, *rest):
    merged = rest[: len(parts)]
    held, sums, sems = rest[-3:]
    outs = rest[-3 - n : -3]
    copies = []
    at = 0
    for (start, offset, rows), ref in zip(parts, merged):
        to = pl.ds(at, rows)
        copies.append(
            pltpu.make_async_copy(
                mine_ref.at[:, pl.ds(start, rows)],
                held.at[pl.ds(0, CAP), to],
                sems.at[len(copies)],
            )
        )
        copies.append(
            pltpu.make_async_copy(
                ref.at[:, pl.ds(offset, rows)],
                held.at[pl.ds(CAP, held.shape[0] - CAP), to],
                sems.at[len(copies)],
            )
        )
        at += rows
    for c in copies:
        c.start()
    for c in copies:
        c.wait()
    add_gradients(slot_ref, weight_ref, lambda s: held[s], sums, outs)


def gradient_chunk(slots, weights, mine, parts, merged, after):
    ends = slots.shape[0]
    virt = mine.shape[2]
    all_slots = CAP + merged[0].shape[0]
    n = all_slots // CAP
    rows = sum(p[2] for p in parts)
    return pl.pallas_call(
        functools.partial(gradient_kernel, parts, n),
        out_shape=[jax.ShapeDtypeStruct((CAP, rows, virt), BF16)] * n,
        in_specs=[SMEM, VMEM, ANY] + [ANY] * (len(parts) + len(after)),
        out_specs=[VMEM] * n,
        scratch_shapes=[
            pltpu.VMEM((all_slots, rows, virt), BF16),
            pltpu.VMEM((all_slots, rows, virt), F32),
            pltpu.SemaphoreType.DMA((2 * len(parts),)),
        ],
        compiler_params=params(),
        cost_estimate=cost(
            2 * ends * rows * virt * virt, 4 * all_slots * rows * virt + ends * virt * virt * 2
        ),
        name="gradient_chunk",
    )(slots, weights, mine, *merged, *after)


def settle_kernel(shape, index_ref, *rest):
    out_ref, sums = rest[-2:]
    sums[...] = jnp.zeros_like(sums)
    at = 0
    for count in shape:
        rows = pl.ds(at, rest[0].shape[1])
        at += rest[0].shape[1]
        for d, ref in enumerate(rest[:count]):
            for k in range(CAP):
                g = index_ref[d, k]
                sums[g, rows] += ref[k].astype(F32)
        rest = rest[count:]
    out_ref[...] = sums[...].astype(BF16)


def settle_chunks(index, returned, local_orbs, after=()):
    rows = sum(r[0].shape[1] for r in returned)
    virt = returned[0][0].shape[2]
    terms = [x for r in returned for x in r]
    return pl.pallas_call(
        functools.partial(settle_kernel, [len(r) for r in returned]),
        out_shape=jax.ShapeDtypeStruct((local_orbs, rows, virt), BF16),
        in_specs=[SMEM] + [VMEM] * len(terms) + [ANY] * len(after),
        out_specs=VMEM,
        scratch_shapes=[pltpu.VMEM((local_orbs, rows, virt), F32)],
        compiler_params=params(),
        cost_estimate=weighed(SETTLE_WEIGHT, 0, (len(returned[0]) * CAP + local_orbs) * 2 * rows * virt),
        name="settle_chunks",
    )(index, *terms, *after)


def add_kernel(groups, *refs):
    count = len(groups)
    grads_ref, wide, sems = refs[-3:]
    copies = []
    at = 0
    for i, group in enumerate(groups):
        mine, other = refs[i], refs[count + i]
        offset = 0
        for c in group:
            rows, source = pl.ds(at, c.count), pl.ds(offset, c.count)
            at, offset = at + c.count, offset + c.count
            for g in range(mine.shape[0]):
                wide[g, rows] = mine[g, source].astype(F32) + other[g, source].astype(F32)
                copies.append(
                    pltpu.make_async_copy(
                        wide.at[g, rows],
                        grads_ref.at[g, pl.ds(c.start, c.count)],
                        sems.at[len(copies)],
                    )
                )
                copies[-1].start()
    for c in copies:
        c.wait()


def add_chunks(waiting, fit_rows, grads=None):
    groups, mine, other = zip(*waiting)
    local_orbs, _, virt = mine[0].shape
    rows = sum(m.shape[1] for m in mine)
    count = len(mine)
    more = [] if grads is None else [grads]
    return pl.pallas_call(
        functools.partial(add_kernel, groups),
        out_shape=jax.ShapeDtypeStruct((local_orbs, fit_rows, virt), F32),
        in_specs=[VMEM] * (2 * count) + [ANY] * len(more),
        out_specs=ANY,
        scratch_shapes=[
            pltpu.VMEM((local_orbs, rows, virt), F32),
            pltpu.SemaphoreType.DMA((local_orbs * sum(len(g) for g in groups),)),
        ],
        input_output_aliases={} if grads is None else {2 * count: 0},
        compiler_params=params(),
        cost_estimate=cost(0, 8 * local_orbs * rows * virt),
        name="add_chunks",
    )(*mine, *other, *more)


def cut_rows(total, weights):
    unit = 16
    units = total // unit
    whole = sum(weights)
    sizes = [max(1, units * w // whole) for w in weights]
    sizes[0] += units - sum(sizes)
    chunks, at = [], 0
    for size in sizes:
        chunks.append(Rows(at, size * unit))
        at += size * unit
    return chunks


def around_fit(x, n_fit):
    return [x] + [lax.ppermute(x, "fit", shifted(n_fit, d)) for d in range(1, n_fit)]


def per_device(blocks, occ_energy, pair_list, pno_sizes, fock_virt):
    n = lax.axis_size("orb")
    n_fit = lax.axis_size("fit")
    n_rep = lax.axis_size("rep")
    local_orbs, fit_rows, virt = blocks.shape
    total_orbs = local_orbs * n
    me = lax.axis_index("orb")

    endpoints = pair_list.reshape(-1)
    relative = (endpoints - me * local_orbs) % total_orbs
    named = jnp.any(
        relative[:, None] == jnp.arange(total_orbs, dtype=jnp.int32)[None, :], axis=0
    ).reshape(n, local_orbs)
    table = named.astype(jnp.int32)
    position = jnp.cumsum(table, axis=1) - 1
    columns = jnp.arange(CAP, dtype=jnp.int32)
    locals_ = jnp.arange(local_orbs, dtype=jnp.int32)
    matches = table[:, :, None] * (position[:, :, None] == columns[None, None, :])
    wanted = jnp.sum(matches * locals_[None, :, None], axis=1)
    end_hot = relative[:, None] == jnp.arange(total_orbs, dtype=jnp.int32)[None, :]
    slots = (relative // local_orbs) * CAP + jnp.sum(
        jnp.where(end_hot, position.reshape(1, -1), 0), axis=1
    )
    slots = slots.astype(jnp.int32)

    energies_here = occ_energy.astype(F32)
    got = {}
    for d in range(1, n):
        note = jnp.concatenate([wanted[d].astype(F32), energies_here])
        got[d] = lax.ppermute(note, "orb", shifted(n, d))
    asked = jnp.stack(
        [wanted[0]] + [got[d][:CAP].astype(jnp.int32) for d in range(1, n)]
    )
    energies = jnp.concatenate([energies_here] + [got[n - d][CAP:] for d in range(1, n)])

    chunks = cut_rows(fit_rows, FORWARD_ROWS)
    fit = lax.axis_index("fit").astype(jnp.int32).reshape(1)
    mine = around_fit(pick_blocks(wanted[:1], blocks, 0, fit_rows)[0], n_fit)
    inverse, off = prepare_pairs(energies, relative, pno_sizes, fock_virt)
    merged, arrived = [], []
    ints = None

    def pass_on(place, after):
        merged.append(around_fit(merge_chunk(arrived[place], after), n_fit))

    def integrals(place, before, after):
        here = slice(place, place + 1)
        return exchange_chunks(slots, fit, chunks[here], mine, merged[here], before, after)

    for place, c in enumerate(chunks):
        after = [mine[0]] if place < 2 else [merged[place - 2][0]]
        picked = pick_blocks(asked[1:], blocks, c.start, c.count, after)
        arrived.append(
            [lax.ppermute(picked[d - 1], "orb", shifted(n, n - d)) for d in range(1, n)]
        )
        if place == 1:
            pass_on(0, [picked[0], inverse])
        elif place == 2:
            pass_on(1, [picked[0]])
        elif place > 2:
            ints = integrals(place - 3, ints, [])
            pass_on(place - 1, [picked[0], ints])
    ints = integrals(len(chunks) - 3, ints, [merged[-1][0]])
    pass_on(len(chunks) - 1, [ints])
    ints = integrals(len(chunks) - 2, ints, [merged[-1][0]])
    amplitudes, weights, *sums = middle_step(
        slots, fit, chunks[-1], mine, merged[-1], ints, inverse, off
    )

    back = [(chunks[-1], sums)]
    for c in reversed(cut_rows(chunks[-1].start, BACK_ROWS)):
        parts, sources = [], []
        for place, chunk in enumerate(chunks[:-1]):
            low = max(c.start, chunk.start)
            high = min(c.start + c.count, chunk.start + chunk.count)
            if low < high:
                parts.append((low, low - chunk.start, high - low))
                sources.append(merged[place][0])
        after = []
        back.append((c, gradient_chunk(slots, weights, mine[0], parts, sources, after)))

    swap = shifted(n_rep, 1)
    waiting = []
    returned = [
        [sums[0]] + [lax.ppermute(sums[d], "orb", shifted(n, d)) for d in range(1, n)]
        for _, sums in back
    ]
    low = 0
    for high in BACK_GROUPS:
        here = settle_chunks(asked, returned[low:high], local_orbs, [w[1] for w in waiting[-1:]])
        group = [c for c, _ in back[low:high]]
        waiting.append((group, here, lax.ppermute(here, "rep", swap)))
        low = high
    grads = add_chunks(waiting[:-1], fit_rows)
    grads = add_chunks(waiting[-1:], fit_rows, grads)
    return amplitudes, grads


def solution(mesh):
    placed = (
        P(("groups", "orb"), "fit", None),
        P(("groups", "orb")),
        P(("groups", "orb", "rep"), None),
        P(("groups", "orb", "rep")),
        P(("groups", "orb", "rep"), None, None),
    )
    return jax.shard_map(
        per_device,
        mesh=mesh,
        in_specs=placed,
        out_specs=(P(("groups", "orb", "rep"), None, None), P(("groups", "orb"), "fit", None)),
        check_vma=False,
    )
```

time: 246 us -> 237 us (0.963)
  waiting for transfers between devices: 130 us -> 79.4 us
  starting transfers between devices: 50.1 us -> 93.5 us
  Pallas kernels: 55.8 us -> 52.4 us
    ppermute x12 -> x15, starting transfers between devices: 11 us -> 44.3 us  [per_device(): lax.ppermute(sums[d], 'orb', shifted(n, d))]
    ppermute x12 -> x15, waiting for transfers between devices: 55.9 us -> 31 us  [per_device(): lax.ppermute(sums[d], 'orb', shifted(n, d))]
    ppermute x12 -> x15, waiting for transfers between devices: 51 us -> 37.9 us  [per_device(): lax.ppermute(picked[d - 1], 'orb', shifted(n, n - d))]
    ppermute x5 -> x10, waiting for transfers between devices: 22.7 us -> 10.6 us  [the longest x6 10.6 us: around_fit(): lax.ppermute(x, 'fit', shifted(n_fit, d))]
    ppermute x5 -> x10, starting transfers between devices: 11.7 us -> 17.8 us  [the longest x4 12.3 us: per_device(): waiting.append((group, here, lax.ppermute(here, 'rep', swap)))]
    ppermute x12 -> x15, starting transfers between devices: 22.7 us -> 27.7 us  [per_device(): lax.ppermute(picked[d - 1], 'orb', shifted(n, n - d))]
    pallas_call x21 -> x27, Pallas kernels: 55.8 us -> 52.4 us  [the longest x4 13.6 us: exchange_chunks(): pl.pallas_call(functools.partial(exchange_kernel, chunks, n_fit, first, l...]
    unnamed x11 -> x25, local copies, waits for them, and re-layouts: 4.48 us -> 6.92 us
  transfers between devices with their start and end apart: 32 -> 43, of which waited for: 19 -> 15; matrix products, arithmetic and copies ran while one was open for 0% -> 0% of each run, Pallas kernels for 16% -> 17%
where the time goes in v3:
time: 237 us; the launch traced here: 236 us
  starting transfers between devices  93.5 us (39%)
  waiting for transfers between devices  79.4 us (34%)
  Pallas kernels  52.4 us (22%)
  local copies, waits for them, and re-layouts  7.47 us (3%)
  other arithmetic  2.41 us (1%)
    ppermute x15, starting transfers between devices, per_device(): lax.ppermute(sums[d], 'orb', shifted(n, d))  44.3 us
    ppermute x15, waiting for transfers between devices, per_device(): lax.ppermute(picked[d - 1], 'orb', shifted(n, n - d))  37.9 us
    ppermute x15, waiting for transfers between devices, per_device(): lax.ppermute(sums[d], 'orb', shifted(n, d))  31 us
    ppermute x15, starting transfers between devices, per_device(): lax.ppermute(picked[d - 1], 'orb', shifted(n, n - d))  27.7 us
    pallas_call x4, Pallas kernels, exchange_chunks(): pl.pallas_call(functools.partial(exchange_kernel, chunks, n_fit, first, l...  13.6 us
    ppermute x4, starting transfers between devices, per_device(): waiting.append((group, here, lax.ppermute(here, 'rep', swap)))  12.3 us
    pallas_call x4, Pallas kernels, gradient_chunk(): pl.pallas_call(functools.partial(gradient_kernel, parts, n), out_shape=[j...  11.8 us
    ppermute x6, waiting for transfers between devices, around_fit(): lax.ppermute(x, 'fit', shifted(n_fit, d))  10.6 us
  transfers between devices with their start and end apart: 43, of which 15 were waited for; matrix products, arithmetic and copies ran while one was open for 0% of the time, Pallas kernels for 17%

profile of v3, /device:TPU:9, one launch (start us, length us, event | category | flops | bytes accessed | tf_op | source)
XLA Modules:
  0.0 236.3 jit_solution(13393742464519721413)
XLA Ops:
  3.0 1.3 collective-permute-start.1
  5.4 1.4 collective-permute-start.3
  6.9 2.2 copy-done
  9.8 1.5 copy-done.1
  11.2 2.0 pick_blocks.7
  13.2 1.1 collective-permute-start.4
  14.5 1.2 collective-permute-start.6
  15.7 1.2 collective-permute-start
  17.2 1.6 pick_blocks.8
  18.9 1.8 prepare_pairs.1
  21.6 15.2 %collective-permute-done.5.refs_1_ = bf16[2,336,256]{2,1,0:T(8,128)(2,1)S(1)} collective-permute-done((bf16[2,336,256]{2,1,0:T(8,128)(2,1)S(1)}, bf16[2,336,256]{2,1,0:T(8,128)(2,1)S(1)}, u32[]{:S(2)}, u32[]{:S(2)}) %collective-permute-start.5) | collective-permute-done | bytes 344096 | tf_op jit(solution)/shard_map/ppermute | solution.py:507
  36.8 7.4 %collective-permute-done.6.refs_2_ = bf16[2,336,256]{2,1,0:T(8,128)(2,1)S(1)} collective-permute-done((bf16[2,336,256]{2,1,0:T(8,128)(2,1)S(1)}, bf16[2,336,256]{2,1,0:T(8,128)(2,1)S(1)}, u32[]{:S(2)}, u32[]{:S(2)}) %collective-permute-start.6) | collective-permute-done | bytes 344096 | tf_op jit(solution)/shard_map/ppermute | solution.py:507
  44.6 1.3 collective-permute-start.13
  46.4 2.9 %collective-permute-start.11 = (bf16[2,256,256]{2,1,0:T(8,128)(2,1)}, bf16[2,256,256]{2,1,0:T(8,128)(2,1)}, u32[]{:S(2)}, u32[]{:S(2)}) collective-permute-start(bf16[2,256,256]{2,1,0:T(8,128)(2,1)} %copy-done.11), channel_id=1, source_target_pairs={{0,8},{4,12},{8,0},{12,4},{1,9},{5,13},{9,1},{13,5},{2,10},{6,14},... | collective-permute-start | bytes 786440 | tf_op jit(solution)/shard_map/ppermute | solution.py:507
  49.6 2.2 copy-done.2
  51.7 1.4 pick_blocks.9
  53.1 10.4 %collective-permute-done.11.refs_1_ = bf16[2,256,256]{2,1,0:T(8,128)(2,1)} collective-permute-done((bf16[2,256,256]{2,1,0:T(8,128)(2,1)}, bf16[2,256,256]{2,1,0:T(8,128)(2,1)}, u32[]{:S(2)}, u32[]{:S(2)}) %collective-permute-start.11) | collective-permute-done | bytes 262176 | tf_op jit(solution)/shard_map/ppermute | solution.py:507
  63.6 8.6 %collective-permute-start.7 = (bf16[2,192,256]{2,1,0:T(8,128)(2,1)S(1)}, bf16[2,192,256]{2,1,0:T(8,128)(2,1)S(1)}, u32[]{:S(2)}, u32[]{:S(2)}) collective-permute-start(bf16[2,192,256]{2,1,0:T(8,128)(2,1)S(1)} %get-tuple-element.46.refs_3_), channel_id=1, source_target_pairs={{0,12},{4,0},{8,4},{12,8},{1,13},{5,1},{9,5},{13,9},{2,14},{6,2},{... | collective-permute-start | bytes 589832 | tf_op jit(solution)/shard_map/ppermute | solution.py:507
  72.2 1.1 merge_chunk.6.rest_0_.rest_2_.rest_1_
  73.4 1.2 pick_blocks.10
  74.9 1.2 collective-permute-start.9
  76.1 1.2 collective-permute-start.18
  77.4 4.6 %exchange_chunks.4.refs_4_.rest_4_ = f32[8,256,256]{2,1,0:T(8,128)S(1)} custom-call(s32[16]{0:T(128)S(1)} %multiply_add_fusion.slot_ref, s32[1]{0:T(128)} %bitcast.fit_ref, bf16[2,1024,256]{2,1,0:T(8,128)(2,1)S(1)} %pick_blocks.6.rest_0_.rest_1_.mine_ref, bf16[2,1024,256]{2,1,0:T(8,128)(2,1)S(1)} %collective-permute-done.rest_1_.rest_2_, ...), custom_call_target="tpu_custom_call" | custom-call | flops 35232153600 | bytes 347340800 | tf_op jit(solution)/shard_map/exchange_chunks/pallas_call | solution.py:177
  81.9 3.6 %collective-permute-done.8.refs_1_ = bf16[2,192,256]{2,1,0:T(8,128)(2,1)S(1)} collective-permute-done((bf16[2,192,256]{2,1,0:T(8,128)(2,1)S(1)}, bf16[2,192,256]{2,1,0:T(8,128)(2,1)S(1)}, u32[]{:S(2)}, u32[]{:S(2)}) %collective-permute-start.8) | collective-permute-done | bytes 196640 | tf_op jit(solution)/shard_map/ppermute | solution.py:507
  85.6 5.6 %collective-permute-start.19 = (bf16[2,144,256]{2,1,0:T(8,128)(2,1)S(1)}, bf16[2,144,256]{2,1,0:T(8,128)(2,1)S(1)}, u32[]{:S(2)}, u32[]{:S(2)}) collective-permute-start(bf16[2,144,256]{2,1,0:T(8,128)(2,1)S(1)} %get-tuple-element.56), channel_id=1, source_target_pairs={{0,4},{4,8},{8,12},{12,0},{1,5},{5,9},{9,13},{13,1},{2,6},{6,10},{... | collective-permute-start | bytes 442376 | tf_op jit(solution)/shard_map/ppermute | solution.py:507
  91.2 1.2 collective-permute-done.9.refs_2_
  94.9 1.2 collective-permute-start.21
  96.1 2.1 collective-permute-start.15
  98.2 3.0 %exchange_chunks.5.refs_4_.rest_5_ = f32[8,256,256]{2,1,0:T(8,128)S(1)} custom-call(s32[16]{0:T(128)S(1)} %multiply_add_fusion.slot_ref, s32[1]{0:T(128)} %bitcast.fit_ref, bf16[2,1024,256]{2,1,0:T(8,128)(2,1)S(1)} %pick_blocks.6.rest_0_.rest_1_.mine_ref, bf16[2,1024,256]{2,1,0:T(8,128)(2,1)S(1)} %collective-permute-done.rest_1_.rest_2_, ...), custom_call_target="tpu_custom_call" | custom-call | flops 26843545600 | bytes 314572800 | tf_op jit(solution)/shard_map/exchange_chunks/pallas_call | solution.py:177
  101.2 2.4 %collective-permute-start.16 = (bf16[2,96,256]{2,1,0:T(8,128)(2,1)S(1)}, bf16[2,96,256]{2,1,0:T(8,128)(2,1)S(1)}, u32[]{:S(2)}, u32[]{:S(2)}) collective-permute-start(bf16[2,96,256]{2,1,0:T(8,128)(2,1)S(1)} %get-tuple-element.54), channel_id=1, source_target_pairs={{0,4},{4,8},{8,12},{12,0},{1,5},{5,9},{9,13},{13,1},{2,6},{6,10},{... | collective-permute-start | bytes 294920 | tf_op jit(solution)/shard_map/ppermute | solution.py:507
  104.6 1.9 collective-permute-done.21.rest_4_
  106.5 3.1 %exchange_chunks.6.refs_3_.rest_5_ = f32[8,256,256]{2,1,0:T(8,128)S(1)} custom-call(s32[16]{0:T(128)S(1)} %multiply_add_fusion.slot_ref, s32[1]{0:T(128)} %bitcast.fit_ref, bf16[6,144,256]{2,1,0:T(8,128)(2,1)S(1)} %merge_chunk.8.rest_0_.rest_3_.rest_1_, bf16[2,1024,256]{2,1,0:T(8,128)(2,1)S(1)} %pick_blocks.6.rest_0_.rest_1_.mine_ref, ...), custom_call_target="tpu_custom_call" | custom-call | flops 20132659200 | bytes 288358400 | tf_op jit(solution)/shard_map/exchange_chunks/pallas_call | solution.py:177
  110.1 1.1 collective-permute-start.22
  111.1 5.4 %collective-permute-done.23.rest_4_ = bf16[6,144,256]{2,1,0:T(8,128)(2,1)S(1)} collective-permute-done((bf16[6,144,256]{2,1,0:T(8,128)(2,1)S(1)}, bf16[6,144,256]{2,1,0:T(8,128)(2,1)S(1)}, u32[]{:S(2)}, u32[]{:S(2)}) %collective-permute-start.23) | collective-permute-done | bytes 442400 | tf_op jit(solution)/shard_map/ppermute | solution.py:451
  116.5 3.0 %exchange_chunks.7.rest_4_ = f32[8,256,256]{2,1,0:T(8,128)S(1)} custom-call(s32[16]{0:T(128)S(1)} %multiply_add_fusion.slot_ref, s32[1]{0:T(128)} %bitcast.fit_ref, bf16[6,96,256]{2,1,0:T(8,128)(2,1)S(1)} %merge_chunk.9.rest_0_.rest_2_, bf16[2,1024,256]{2,1,0:T(8,128)(2,1)S(1)} %pick_blocks.6.rest_0_.rest_1_.mine_ref, ...), custom_call_target="tpu_custom_call" | custom-call | flops 15099494400 | bytes 268697600 | tf_op jit(solution)/shard_map/exchange_chunks/pallas_call | solution.py:177
  119.6 3.3 %collective-permute-done.22.rest_3_ = bf16[6,96,256]{2,1,0:T(8,128)(2,1)S(1)} collective-permute-done((bf16[6,96,256]{2,1,0:T(8,128)(2,1)S(1)}, bf16[6,96,256]{2,1,0:T(8,128)(2,1)S(1)}, u32[]{:S(2)}, u32[]{:S(2)}) %collective-permute-start.22) | collective-permute-done | bytes 294944 | tf_op jit(solution)/shard_map/ppermute | solution.py:451
  122.9 5.7 %middle_step.1 = (bf16[8,256,256]{2,1,0:T(8,128)(2,1)}, bf16[16,256,256]{2,1,0:T(8,128)(2,1)S(1)}, bf16[2,96,256]{2,1,0:T(8,128)(2,1)S(1)}, bf16[2,96,256]{2,1,0...) custom-call(s32[16]{0:T(128)S(1)} %multiply_add_fusion.slot_ref, s32[1]{0:T(128)} %bitcast.fit_ref, ...), custom_call_target="tpu_custom_call" | custom-call | flops 1140850688 | bytes 8388608 | tf_op jit(solution)/shard_map/middle_step/pallas_call | solution.py:282
  128.6 3.0 %gradient_chunk.7 = (bf16[2,240,256]{2,1,0:T(8,128)(2,1)S(1)}, bf16[2,240,256]{2,1,0:T(8,128)(2,1)S(1)}, bf16[2,240,256]{2,1,0:T(8,128)(2,1)S(1)}, bf16[2,240,256]{2,1,0:T(8,128)(2,1)S(1)}) custom-call(s32[16]{0:T(128)S(1)} %multiply_add_fusion.slot_ref, bf16[16,256,256]{2,1,0:T(8,128)(2,1)S(1)} %get-tuple-element.59.weight_ref, ...), custom_call_target="tpu_custom_call" | custom-call | flops 503316480 | bytes 4063232 | tf_op jit(solution)/shard_map/gradient_chunk/pallas_call | solution.py:341
  131.6 2.8 %collective-permute-start.36 = (bf16[2,240,256]{2,1,0:T(8,128)(2,1)S(1)}, bf16[2,240,256]{2,1,0:T(8,128)(2,1)S(1)}, u32[]{:S(2)}, u32[]{:S(2)}) collective-permute-start(bf16[2,240,256]{2,1,0:T(8,128)(2,1)S(1)} %get-tuple-element.77), channel_id=1, source_target_pairs={{0,4},{4,8},{8,12},{12,0},{1,5},{5,9},{9,13},{13,1},{2,6},{6,10},{... | collective-permute-start | bytes 737288 | tf_op jit(solution)/shard_map/ppermute | solution.py:538
  134.4 1.8 collective-permute-start.37
  136.2 1.5 collective-permute-start.33
  137.6 2.4 collective-permute-start.34
  140.0 2.9 %gradient_chunk.5 = (bf16[2,224,256]{2,1,0:T(8,128)(2,1)S(1)}, bf16[2,224,256]{2,1,0:T(8,128)(2,1)S(1)}, bf16[2,224,256]{2,1,0:T(8,128)(2,1)S(1)}, bf16[2,224,256]{2,1,0:T(8,128)(2,1)S(1)}) custom-call(s32[16]{0:T(128)S(1)} %multiply_add_fusion.slot_ref, bf16[16,256,256]{2,1,0:T(8,128)(2,1)S(1)} %get-tuple-element.59.weight_ref, ...), custom_call_target="tpu_custom_call" | custom-call | flops 469762048 | bytes 3932160 | tf_op jit(solution)/shard_map/gradient_chunk/pallas_call | solution.py:341
  142.9 15.0 %collective-permute-done.33.rest_1_ = bf16[2,96,256]{2,1,0:T(8,128)(2,1)S(1)} collective-permute-done((bf16[2,96,256]{2,1,0:T(8,128)(2,1)S(1)}, bf16[2,96,256]{2,1,0:T(8,128)(2,1)S(1)}, u32[]{:S(2)}, u32[]{:S(2)}) %collective-permute-start.33) | collective-permute-done | bytes 98336 | tf_op jit(solution)/shard_map/ppermute | solution.py:538
  157.9 1.9 collective-permute-start.27
  160.0 9.2 %collective-permute-start.35 = (bf16[2,96,256]{2,1,0:T(8,128)(2,1)S(1)}, bf16[2,96,256]{2,1,0:T(8,128)(2,1)S(1)}, u32[]{:S(2)}, u32[]{:S(2)}) collective-permute-start(bf16[2,96,256]{2,1,0:T(8,128)(2,1)S(1)} %get-tuple-element.75), channel_id=1, source_target_pairs={{0,12},{4,0},{8,4},{12,8},{1,13},{5,1},{9,5},{13,9},{2,14},{6,2},{... | collective-permute-start | bytes 294920 | tf_op jit(solution)/shard_map/ppermute | solution.py:538
  169.2 3.0 %gradient_chunk.6 = (bf16[2,240,256]{2,1,0:T(8,128)(2,1)S(1)}, bf16[2,240,256]{2,1,0:T(8,128)(2,1)S(1)}, bf16[2,240,256]{2,1,0:T(8,128)(2,1)S(1)}, bf16[2,240,256]{2,1,0:T(8,128)(2,1)S(1)}) custom-call(s32[16]{0:T(128)S(1)} %multiply_add_fusion.slot_ref, bf16[16,256,256]{2,1,0:T(8,128)(2,1)S(1)} %get-tuple-element.59.weight_ref, ...), custom_call_target="tpu_custom_call" | custom-call | flops 503316480 | bytes 4063232 | tf_op jit(solution)/shard_map/gradient_chunk/pallas_call | solution.py:341
  174.7 1.4 collective-permute-start.32
  176.1 1.1 settle_chunks.4.rest_4_.refs_0_
  177.3 3.2 %collective-permute-start.40 = (bf16[8,336,256]{2,1,0:T(8,128)(2,1)S(1)}, bf16[8,336,256]{2,1,0:T(8,128)(2,1)S(1)}, u32[]{:S(2)}, u32[]{:S(2)}) collective-permute-start(bf16[8,336,256]{2,1,0:T(8,128)(2,1)S(1)} %settle_chunks.4.rest_4_.refs_0_), channel_id=1, source_target_pairs={{0,1},{1,0},{2,3},{3,2},{4,5},{5,4},{6,7},{7,6},{8,9},{9,8},{10,11... | collective-permute-start | bytes 4128776 | tf_op jit(solution)/shard_map/ppermute | solution.py:545
  180.5 2.0 collective-permute-done.28.rest_2_
  182.5 13.1 %collective-permute-start.29 = (bf16[2,224,256]{2,1,0:T(8,128)(2,1)S(1)}, bf16[2,224,256]{2,1,0:T(8,128)(2,1)S(1)}, u32[]{:S(2)}, u32[]{:S(2)}) collective-permute-start(bf16[2,224,256]{2,1,0:T(8,128)(2,1)S(1)} %get-tuple-element.67), channel_id=1, source_target_pairs={{0,12},{4,0},{8,4},{12,8},{1,13},{5,1},{9,5},{13,9},{2,14},{6,2},{... | collective-permute-start | bytes 688136 | tf_op jit(solution)/shard_map/ppermute | solution.py:538
  195.6 2.9 %gradient_chunk.4 = (bf16[2,224,256]{2,1,0:T(8,128)(2,1)S(1)}, bf16[2,224,256]{2,1,0:T(8,128)(2,1)S(1)}, bf16[2,224,256]{2,1,0:T(8,128)(2,1)S(1)}, bf16[2,224,256]{2,1,0:T(8,128)(2,1)S(1)}) custom-call(s32[16]{0:T(128)S(1)} %multiply_add_fusion.slot_ref, bf16[16,256,256]{2,1,0:T(8,128)(2,1)S(1)} %get-tuple-element.59.weight_ref, ...), custom_call_target="tpu_custom_call" | custom-call | flops 469762048 | bytes 3932160 | tf_op jit(solution)/shard_map/gradient_chunk/pallas_call | solution.py:341
  198.5 1.2 collective-permute-done.30.rest_1_
  199.7 2.2 collective-permute-start.24
  201.9 8.0 %collective-permute-done.31.rest_2_ = bf16[2,240,256]{2,1,0:T(8,128)(2,1)S(1)} collective-permute-done((bf16[2,240,256]{2,1,0:T(8,128)(2,1)S(1)}, bf16[2,240,256]{2,1,0:T(8,128)(2,1)S(1)}, u32[]{:S(2)}, u32[]{:S(2)}) %collective-permute-start.31) | collective-permute-done | bytes 245792 | tf_op jit(solution)/shard_map/ppermute | solution.py:538
  209.9 5.6 %collective-permute-start.25 = (bf16[2,224,256]{2,1,0:T(8,128)(2,1)S(1)}, bf16[2,224,256]{2,1,0:T(8,128)(2,1)S(1)}, u32[]{:S(2)}, u32[]{:S(2)}) collective-permute-start(bf16[2,224,256]{2,1,0:T(8,128)(2,1)S(1)} %get-tuple-element.62), channel_id=1, source_target_pairs={{0,8},{4,12},{8,0},{12,4},{1,9},{5,13},{9,1},{13,5},{2,10},{6,14},... | collective-permute-start | bytes 688136 | tf_op jit(solution)/shard_map/ppermute | solution.py:538
  216.5 3.2 %collective-permute-start.41 = (bf16[8,240,256]{2,1,0:T(8,128)(2,1)S(1)}, bf16[8,240,256]{2,1,0:T(8,128)(2,1)S(1)}, u32[]{:S(2)}, u32[]{:S(2)}) collective-permute-start(bf16[8,240,256]{2,1,0:T(8,128)(2,1)S(1)} %settle_chunks.5.rest_4_.refs_1_), channel_id=1, source_target_pairs={{0,1},{1,0},{2,3},{3,2},{4,5},{5,4},{6,7},{7,6},{8,9},{9,8},{10,11... | collective-permute-start | bytes 2949128 | tf_op jit(solution)/shard_map/ppermute | solution.py:545
  220.6 4.4 %collective-permute-start.42 = (bf16[8,224,256]{2,1,0:T(8,128)(2,1)S(1)}, bf16[8,224,256]{2,1,0:T(8,128)(2,1)S(1)}, u32[]{:S(2)}, u32[]{:S(2)}) collective-permute-start(bf16[8,224,256]{2,1,0:T(8,128)(2,1)S(1)} %settle_chunks.6.rest_4_.refs_2_), channel_id=1, source_target_pairs={{0,1},{1,0},{2,3},{3,2},{4,5},{5,4},{6,7},{7,6},{8,9},{9,8},{10,11... | collective-permute-start | bytes 2752520 | tf_op jit(solution)/shard_map/ppermute | solution.py:545
  225.1 2.1 collective-permute-done.25.rest_2_
  227.2 2.4 %collective-permute-done.26.rest_3_ = bf16[2,224,256]{2,1,0:T(8,128)(2,1)S(1)} collective-permute-done((bf16[2,224,256]{2,1,0:T(8,128)(2,1)S(1)}, bf16[2,224,256]{2,1,0:T(8,128)(2,1)S(1)}, u32[]{:S(2)}, u32[]{:S(2)}) %collective-permute-start.26) | collective-permute-done | bytes 229408 | tf_op jit(solution)/shard_map/ppermute | solution.py:538
  230.5 1.4 collective-permute-start.39
  232.0 3.0 %add_chunks.2.refs_2_ = f32[8,1024,256]{2,1,0:T(8,128)} custom-call(bf16[8,336,256]{2,1,0:T(8,128)(2,1)S(1)} %settle_chunks.4.rest_4_.refs_0_, bf16[8,240,256]{2,1,0:T(8,128)(2,1)S(1)} %settle_chunks.5.rest_4_.refs_1_, bf16[8,224,256]{2,1,0:T(8,128)(2,1)S(1)} %settle_chunks.6.rest_4_.refs_2_, bf16[8,336,256]{2,1,0:T(8,128)(2,1)S(1)} %collective-permute-done.40.refs_3_, ...), custom_call_target="tpu_custom_call" | custom-call | bytes 13107200 | tf_op jit(solution)/shard_map/add_chunks/pallas_call | solution.py:421
  235.0 1.3 add_chunks.3
  (99 shorter events, 16.6 us)
Async XLA Ops:
  3.0 6.7 %collective-permute-start.1 = (f32[10]{0:T(128)S(1)}, f32[10]{0:T(128)S(1)}, u32[]{:S(2)}, u32[]{:S(2)}) collective-permute-start(f32[10]{0:T(128)S(1)} %get-tuple-element.83), channel_id=1, source_target_pairs={{0,4},{4,8},{8,12},{12,0},{1,5},{5,9},{9,13},{13,1},{2,6},{6,10},{... | collective-permute-start | bytes 128 | tf_op jit(solution)/shard_map/ppermute | solution.py:483
  4.3 5.4 %collective-permute-start.2 = (f32[10]{0:T(128)S(1)}, f32[10]{0:T(128)S(1)}, u32[]{:S(2)}, u32[]{:S(2)}) collective-permute-start(f32[10]{0:T(128)S(1)} %get-tuple-element.84), channel_id=1, source_target_pairs={{0,8},{4,12},{8,0},{12,4},{1,9},{5,13},{9,1},{13,5},{2,10},{6,14},... | collective-permute-start | bytes 128 | tf_op jit(solution)/shard_map/ppermute | solution.py:483
  5.4 4.4 %collective-permute-start.3 = (f32[10]{0:T(128)S(1)}, f32[10]{0:T(128)S(1)}, u32[]{:S(2)}, u32[]{:S(2)}) collective-permute-start(f32[10]{0:T(128)S(1)} %get-tuple-element.85), channel_id=1, source_target_pairs={{0,12},{4,0},{8,4},{12,8},{1,13},{5,1},{9,5},{13,9},{2,14},{6,2},{... | collective-permute-start | bytes 128 | tf_op jit(solution)/shard_map/ppermute | solution.py:483
  6.9 2.2 copy-start
  9.1 2.2 copy-start.1
  13.2 8.4 %collective-permute-start.4 = (bf16[2,336,256]{2,1,0:T(8,128)(2,1)S(1)}, bf16[2,336,256]{2,1,0:T(8,128)(2,1)S(1)}, u32[]{:S(2)}, u32[]{:S(2)}) collective-permute-start(bf16[2,336,256]{2,1,0:T(8,128)(2,1)S(1)} %get-tuple-element.41), channel_id=1, source_target_pairs={{0,12},{4,0},{8,4},{12,8},{1,13},{5,1},{9,5},{13,9},{2,14},{6,2},{... | collective-permute-start | bytes 1032200 | tf_op jit(solution)/shard_map/ppermute | solution.py:507
  14.3 22.5 %collective-permute-start.5 = (bf16[2,336,256]{2,1,0:T(8,128)(2,1)S(1)}, bf16[2,336,256]{2,1,0:T(8,128)(2,1)S(1)}, u32[]{:S(2)}, u32[]{:S(2)}) collective-permute-start(bf16[2,336,256]{2,1,0:T(8,128)(2,1)S(1)} %get-tuple-element.42), channel_id=1, source_target_pairs={{0,8},{4,12},{8,0},{12,4},{1,9},{5,13},{9,1},{13,5},{2,10},{6,14},... | collective-permute-start | bytes 1032200 | tf_op jit(solution)/shard_map/ppermute | solution.py:507
  14.5 29.7 %collective-permute-start.6 = (bf16[2,336,256]{2,1,0:T(8,128)(2,1)S(1)}, bf16[2,336,256]{2,1,0:T(8,128)(2,1)S(1)}, u32[]{:S(2)}, u32[]{:S(2)}) collective-permute-start(bf16[2,336,256]{2,1,0:T(8,128)(2,1)S(1)} %get-tuple-element.43), channel_id=1, source_target_pairs={{0,4},{4,8},{8,12},{12,0},{1,5},{5,9},{9,13},{13,1},{2,6},{6,10},{... | collective-permute-start | bytes 1032200 | tf_op jit(solution)/shard_map/ppermute | solution.py:507
  15.7 59.2 %collective-permute-start = (bf16[2,1024,256]{2,1,0:T(8,128)(2,1)S(1)}, bf16[2,1024,256]{2,1,0:T(8,128)(2,1)S(1)}, u32[]{:S(2)}, u32[]{:S(2)}) collective-permute-start(bf16[2,1024,256]{2,1,0:T(8,128)(2,1)S(1)} %pick_blocks.6.rest_0_.rest_1_.mine_ref), channel_id=1, source_target_pairs={{0,2},{2,0},{1,3},{3,1},{4,6},{6,4},{5,7},{7,5},{8,10},{10,8},{9,1... | collective-permute-start | bytes 3145736 | tf_op jit(solution)/shard_map/ppermute | solution.py:451
  17.2 1.7 copy-start.6
  17.2 1.7 copy-start.9
  18.9 25.7 %copy-start.10 = (bf16[2,256,256]{2,1,0:T(8,128)(2,1)}, bf16[2,256,256]{2,1,0:T(8,128)(2,1)S(1)}, u32[]{:S(2)}) copy-start(bf16[2,256,256]{2,1,0:T(8,128)(2,1)S(1)} %get-tuple-element.50) | copy-start | bytes 786436
  18.9 25.7 %copy-start.11 = (bf16[2,256,256]{2,1,0:T(8,128)(2,1)}, bf16[2,256,256]{2,1,0:T(8,128)(2,1)S(1)}, u32[]{:S(2)}) copy-start(bf16[2,256,256]{2,1,0:T(8,128)(2,1)S(1)} %get-tuple-element.49) | copy-start | bytes 786436
  20.7 1.0 copy-start.7
  21.6 23.0 %copy-start.4 = (f32[8,256,256]{2,1,0:T(8,128)}, f32[8,256,256]{2,1,0:T(8,128)S(1)}, u32[]{:S(2)}) copy-start(f32[8,256,256]{2,1,0:T(8,128)S(1)} %get-tuple-element.45.refs_4_.rest_5_) | copy-start | bytes 6291460
  44.6 31.5 %collective-permute-start.13 = (bf16[6,336,256]{2,1,0:T(8,128)(2,1)S(1)}, bf16[6,336,256]{2,1,0:T(8,128)(2,1)}, u32[]{:S(2)}, u32[]{:S(2)}) collective-permute-start(bf16[6,336,256]{2,1,0:T(8,128)(2,1)S(1)} %merge_chunk.5.rest_0_.rest_2_), channel_id=1, source_target_pairs={{0,2},{2,0},{1,3},{3,1},{4,6},{6,4},{5,7},{7,5},{8,10},{10,8},{9,1... | collective-permute-start | bytes 3096584 | tf_op jit(solution)/shard_map/ppermute | solution.py:451
  46.0 26.3 %collective-permute-start.10 = (bf16[2,256,256]{2,1,0:T(8,128)(2,1)S(1)}, bf16[2,256,256]{2,1,0:T(8,128)(2,1)}, u32[]{:S(2)}, u32[]{:S(2)}) collective-permute-start(bf16[2,256,256]{2,1,0:T(8,128)(2,1)S(1)} %get-tuple-element.44.refs_3_), channel_id=1, source_target_pairs={{0,12},{4,0},{8,4},{12,8},{1,13},{5,1},{9,5},{13,9},{2,14},{6,2},{... | collective-permute-start | bytes 786440 | tf_op jit(solution)/shard_map/ppermute | solution.py:507
  46.4 17.2 %collective-permute-start.11 = (bf16[2,256,256]{2,1,0:T(8,128)(2,1)}, bf16[2,256,256]{2,1,0:T(8,128)(2,1)}, u32[]{:S(2)}, u32[]{:S(2)}) collective-permute-start(bf16[2,256,256]{2,1,0:T(8,128)(2,1)} %copy-done.11), channel_id=1, source_target_pairs={{0,8},{4,12},{8,0},{12,4},{1,9},{5,13},{9,1},{13,5},{2,10},{6,14},... | collective-permute-start | bytes 786440 | tf_op jit(solution)/shard_map/ppermute | solution.py:507
  49.3 22.9 %collective-permute-start.12 = (bf16[2,256,256]{2,1,0:T(8,128)(2,1)}, bf16[2,256,256]{2,1,0:T(8,128)(2,1)}, u32[]{:S(2)}, u32[]{:S(2)}) collective-permute-start(bf16[2,256,256]{2,1,0:T(8,128)(2,1)} %copy-done.10), channel_id=1, source_target_pairs={{0,4},{4,8},{8,12},{12,0},{1,5},{5,9},{9,13},{13,1},{2,6},{6,10},{... | collective-permute-start | bytes 786440 | tf_op jit(solution)/shard_map/ppermute | solution.py:507
  49.5 2.2 copy-start.2
  51.7 21.6 %copy-start.3 = (bf16[8,1024,256]{2,1,0:T(8,128)(2,1)S(1)}, bf16[8,1024,256]{2,1,0:T(8,128)(2,1)}, u32[]{:S(2)}) copy-start(bf16[8,1024,256]{2,1,0:T(8,128)(2,1)} %blocks_ref.11) | copy-start | bytes 12582916
  63.6 29.5 %collective-permute-start.7 = (bf16[2,192,256]{2,1,0:T(8,128)(2,1)S(1)}, bf16[2,192,256]{2,1,0:T(8,128)(2,1)S(1)}, u32[]{:S(2)}, u32[]{:S(2)}) collective-permute-start(bf16[2,192,256]{2,1,0:T(8,128)(2,1)S(1)} %get-tuple-element.46.refs_3_), channel_id=1, source_target_pairs={{0,12},{4,0},{8,4},{12,8},{1,13},{5,1},{9,5},{13,9},{2,14},{6,2},{... | collective-permute-start | bytes 589832 | tf_op jit(solution)/shard_map/ppermute | solution.py:507
  74.6 21.5 %collective-permute-start.20 = (bf16[6,256,256]{2,1,0:T(8,128)(2,1)S(1)}, bf16[6,256,256]{2,1,0:T(8,128)(2,1)S(1)}, u32[]{:S(2)}, u32[]{:S(2)}) collective-permute-start(bf16[6,256,256]{2,1,0:T(8,128)(2,1)S(1)} %merge_chunk.6.rest_0_.rest_2_.rest_1_), channel_id=1, source_target_pairs={{0,2},{2,0},{1,3},{3,1},{4,6},{6,4},{5,7},{7,5},{8,10},{10,8},{9,1... | collective-permute-start | bytes 2359304 | tf_op jit(solution)/shard_map/ppermute | solution.py:451
  74.9 10.7 %collective-permute-start.8 = (bf16[2,192,256]{2,1,0:T(8,128)(2,1)S(1)}, bf16[2,192,256]{2,1,0:T(8,128)(2,1)S(1)}, u32[]{:S(2)}, u32[]{:S(2)}) collective-permute-start(bf16[2,192,256]{2,1,0:T(8,128)(2,1)S(1)} %get-tuple-element.47), channel_id=1, source_target_pairs={{0,8},{4,12},{8,0},{12,4},{1,9},{5,13},{9,1},{13,5},{2,10},{6,14},... | collective-permute-start | bytes 589832 | tf_op jit(solution)/shard_map/ppermute | solution.py:507
  74.9 17.5 %collective-permute-start.9 = (bf16[2,192,256]{2,1,0:T(8,128)(2,1)S(1)}, bf16[2,192,256]{2,1,0:T(8,128)(2,1)S(1)}, u32[]{:S(2)}, u32[]{:S(2)}) collective-permute-start(bf16[2,192,256]{2,1,0:T(8,128)(2,1)S(1)} %get-tuple-element.48), channel_id=1, source_target_pairs={{0,4},{4,8},{8,12},{12,0},{1,5},{5,9},{9,13},{13,1},{2,6},{6,10},{... | collective-permute-start | bytes 589832 | tf_op jit(solution)/shard_map/ppermute | solution.py:507
  76.1 25.1 %collective-permute-start.18 = (bf16[2,144,256]{2,1,0:T(8,128)(2,1)S(1)}, bf16[2,144,256]{2,1,0:T(8,128)(2,1)S(1)}, u32[]{:S(2)}, u32[]{:S(2)}) collective-permute-start(bf16[2,144,256]{2,1,0:T(8,128)(2,1)S(1)} %get-tuple-element.55), channel_id=1, source_target_pairs={{0,8},{4,12},{8,0},{12,4},{1,9},{5,13},{9,1},{13,5},{2,10},{6,14},... | collective-permute-start | bytes 442376 | tf_op jit(solution)/shard_map/ppermute | solution.py:507
  85.6 18.0 %collective-permute-start.19 = (bf16[2,144,256]{2,1,0:T(8,128)(2,1)S(1)}, bf16[2,144,256]{2,1,0:T(8,128)(2,1)S(1)}, u32[]{:S(2)}, u32[]{:S(2)}) collective-permute-start(bf16[2,144,256]{2,1,0:T(8,128)(2,1)S(1)} %get-tuple-element.56), channel_id=1, source_target_pairs={{0,4},{4,8},{8,12},{12,0},{1,5},{5,9},{9,13},{13,1},{2,6},{6,10},{... | collective-permute-start | bytes 442376 | tf_op jit(solution)/shard_map/ppermute | solution.py:507
  92.4 11.2 %collective-permute-start.17 = (bf16[2,144,256]{2,1,0:T(8,128)(2,1)S(1)}, bf16[2,144,256]{2,1,0:T(8,128)(2,1)S(1)}, u32[]{:S(2)}, u32[]{:S(2)}) collective-permute-start(bf16[2,144,256]{2,1,0:T(8,128)(2,1)S(1)} %get-tuple-element.51.refs_3_), channel_id=1, source_target_pairs={{0,12},{4,0},{8,4},{12,8},{1,13},{5,1},{9,5},{13,9},{2,14},{6,2},{... | collective-permute-start | bytes 442376 | tf_op jit(solution)/shard_map/ppermute | solution.py:507
  94.9 11.6 %collective-permute-start.21 = (bf16[6,192,256]{2,1,0:T(8,128)(2,1)S(1)}, bf16[6,192,256]{2,1,0:T(8,128)(2,1)S(1)}, u32[]{:S(2)}, u32[]{:S(2)}) collective-permute-start(bf16[6,192,256]{2,1,0:T(8,128)(2,1)S(1)} %merge_chunk.7.rest_0_.rest_3_.rest_1_), channel_id=1, source_target_pairs={{0,2},{2,0},{1,3},{3,1},{4,6},{6,4},{5,7},{7,5},{8,10},{10,8},{9,1... | collective-permute-start | bytes 1769480 | tf_op jit(solution)/shard_map/ppermute | solution.py:451
  96.1 13.5 %collective-permute-start.15 = (bf16[2,96,256]{2,1,0:T(8,128)(2,1)S(1)}, bf16[2,96,256]{2,1,0:T(8,128)(2,1)S(1)}, u32[]{:S(2)}, u32[]{:S(2)}) collective-permute-start(bf16[2,96,256]{2,1,0:T(8,128)(2,1)S(1)} %get-tuple-element.53), channel_id=1, source_target_pairs={{0,8},{4,12},{8,0},{12,4},{1,9},{5,13},{9,1},{13,5},{2,10},{6,14},... | collective-permute-start | bytes 294920 | tf_op jit(solution)/shard_map/ppermute | solution.py:507
  101.2 8.4 %collective-permute-start.16 = (bf16[2,96,256]{2,1,0:T(8,128)(2,1)S(1)}, bf16[2,96,256]{2,1,0:T(8,128)(2,1)S(1)}, u32[]{:S(2)}, u32[]{:S(2)}) collective-permute-start(bf16[2,96,256]{2,1,0:T(8,128)(2,1)S(1)} %get-tuple-element.54), channel_id=1, source_target_pairs={{0,4},{4,8},{8,12},{12,0},{1,5},{5,9},{9,13},{13,1},{2,6},{6,10},{... | collective-permute-start | bytes 294920 | tf_op jit(solution)/shard_map/ppermute | solution.py:507
  103.6 6.0 %collective-permute-start.14 = (bf16[2,96,256]{2,1,0:T(8,128)(2,1)S(1)}, bf16[2,96,256]{2,1,0:T(8,128)(2,1)S(1)}, u32[]{:S(2)}, u32[]{:S(2)}) collective-permute-start(bf16[2,96,256]{2,1,0:T(8,128)(2,1)S(1)} %get-tuple-element.52.refs_3_), channel_id=1, source_target_pairs={{0,12},{4,0},{8,4},{12,8},{1,13},{5,1},{9,5},{13,9},{2,14},{6,2},{... | collective-permute-start | bytes 294920 | tf_op jit(solution)/shard_map/ppermute | solution.py:507
  104.2 12.3 %collective-permute-start.23 = (bf16[6,144,256]{2,1,0:T(8,128)(2,1)S(1)}, bf16[6,144,256]{2,1,0:T(8,128)(2,1)S(1)}, u32[]{:S(2)}, u32[]{:S(2)}) collective-permute-start(bf16[6,144,256]{2,1,0:T(8,128)(2,1)S(1)} %merge_chunk.8.rest_0_.rest_3_.rest_1_), channel_id=1, source_target_pairs={{0,2},{2,0},{1,3},{3,1},{4,6},{6,4},{5,7},{7,5},{8,10},{10,8},{9,1... | collective-permute-start | bytes 1327112 | tf_op jit(solution)/shard_map/ppermute | solution.py:451
  110.0 12.8 %copy-start.5 = (f32[8,256,256]{2,1,0:T(8,128)S(1)}, f32[8,256,256]{2,1,0:T(8,128)}, u32[]{:S(2)}) copy-start(f32[8,256,256]{2,1,0:T(8,128)} %copy-done.4) | copy-start | bytes 6291460
  110.1 12.8 %copy-start.8 = (bf16[8,256,256]{2,1,0:T(8,128)(2,1)S(1)}, bf16[8,256,256]{2,1,0:T(8,128)(2,1)}, u32[]{:S(2)}) copy-start(bf16[8,256,256]{2,1,0:T(8,128)(2,1)} %copy-done.7) | copy-start | bytes 3145732
  110.1 12.8 %collective-permute-start.22 = (bf16[6,96,256]{2,1,0:T(8,128)(2,1)S(1)}, bf16[6,96,256]{2,1,0:T(8,128)(2,1)S(1)}, u32[]{:S(2)}, u32[]{:S(2)}) collective-permute-start(bf16[6,96,256]{2,1,0:T(8,128)(2,1)S(1)} %merge_chunk.9.rest_0_.rest_2_), channel_id=1, source_target_pairs={{0,2},{2,0},{1,3},{3,1},{4,6},{6,4},{5,7},{7,5},{8,10},{10,8},{9,1... | collective-permute-start | bytes 884744 | tf_op jit(solution)/shard_map/ppermute | solution.py:451
  131.6 41.7 %collective-permute-start.36 = (bf16[2,240,256]{2,1,0:T(8,128)(2,1)S(1)}, bf16[2,240,256]{2,1,0:T(8,128)(2,1)S(1)}, u32[]{:S(2)}, u32[]{:S(2)}) collective-permute-start(bf16[2,240,256]{2,1,0:T(8,128)(2,1)S(1)} %get-tuple-element.77), channel_id=1, source_target_pairs={{0,4},{4,8},{8,12},{12,0},{1,5},{5,9},{9,13},{13,1},{2,6},{6,10},{... | collective-permute-start | bytes 737288 | tf_op jit(solution)/shard_map/ppermute | solution.py:538
  134.4 39.5 %collective-permute-start.37 = (bf16[2,240,256]{2,1,0:T(8,128)(2,1)S(1)}, bf16[2,240,256]{2,1,0:T(8,128)(2,1)S(1)}, u32[]{:S(2)}, u32[]{:S(2)}) collective-permute-start(bf16[2,240,256]{2,1,0:T(8,128)(2,1)S(1)} %get-tuple-element.78), channel_id=1, source_target_pairs={{0,8},{4,12},{8,0},{12,4},{1,9},{5,13},{9,1},{13,5},{2,10},{6,14},... | collective-permute-start | bytes 737288 | tf_op jit(solution)/shard_map/ppermute | solution.py:538
  136.2 38.6 %collective-permute-start.38 = (bf16[2,240,256]{2,1,0:T(8,128)(2,1)S(1)}, bf16[2,240,256]{2,1,0:T(8,128)(2,1)S(1)}, u32[]{:S(2)}, u32[]{:S(2)}) collective-permute-start(bf16[2,240,256]{2,1,0:T(8,128)(2,1)S(1)} %get-tuple-element.79), channel_id=1, source_target_pairs={{0,12},{4,0},{8,4},{12,8},{1,13},{5,1},{9,5},{13,9},{2,14},{6,2},{... | collective-permute-start | bytes 737288 | tf_op jit(solution)/shard_map/ppermute | solution.py:538
  136.2 21.7 %collective-permute-start.33 = (bf16[2,96,256]{2,1,0:T(8,128)(2,1)S(1)}, bf16[2,96,256]{2,1,0:T(8,128)(2,1)S(1)}, u32[]{:S(2)}, u32[]{:S(2)}) collective-permute-start(bf16[2,96,256]{2,1,0:T(8,128)(2,1)S(1)} %get-tuple-element.73), channel_id=1, source_target_pairs={{0,4},{4,8},{8,12},{12,0},{1,5},{5,9},{9,13},{13,1},{2,6},{6,10},{... | collective-permute-start | bytes 294920 | tf_op jit(solution)/shard_map/ppermute | solution.py:538
  137.6 22.4 %collective-permute-start.34 = (bf16[2,96,256]{2,1,0:T(8,128)(2,1)S(1)}, bf16[2,96,256]{2,1,0:T(8,128)(2,1)S(1)}, u32[]{:S(2)}, u32[]{:S(2)}) collective-permute-start(bf16[2,96,256]{2,1,0:T(8,128)(2,1)S(1)} %get-tuple-element.74), channel_id=1, source_target_pairs={{0,8},{4,12},{8,0},{12,4},{1,9},{5,13},{9,1},{13,5},{2,10},{6,14},... | collective-permute-start | bytes 294920 | tf_op jit(solution)/shard_map/ppermute | solution.py:538
  157.9 19.4 %collective-permute-start.27 = (bf16[2,224,256]{2,1,0:T(8,128)(2,1)S(1)}, bf16[2,224,256]{2,1,0:T(8,128)(2,1)S(1)}, u32[]{:S(2)}, u32[]{:S(2)}) collective-permute-start(bf16[2,224,256]{2,1,0:T(8,128)(2,1)S(1)} %get-tuple-element.65), channel_id=1, source_target_pairs={{0,4},{4,8},{8,12},{12,0},{1,5},{5,9},{9,13},{13,1},{2,6},{6,10},{... | collective-permute-start | bytes 688136 | tf_op jit(solution)/shard_map/ppermute | solution.py:538
  160.0 12.2 %collective-permute-start.35 = (bf16[2,96,256]{2,1,0:T(8,128)(2,1)S(1)}, bf16[2,96,256]{2,1,0:T(8,128)(2,1)S(1)}, u32[]{:S(2)}, u32[]{:S(2)}) collective-permute-start(bf16[2,96,256]{2,1,0:T(8,128)(2,1)S(1)} %get-tuple-element.75), channel_id=1, source_target_pairs={{0,12},{4,0},{8,4},{12,8},{1,13},{5,1},{9,5},{13,9},{2,14},{6,2},{... | collective-permute-start | bytes 294920 | tf_op jit(solution)/shard_map/ppermute | solution.py:538
  172.2 10.3 %collective-permute-start.28 = (bf16[2,224,256]{2,1,0:T(8,128)(2,1)S(1)}, bf16[2,224,256]{2,1,0:T(8,128)(2,1)S(1)}, u32[]{:S(2)}, u32[]{:S(2)}) collective-permute-start(bf16[2,224,256]{2,1,0:T(8,128)(2,1)S(1)} %get-tuple-element.66), channel_id=1, source_target_pairs={{0,8},{4,12},{8,0},{12,4},{1,9},{5,13},{9,1},{13,5},{2,10},{6,14},... | collective-permute-start | bytes 688136 | tf_op jit(solution)/shard_map/ppermute | solution.py:538
  173.3 26.5 %collective-permute-start.30 = (bf16[2,240,256]{2,1,0:T(8,128)(2,1)S(1)}, bf16[2,240,256]{2,1,0:T(8,128)(2,1)S(1)}, u32[]{:S(2)}, u32[]{:S(2)}) collective-permute-start(bf16[2,240,256]{2,1,0:T(8,128)(2,1)S(1)} %get-tuple-element.69), channel_id=1, source_target_pairs={{0,4},{4,8},{8,12},{12,0},{1,5},{5,9},{9,13},{13,1},{2,6},{6,10},{... | collective-permute-start | bytes 737288 | tf_op jit(solution)/shard_map/ppermute | solution.py:538
  173.8 36.1 %collective-permute-start.31 = (bf16[2,240,256]{2,1,0:T(8,128)(2,1)S(1)}, bf16[2,240,256]{2,1,0:T(8,128)(2,1)S(1)}, u32[]{:S(2)}, u32[]{:S(2)}) collective-permute-start(bf16[2,240,256]{2,1,0:T(8,128)(2,1)S(1)} %get-tuple-element.70), channel_id=1, source_target_pairs={{0,8},{4,12},{8,0},{12,4},{1,9},{5,13},{9,1},{13,5},{2,10},{6,14},... | collective-permute-start | bytes 737288 | tf_op jit(solution)/shard_map/ppermute | solution.py:538
  174.7 40.8 %collective-permute-start.32 = (bf16[2,240,256]{2,1,0:T(8,128)(2,1)S(1)}, bf16[2,240,256]{2,1,0:T(8,128)(2,1)S(1)}, u32[]{:S(2)}, u32[]{:S(2)}) collective-permute-start(bf16[2,240,256]{2,1,0:T(8,128)(2,1)S(1)} %get-tuple-element.71), channel_id=1, source_target_pairs={{0,12},{4,0},{8,4},{12,8},{1,13},{5,1},{9,5},{13,9},{2,14},{6,2},{... | collective-permute-start | bytes 737288 | tf_op jit(solution)/shard_map/ppermute | solution.py:538
  177.3 54.7 %collective-permute-start.40 = (bf16[8,336,256]{2,1,0:T(8,128)(2,1)S(1)}, bf16[8,336,256]{2,1,0:T(8,128)(2,1)S(1)}, u32[]{:S(2)}, u32[]{:S(2)}) collective-permute-start(bf16[8,336,256]{2,1,0:T(8,128)(2,1)S(1)} %settle_chunks.4.rest_4_.refs_0_), channel_id=1, source_target_pairs={{0,1},{1,0},{2,3},{3,2},{4,5},{5,4},{6,7},{7,6},{8,9},{9,8},{10,11... | collective-permute-start | bytes 4128776 | tf_op jit(solution)/shard_map/ppermute | solution.py:545
  182.5 34.0 %collective-permute-start.29 = (bf16[2,224,256]{2,1,0:T(8,128)(2,1)S(1)}, bf16[2,224,256]{2,1,0:T(8,128)(2,1)S(1)}, u32[]{:S(2)}, u32[]{:S(2)}) collective-permute-start(bf16[2,224,256]{2,1,0:T(8,128)(2,1)S(1)} %get-tuple-element.67), channel_id=1, source_target_pairs={{0,12},{4,0},{8,4},{12,8},{1,13},{5,1},{9,5},{13,9},{2,14},{6,2},{... | collective-permute-start | bytes 688136 | tf_op jit(solution)/shard_map/ppermute | solution.py:538
  199.7 20.9 %collective-permute-start.24 = (bf16[2,224,256]{2,1,0:T(8,128)(2,1)S(1)}, bf16[2,224,256]{2,1,0:T(8,128)(2,1)S(1)}, u32[]{:S(2)}, u32[]{:S(2)}) collective-permute-start(bf16[2,224,256]{2,1,0:T(8,128)(2,1)S(1)} %get-tuple-element.61), channel_id=1, source_target_pairs={{0,4},{4,8},{8,12},{12,0},{1,5},{5,9},{9,13},{13,1},{2,6},{6,10},{... | collective-permute-start | bytes 688136 | tf_op jit(solution)/shard_map/ppermute | solution.py:538
  209.9 17.2 %collective-permute-start.25 = (bf16[2,224,256]{2,1,0:T(8,128)(2,1)S(1)}, bf16[2,224,256]{2,1,0:T(8,128)(2,1)S(1)}, u32[]{:S(2)}, u32[]{:S(2)}) collective-permute-start(bf16[2,224,256]{2,1,0:T(8,128)(2,1)S(1)} %get-tuple-element.62), channel_id=1, source_target_pairs={{0,8},{4,12},{8,0},{12,4},{1,9},{5,13},{9,1},{13,5},{2,10},{6,14},... | collective-permute-start | bytes 688136 | tf_op jit(solution)/shard_map/ppermute | solution.py:538
  215.5 14.0 %collective-permute-start.26 = (bf16[2,224,256]{2,1,0:T(8,128)(2,1)S(1)}, bf16[2,224,256]{2,1,0:T(8,128)(2,1)S(1)}, u32[]{:S(2)}, u32[]{:S(2)}) collective-permute-start(bf16[2,224,256]{2,1,0:T(8,128)(2,1)S(1)} %get-tuple-element.63), channel_id=1, source_target_pairs={{0,12},{4,0},{8,4},{12,8},{1,13},{5,1},{9,5},{13,9},{2,14},{6,2},{... | collective-permute-start | bytes 688136 | tf_op jit(solution)/shard_map/ppermute | solution.py:538
  216.5 15.4 %collective-permute-start.41 = (bf16[8,240,256]{2,1,0:T(8,128)(2,1)S(1)}, bf16[8,240,256]{2,1,0:T(8,128)(2,1)S(1)}, u32[]{:S(2)}, u32[]{:S(2)}) collective-permute-start(bf16[8,240,256]{2,1,0:T(8,128)(2,1)S(1)} %settle_chunks.5.rest_4_.refs_1_), channel_id=1, source_target_pairs={{0,1},{1,0},{2,3},{3,2},{4,5},{5,4},{6,7},{7,6},{8,9},{9,8},{10,11... | collective-permute-start | bytes 2949128 | tf_op jit(solution)/shard_map/ppermute | solution.py:545
  220.6 11.3 %collective-permute-start.42 = (bf16[8,224,256]{2,1,0:T(8,128)(2,1)S(1)}, bf16[8,224,256]{2,1,0:T(8,128)(2,1)S(1)}, u32[]{:S(2)}, u32[]{:S(2)}) collective-permute-start(bf16[8,224,256]{2,1,0:T(8,128)(2,1)S(1)} %settle_chunks.6.rest_4_.refs_2_), channel_id=1, source_target_pairs={{0,1},{1,0},{2,3},{3,2},{4,5},{5,4},{6,7},{7,6},{8,9},{9,8},{10,11... | collective-permute-start | bytes 2752520 | tf_op jit(solution)/shard_map/ppermute | solution.py:545
  230.5 4.5 %collective-permute-start.39 = (bf16[8,224,256]{2,1,0:T(8,128)(2,1)S(1)}, bf16[8,224,256]{2,1,0:T(8,128)(2,1)S(1)}, u32[]{:S(2)}, u32[]{:S(2)}) collective-permute-start(bf16[8,224,256]{2,1,0:T(8,128)(2,1)S(1)} %settle_chunks.7.refs_0_), channel_id=1, source_target_pairs={{0,1},{1,0},{2,3},{3,2},{4,5},{5,4},{6,7},{7,6},{8,9},{9,8},{10,11... | collective-permute-start | bytes 2752520 | tf_op jit(solution)/shard_map/ppermute | solution.py:545

commit v4 on v3

--- a/solution.py
+++ b/solution.py
@@ -9,12 +9,19 @@
 from jax.sharding import PartitionSpec as P
 
 CAP = 2
-FORWARD_ROWS = (21, 16, 12, 9, 6)
+FORWARD_ROWS = (16, 13, 10, 9, 8, 8)
+MIDDLE_CHUNKS = 2
+INTEGRAL_LAG = 3
 BACK_ROWS = (14, 14, 15, 15)
 BACK_GROUPS = (2, 3, 4, 5)
+CHAIN_GRADIENTS = False
+SETTLE_FROM = 99
 SETTLE_WEIGHT = 50
 MERGE_WEIGHT = 50
 EXCHANGE_WEIGHT = 50
+PICK_WEIGHT = 1
+PREPARE_WEIGHT = 1
+SWAP_FIRST = 9
 VMEM_LIMIT = 40 * 1024 * 1024
 
 F32 = jnp.float32
@@ -70,7 +77,7 @@
         out_specs=[ANY] * count,
         scratch_shapes=[pltpu.SemaphoreType.DMA((count * CAP,))],
         compiler_params=params(),
-        cost_estimate=cost(0, 2 * count * CAP * rows * virt * 2),
+        cost_estimate=weighed(PICK_WEIGHT, 0, 2 * count * CAP * rows * virt * 2),
         name="pick_blocks",
     )(index, blocks, *after)
 
@@ -223,7 +230,7 @@
         in_specs=[SMEM, SMEM, SMEM, block],
         out_specs=[block, block],
         compiler_params=params(),
-        cost_estimate=cost(10 * pairs * virt * virt, pairs * virt * virt * 10),
+        cost_estimate=weighed(PREPARE_WEIGHT, 10 * pairs * virt * virt, pairs * virt * virt * 10),
         name="prepare_pairs",
     )(energies, ends, sizes, fock)
 
@@ -244,12 +251,12 @@
             out[k] = sums[d * CAP + k].astype(BF16)
 
 
-def middle_kernel(chunk, n, n_fit, slot_ref, fit_ref, *rest):
-    mine, merged, rest = split_refs(rest, n_fit, [chunk])
+def middle_kernel(chunks, n, n_fit, slot_ref, fit_ref, *rest):
+    mine, merged, rest = split_refs(rest, n_fit, chunks)
     before_ref, inverse_ref, off_ref, amp_ref, weight_ref = rest[:5]
     outs = rest[5 : 5 + n]
     held, sums, sems = rest[5 + n :]
-    for c in load_all(fit_ref, [chunk], mine, merged, held, sems):
+    for c in load_all(fit_ref, chunks, mine, merged, held, sems):
         c.wait()
 
     def step(p, carry):
@@ -270,36 +277,38 @@
         return carry
 
     lax.fori_loop(0, amp_ref.shape[0], step, 0, unroll=2)
-    here = pl.ds(pl.multiple_of(fit_ref[0] * chunk.count, 16), chunk.count)
+    total = sum(c.count for c in chunks)
+    last = chunks[-1].count
+    here = pl.ds(pl.multiple_of(fit_ref[0] * total + total - last, 16), last)
     add_gradients(slot_ref, weight_ref, lambda s: held[s, here], sums, outs)
 
 
-def middle_step(slots, fit, chunk, mine, merged, before, inverse, off):
+def middle_step(slots, fit, chunks, mine, merged, before, inverse, off):
     n_fit = len(mine)
     pairs, virt, _ = before.shape
-    all_slots = CAP + merged[0].shape[0]
+    all_slots = CAP + merged[0][0].shape[0]
     n = all_slots // CAP
-    return pl.pallas_call(
-        functools.partial(middle_kernel, chunk, n, n_fit),
+    rows = sum(c.count for c in chunks)
+    return pl.pallas_call(
+        functools.partial(middle_kernel, chunks, n, n_fit),
         out_shape=[
             jax.ShapeDtypeStruct((pairs, virt, virt), BF16),
             jax.ShapeDtypeStruct((2 * pairs, virt, virt), BF16),
         ]
-        + [jax.ShapeDtypeStruct((CAP, chunk.count, virt), BF16)] * n,
-        in_specs=[SMEM, SMEM] + [ANY] * (2 * n_fit) + [VMEM] * 3,
+        + [jax.ShapeDtypeStruct((CAP, chunks[-1].count, virt), BF16)] * n,
+        in_specs=[SMEM, SMEM] + [ANY] * (n_fit * (1 + len(chunks))) + [VMEM] * 3,
         out_specs=[VMEM] * (2 + n),
         scratch_shapes=[
-            pltpu.VMEM((all_slots, n_fit * chunk.count, virt), BF16),
-            pltpu.VMEM((all_slots, chunk.count, virt), F32),
-            pltpu.SemaphoreType.DMA((2 * n_fit,)),
+            pltpu.VMEM((all_slots, n_fit * rows, virt), BF16),
+            pltpu.VMEM((all_slots, chunks[-1].count, virt), F32),
+            pltpu.SemaphoreType.DMA((2 * n_fit * len(chunks),)),
         ],
         compiler_params=params(),
         cost_estimate=cost(
-            pairs * (4 * virt**3 + 6 * chunk.count * n_fit * virt * virt),
-            pairs * virt * virt * 16,
+            pairs * (4 * virt**3 + 6 * rows * n_fit * virt * virt), pairs * virt * virt * 16
         ),
         name="middle_step",
-    )(slots, fit, *mine, *merged, before, inverse, off)
+    )(slots, fit, *mine, *[x for m in merged for x in m], before, inverse, off)
 
 
 def gradient_kernel(parts, n, slot_ref, weight_ref, mine_ref, *rest):
@@ -459,6 +468,7 @@
     total_orbs = local_orbs * n
     me = lax.axis_index("orb")
 
+    blocks = pltpu.with_memory_space_constraint(blocks, pltpu.HBM)
     endpoints = pair_list.reshape(-1)
     relative = (endpoints - me * local_orbs) % total_orbs
     named = jnp.any(
@@ -500,28 +510,34 @@
         here = slice(place, place + 1)
         return exchange_chunks(slots, fit, chunks[here], mine, merged[here], before, after)
 
-    for place, c in enumerate(chunks):
-        after = [mine[0]] if place < 2 else [merged[place - 2][0]]
-        picked = pick_blocks(asked[1:], blocks, c.start, c.count, after)
-        arrived.append(
-            [lax.ppermute(picked[d - 1], "orb", shifted(n, n - d)) for d in range(1, n)]
-        )
-        if place == 1:
-            pass_on(0, [picked[0], inverse])
-        elif place == 2:
-            pass_on(1, [picked[0]])
-        elif place > 2:
-            ints = integrals(place - 3, ints, [])
-            pass_on(place - 1, [picked[0], ints])
-    ints = integrals(len(chunks) - 3, ints, [merged[-1][0]])
-    pass_on(len(chunks) - 1, [ints])
-    ints = integrals(len(chunks) - 2, ints, [merged[-1][0]])
+    count = len(chunks)
+    early = count - MIDDLE_CHUNKS
+    for place in range(count + 1):
+        if place < count:
+            c = chunks[place]
+            after = [mine[0]] if place < 2 else [merged[place - 2][0]]
+            picked = pick_blocks(asked[1:], blocks, c.start, c.count, after)
+            arrived.append(
+                [lax.ppermute(picked[d - 1], "orb", shifted(n, n - d)) for d in range(1, n)]
+            )
+        if place > 0:
+            after = [picked[0]] if place < count else []
+            after += [inverse] if place == 1 else []
+            after += merged[-1][1:] if place > SWAP_FIRST else []
+            done = place - 1 - INTEGRAL_LAG
+            if 0 <= done < early:
+                ints = integrals(done, ints, [])
+                after.append(ints)
+            pass_on(place - 1, after)
+    for place in range(max(count - INTEGRAL_LAG, 0), early):
+        ints = integrals(place, ints, [merged[-1][0]])
     amplitudes, weights, *sums = middle_step(
-        slots, fit, chunks[-1], mine, merged[-1], ints, inverse, off
+        slots, fit, chunks[early:], mine, merged[early:], ints, inverse, off
     )
 
-    back = [(chunks[-1], sums)]
-    for c in reversed(cut_rows(chunks[-1].start, BACK_ROWS)):
+    first = chunks[-1]
+    back = [(first, sums)]
+    for c in reversed(cut_rows(first.start, BACK_ROWS)):
         parts, sources = [], []
         for place, chunk in enumerate(chunks[:-1]):
             low = max(c.start, chunk.start)
@@ -529,7 +545,7 @@
             if low < high:
                 parts.append((low, low - chunk.start, high - low))
                 sources.append(merged[place][0])
-        after = []
+        after = back[-1][1][:1] if CHAIN_GRADIENTS else []
         back.append((c, gradient_chunk(slots, weights, mine[0], parts, sources, after)))
 
     swap = shifted(n_rep, 1)
@@ -540,7 +556,10 @@
     ]
     low = 0
     for high in BACK_GROUPS:
-        here = settle_chunks(asked, returned[low:high], local_orbs, [w[1] for w in waiting[-1:]])
+        after = [w[1] for w in waiting[-1:]]
+        if high == len(back):
+            after = [w[2] for w in waiting[SETTLE_FROM:]]
+        here = settle_chunks(asked, returned[low:high], local_orbs, after)
         group = [c for c, _ in back[low:high]]
         waiting.append((group, here, lax.ppermute(here, "rep", swap)))
         low = high

time: 237 us -> 229 us (0.966)
  starting transfers between devices: 93.5 us -> 62.8 us
  Pallas kernels: 52.4 us -> 76.1 us
  local copies, waits for them, and re-layouts: 7.47 us -> 3.39 us
    ppermute x15, starting transfers between devices: 44.3 us -> 16.3 us  [per_device(): lax.ppermute(sums[d], 'orb', shifted(n, d))]
    pallas_call x6 -> x7, Pallas kernels: 7.87 us -> 31.3 us  [pick_blocks(): pl.pallas_call(functools.partial(pick_kernel, start, rows, len(after)), o...]
    ppermute x15, waiting for transfers between devices: 31 us -> 54 us  [per_device(): lax.ppermute(sums[d], 'orb', shifted(n, d))]
    ppermute x15 -> x18, waiting for transfers between devices: 37.9 us -> 19 us  [per_device(): lax.ppermute(picked[d - 1], 'orb', shifted(n, n - d))]
    ppermute x6 -> x7, starting transfers between devices: 5.49 us -> 11.6 us  [around_fit(): lax.ppermute(x, 'fit', shifted(n_fit, d))]
    unnamed x25 -> x13, local copies, waits for them, and re-layouts: 6.92 us -> 2.27 us
    ppermute x15 -> x18, starting transfers between devices: 27.7 us -> 23.2 us  [per_device(): lax.ppermute(picked[d - 1], 'orb', shifted(n, n - d))]
    ppermute x4, starting transfers between devices: 12.3 us -> 7.92 us  [per_device(): waiting.append((group, here, lax.ppermute(here, 'rep', swap)))]
  transfers between devices with their start and end apart: 43 -> 47, of which waited for: 15 -> 13; matrix products, arithmetic and copies ran while one was open for 0% -> 1% of each run, Pallas kernels for 17% -> 29%
where the time goes in v4:
time: 229 us; the launch traced here: 228 us
  waiting for transfers between devices  81.6 us (36%)
  Pallas kernels  76.1 us (33%)
  starting transfers between devices  62.8 us (27%)
  local copies, waits for them, and re-layouts  3.39 us (1%)
  other arithmetic  3.07 us (1%)
    ppermute x15, waiting for transfers between devices, per_device(): lax.ppermute(sums[d], 'orb', shifted(n, d))  54 us
    pallas_call x7, Pallas kernels, pick_blocks(): pl.pallas_call(functools.partial(pick_kernel, start, rows, len(after)), o...  31.3 us
    ppermute x18, starting transfers between devices, per_device(): lax.ppermute(picked[d - 1], 'orb', shifted(n, n - d))  23.2 us
    ppermute x18, waiting for transfers between devices, per_device(): lax.ppermute(picked[d - 1], 'orb', shifted(n, n - d))  19 us
    ppermute x15, starting transfers between devices, per_device(): lax.ppermute(sums[d], 'orb', shifted(n, d))  16.3 us
    pallas_call x4, Pallas kernels, exchange_chunks(): pl.pallas_call(functools.partial(exchange_kernel, chunks, n_fit, first, l...  13.3 us
    pallas_call x4, Pallas kernels, gradient_chunk(): pl.pallas_call(functools.partial(gradient_kernel, parts, n), out_shape=[j...  11.7 us
    ppermute x7, starting transfers between devices, around_fit(): lax.ppermute(x, 'fit', shifted(n_fit, d))  11.6 us
  transfers between devices with their start and end apart: 47, of which 13 were waited for; matrix products, arithmetic and copies ran while one was open for 1% of the time, Pallas kernels for 29%

profile of v4, /device:TPU:9, one launch (start us, length us, event | category | flops | bytes accessed | tf_op | source)
XLA Modules:
  0.0 228.3 jit_solution(13888292928493781697)
XLA Ops:
  3.0 1.3 collective-permute-start.1
  4.3 1.1 collective-permute-start.2
  5.4 1.4 collective-permute-start.3
  6.9 1.8 pick_blocks.7.rest_0_.rest_1_.mine_ref
  8.7 1.8 pick_blocks.8
  10.5 1.1 collective-permute-start.4
  11.7 1.2 collective-permute-start.5
  12.8 2.3 %collective-permute-start.6 = (bf16[2,256,256]{2,1,0:T(8,128)(2,1)S(1)}, bf16[2,256,256]{2,1,0:T(8,128)(2,1)S(1)}, u32[]{:S(2)}, u32[]{:S(2)}) collective-permute-start(bf16[2,256,256]{2,1,0:T(8,128)(2,1)S(1)} %get-tuple-element.46), channel_id=1, source_target_pairs={{0,4},{4,8},{8,12},{12,0},{1,5},{5,9},{9,13},{13,1},{2,6},{6,10},{... | collective-permute-start | bytes 786440 | tf_op jit(solution)/shard_map/ppermute | solution.py:521
  15.1 1.2 collective-permute-start
  16.3 21.1 %pick_blocks.9 = (bf16[2,208,256]{2,1,0:T(8,128)(2,1)}, bf16[2,208,256]{2,1,0:T(8,128)(2,1)}, bf16[2,208,256]{2,1,0:T(8,128)(2,1)}) custom-call(s32[3,2]{1,0:T(4,128)S(1)} %pad_add_fusion.index_ref, bf16[8,1024,256]{2,1,0:T(8,128)(2,1)} %blocks_ref.13, bf16[2,1024,256]{2,1,0:T(8,128)(2,1)S(1)} %pick_blocks.7.rest_0_.rest_1_.mine_ref), custom_call_target="tpu_custom_call" | custom-call | bytes 1277952 | tf_op jit(solution)/shard_map/pick_blocks/pallas_call | solution.py:73
  37.7 1.7 prepare_pairs.1
  40.4 1.3 copy-done
  42.9 1.5 collective-permute-start.10
  45.9 1.7 pick_blocks.10
  47.6 5.4 %collective-permute-done.11.refs_1_ = bf16[2,208,256]{2,1,0:T(8,128)(2,1)S(1)} collective-permute-done((bf16[2,208,256]{2,1,0:T(8,128)(2,1)}, bf16[2,208,256]{2,1,0:T(8,128)(2,1)S(1)}, u32[]{:S(2)}, u32[]{:S(2)}) %collective-permute-start.11) | collective-permute-done | bytes 213024 | tf_op jit(solution)/shard_map/ppermute | solution.py:521
  53.0 3.5 %collective-permute-start.8 = (bf16[2,160,256]{2,1,0:T(8,128)(2,1)S(1)}, bf16[2,160,256]{2,1,0:T(8,128)(2,1)S(1)}, u32[]{:S(2)}, u32[]{:S(2)}) collective-permute-start(bf16[2,160,256]{2,1,0:T(8,128)(2,1)S(1)} %get-tuple-element.50), channel_id=1, source_target_pairs={{0,8},{4,12},{8,0},{12,4},{1,9},{5,13},{9,1},{13,5},{2,10},{6,14},... | collective-permute-start | bytes 491528 | tf_op jit(solution)/shard_map/ppermute | solution.py:521
  56.5 5.7 %collective-permute-done.12.refs_2_ = bf16[2,208,256]{2,1,0:T(8,128)(2,1)S(1)} collective-permute-done((bf16[2,208,256]{2,1,0:T(8,128)(2,1)}, bf16[2,208,256]{2,1,0:T(8,128)(2,1)S(1)}, u32[]{:S(2)}, u32[]{:S(2)}) %collective-permute-start.12) | collective-permute-done | bytes 213024 | tf_op jit(solution)/shard_map/ppermute | solution.py:521
  62.1 2.1 collective-permute-start.9
  65.1 1.7 pick_blocks.11
  66.8 1.3 collective-permute-start.20
  68.1 6.2 %collective-permute-done.9.refs_2_ = bf16[2,160,256]{2,1,0:T(8,128)(2,1)S(1)} collective-permute-done((bf16[2,160,256]{2,1,0:T(8,128)(2,1)S(1)}, bf16[2,160,256]{2,1,0:T(8,128)(2,1)S(1)}, u32[]{:S(2)}, u32[]{:S(2)}) %collective-permute-start.9) | collective-permute-done | bytes 163872 | tf_op jit(solution)/shard_map/ppermute | solution.py:521
  74.3 3.4 %collective-permute-start.16 = (bf16[2,144,256]{2,1,0:T(8,128)(2,1)S(1)}, bf16[2,144,256]{2,1,0:T(8,128)(2,1)S(1)}, u32[]{:S(2)}, u32[]{:S(2)}) collective-permute-start(bf16[2,144,256]{2,1,0:T(8,128)(2,1)S(1)} %get-tuple-element.54.refs_3_), channel_id=1, source_target_pairs={{0,12},{4,0},{8,4},{12,8},{1,13},{5,1},{9,5},{13,9},{2,14},{6,2},{... | collective-permute-start | bytes 442376 | tf_op jit(solution)/shard_map/ppermute | solution.py:521
  78.3 1.6 pick_blocks.12
  80.0 1.3 collective-permute-start.25
  81.3 4.0 %exchange_chunks.4.refs_4_.rest_4_ = f32[8,256,256]{2,1,0:T(8,128)S(1)} custom-call(s32[16]{0:T(128)S(1)} %multiply_add_fusion.slot_ref, s32[1]{0:T(128)} %bitcast.fit_ref, bf16[2,1024,256]{2,1,0:T(8,128)(2,1)S(1)} %pick_blocks.7.rest_0_.rest_1_.mine_ref, bf16[2,1024,256]{2,1,0:T(8,128)(2,1)S(1)} %collective-permute-done.rest_1_.rest_2_, ...), custom_call_target="tpu_custom_call" | custom-call | flops 26843545600 | bytes 314572800 | tf_op jit(solution)/shard_map/exchange_chunks/pallas_call | solution.py:184
  85.4 2.2 collective-permute-start.14
  87.6 2.3 %collective-permute-start.15 = (bf16[2,128,256]{2,1,0:T(8,128)(2,1)S(1)}, bf16[2,128,256]{2,1,0:T(8,128)(2,1)S(1)}, u32[]{:S(2)}, u32[]{:S(2)}) collective-permute-start(bf16[2,128,256]{2,1,0:T(8,128)(2,1)S(1)} %get-tuple-element.57), channel_id=1, source_target_pairs={{0,4},{4,8},{8,12},{12,0},{1,5},{5,9},{9,13},{13,1},{2,6},{6,10},{... | collective-permute-start | bytes 393224 | tf_op jit(solution)/shard_map/ppermute | solution.py:521
  90.5 2.4 %collective-permute-start.27 = (bf16[6,144,256]{2,1,0:T(8,128)(2,1)S(1)}, bf16[6,144,256]{2,1,0:T(8,128)(2,1)S(1)}, u32[]{:S(2)}, u32[]{:S(2)}) collective-permute-start(bf16[6,144,256]{2,1,0:T(8,128)(2,1)S(1)} %merge_chunk.9.rest_0_.rest_3_.rest_2_), channel_id=1, source_target_pairs={{0,2},{2,0},{1,3},{3,1},{4,6},{6,4},{5,7},{7,5},{8,10},{10,8},{9,1... | collective-permute-start | bytes 1327112 | tf_op jit(solution)/shard_map/ppermute | solution.py:460
  92.9 3.2 %exchange_chunks.5.refs_4_.rest_4_ = f32[8,256,256]{2,1,0:T(8,128)S(1)} custom-call(s32[16]{0:T(128)S(1)} %multiply_add_fusion.slot_ref, s32[1]{0:T(128)} %bitcast.fit_ref, bf16[2,1024,256]{2,1,0:T(8,128)(2,1)S(1)} %pick_blocks.7.rest_0_.rest_1_.mine_ref, bf16[2,1024,256]{2,1,0:T(8,128)(2,1)S(1)} %collective-permute-done.rest_1_.rest_2_, ...), custom_call_target="tpu_custom_call" | custom-call | flops 21810380800 | bytes 294912000 | tf_op jit(solution)/shard_map/exchange_chunks/pallas_call | solution.py:184
  96.1 1.6 pick_blocks.13
  97.7 1.2 collective-permute-start.23
  98.9 1.3 collective-permute-start.24
  101.0 1.7 collective-permute-start.21
  102.7 3.1 %exchange_chunks.6.refs_3_.rest_5_ = f32[8,256,256]{2,1,0:T(8,128)S(1)} custom-call(s32[16]{0:T(128)S(1)} %multiply_add_fusion.slot_ref, s32[1]{0:T(128)} %bitcast.fit_ref, bf16[2,1024,256]{2,1,0:T(8,128)(2,1)S(1)} %pick_blocks.7.rest_0_.rest_1_.mine_ref, bf16[2,1024,256]{2,1,0:T(8,128)(2,1)S(1)} %collective-permute-done.rest_1_.rest_2_, ...), custom_call_target="tpu_custom_call" | custom-call | flops 16777216000 | bytes 275251200 | tf_op jit(solution)/shard_map/exchange_chunks/pallas_call | solution.py:184
  106.5 1.1 collective-permute-done.22.refs_0_
  108.1 3.4 %collective-permute-start.26 = (bf16[6,128,256]{2,1,0:T(8,128)(2,1)S(1)}, bf16[6,128,256]{2,1,0:T(8,128)(2,1)S(1)}, u32[]{:S(2)}, u32[]{:S(2)}) collective-permute-start(bf16[6,128,256]{2,1,0:T(8,128)(2,1)S(1)} %merge_chunk.11.rest_0_.rest_4_), channel_id=1, source_target_pairs={{0,2},{2,0},{1,3},{3,1},{4,6},{6,4},{5,7},{7,5},{8,10},{10,8},{9,1... | collective-permute-start | bytes 1179656 | tf_op jit(solution)/shard_map/ppermute | solution.py:460
  111.5 3.0 %exchange_chunks.7.rest_6_ = f32[8,256,256]{2,1,0:T(8,128)S(1)} custom-call(s32[16]{0:T(128)S(1)} %multiply_add_fusion.slot_ref, s32[1]{0:T(128)} %bitcast.fit_ref, bf16[6,128,256]{2,1,0:T(8,128)(2,1)S(1)} %merge_chunk.11.rest_0_.rest_4_, bf16[2,1024,256]{2,1,0:T(8,128)(2,1)S(1)} %pick_blocks.7.rest_0_.rest_1_.mine_ref, ...), custom_call_target="tpu_custom_call" | custom-call | flops 15099494400 | bytes 268697600 | tf_op jit(solution)/shard_map/exchange_chunks/pallas_call | solution.py:184
  114.6 6.6 %collective-permute-done.26.rest_5_ = bf16[6,128,256]{2,1,0:T(8,128)(2,1)S(1)} collective-permute-done((bf16[6,128,256]{2,1,0:T(8,128)(2,1)S(1)}, bf16[6,128,256]{2,1,0:T(8,128)(2,1)S(1)}, u32[]{:S(2)}, u32[]{:S(2)}) %collective-permute-start.26) | collective-permute-done | bytes 393248 | tf_op jit(solution)/shard_map/ppermute | solution.py:460
  121.2 6.6 %middle_step.1 = (bf16[8,256,256]{2,1,0:T(8,128)(2,1)}, bf16[16,256,256]{2,1,0:T(8,128)(2,1)S(1)}, bf16[2,128,256]{2,1,0:T(8,128)(2,1)S(1)}, bf16[2,128,256]{2,1...) custom-call(s32[16]{0:T(128)S(1)} %multiply_add_fusion.slot_ref, ...), custom_call_target="tpu_custom_call" | custom-call | flops 2147483648 | bytes 8388608 | tf_op jit(solution)/shard_map/middle_step/pallas_call | solution.py:292
  127.9 2.9 %gradient_chunk.5 = (bf16[2,224,256]{2,1,0:T(8,128)(2,1)S(1)}, bf16[2,224,256]{2,1,0:T(8,128)(2,1)S(1)}, bf16[2,224,256]{2,1,0:T(8,128)(2,1)S(1)}, bf16[2,224,256]{2,1,0:T(8,128)(2,1)S(1)}) custom-call(s32[16]{0:T(128)S(1)} %multiply_add_fusion.slot_ref, bf16[16,256,256]{2,1,0:T(8,128)(2,1)S(1)} %get-tuple-element.65.weight_ref, ...), custom_call_target="tpu_custom_call" | custom-call | flops 469762048 | bytes 3932160 | tf_op jit(solution)/shard_map/gradient_chunk/pallas_call | solution.py:350
  130.8 2.6 %collective-permute-start.35 = (bf16[2,224,256]{2,1,0:T(8,128)(2,1)S(1)}, bf16[2,224,256]{2,1,0:T(8,128)(2,1)S(1)}, u32[]{:S(2)}, u32[]{:S(2)}) collective-permute-start(bf16[2,224,256]{2,1,0:T(8,128)(2,1)S(1)} %get-tuple-element.75), channel_id=1, source_target_pairs={{0,4},{4,8},{8,12},{12,0},{1,5},{5,9},{9,13},{13,1},{2,6},{6,10},{... | collective-permute-start | bytes 688136 | tf_op jit(solution)/shard_map/ppermute | solution.py:554
  134.7 2.3 %collective-permute-start.34 = (bf16[2,128,256]{2,1,0:T(8,128)(2,1)S(1)}, bf16[2,128,256]{2,1,0:T(8,128)(2,1)S(1)}, u32[]{:S(2)}, u32[]{:S(2)}) collective-permute-start(bf16[2,128,256]{2,1,0:T(8,128)(2,1)S(1)} %get-tuple-element.73), channel_id=1, source_target_pairs={{0,12},{4,0},{8,4},{12,8},{1,13},{5,1},{9,5},{13,9},{2,14},{6,2},{... | collective-permute-start | bytes 393224 | tf_op jit(solution)/shard_map/ppermute | solution.py:554
  137.0 3.0 %gradient_chunk.6 = (bf16[2,224,256]{2,1,0:T(8,128)(2,1)S(1)}, bf16[2,224,256]{2,1,0:T(8,128)(2,1)S(1)}, bf16[2,224,256]{2,1,0:T(8,128)(2,1)S(1)}, bf16[2,224,256]{2,1,0:T(8,128)(2,1)S(1)}) custom-call(s32[16]{0:T(128)S(1)} %multiply_add_fusion.slot_ref, bf16[16,256,256]{2,1,0:T(8,128)(2,1)S(1)} %get-tuple-element.65.weight_ref, ...), custom_call_target="tpu_custom_call" | custom-call | flops 469762048 | bytes 3932160 | tf_op jit(solution)/shard_map/gradient_chunk/pallas_call | solution.py:350
  140.0 24.7 %collective-permute-done.34.rest_3_ = bf16[2,128,256]{2,1,0:T(8,128)(2,1)S(1)} collective-permute-done((bf16[2,128,256]{2,1,0:T(8,128)(2,1)S(1)}, bf16[2,128,256]{2,1,0:T(8,128)(2,1)S(1)}, u32[]{:S(2)}, u32[]{:S(2)}) %collective-permute-start.34) | collective-permute-done | bytes 131104 | tf_op jit(solution)/shard_map/ppermute | solution.py:554
  164.8 1.2 settle_chunks.5.rest_4_.refs_0_
  166.0 2.9 %collective-permute-start.44 = (bf16[8,352,256]{2,1,0:T(8,128)(2,1)S(1)}, bf16[8,352,256]{2,1,0:T(8,128)(2,1)S(1)}, u32[]{:S(2)}, u32[]{:S(2)}) collective-permute-start(bf16[8,352,256]{2,1,0:T(8,128)(2,1)S(1)} %settle_chunks.5.rest_4_.refs_0_), channel_id=1, source_target_pairs={{0,1},{1,0},{2,3},{3,2},{4,5},{5,4},{6,7},{7,6},{8,9},{9,8},{10,11... | collective-permute-start | bytes 4325384 | tf_op jit(solution)/shard_map/ppermute | solution.py:564
  168.8 3.0 %gradient_chunk.4 = (bf16[2,240,256]{2,1,0:T(8,128)(2,1)S(1)}, bf16[2,240,256]{2,1,0:T(8,128)(2,1)S(1)}, bf16[2,240,256]{2,1,0:T(8,128)(2,1)S(1)}, bf16[2,240,256]{2,1,0:T(8,128)(2,1)S(1)}) custom-call(s32[16]{0:T(128)S(1)} %multiply_add_fusion.slot_ref, bf16[16,256,256]{2,1,0:T(8,128)(2,1)S(1)} %get-tuple-element.65.weight_ref, ...), custom_call_target="tpu_custom_call" | custom-call | flops 503316480 | bytes 4063232 | tf_op jit(solution)/shard_map/gradient_chunk/pallas_call | solution.py:350
  171.9 2.8 %collective-permute-start.29 = (bf16[2,240,256]{2,1,0:T(8,128)(2,1)S(1)}, bf16[2,240,256]{2,1,0:T(8,128)(2,1)S(1)}, u32[]{:S(2)}, u32[]{:S(2)}) collective-permute-start(bf16[2,240,256]{2,1,0:T(8,128)(2,1)S(1)} %get-tuple-element.68), channel_id=1, source_target_pairs={{0,8},{4,12},{8,0},{12,4},{1,9},{5,13},{9,1},{13,5},{2,10},{6,14},... | collective-permute-start | bytes 737288 | tf_op jit(solution)/shard_map/ppermute | solution.py:554
  174.7 1.3 collective-permute-start.30
  176.1 2.9 %gradient_chunk.7 = (bf16[2,208,256]{2,1,0:T(8,128)(2,1)S(1)}, bf16[2,208,256]{2,1,0:T(8,128)(2,1)S(1)}, bf16[2,208,256]{2,1,0:T(8,128)(2,1)S(1)}, bf16[2,208,256]{2,1,0:T(8,128)(2,1)S(1)}) custom-call(s32[16]{0:T(128)S(1)} %multiply_add_fusion.slot_ref, bf16[16,256,256]{2,1,0:T(8,128)(2,1)S(1)} %get-tuple-element.65.weight_ref, ...), custom_call_target="tpu_custom_call" | custom-call | flops 436207616 | bytes 3801088 | tf_op jit(solution)/shard_map/gradient_chunk/pallas_call | solution.py:350
  178.9 16.3 %collective-permute-done.28.rest_1_ = bf16[2,240,256]{2,1,0:T(8,128)(2,1)S(1)} collective-permute-done((bf16[2,240,256]{2,1,0:T(8,128)(2,1)S(1)}, bf16[2,240,256]{2,1,0:T(8,128)(2,1)S(1)}, u32[]{:S(2)}, u32[]{:S(2)}) %collective-permute-start.28) | collective-permute-done | bytes 245792 | tf_op jit(solution)/shard_map/ppermute | solution.py:554
  195.2 2.2 collective-permute-start.41
  197.4 3.8 %collective-permute-done.29.rest_2_ = bf16[2,240,256]{2,1,0:T(8,128)(2,1)S(1)} collective-permute-done((bf16[2,240,256]{2,1,0:T(8,128)(2,1)S(1)}, bf16[2,240,256]{2,1,0:T(8,128)(2,1)S(1)}, u32[]{:S(2)}, u32[]{:S(2)}) %collective-permute-start.29) | collective-permute-done | bytes 245792 | tf_op jit(solution)/shard_map/ppermute | solution.py:554
  201.2 3.6 %collective-permute-start.42 = (bf16[2,208,256]{2,1,0:T(8,128)(2,1)S(1)}, bf16[2,208,256]{2,1,0:T(8,128)(2,1)S(1)}, u32[]{:S(2)}, u32[]{:S(2)}) collective-permute-start(bf16[2,208,256]{2,1,0:T(8,128)(2,1)S(1)} %get-tuple-element.84), channel_id=1, source_target_pairs={{0,8},{4,12},{8,0},{12,4},{1,9},{5,13},{9,1},{13,5},{2,10},{6,14},... | collective-permute-start | bytes 638984 | tf_op jit(solution)/shard_map/ppermute | solution.py:554
  204.8 1.0 settle_chunks.4.refs_0_
  205.8 3.2 %collective-permute-done.40.rest_3_ = bf16[2,224,256]{2,1,0:T(8,128)(2,1)S(1)} collective-permute-done((bf16[2,224,256]{2,1,0:T(8,128)(2,1)S(1)}, bf16[2,224,256]{2,1,0:T(8,128)(2,1)S(1)}, u32[]{:S(2)}, u32[]{:S(2)}) %collective-permute-start.40) | collective-permute-done | bytes 229408 | tf_op jit(solution)/shard_map/ppermute | solution.py:554
  209.0 4.4 %collective-permute-start.31 = (bf16[8,240,256]{2,1,0:T(8,128)(2,1)S(1)}, bf16[8,240,256]{2,1,0:T(8,128)(2,1)S(1)}, u32[]{:S(2)}, u32[]{:S(2)}) collective-permute-start(bf16[8,240,256]{2,1,0:T(8,128)(2,1)S(1)} %settle_chunks.4.refs_0_), channel_id=1, source_target_pairs={{0,1},{1,0},{2,3},{3,2},{4,5},{5,4},{6,7},{7,6},{8,9},{9,8},{10,11... | collective-permute-start | bytes 2949128 | tf_op jit(solution)/shard_map/ppermute | solution.py:564
  213.4 0.9 settle_chunks.6.rest_4_.refs_1_
  214.5 4.3 %collective-permute-done.42.rest_2_ = bf16[2,208,256]{2,1,0:T(8,128)(2,1)S(1)} collective-permute-done((bf16[2,208,256]{2,1,0:T(8,128)(2,1)S(1)}, bf16[2,208,256]{2,1,0:T(8,128)(2,1)S(1)}, u32[]{:S(2)}, u32[]{:S(2)}) %collective-permute-start.42) | collective-permute-done | bytes 213024 | tf_op jit(solution)/shard_map/ppermute | solution.py:554
  218.8 1.5 collective-permute-done.43.rest_3_
  220.3 0.9 settle_chunks.7.refs_2_
  221.8 2.0 collective-permute-done.46.refs_5_
  223.8 3.0 %add_chunks.2.refs_2_ = f32[8,1024,256]{2,1,0:T(8,128)} custom-call(bf16[8,352,256]{2,1,0:T(8,128)(2,1)S(1)} %settle_chunks.5.rest_4_.refs_0_, bf16[8,224,256]{2,1,0:T(8,128)(2,1)S(1)} %settle_chunks.6.rest_4_.refs_1_, bf16[8,208,256]{2,1,0:T(8,128)(2,1)S(1)} %settle_chunks.7.refs_2_, bf16[8,352,256]{2,1,0:T(8,128)(2,1)S(1)} %collective-permute-done.44.refs_3_, ...), custom_call_target="tpu_custom_call" | custom-call | bytes 12845056 | tf_op jit(solution)/shard_map/add_chunks/pallas_call | solution.py:430
  226.8 1.4 add_chunks.3
  (97 shorter events, 12.7 us)
Async XLA Ops:
  3.0 5.6 %collective-permute-start.1 = (f32[10]{0:T(128)S(1)}, f32[10]{0:T(128)S(1)}, u32[]{:S(2)}, u32[]{:S(2)}) collective-permute-start(f32[10]{0:T(128)S(1)} %get-tuple-element.89), channel_id=1, source_target_pairs={{0,4},{4,8},{8,12},{12,0},{1,5},{5,9},{9,13},{13,1},{2,6},{6,10},{... | collective-permute-start | bytes 128 | tf_op jit(solution)/shard_map/ppermute | solution.py:493
  4.3 4.4 %collective-permute-start.2 = (f32[10]{0:T(128)S(1)}, f32[10]{0:T(128)S(1)}, u32[]{:S(2)}, u32[]{:S(2)}) collective-permute-start(f32[10]{0:T(128)S(1)} %get-tuple-element.90), channel_id=1, source_target_pairs={{0,8},{4,12},{8,0},{12,4},{1,9},{5,13},{9,1},{13,5},{2,10},{6,14},... | collective-permute-start | bytes 128 | tf_op jit(solution)/shard_map/ppermute | solution.py:493
  5.4 3.3 %collective-permute-start.3 = (f32[10]{0:T(128)S(1)}, f32[10]{0:T(128)S(1)}, u32[]{:S(2)}, u32[]{:S(2)}) collective-permute-start(f32[10]{0:T(128)S(1)} %get-tuple-element.91), channel_id=1, source_target_pairs={{0,12},{4,0},{8,4},{12,8},{1,13},{5,1},{9,5},{13,9},{2,14},{6,2},{... | collective-permute-start | bytes 128 | tf_op jit(solution)/shard_map/ppermute | solution.py:493
  10.5 28.9 %collective-permute-start.4 = (bf16[2,256,256]{2,1,0:T(8,128)(2,1)S(1)}, bf16[2,256,256]{2,1,0:T(8,128)(2,1)S(1)}, u32[]{:S(2)}, u32[]{:S(2)}) collective-permute-start(bf16[2,256,256]{2,1,0:T(8,128)(2,1)S(1)} %get-tuple-element.44), channel_id=1, source_target_pairs={{0,12},{4,0},{8,4},{12,8},{1,13},{5,1},{9,5},{13,9},{2,14},{6,2},{... | collective-permute-start | bytes 786440 | tf_op jit(solution)/shard_map/ppermute | solution.py:521
  11.7 27.8 %collective-permute-start.5 = (bf16[2,256,256]{2,1,0:T(8,128)(2,1)S(1)}, bf16[2,256,256]{2,1,0:T(8,128)(2,1)S(1)}, u32[]{:S(2)}, u32[]{:S(2)}) collective-permute-start(bf16[2,256,256]{2,1,0:T(8,128)(2,1)S(1)} %get-tuple-element.45), channel_id=1, source_target_pairs={{0,8},{4,12},{8,0},{12,4},{1,9},{5,13},{9,1},{13,5},{2,10},{6,14},... | collective-permute-start | bytes 786440 | tf_op jit(solution)/shard_map/ppermute | solution.py:521
  12.8 24.9 %copy-start.2 = (f32[8,256,256]{2,1,0:T(8,128)S(1)}, f32[8,256,256]{2,1,0:T(8,128)}, u32[]{:S(2)}) copy-start(f32[8,256,256]{2,1,0:T(8,128)} %fock_ref.1) | copy-start | bytes 6291460
  12.8 24.9 %copy-start.5 = (s32[8]{0:T(128)S(1)}, s32[8]{0:T(128)}, u32[]{:S(2)}) copy-start(s32[8]{0:T(128)} %size_ref.1) | copy-start | bytes 100
  12.8 26.7 %collective-permute-start.6 = (bf16[2,256,256]{2,1,0:T(8,128)(2,1)S(1)}, bf16[2,256,256]{2,1,0:T(8,128)(2,1)S(1)}, u32[]{:S(2)}, u32[]{:S(2)}) collective-permute-start(bf16[2,256,256]{2,1,0:T(8,128)(2,1)S(1)} %get-tuple-element.46), channel_id=1, source_target_pairs={{0,4},{4,8},{8,12},{12,0},{1,5},{5,9},{9,13},{13,1},{2,6},{6,10},{... | collective-permute-start | bytes 786440 | tf_op jit(solution)/shard_map/ppermute | solution.py:521
  15.1 64.8 %collective-permute-start = (bf16[2,1024,256]{2,1,0:T(8,128)(2,1)S(1)}, bf16[2,1024,256]{2,1,0:T(8,128)(2,1)S(1)}, u32[]{:S(2)}, u32[]{:S(2)}) collective-permute-start(bf16[2,1024,256]{2,1,0:T(8,128)(2,1)S(1)} %pick_blocks.7.rest_0_.rest_1_.mine_ref), channel_id=1, source_target_pairs={{0,2},{2,0},{1,3},{3,1},{4,6},{6,4},{5,7},{7,5},{8,10},{10,8},{9,1... | collective-permute-start | bytes 3145736 | tf_op jit(solution)/shard_map/ppermute | solution.py:460
  39.5 1.0 copy-start.3
  40.4 1.3 copy-start
  41.8 38.3 %collective-permute-start.19 = (bf16[6,256,256]{2,1,0:T(8,128)(2,1)S(1)}, bf16[6,256,256]{2,1,0:T(8,128)(2,1)}, u32[]{:S(2)}, u32[]{:S(2)}) collective-permute-start(bf16[6,256,256]{2,1,0:T(8,128)(2,1)S(1)} %merge_chunk.6.rest_0_.rest_2_), channel_id=1, source_target_pairs={{0,2},{2,0},{1,3},{3,1},{4,6},{6,4},{5,7},{7,5},{8,10},{10,8},{9,1... | collective-permute-start | bytes 2359304 | tf_op jit(solution)/shard_map/ppermute | solution.py:460
  42.0 10.9 %collective-permute-start.11 = (bf16[2,208,256]{2,1,0:T(8,128)(2,1)}, bf16[2,208,256]{2,1,0:T(8,128)(2,1)S(1)}, u32[]{:S(2)}, u32[]{:S(2)}) collective-permute-start(bf16[2,208,256]{2,1,0:T(8,128)(2,1)} %get-tuple-element.52), channel_id=1, source_target_pairs={{0,8},{4,12},{8,0},{12,4},{1,9},{5,13},{9,1},{13,5},{2,10},{6,14},... | collective-permute-start | bytes 638984 | tf_op jit(solution)/shard_map/ppermute | solution.py:521
  42.9 19.2 %collective-permute-start.12 = (bf16[2,208,256]{2,1,0:T(8,128)(2,1)}, bf16[2,208,256]{2,1,0:T(8,128)(2,1)S(1)}, u32[]{:S(2)}, u32[]{:S(2)}) collective-permute-start(bf16[2,208,256]{2,1,0:T(8,128)(2,1)} %get-tuple-element.53), channel_id=1, source_target_pairs={{0,4},{4,8},{8,12},{12,0},{1,5},{5,9},{9,13},{13,1},{2,6},{6,10},{... | collective-permute-start | bytes 638984 | tf_op jit(solution)/shard_map/ppermute | solution.py:521
  42.9 21.3 %collective-permute-start.10 = (bf16[2,208,256]{2,1,0:T(8,128)(2,1)}, bf16[2,208,256]{2,1,0:T(8,128)(2,1)S(1)}, u32[]{:S(2)}, u32[]{:S(2)}) collective-permute-start(bf16[2,208,256]{2,1,0:T(8,128)(2,1)} %get-tuple-element.47.refs_3_), channel_id=1, source_target_pairs={{0,12},{4,0},{8,4},{12,8},{1,13},{5,1},{9,5},{13,9},{2,14},{6,2},{... | collective-permute-start | bytes 638984 | tf_op jit(solution)/shard_map/ppermute | solution.py:521
  53.0 13.8 %collective-permute-start.8 = (bf16[2,160,256]{2,1,0:T(8,128)(2,1)S(1)}, bf16[2,160,256]{2,1,0:T(8,128)(2,1)S(1)}, u32[]{:S(2)}, u32[]{:S(2)}) collective-permute-start(bf16[2,160,256]{2,1,0:T(8,128)(2,1)S(1)} %get-tuple-element.50), channel_id=1, source_target_pairs={{0,8},{4,12},{8,0},{12,4},{1,9},{5,13},{9,1},{13,5},{2,10},{6,14},... | collective-permute-start | bytes 491528 | tf_op jit(solution)/shard_map/ppermute | solution.py:521
  62.1 12.2 %collective-permute-start.9 = (bf16[2,160,256]{2,1,0:T(8,128)(2,1)S(1)}, bf16[2,160,256]{2,1,0:T(8,128)(2,1)S(1)}, u32[]{:S(2)}, u32[]{:S(2)}) collective-permute-start(bf16[2,160,256]{2,1,0:T(8,128)(2,1)S(1)} %get-tuple-element.51), channel_id=1, source_target_pairs={{0,4},{4,8},{8,12},{12,0},{1,5},{5,9},{9,13},{13,1},{2,6},{6,10},{... | collective-permute-start | bytes 491528 | tf_op jit(solution)/shard_map/ppermute | solution.py:521
  64.2 10.1 %collective-permute-start.7 = (bf16[2,160,256]{2,1,0:T(8,128)(2,1)S(1)}, bf16[2,160,256]{2,1,0:T(8,128)(2,1)S(1)}, u32[]{:S(2)}, u32[]{:S(2)}) collective-permute-start(bf16[2,160,256]{2,1,0:T(8,128)(2,1)S(1)} %get-tuple-element.49.refs_3_), channel_id=1, source_target_pairs={{0,12},{4,0},{8,4},{12,8},{1,13},{5,1},{9,5},{13,9},{2,14},{6,2},{... | collective-permute-start | bytes 491528 | tf_op jit(solution)/shard_map/ppermute | solution.py:521
  66.8 23.7 %collective-permute-start.20 = (bf16[6,208,256]{2,1,0:T(8,128)(2,1)S(1)}, bf16[6,208,256]{2,1,0:T(8,128)(2,1)S(1)}, u32[]{:S(2)}, u32[]{:S(2)}) collective-permute-start(bf16[6,208,256]{2,1,0:T(8,128)(2,1)S(1)} %merge_chunk.7.rest_0_.rest_2_.rest_1_), channel_id=1, source_target_pairs={{0,2},{2,0},{1,3},{3,1},{4,6},{6,4},{5,7},{7,5},{8,10},{10,8},{9,1... | collective-permute-start | bytes 1916936 | tf_op jit(solution)/shard_map/ppermute | solution.py:460
  74.3 11.1 %collective-permute-start.17 = (bf16[2,144,256]{2,1,0:T(8,128)(2,1)S(1)}, bf16[2,144,256]{2,1,0:T(8,128)(2,1)S(1)}, u32[]{:S(2)}, u32[]{:S(2)}) collective-permute-start(bf16[2,144,256]{2,1,0:T(8,128)(2,1)S(1)} %get-tuple-element.58), channel_id=1, source_target_pairs={{0,8},{4,12},{8,0},{12,4},{1,9},{5,13},{9,1},{13,5},{2,10},{6,14},... | collective-permute-start | bytes 442376 | tf_op jit(solution)/shard_map/ppermute | solution.py:521
  74.3 15.6 %collective-permute-start.16 = (bf16[2,144,256]{2,1,0:T(8,128)(2,1)S(1)}, bf16[2,144,256]{2,1,0:T(8,128)(2,1)S(1)}, u32[]{:S(2)}, u32[]{:S(2)}) collective-permute-start(bf16[2,144,256]{2,1,0:T(8,128)(2,1)S(1)} %get-tuple-element.54.refs_3_), channel_id=1, source_target_pairs={{0,12},{4,0},{8,4},{12,8},{1,13},{5,1},{9,5},{13,9},{2,14},{6,2},{... | collective-permute-start | bytes 442376 | tf_op jit(solution)/shard_map/ppermute | solution.py:521
  80.0 7.6 %collective-permute-start.18 = (bf16[2,144,256]{2,1,0:T(8,128)(2,1)S(1)}, bf16[2,144,256]{2,1,0:T(8,128)(2,1)S(1)}, u32[]{:S(2)}, u32[]{:S(2)}) collective-permute-start(bf16[2,144,256]{2,1,0:T(8,128)(2,1)S(1)} %get-tuple-element.59), channel_id=1, source_target_pairs={{0,4},{4,8},{8,12},{12,0},{1,5},{5,9},{9,13},{13,1},{2,6},{6,10},{... | collective-permute-start | bytes 442376 | tf_op jit(solution)/shard_map/ppermute | solution.py:521
  80.0 21.0 %collective-permute-start.25 = (bf16[6,160,256]{2,1,0:T(8,128)(2,1)S(1)}, bf16[6,160,256]{2,1,0:T(8,128)(2,1)S(1)}, u32[]{:S(2)}, u32[]{:S(2)}) collective-permute-start(bf16[6,160,256]{2,1,0:T(8,128)(2,1)S(1)} %merge_chunk.8.rest_0_.rest_2_.rest_1_), channel_id=1, source_target_pairs={{0,2},{2,0},{1,3},{3,1},{4,6},{6,4},{5,7},{7,5},{8,10},{10,8},{9,1... | collective-permute-start | bytes 1474568 | tf_op jit(solution)/shard_map/ppermute | solution.py:460
  85.4 12.3 %collective-permute-start.14 = (bf16[2,128,256]{2,1,0:T(8,128)(2,1)S(1)}, bf16[2,128,256]{2,1,0:T(8,128)(2,1)S(1)}, u32[]{:S(2)}, u32[]{:S(2)}) collective-permute-start(bf16[2,128,256]{2,1,0:T(8,128)(2,1)S(1)} %get-tuple-element.56), channel_id=1, source_target_pairs={{0,8},{4,12},{8,0},{12,4},{1,9},{5,13},{9,1},{13,5},{2,10},{6,14},... | collective-permute-start | bytes 393224 | tf_op jit(solution)/shard_map/ppermute | solution.py:521
  87.6 11.4 %collective-permute-start.15 = (bf16[2,128,256]{2,1,0:T(8,128)(2,1)S(1)}, bf16[2,128,256]{2,1,0:T(8,128)(2,1)S(1)}, u32[]{:S(2)}, u32[]{:S(2)}) collective-permute-start(bf16[2,128,256]{2,1,0:T(8,128)(2,1)S(1)} %get-tuple-element.57), channel_id=1, source_target_pairs={{0,4},{4,8},{8,12},{12,0},{1,5},{5,9},{9,13},{13,1},{2,6},{6,10},{... | collective-permute-start | bytes 393224 | tf_op jit(solution)/shard_map/ppermute | solution.py:521
  89.9 10.4 %collective-permute-start.13 = (bf16[2,128,256]{2,1,0:T(8,128)(2,1)S(1)}, bf16[2,128,256]{2,1,0:T(8,128)(2,1)S(1)}, u32[]{:S(2)}, u32[]{:S(2)}) collective-permute-start(bf16[2,128,256]{2,1,0:T(8,128)(2,1)S(1)} %get-tuple-element.55.refs_3_), channel_id=1, source_target_pairs={{0,12},{4,0},{8,4},{12,8},{1,13},{5,1},{9,5},{13,9},{2,14},{6,2},{... | collective-permute-start | bytes 393224 | tf_op jit(solution)/shard_map/ppermute | solution.py:521
  90.5 21.0 %collective-permute-start.27 = (bf16[6,144,256]{2,1,0:T(8,128)(2,1)S(1)}, bf16[6,144,256]{2,1,0:T(8,128)(2,1)S(1)}, u32[]{:S(2)}, u32[]{:S(2)}) collective-permute-start(bf16[6,144,256]{2,1,0:T(8,128)(2,1)S(1)} %merge_chunk.9.rest_0_.rest_3_.rest_2_), channel_id=1, source_target_pairs={{0,2},{2,0},{1,3},{3,1},{4,6},{6,4},{5,7},{7,5},{8,10},{10,8},{9,1... | collective-permute-start | bytes 1327112 | tf_op jit(solution)/shard_map/ppermute | solution.py:460
  97.7 8.1 %collective-permute-start.23 = (bf16[2,128,256]{2,1,0:T(8,128)(2,1)S(1)}, bf16[2,128,256]{2,1,0:T(8,128)(2,1)S(1)}, u32[]{:S(2)}, u32[]{:S(2)}) collective-permute-start(bf16[2,128,256]{2,1,0:T(8,128)(2,1)S(1)} %get-tuple-element.61), channel_id=1, source_target_pairs={{0,8},{4,12},{8,0},{12,4},{1,9},{5,13},{9,1},{13,5},{2,10},{6,14},... | collective-permute-start | bytes 393224 | tf_op jit(solution)/shard_map/ppermute | solution.py:521
  98.9 7.5 %collective-permute-start.24 = (bf16[2,128,256]{2,1,0:T(8,128)(2,1)S(1)}, bf16[2,128,256]{2,1,0:T(8,128)(2,1)S(1)}, u32[]{:S(2)}, u32[]{:S(2)}) collective-permute-start(bf16[2,128,256]{2,1,0:T(8,128)(2,1)S(1)} %get-tuple-element.62), channel_id=1, source_target_pairs={{0,4},{4,8},{8,12},{12,0},{1,5},{5,9},{9,13},{13,1},{2,6},{6,10},{... | collective-permute-start | bytes 393224 | tf_op jit(solution)/shard_map/ppermute | solution.py:521
  100.3 7.3 %collective-permute-start.22 = (bf16[2,128,256]{2,1,0:T(8,128)(2,1)S(1)}, bf16[2,128,256]{2,1,0:T(8,128)(2,1)S(1)}, u32[]{:S(2)}, u32[]{:S(2)}) collective-permute-start(bf16[2,128,256]{2,1,0:T(8,128)(2,1)S(1)} %get-tuple-element.60.refs_3_), channel_id=1, source_target_pairs={{0,12},{4,0},{8,4},{12,8},{1,13},{5,1},{9,5},{13,9},{2,14},{6,2},{... | collective-permute-start | bytes 393224 | tf_op jit(solution)/shard_map/ppermute | solution.py:521
  101.0 13.6 %collective-permute-start.21 = (bf16[6,128,256]{2,1,0:T(8,128)(2,1)S(1)}, bf16[6,128,256]{2,1,0:T(8,128)(2,1)S(1)}, u32[]{:S(2)}, u32[]{:S(2)}) collective-permute-start(bf16[6,128,256]{2,1,0:T(8,128)(2,1)S(1)} %merge_chunk.10.rest_2_.rest_1_), channel_id=1, source_target_pairs={{0,2},{2,0},{1,3},{3,1},{4,6},{6,4},{5,7},{7,5},{8,10},{10,8},{9,1... | collective-permute-start | bytes 1179656 | tf_op jit(solution)/shard_map/ppermute | solution.py:460
  108.1 13.1 %copy-start.1 = (f32[8,256,256]{2,1,0:T(8,128)S(1)}, f32[8,256,256]{2,1,0:T(8,128)}, u32[]{:S(2)}) copy-start(f32[8,256,256]{2,1,0:T(8,128)} %copy-done) | copy-start | bytes 6291460
  108.1 13.1 %copy-start.4 = (bf16[8,256,256]{2,1,0:T(8,128)(2,1)S(1)}, bf16[8,256,256]{2,1,0:T(8,128)(2,1)}, u32[]{:S(2)}) copy-start(bf16[8,256,256]{2,1,0:T(8,128)(2,1)} %copy-done.3) | copy-start | bytes 3145732
  108.1 13.1 %collective-permute-start.26 = (bf16[6,128,256]{2,1,0:T(8,128)(2,1)S(1)}, bf16[6,128,256]{2,1,0:T(8,128)(2,1)S(1)}, u32[]{:S(2)}, u32[]{:S(2)}) collective-permute-start(bf16[6,128,256]{2,1,0:T(8,128)(2,1)S(1)} %merge_chunk.11.rest_0_.rest_4_), channel_id=1, source_target_pairs={{0,2},{2,0},{1,3},{3,1},{4,6},{6,4},{5,7},{7,5},{8,10},{10,8},{9,1... | collective-permute-start | bytes 1179656 | tf_op jit(solution)/shard_map/ppermute | solution.py:460
  127.8 6.9 %collective-permute-start.32 = (bf16[2,128,256]{2,1,0:T(8,128)(2,1)S(1)}, bf16[2,128,256]{2,1,0:T(8,128)(2,1)S(1)}, u32[]{:S(2)}, u32[]{:S(2)}) collective-permute-start(bf16[2,128,256]{2,1,0:T(8,128)(2,1)S(1)} %get-tuple-element.71), channel_id=1, source_target_pairs={{0,4},{4,8},{8,12},{12,0},{1,5},{5,9},{9,13},{13,1},{2,6},{6,10},{... | collective-permute-start | bytes 393224 | tf_op jit(solution)/shard_map/ppermute | solution.py:554
  127.8 12.1 %collective-permute-start.33 = (bf16[2,128,256]{2,1,0:T(8,128)(2,1)S(1)}, bf16[2,128,256]{2,1,0:T(8,128)(2,1)S(1)}, u32[]{:S(2)}, u32[]{:S(2)}) collective-permute-start(bf16[2,128,256]{2,1,0:T(8,128)(2,1)S(1)} %get-tuple-element.72), channel_id=1, source_target_pairs={{0,8},{4,12},{8,0},{12,4},{1,9},{5,13},{9,1},{13,5},{2,10},{6,14},... | collective-permute-start | bytes 393224 | tf_op jit(solution)/shard_map/ppermute | solution.py:554
  130.8 34.0 %collective-permute-start.35 = (bf16[2,224,256]{2,1,0:T(8,128)(2,1)S(1)}, bf16[2,224,256]{2,1,0:T(8,128)(2,1)S(1)}, u32[]{:S(2)}, u32[]{:S(2)}) collective-permute-start(bf16[2,224,256]{2,1,0:T(8,128)(2,1)S(1)} %get-tuple-element.75), channel_id=1, source_target_pairs={{0,4},{4,8},{8,12},{12,0},{1,5},{5,9},{9,13},{13,1},{2,6},{6,10},{... | collective-permute-start | bytes 688136 | tf_op jit(solution)/shard_map/ppermute | solution.py:554
  133.4 31.4 %collective-permute-start.36 = (bf16[2,224,256]{2,1,0:T(8,128)(2,1)S(1)}, bf16[2,224,256]{2,1,0:T(8,128)(2,1)S(1)}, u32[]{:S(2)}, u32[]{:S(2)}) collective-permute-start(bf16[2,224,256]{2,1,0:T(8,128)(2,1)S(1)} %get-tuple-element.76), channel_id=1, source_target_pairs={{0,8},{4,12},{8,0},{12,4},{1,9},{5,13},{9,1},{13,5},{2,10},{6,14},... | collective-permute-start | bytes 688136 | tf_op jit(solution)/shard_map/ppermute | solution.py:554
  134.3 30.5 %collective-permute-start.37 = (bf16[2,224,256]{2,1,0:T(8,128)(2,1)S(1)}, bf16[2,224,256]{2,1,0:T(8,128)(2,1)S(1)}, u32[]{:S(2)}, u32[]{:S(2)}) collective-permute-start(bf16[2,224,256]{2,1,0:T(8,128)(2,1)S(1)} %get-tuple-element.77), channel_id=1, source_target_pairs={{0,12},{4,0},{8,4},{12,8},{1,13},{5,1},{9,5},{13,9},{2,14},{6,2},{... | collective-permute-start | bytes 688136 | tf_op jit(solution)/shard_map/ppermute | solution.py:554
  134.7 30.1 %collective-permute-start.34 = (bf16[2,128,256]{2,1,0:T(8,128)(2,1)S(1)}, bf16[2,128,256]{2,1,0:T(8,128)(2,1)S(1)}, u32[]{:S(2)}, u32[]{:S(2)}) collective-permute-start(bf16[2,128,256]{2,1,0:T(8,128)(2,1)S(1)} %get-tuple-element.73), channel_id=1, source_target_pairs={{0,12},{4,0},{8,4},{12,8},{1,13},{5,1},{9,5},{13,9},{2,14},{6,2},{... | collective-permute-start | bytes 393224 | tf_op jit(solution)/shard_map/ppermute | solution.py:554
  140.0 34.8 %collective-permute-start.38 = (bf16[2,224,256]{2,1,0:T(8,128)(2,1)S(1)}, bf16[2,224,256]{2,1,0:T(8,128)(2,1)S(1)}, u32[]{:S(2)}, u32[]{:S(2)}) collective-permute-start(bf16[2,224,256]{2,1,0:T(8,128)(2,1)S(1)} %get-tuple-element.79), channel_id=1, source_target_pairs={{0,4},{4,8},{8,12},{12,0},{1,5},{5,9},{9,13},{13,1},{2,6},{6,10},{... | collective-permute-start | bytes 688136 | tf_op jit(solution)/shard_map/ppermute | solution.py:554
  164.8 11.2 %collective-permute-start.39 = (bf16[2,224,256]{2,1,0:T(8,128)(2,1)S(1)}, bf16[2,224,256]{2,1,0:T(8,128)(2,1)S(1)}, u32[]{:S(2)}, u32[]{:S(2)}) collective-permute-start(bf16[2,224,256]{2,1,0:T(8,128)(2,1)S(1)} %get-tuple-element.80), channel_id=1, source_target_pairs={{0,8},{4,12},{8,0},{12,4},{1,9},{5,13},{9,1},{13,5},{2,10},{6,14},... | collective-permute-start | bytes 688136 | tf_op jit(solution)/shard_map/ppermute | solution.py:554
  166.0 57.9 %collective-permute-start.44 = (bf16[8,352,256]{2,1,0:T(8,128)(2,1)S(1)}, bf16[8,352,256]{2,1,0:T(8,128)(2,1)S(1)}, u32[]{:S(2)}, u32[]{:S(2)}) collective-permute-start(bf16[8,352,256]{2,1,0:T(8,128)(2,1)S(1)} %settle_chunks.5.rest_4_.refs_0_), channel_id=1, source_target_pairs={{0,1},{1,0},{2,3},{3,2},{4,5},{5,4},{6,7},{7,6},{8,9},{9,8},{10,11... | collective-permute-start | bytes 4325384 | tf_op jit(solution)/shard_map/ppermute | solution.py:564
  171.9 23.4 %collective-permute-start.28 = (bf16[2,240,256]{2,1,0:T(8,128)(2,1)S(1)}, bf16[2,240,256]{2,1,0:T(8,128)(2,1)S(1)}, u32[]{:S(2)}, u32[]{:S(2)}) collective-permute-start(bf16[2,240,256]{2,1,0:T(8,128)(2,1)S(1)} %get-tuple-element.67), channel_id=1, source_target_pairs={{0,4},{4,8},{8,12},{12,0},{1,5},{5,9},{9,13},{13,1},{2,6},{6,10},{... | collective-permute-start | bytes 737288 | tf_op jit(solution)/shard_map/ppermute | solution.py:554
  171.9 29.3 %collective-permute-start.29 = (bf16[2,240,256]{2,1,0:T(8,128)(2,1)S(1)}, bf16[2,240,256]{2,1,0:T(8,128)(2,1)S(1)}, u32[]{:S(2)}, u32[]{:S(2)}) collective-permute-start(bf16[2,240,256]{2,1,0:T(8,128)(2,1)S(1)} %get-tuple-element.68), channel_id=1, source_target_pairs={{0,8},{4,12},{8,0},{12,4},{1,9},{5,13},{9,1},{13,5},{2,10},{6,14},... | collective-permute-start | bytes 737288 | tf_op jit(solution)/shard_map/ppermute | solution.py:554
  174.7 30.1 %collective-permute-start.30 = (bf16[2,240,256]{2,1,0:T(8,128)(2,1)S(1)}, bf16[2,240,256]{2,1,0:T(8,128)(2,1)S(1)}, u32[]{:S(2)}, u32[]{:S(2)}) collective-permute-start(bf16[2,240,256]{2,1,0:T(8,128)(2,1)S(1)} %get-tuple-element.69), channel_id=1, source_target_pairs={{0,12},{4,0},{8,4},{12,8},{1,13},{5,1},{9,5},{13,9},{2,14},{6,2},{... | collective-permute-start | bytes 737288 | tf_op jit(solution)/shard_map/ppermute | solution.py:554
  176.0 33.0 %collective-permute-start.40 = (bf16[2,224,256]{2,1,0:T(8,128)(2,1)S(1)}, bf16[2,224,256]{2,1,0:T(8,128)(2,1)S(1)}, u32[]{:S(2)}, u32[]{:S(2)}) collective-permute-start(bf16[2,224,256]{2,1,0:T(8,128)(2,1)S(1)} %get-tuple-element.81), channel_id=1, source_target_pairs={{0,12},{4,0},{8,4},{12,8},{1,13},{5,1},{9,5},{13,9},{2,14},{6,2},{... | collective-permute-start | bytes 688136 | tf_op jit(solution)/shard_map/ppermute | solution.py:554
  195.2 19.1 %collective-permute-start.41 = (bf16[2,208,256]{2,1,0:T(8,128)(2,1)S(1)}, bf16[2,208,256]{2,1,0:T(8,128)(2,1)S(1)}, u32[]{:S(2)}, u32[]{:S(2)}) collective-permute-start(bf16[2,208,256]{2,1,0:T(8,128)(2,1)S(1)} %get-tuple-element.83), channel_id=1, source_target_pairs={{0,4},{4,8},{8,12},{12,0},{1,5},{5,9},{9,13},{13,1},{2,6},{6,10},{... | collective-permute-start | bytes 638984 | tf_op jit(solution)/shard_map/ppermute | solution.py:554
  201.2 17.6 %collective-permute-start.42 = (bf16[2,208,256]{2,1,0:T(8,128)(2,1)S(1)}, bf16[2,208,256]{2,1,0:T(8,128)(2,1)S(1)}, u32[]{:S(2)}, u32[]{:S(2)}) collective-permute-start(bf16[2,208,256]{2,1,0:T(8,128)(2,1)S(1)} %get-tuple-element.84), channel_id=1, source_target_pairs={{0,8},{4,12},{8,0},{12,4},{1,9},{5,13},{9,1},{13,5},{2,10},{6,14},... | collective-permute-start | bytes 638984 | tf_op jit(solution)/shard_map/ppermute | solution.py:554
  204.8 15.5 %collective-permute-start.43 = (bf16[2,208,256]{2,1,0:T(8,128)(2,1)S(1)}, bf16[2,208,256]{2,1,0:T(8,128)(2,1)S(1)}, u32[]{:S(2)}, u32[]{:S(2)}) collective-permute-start(bf16[2,208,256]{2,1,0:T(8,128)(2,1)S(1)} %get-tuple-element.85), channel_id=1, source_target_pairs={{0,12},{4,0},{8,4},{12,8},{1,13},{5,1},{9,5},{13,9},{2,14},{6,2},{... | collective-permute-start | bytes 638984 | tf_op jit(solution)/shard_map/ppermute | solution.py:554
  209.0 17.8 %collective-permute-start.31 = (bf16[8,240,256]{2,1,0:T(8,128)(2,1)S(1)}, bf16[8,240,256]{2,1,0:T(8,128)(2,1)S(1)}, u32[]{:S(2)}, u32[]{:S(2)}) collective-permute-start(bf16[8,240,256]{2,1,0:T(8,128)(2,1)S(1)} %settle_chunks.4.refs_0_), channel_id=1, source_target_pairs={{0,1},{1,0},{2,3},{3,2},{4,5},{5,4},{6,7},{7,6},{8,9},{9,8},{10,11... | collective-permute-start | bytes 2949128 | tf_op jit(solution)/shard_map/ppermute | solution.py:564
  214.4 9.4 %collective-permute-start.45 = (bf16[8,224,256]{2,1,0:T(8,128)(2,1)S(1)}, bf16[8,224,256]{2,1,0:T(8,128)(2,1)S(1)}, u32[]{:S(2)}, u32[]{:S(2)}) collective-permute-start(bf16[8,224,256]{2,1,0:T(8,128)(2,1)S(1)} %settle_chunks.6.rest_4_.refs_1_), channel_id=1, source_target_pairs={{0,1},{1,0},{2,3},{3,2},{4,5},{5,4},{6,7},{7,6},{8,9},{9,8},{10,11... | collective-permute-start | bytes 2752520 | tf_op jit(solution)/shard_map/ppermute | solution.py:564
  221.3 2.6 %collective-permute-start.46 = (bf16[8,208,256]{2,1,0:T(8,128)(2,1)S(1)}, bf16[8,208,256]{2,1,0:T(8,128)(2,1)S(1)}, u32[]{:S(2)}, u32[]{:S(2)}) collective-permute-start(bf16[8,208,256]{2,1,0:T(8,128)(2,1)S(1)} %settle_chunks.7.refs_2_), channel_id=1, source_target_pairs={{0,1},{1,0},{2,3},{3,2},{4,5},{5,4},{6,7},{7,6},{8,9},{9,8},{10,11... | collective-permute-start | bytes 2555912 | tf_op jit(solution)/shard_map/ppermute | solution.py:564

commit v5 on v4

--- a/solution.py
+++ b/solution.py
@@ -16,6 +16,9 @@
 BACK_GROUPS = (2, 3, 4, 5)
 CHAIN_GRADIENTS = False
 SETTLE_FROM = 99
+UNROLL = 4
+PREPARE_AT = 3
+FIRST_WAITS = (2,)
 SETTLE_WEIGHT = 50
 MERGE_WEIGHT = 50
 EXCHANGE_WEIGHT = 50
@@ -276,7 +279,7 @@
         weight_ref[2 * p + 1] = (2.0 * wide - flipped).astype(BF16)
         return carry
 
-    lax.fori_loop(0, amp_ref.shape[0], step, 0, unroll=2)
+    lax.fori_loop(0, amp_ref.shape[0], step, 0, unroll=UNROLL)
     total = sum(c.count for c in chunks)
     last = chunks[-1].count
     here = pl.ds(pl.multiple_of(fit_ref[0] * total + total - last, 16), last)
@@ -522,7 +525,8 @@
             )
         if place > 0:
             after = [picked[0]] if place < count else []
-            after += [inverse] if place == 1 else []
+            after += [inverse] if place == PREPARE_AT else []
+            after += [arrived[1][j] for j in FIRST_WAITS] if place == 1 else []
             after += merged[-1][1:] if place > SWAP_FIRST else []
             done = place - 1 - INTEGRAL_LAG
             if 0 <= done < early:

time: 229 us -> 230 us (level)
  starting transfers between devices: 62.8 us -> 48.7 us
  Pallas kernels: 76.1 us -> 84.1 us
  waiting for transfers between devices: 81.6 us -> 88.8 us
    pallas_call x7, Pallas kernels: 31.3 us -> 39.8 us  [pick_blocks(): pl.pallas_call(functools.partial(pick_kernel, start, rows, len(after)), o...]
    ppermute x7, starting transfers between devices: 11.6 us -> 4.72 us  [around_fit(): lax.ppermute(x, 'fit', shifted(n_fit, d))]
    ppermute x18, starting transfers between devices: 23.2 us -> 18.7 us  [per_device(): lax.ppermute(picked[d - 1], 'orb', shifted(n, n - d))]
    ppermute x15, waiting for transfers between devices: 54 us -> 57.7 us  [per_device(): lax.ppermute(sums[d], 'orb', shifted(n, d))]
    ppermute x4, starting transfers between devices: 7.92 us -> 5.16 us  [per_device(): waiting.append((group, here, lax.ppermute(here, 'rep', swap)))]
  transfers between devices with their start and end apart: 47 -> 47, of which waited for: 13 -> 16; matrix products, arithmetic and copies ran while one was open for 1% -> 1% of each run, Pallas kernels for 29% -> 33%
where the time goes in v5:
time: 230 us
  waiting for transfers between devices  88.8 us (39%)
  Pallas kernels  84.1 us (37%)
  starting transfers between devices  48.7 us (21%)
  local copies, waits for them, and re-layouts  4.66 us (2%)
  other arithmetic  2.41 us (1%)
    ppermute x15, waiting for transfers between devices, per_device(): lax.ppermute(sums[d], 'orb', shifted(n, d))  57.7 us
    pallas_call x7, Pallas kernels, pick_blocks(): pl.pallas_call(functools.partial(pick_kernel, start, rows, len(after)), o...  39.8 us
    ppermute x18, waiting for transfers between devices, per_device(): lax.ppermute(picked[d - 1], 'orb', shifted(n, n - d))  20.9 us
    ppermute x18, starting transfers between devices, per_device(): lax.ppermute(picked[d - 1], 'orb', shifted(n, n - d))  18.7 us
    ppermute x15, starting transfers between devices, per_device(): lax.ppermute(sums[d], 'orb', shifted(n, d))  16.4 us
    pallas_call x4, Pallas kernels, exchange_chunks(): pl.pallas_call(functools.partial(exchange_kernel, chunks, n_fit, first, l...  13.3 us
    pallas_call x4, Pallas kernels, gradient_chunk(): pl.pallas_call(functools.partial(gradient_kernel, parts, n), out_shape=[j...  11.7 us
    ppermute x7, waiting for transfers between devices, around_fit(): lax.ppermute(x, 'fit', shifted(n_fit, d))  8.14 us
  transfers between devices with their start and end apart: 47, of which 16 were waited for; matrix products, arithmetic and copies ran while one was open for 1% of the time, Pallas kernels for 33%

profile of v5, /device:TPU:9, one launch (start us, length us, event | category | flops | bytes accessed | tf_op | source)
XLA Modules:
  0.0 230.0 jit_solution(7684604401091346678)
XLA Ops:
  3.0 1.3 collective-permute-start.1
  4.3 1.1 collective-permute-start.2
  5.4 1.4 collective-permute-start.3
  6.9 1.8 pick_blocks.7.rest_0_.rest_1_.mine_ref
  9.3 1.8 pick_blocks.8
  11.1 1.1 collective-permute-start.4
  12.2 1.1 collective-permute-start.5
  13.3 2.3 collective-permute-start.6
  15.6 1.2 collective-permute-start
  16.8 14.6 %pick_blocks.9 = (bf16[2,208,256]{2,1,0:T(8,128)(2,1)}, bf16[2,208,256]{2,1,0:T(8,128)(2,1)}, bf16[2,208,256]{2,1,0:T(8,128)(2,1)S(1)}) custom-call(s32[3,2]{1,0:T(4,128)S(1)} %pad_add_fusion.index_ref, bf16[8,1024,256]{2,1,0:T(8,128)(2,1)} %blocks_ref.13, bf16[2,1024,256]{2,1,0:T(8,128)(2,1)S(1)} %pick_blocks.7.rest_0_.rest_1_.mine_ref), custom_call_target="tpu_custom_call" | custom-call | bytes 1277952 | tf_op jit(solution)/shard_map/pick_blocks/pallas_call | solution.py:76
  31.5 8.4 %collective-permute-done.7.refs_4_.refs_2_ = bf16[2,208,256]{2,1,0:T(8,128)(2,1)S(1)} collective-permute-done((bf16[2,208,256]{2,1,0:T(8,128)(2,1)S(1)}, bf16[2,208,256]{2,1,0:T(8,128)(2,1)S(1)}, u32[]{:S(2)}, u32[]{:S(2)}) %collective-permute-start.7) | collective-permute-done | bytes 213024 | tf_op jit(solution)/shard_map/ppermute | solution.py:524
  40.1 1.3 collective-permute-start.19
  41.3 3.4 %collective-permute-start.11 = (bf16[2,208,256]{2,1,0:T(8,128)(2,1)}, bf16[2,208,256]{2,1,0:T(8,128)(2,1)S(1)}, u32[]{:S(2)}, u32[]{:S(2)}) collective-permute-start(bf16[2,208,256]{2,1,0:T(8,128)(2,1)} %get-tuple-element.47.refs_3_), channel_id=1, source_target_pairs={{0,12},{4,0},{8,4},{12,8},{1,13},{5,1},{9,5},{13,9},{2,14},{6,2},{... | collective-permute-start | bytes 638984 | tf_op jit(solution)/shard_map/ppermute | solution.py:524
  45.0 16.6 %pick_blocks.10 = (bf16[2,160,256]{2,1,0:T(8,128)(2,1)}, bf16[2,160,256]{2,1,0:T(8,128)(2,1)}, bf16[2,160,256]{2,1,0:T(8,128)(2,1)}) custom-call(s32[3,2]{1,0:T(4,128)S(1)} %pad_add_fusion.index_ref, bf16[8,1024,256]{2,1,0:T(8,128)(2,1)} %blocks_ref.13, bf16[6,256,256]{2,1,0:T(8,128)(2,1)S(1)} %merge_chunk.6.rest_0_.rest_2_), custom_call_target="tpu_custom_call" | custom-call | bytes 983040 | tf_op jit(solution)/shard_map/pick_blocks/pallas_call | solution.py:76
  61.7 1.3 collective-permute-start.10
  65.4 1.6 copy-done
  67.0 1.7 prepare_pairs.1
  69.6 1.7 pick_blocks.11
  71.6 3.8 %collective-permute-done.10.refs_2_ = bf16[2,160,256]{2,1,0:T(8,128)(2,1)} collective-permute-done((bf16[2,160,256]{2,1,0:T(8,128)(2,1)}, bf16[2,160,256]{2,1,0:T(8,128)(2,1)}, u32[]{:S(2)}, u32[]{:S(2)}) %collective-permute-start.10) | collective-permute-done | bytes 163872 | tf_op jit(solution)/shard_map/ppermute | solution.py:524
  75.4 2.0 collective-permute-done.8.refs_0_
  77.4 1.4 collective-permute-start.16
  78.8 1.1 merge_chunk.8.rest_0_.rest_2_.rest_1_
  79.9 1.6 pick_blocks.12
  82.0 4.1 %exchange_chunks.4.refs_4_.rest_4_ = f32[8,256,256]{2,1,0:T(8,128)S(1)} custom-call(s32[16]{0:T(128)S(1)} %multiply_add_fusion.slot_ref, s32[1]{0:T(128)} %bitcast.fit_ref, bf16[2,1024,256]{2,1,0:T(8,128)(2,1)S(1)} %pick_blocks.7.rest_0_.rest_1_.mine_ref, bf16[2,1024,256]{2,1,0:T(8,128)(2,1)S(1)} %collective-permute-done.rest_1_.rest_2_, ...), custom_call_target="tpu_custom_call" | custom-call | flops 26843545600 | bytes 314572800 | tf_op jit(solution)/shard_map/exchange_chunks/pallas_call | solution.py:187
  86.0 2.2 collective-permute-start.14
  89.0 2.7 %collective-permute-start.15 = (bf16[2,128,256]{2,1,0:T(8,128)(2,1)S(1)}, bf16[2,128,256]{2,1,0:T(8,128)(2,1)S(1)}, u32[]{:S(2)}, u32[]{:S(2)}) collective-permute-start(bf16[2,128,256]{2,1,0:T(8,128)(2,1)S(1)} %get-tuple-element.57), channel_id=1, source_target_pairs={{0,4},{4,8},{8,12},{12,0},{1,5},{5,9},{9,13},{13,1},{2,6},{6,10},{... | collective-permute-start | bytes 393224 | tf_op jit(solution)/shard_map/ppermute | solution.py:524
  91.6 1.8 collective-permute-done.16.refs_0_
  94.0 1.6 pick_blocks.13
  95.7 3.2 %exchange_chunks.5.refs_4_.rest_4_ = f32[8,256,256]{2,1,0:T(8,128)S(1)} custom-call(s32[16]{0:T(128)S(1)} %multiply_add_fusion.slot_ref, s32[1]{0:T(128)} %bitcast.fit_ref, bf16[2,1024,256]{2,1,0:T(8,128)(2,1)S(1)} %pick_blocks.7.rest_0_.rest_1_.mine_ref, bf16[2,1024,256]{2,1,0:T(8,128)(2,1)S(1)} %collective-permute-done.rest_1_.rest_2_, ...), custom_call_target="tpu_custom_call" | custom-call | flops 21810380800 | bytes 294912000 | tf_op jit(solution)/shard_map/exchange_chunks/pallas_call | solution.py:187
  99.3 2.1 collective-permute-start.24
  102.2 1.5 collective-permute-start.21
  103.7 3.1 %exchange_chunks.6.refs_3_.rest_5_ = f32[8,256,256]{2,1,0:T(8,128)S(1)} custom-call(s32[16]{0:T(128)S(1)} %multiply_add_fusion.slot_ref, s32[1]{0:T(128)} %bitcast.fit_ref, bf16[2,1024,256]{2,1,0:T(8,128)(2,1)S(1)} %pick_blocks.7.rest_0_.rest_1_.mine_ref, bf16[2,1024,256]{2,1,0:T(8,128)(2,1)S(1)} %collective-permute-done.rest_1_.rest_2_, ...), custom_call_target="tpu_custom_call" | custom-call | flops 16777216000 | bytes 275251200 | tf_op jit(solution)/shard_map/exchange_chunks/pallas_call | solution.py:187
  106.8 1.5 collective-permute-done.24.refs_2_
  108.3 2.6 %collective-permute-done.22.refs_0_ = bf16[2,128,256]{2,1,0:T(8,128)(2,1)S(1)} collective-permute-done((bf16[2,128,256]{2,1,0:T(8,128)(2,1)S(1)}, bf16[2,128,256]{2,1,0:T(8,128)(2,1)S(1)}, u32[]{:S(2)}, u32[]{:S(2)}) %collective-permute-start.22) | collective-permute-done | bytes 131104 | tf_op jit(solution)/shard_map/ppermute | solution.py:524
  111.6 3.0 %exchange_chunks.7.rest_6_ = f32[8,256,256]{2,1,0:T(8,128)S(1)} custom-call(s32[16]{0:T(128)S(1)} %multiply_add_fusion.slot_ref, s32[1]{0:T(128)} %bitcast.fit_ref, bf16[6,128,256]{2,1,0:T(8,128)(2,1)S(1)} %merge_chunk.11.rest_0_.rest_4_, bf16[2,1024,256]{2,1,0:T(8,128)(2,1)S(1)} %pick_blocks.7.rest_0_.rest_1_.mine_ref, ...), custom_call_target="tpu_custom_call" | custom-call | flops 15099494400 | bytes 268697600 | tf_op jit(solution)/shard_map/exchange_chunks/pallas_call | solution.py:187
  114.6 8.1 %collective-permute-done.26.rest_5_ = bf16[6,128,256]{2,1,0:T(8,128)(2,1)S(1)} collective-permute-done((bf16[6,128,256]{2,1,0:T(8,128)(2,1)S(1)}, bf16[6,128,256]{2,1,0:T(8,128)(2,1)S(1)}, u32[]{:S(2)}, u32[]{:S(2)}) %collective-permute-start.26) | collective-permute-done | bytes 393248 | tf_op jit(solution)/shard_map/ppermute | solution.py:463
  122.8 5.7 %middle_step.1 = (bf16[8,256,256]{2,1,0:T(8,128)(2,1)}, bf16[16,256,256]{2,1,0:T(8,128)(2,1)S(1)}, bf16[2,128,256]{2,1,0:T(8,128)(2,1)S(1)}, bf16[2,128,256]{2,1...) custom-call(s32[16]{0:T(128)S(1)} %multiply_add_fusion.slot_ref, ...), custom_call_target="tpu_custom_call" | custom-call | flops 2147483648 | bytes 8388608 | tf_op jit(solution)/shard_map/middle_step/pallas_call | solution.py:295
  128.5 1.0 collective-permute-start.32
  129.5 2.9 %gradient_chunk.5 = (bf16[2,224,256]{2,1,0:T(8,128)(2,1)S(1)}, bf16[2,224,256]{2,1,0:T(8,128)(2,1)S(1)}, bf16[2,224,256]{2,1,0:T(8,128)(2,1)S(1)}, bf16[2,224,256]{2,1,0:T(8,128)(2,1)S(1)}) custom-call(s32[16]{0:T(128)S(1)} %multiply_add_fusion.slot_ref, bf16[16,256,256]{2,1,0:T(8,128)(2,1)S(1)} %get-tuple-element.65.weight_ref, ...), custom_call_target="tpu_custom_call" | custom-call | flops 469762048 | bytes 3932160 | tf_op jit(solution)/shard_map/gradient_chunk/pallas_call | solution.py:353
  132.4 1.7 collective-permute-start.35
  134.1 1.7 collective-permute-start.36
  136.3 1.4 collective-permute-start.34
  137.7 3.0 %gradient_chunk.6 = (bf16[2,224,256]{2,1,0:T(8,128)(2,1)S(1)}, bf16[2,224,256]{2,1,0:T(8,128)(2,1)S(1)}, bf16[2,224,256]{2,1,0:T(8,128)(2,1)S(1)}, bf16[2,224,256]{2,1,0:T(8,128)(2,1)S(1)}) custom-call(s32[16]{0:T(128)S(1)} %multiply_add_fusion.slot_ref, bf16[16,256,256]{2,1,0:T(8,128)(2,1)S(1)} %get-tuple-element.65.weight_ref, ...), custom_call_target="tpu_custom_call" | custom-call | flops 469762048 | bytes 3932160 | tf_op jit(solution)/shard_map/gradient_chunk/pallas_call | solution.py:353
  140.8 25.8 %collective-permute-done.34.rest_3_ = bf16[2,128,256]{2,1,0:T(8,128)(2,1)S(1)} collective-permute-done((bf16[2,128,256]{2,1,0:T(8,128)(2,1)S(1)}, bf16[2,128,256]{2,1,0:T(8,128)(2,1)S(1)}, u32[]{:S(2)}, u32[]{:S(2)}) %collective-permute-start.34) | collective-permute-done | bytes 131104 | tf_op jit(solution)/shard_map/ppermute | solution.py:558
  166.6 1.1 settle_chunks.5.rest_4_.refs_0_
  167.8 2.6 %collective-permute-start.44 = (bf16[8,352,256]{2,1,0:T(8,128)(2,1)S(1)}, bf16[8,352,256]{2,1,0:T(8,128)(2,1)S(1)}, u32[]{:S(2)}, u32[]{:S(2)}) collective-permute-start(bf16[8,352,256]{2,1,0:T(8,128)(2,1)S(1)} %settle_chunks.5.rest_4_.refs_0_), channel_id=1, source_target_pairs={{0,1},{1,0},{2,3},{3,2},{4,5},{5,4},{6,7},{7,6},{8,9},{9,8},{10,11... | collective-permute-start | bytes 4325384 | tf_op jit(solution)/shard_map/ppermute | solution.py:568
  170.4 3.0 %gradient_chunk.4 = (bf16[2,240,256]{2,1,0:T(8,128)(2,1)S(1)}, bf16[2,240,256]{2,1,0:T(8,128)(2,1)S(1)}, bf16[2,240,256]{2,1,0:T(8,128)(2,1)S(1)}, bf16[2,240,256]{2,1,0:T(8,128)(2,1)S(1)}) custom-call(s32[16]{0:T(128)S(1)} %multiply_add_fusion.slot_ref, bf16[16,256,256]{2,1,0:T(8,128)(2,1)S(1)} %get-tuple-element.65.weight_ref, ...), custom_call_target="tpu_custom_call" | custom-call | flops 503316480 | bytes 4063232 | tf_op jit(solution)/shard_map/gradient_chunk/pallas_call | solution.py:353
  173.5 2.8 %collective-permute-start.29 = (bf16[2,240,256]{2,1,0:T(8,128)(2,1)S(1)}, bf16[2,240,256]{2,1,0:T(8,128)(2,1)S(1)}, u32[]{:S(2)}, u32[]{:S(2)}) collective-permute-start(bf16[2,240,256]{2,1,0:T(8,128)(2,1)S(1)} %get-tuple-element.68), channel_id=1, source_target_pairs={{0,8},{4,12},{8,0},{12,4},{1,9},{5,13},{9,1},{13,5},{2,10},{6,14},... | collective-permute-start | bytes 737288 | tf_op jit(solution)/shard_map/ppermute | solution.py:558
  176.3 1.3 collective-permute-start.30
  177.6 2.8 %gradient_chunk.7 = (bf16[2,208,256]{2,1,0:T(8,128)(2,1)S(1)}, bf16[2,208,256]{2,1,0:T(8,128)(2,1)S(1)}, bf16[2,208,256]{2,1,0:T(8,128)(2,1)S(1)}, bf16[2,208,256]{2,1,0:T(8,128)(2,1)S(1)}) custom-call(s32[16]{0:T(128)S(1)} %multiply_add_fusion.slot_ref, bf16[16,256,256]{2,1,0:T(8,128)(2,1)S(1)} %get-tuple-element.65.weight_ref, ...), custom_call_target="tpu_custom_call" | custom-call | flops 436207616 | bytes 3801088 | tf_op jit(solution)/shard_map/gradient_chunk/pallas_call | solution.py:353
  180.4 16.9 %collective-permute-done.28.rest_1_ = bf16[2,240,256]{2,1,0:T(8,128)(2,1)S(1)} collective-permute-done((bf16[2,240,256]{2,1,0:T(8,128)(2,1)S(1)}, bf16[2,240,256]{2,1,0:T(8,128)(2,1)S(1)}, u32[]{:S(2)}, u32[]{:S(2)}) %collective-permute-start.28) | collective-permute-done | bytes 245792 | tf_op jit(solution)/shard_map/ppermute | solution.py:558
  197.4 2.2 collective-permute-start.41
  199.6 3.2 %collective-permute-done.29.rest_2_ = bf16[2,240,256]{2,1,0:T(8,128)(2,1)S(1)} collective-permute-done((bf16[2,240,256]{2,1,0:T(8,128)(2,1)S(1)}, bf16[2,240,256]{2,1,0:T(8,128)(2,1)S(1)}, u32[]{:S(2)}, u32[]{:S(2)}) %collective-permute-start.29) | collective-permute-done | bytes 245792 | tf_op jit(solution)/shard_map/ppermute | solution.py:558
  202.7 3.6 %collective-permute-start.42 = (bf16[2,208,256]{2,1,0:T(8,128)(2,1)S(1)}, bf16[2,208,256]{2,1,0:T(8,128)(2,1)S(1)}, u32[]{:S(2)}, u32[]{:S(2)}) collective-permute-start(bf16[2,208,256]{2,1,0:T(8,128)(2,1)S(1)} %get-tuple-element.84), channel_id=1, source_target_pairs={{0,8},{4,12},{8,0},{12,4},{1,9},{5,13},{9,1},{13,5},{2,10},{6,14},... | collective-permute-start | bytes 638984 | tf_op jit(solution)/shard_map/ppermute | solution.py:558
  206.3 1.0 settle_chunks.4.refs_0_
  207.3 4.5 %collective-permute-done.40.rest_3_ = bf16[2,224,256]{2,1,0:T(8,128)(2,1)S(1)} collective-permute-done((bf16[2,224,256]{2,1,0:T(8,128)(2,1)S(1)}, bf16[2,224,256]{2,1,0:T(8,128)(2,1)S(1)}, u32[]{:S(2)}, u32[]{:S(2)}) %collective-permute-start.40) | collective-permute-done | bytes 229408 | tf_op jit(solution)/shard_map/ppermute | solution.py:558
  211.8 1.0 collective-permute-start.31
  213.7 2.7 %collective-permute-done.41.rest_1_ = bf16[2,208,256]{2,1,0:T(8,128)(2,1)S(1)} collective-permute-done((bf16[2,208,256]{2,1,0:T(8,128)(2,1)S(1)}, bf16[2,208,256]{2,1,0:T(8,128)(2,1)S(1)}, u32[]{:S(2)}, u32[]{:S(2)}) %collective-permute-start.41) | collective-permute-done | bytes 213024 | tf_op jit(solution)/shard_map/ppermute | solution.py:558
  216.4 1.0 collective-permute-start.45
  217.3 3.6 %collective-permute-done.42.rest_2_ = bf16[2,208,256]{2,1,0:T(8,128)(2,1)S(1)} collective-permute-done((bf16[2,208,256]{2,1,0:T(8,128)(2,1)S(1)}, bf16[2,208,256]{2,1,0:T(8,128)(2,1)S(1)}, u32[]{:S(2)}, u32[]{:S(2)}) %collective-permute-start.42) | collective-permute-done | bytes 213024 | tf_op jit(solution)/shard_map/ppermute | solution.py:558
  220.9 1.1 collective-permute-done.43.rest_3_
  223.5 2.0 collective-permute-done.46.refs_5_
  225.5 3.0 %add_chunks.2.refs_2_ = f32[8,1024,256]{2,1,0:T(8,128)} custom-call(bf16[8,352,256]{2,1,0:T(8,128)(2,1)S(1)} %settle_chunks.5.rest_4_.refs_0_, bf16[8,224,256]{2,1,0:T(8,128)(2,1)S(1)} %settle_chunks.6.rest_4_.refs_1_, bf16[8,208,256]{2,1,0:T(8,128)(2,1)S(1)} %settle_chunks.7.refs_2_, bf16[8,352,256]{2,1,0:T(8,128)(2,1)S(1)} %collective-permute-done.44.refs_3_, ...), custom_call_target="tpu_custom_call" | custom-call | bytes 12845056 | tf_op jit(solution)/shard_map/add_chunks/pallas_call | solution.py:433
  228.5 1.4 add_chunks.3
  (103 shorter events, 13.9 us)
Async XLA Ops:
  2.1 4.6 %copy-start.4 = (s32[16]{0:T(128)}, s32[16]{0:T(128)S(1)}, u32[]{:S(2)}) copy-start(s32[16]{0:T(128)S(1)} %sub.25) | copy-start | bytes 196
  3.0 5.6 %collective-permute-start.1 = (f32[10]{0:T(128)S(1)}, f32[10]{0:T(128)S(1)}, u32[]{:S(2)}, u32[]{:S(2)}) collective-permute-start(f32[10]{0:T(128)S(1)} %get-tuple-element.89), channel_id=1, source_target_pairs={{0,4},{4,8},{8,12},{12,0},{1,5},{5,9},{9,13},{13,1},{2,6},{6,10},{... | collective-permute-start | bytes 128 | tf_op jit(solution)/shard_map/ppermute | solution.py:496
  4.3 4.4 %collective-permute-start.2 = (f32[10]{0:T(128)S(1)}, f32[10]{0:T(128)S(1)}, u32[]{:S(2)}, u32[]{:S(2)}) collective-permute-start(f32[10]{0:T(128)S(1)} %get-tuple-element.90), channel_id=1, source_target_pairs={{0,8},{4,12},{8,0},{12,4},{1,9},{5,13},{9,1},{13,5},{2,10},{6,14},... | collective-permute-start | bytes 128 | tf_op jit(solution)/shard_map/ppermute | solution.py:496
  5.4 3.3 %collective-permute-start.3 = (f32[10]{0:T(128)S(1)}, f32[10]{0:T(128)S(1)}, u32[]{:S(2)}, u32[]{:S(2)}) collective-permute-start(f32[10]{0:T(128)S(1)} %get-tuple-element.91), channel_id=1, source_target_pairs={{0,12},{4,0},{8,4},{12,8},{1,13},{5,1},{9,5},{13,9},{2,14},{6,2},{... | collective-permute-start | bytes 128 | tf_op jit(solution)/shard_map/ppermute | solution.py:496
  8.6 0.5 copy-start.6
  8.7 0.6 copy-start.7
  8.7 0.5 copy-start.8
  9.3 1.8 copy-start.2
  11.1 28.8 %collective-permute-start.4 = (bf16[2,256,256]{2,1,0:T(8,128)(2,1)S(1)}, bf16[2,256,256]{2,1,0:T(8,128)(2,1)S(1)}, u32[]{:S(2)}, u32[]{:S(2)}) collective-permute-start(bf16[2,256,256]{2,1,0:T(8,128)(2,1)S(1)} %get-tuple-element.44), channel_id=1, source_target_pairs={{0,12},{4,0},{8,4},{12,8},{1,13},{5,1},{9,5},{13,9},{2,14},{6,2},{... | collective-permute-start | bytes 786440 | tf_op jit(solution)/shard_map/ppermute | solution.py:524
  12.2 27.7 %collective-permute-start.5 = (bf16[2,256,256]{2,1,0:T(8,128)(2,1)S(1)}, bf16[2,256,256]{2,1,0:T(8,128)(2,1)S(1)}, u32[]{:S(2)}, u32[]{:S(2)}) collective-permute-start(bf16[2,256,256]{2,1,0:T(8,128)(2,1)S(1)} %get-tuple-element.45), channel_id=1, source_target_pairs={{0,8},{4,12},{8,0},{12,4},{1,9},{5,13},{9,1},{13,5},{2,10},{6,14},... | collective-permute-start | bytes 786440 | tf_op jit(solution)/shard_map/ppermute | solution.py:524
  13.3 26.6 %collective-permute-start.6 = (bf16[2,256,256]{2,1,0:T(8,128)(2,1)S(1)}, bf16[2,256,256]{2,1,0:T(8,128)(2,1)S(1)}, u32[]{:S(2)}, u32[]{:S(2)}) collective-permute-start(bf16[2,256,256]{2,1,0:T(8,128)(2,1)S(1)} %get-tuple-element.46), channel_id=1, source_target_pairs={{0,4},{4,8},{8,12},{12,0},{1,5},{5,9},{9,13},{13,1},{2,6},{6,10},{... | collective-permute-start | bytes 786440 | tf_op jit(solution)/shard_map/ppermute | solution.py:524
  15.6 65.9 %collective-permute-start = (bf16[2,1024,256]{2,1,0:T(8,128)(2,1)S(1)}, bf16[2,1024,256]{2,1,0:T(8,128)(2,1)S(1)}, u32[]{:S(2)}, u32[]{:S(2)}) collective-permute-start(bf16[2,1024,256]{2,1,0:T(8,128)(2,1)S(1)} %pick_blocks.7.rest_0_.rest_1_.mine_ref), channel_id=1, source_target_pairs={{0,2},{2,0},{1,3},{3,1},{4,6},{6,4},{5,7},{7,5},{8,10},{10,8},{9,1... | collective-permute-start | bytes 3145736 | tf_op jit(solution)/shard_map/ppermute | solution.py:463
  31.5 8.5 %collective-permute-start.7 = (bf16[2,208,256]{2,1,0:T(8,128)(2,1)S(1)}, bf16[2,208,256]{2,1,0:T(8,128)(2,1)S(1)}, u32[]{:S(2)}, u32[]{:S(2)}) collective-permute-start(bf16[2,208,256]{2,1,0:T(8,128)(2,1)S(1)} %get-tuple-element.48), channel_id=1, source_target_pairs={{0,4},{4,8},{8,12},{12,0},{1,5},{5,9},{9,13},{13,1},{2,6},{6,10},{... | collective-permute-start | bytes 638984 | tf_op jit(solution)/shard_map/ppermute | solution.py:524
  40.1 41.7 %collective-permute-start.19 = (bf16[6,256,256]{2,1,0:T(8,128)(2,1)S(1)}, bf16[6,256,256]{2,1,0:T(8,128)(2,1)}, u32[]{:S(2)}, u32[]{:S(2)}) collective-permute-start(bf16[6,256,256]{2,1,0:T(8,128)(2,1)S(1)} %merge_chunk.6.rest_0_.rest_2_), channel_id=1, source_target_pairs={{0,2},{2,0},{1,3},{3,1},{4,6},{6,4},{5,7},{7,5},{8,10},{10,8},{9,1... | collective-permute-start | bytes 2359304 | tf_op jit(solution)/shard_map/ppermute | solution.py:463
  41.3 20.4 %collective-permute-start.12 = (bf16[2,208,256]{2,1,0:T(8,128)(2,1)}, bf16[2,208,256]{2,1,0:T(8,128)(2,1)S(1)}, u32[]{:S(2)}, u32[]{:S(2)}) collective-permute-start(bf16[2,208,256]{2,1,0:T(8,128)(2,1)} %get-tuple-element.52), channel_id=1, source_target_pairs={{0,8},{4,12},{8,0},{12,4},{1,9},{5,13},{9,1},{13,5},{2,10},{6,14},... | collective-permute-start | bytes 638984 | tf_op jit(solution)/shard_map/ppermute | solution.py:524
  41.3 21.7 %collective-permute-start.11 = (bf16[2,208,256]{2,1,0:T(8,128)(2,1)}, bf16[2,208,256]{2,1,0:T(8,128)(2,1)S(1)}, u32[]{:S(2)}, u32[]{:S(2)}) collective-permute-start(bf16[2,208,256]{2,1,0:T(8,128)(2,1)} %get-tuple-element.47.refs_3_), channel_id=1, source_target_pairs={{0,12},{4,0},{8,4},{12,8},{1,13},{5,1},{9,5},{13,9},{2,14},{6,2},{... | collective-permute-start | bytes 638984 | tf_op jit(solution)/shard_map/ppermute | solution.py:524
  45.0 18.3 %copy-start.5 = (s32[16]{0:T(128)S(1)}, s32[16]{0:T(128)}, u32[]{:S(2)}) copy-start(s32[16]{0:T(128)} %copy-done.4) | copy-start | bytes 196
  45.0 20.4 %copy-start.1 = (s32[8]{0:T(128)S(1)}, s32[8]{0:T(128)}, u32[]{:S(2)}) copy-start(s32[8]{0:T(128)} %size_ref.1) | copy-start | bytes 100
  61.6 9.7 %collective-permute-start.9 = (bf16[2,160,256]{2,1,0:T(8,128)(2,1)}, bf16[2,160,256]{2,1,0:T(8,128)(2,1)}, u32[]{:S(2)}, u32[]{:S(2)}) collective-permute-start(bf16[2,160,256]{2,1,0:T(8,128)(2,1)} %get-tuple-element.50), channel_id=1, source_target_pairs={{0,8},{4,12},{8,0},{12,4},{1,9},{5,13},{9,1},{13,5},{2,10},{6,14},... | collective-permute-start | bytes 491528 | tf_op jit(solution)/shard_map/ppermute | solution.py:524
  61.7 13.7 %collective-permute-start.10 = (bf16[2,160,256]{2,1,0:T(8,128)(2,1)}, bf16[2,160,256]{2,1,0:T(8,128)(2,1)}, u32[]{:S(2)}, u32[]{:S(2)}) collective-permute-start(bf16[2,160,256]{2,1,0:T(8,128)(2,1)} %get-tuple-element.51), channel_id=1, source_target_pairs={{0,4},{4,8},{8,12},{12,0},{1,5},{5,9},{9,13},{13,1},{2,6},{6,10},{... | collective-permute-start | bytes 491528 | tf_op jit(solution)/shard_map/ppermute | solution.py:524
  63.0 14.4 %collective-permute-start.8 = (bf16[2,160,256]{2,1,0:T(8,128)(2,1)}, bf16[2,160,256]{2,1,0:T(8,128)(2,1)}, u32[]{:S(2)}, u32[]{:S(2)}) collective-permute-start(bf16[2,160,256]{2,1,0:T(8,128)(2,1)} %get-tuple-element.49.refs_3_), channel_id=1, source_target_pairs={{0,12},{4,0},{8,4},{12,8},{1,13},{5,1},{9,5},{13,9},{2,14},{6,2},{... | collective-permute-start | bytes 491528 | tf_op jit(solution)/shard_map/ppermute | solution.py:524
  65.4 1.6 copy-start
  71.3 24.3 %collective-permute-start.20 = (bf16[6,208,256]{2,1,0:T(8,128)(2,1)S(1)}, bf16[6,208,256]{2,1,0:T(8,128)(2,1)S(1)}, u32[]{:S(2)}, u32[]{:S(2)}) collective-permute-start(bf16[6,208,256]{2,1,0:T(8,128)(2,1)S(1)} %merge_chunk.7.rest_0_.rest_2_.rest_1_), channel_id=1, source_target_pairs={{0,2},{2,0},{1,3},{3,1},{4,6},{6,4},{5,7},{7,5},{8,10},{10,8},{9,1... | collective-permute-start | bytes 1916936 | tf_op jit(solution)/shard_map/ppermute | solution.py:463
  75.4 10.6 %collective-permute-start.17 = (bf16[2,144,256]{2,1,0:T(8,128)(2,1)S(1)}, bf16[2,144,256]{2,1,0:T(8,128)(2,1)S(1)}, u32[]{:S(2)}, u32[]{:S(2)}) collective-permute-start(bf16[2,144,256]{2,1,0:T(8,128)(2,1)S(1)} %get-tuple-element.58), channel_id=1, source_target_pairs={{0,8},{4,12},{8,0},{12,4},{1,9},{5,13},{9,1},{13,5},{2,10},{6,14},... | collective-permute-start | bytes 442376 | tf_op jit(solution)/shard_map/ppermute | solution.py:524
  77.4 16.0 %collective-permute-start.16 = (bf16[2,144,256]{2,1,0:T(8,128)(2,1)S(1)}, bf16[2,144,256]{2,1,0:T(8,128)(2,1)S(1)}, u32[]{:S(2)}, u32[]{:S(2)}) collective-permute-start(bf16[2,144,256]{2,1,0:T(8,128)(2,1)S(1)} %get-tuple-element.53.refs_3_), channel_id=1, source_target_pairs={{0,12},{4,0},{8,4},{12,8},{1,13},{5,1},{9,5},{13,9},{2,14},{6,2},{... | collective-permute-start | bytes 442376 | tf_op jit(solution)/shard_map/ppermute | solution.py:524
  81.6 7.4 %collective-permute-start.18 = (bf16[2,144,256]{2,1,0:T(8,128)(2,1)S(1)}, bf16[2,144,256]{2,1,0:T(8,128)(2,1)S(1)}, u32[]{:S(2)}, u32[]{:S(2)}) collective-permute-start(bf16[2,144,256]{2,1,0:T(8,128)(2,1)S(1)} %get-tuple-element.59), channel_id=1, source_target_pairs={{0,4},{4,8},{8,12},{12,0},{1,5},{5,9},{9,13},{13,1},{2,6},{6,10},{... | collective-permute-start | bytes 442376 | tf_op jit(solution)/shard_map/ppermute | solution.py:524
  81.7 20.5 %collective-permute-start.25 = (bf16[6,160,256]{2,1,0:T(8,128)(2,1)S(1)}, bf16[6,160,256]{2,1,0:T(8,128)(2,1)S(1)}, u32[]{:S(2)}, u32[]{:S(2)}) collective-permute-start(bf16[6,160,256]{2,1,0:T(8,128)(2,1)S(1)} %merge_chunk.8.rest_0_.rest_2_.rest_1_), channel_id=1, source_target_pairs={{0,2},{2,0},{1,3},{3,1},{4,6},{6,4},{5,7},{7,5},{8,10},{10,8},{9,1... | collective-permute-start | bytes 1474568 | tf_op jit(solution)/shard_map/ppermute | solution.py:463
  86.0 12.9 %collective-permute-start.14 = (bf16[2,128,256]{2,1,0:T(8,128)(2,1)S(1)}, bf16[2,128,256]{2,1,0:T(8,128)(2,1)S(1)}, u32[]{:S(2)}, u32[]{:S(2)}) collective-permute-start(bf16[2,128,256]{2,1,0:T(8,128)(2,1)S(1)} %get-tuple-element.56), channel_id=1, source_target_pairs={{0,8},{4,12},{8,0},{12,4},{1,9},{5,13},{9,1},{13,5},{2,10},{6,14},... | collective-permute-start | bytes 393224 | tf_op jit(solution)/shard_map/ppermute | solution.py:524
  89.0 10.3 %collective-permute-start.15 = (bf16[2,128,256]{2,1,0:T(8,128)(2,1)S(1)}, bf16[2,128,256]{2,1,0:T(8,128)(2,1)S(1)}, u32[]{:S(2)}, u32[]{:S(2)}) collective-permute-start(bf16[2,128,256]{2,1,0:T(8,128)(2,1)S(1)} %get-tuple-element.57), channel_id=1, source_target_pairs={{0,4},{4,8},{8,12},{12,0},{1,5},{5,9},{9,13},{13,1},{2,6},{6,10},{... | collective-permute-start | bytes 393224 | tf_op jit(solution)/shard_map/ppermute | solution.py:524
  93.4 8.0 %collective-permute-start.13 = (bf16[2,128,256]{2,1,0:T(8,128)(2,1)S(1)}, bf16[2,128,256]{2,1,0:T(8,128)(2,1)S(1)}, u32[]{:S(2)}, u32[]{:S(2)}) collective-permute-start(bf16[2,128,256]{2,1,0:T(8,128)(2,1)S(1)} %get-tuple-element.55.refs_3_), channel_id=1, source_target_pairs={{0,12},{4,0},{8,4},{12,8},{1,13},{5,1},{9,5},{13,9},{2,14},{6,2},{... | collective-permute-start | bytes 393224 | tf_op jit(solution)/shard_map/ppermute | solution.py:524
  95.6 15.9 %collective-permute-start.27 = (bf16[6,144,256]{2,1,0:T(8,128)(2,1)S(1)}, bf16[6,144,256]{2,1,0:T(8,128)(2,1)S(1)}, u32[]{:S(2)}, u32[]{:S(2)}) collective-permute-start(bf16[6,144,256]{2,1,0:T(8,128)(2,1)S(1)} %merge_chunk.9.rest_0_.rest_3_.rest_2_), channel_id=1, source_target_pairs={{0,2},{2,0},{1,3},{3,1},{4,6},{6,4},{5,7},{7,5},{8,10},{10,8},{9,1... | collective-permute-start | bytes 1327112 | tf_op jit(solution)/shard_map/ppermute | solution.py:463
  98.9 7.9 %collective-permute-start.23 = (bf16[2,128,256]{2,1,0:T(8,128)(2,1)S(1)}, bf16[2,128,256]{2,1,0:T(8,128)(2,1)S(1)}, u32[]{:S(2)}, u32[]{:S(2)}) collective-permute-start(bf16[2,128,256]{2,1,0:T(8,128)(2,1)S(1)} %get-tuple-element.61), channel_id=1, source_target_pairs={{0,8},{4,12},{8,0},{12,4},{1,9},{5,13},{9,1},{13,5},{2,10},{6,14},... | collective-permute-start | bytes 393224 | tf_op jit(solution)/shard_map/ppermute | solution.py:524
  99.3 9.1 %collective-permute-start.24 = (bf16[2,128,256]{2,1,0:T(8,128)(2,1)S(1)}, bf16[2,128,256]{2,1,0:T(8,128)(2,1)S(1)}, u32[]{:S(2)}, u32[]{:S(2)}) collective-permute-start(bf16[2,128,256]{2,1,0:T(8,128)(2,1)S(1)} %get-tuple-element.62), channel_id=1, source_target_pairs={{0,4},{4,8},{8,12},{12,0},{1,5},{5,9},{9,13},{13,1},{2,6},{6,10},{... | collective-permute-start | bytes 393224 | tf_op jit(solution)/shard_map/ppermute | solution.py:524
  101.4 9.6 %collective-permute-start.22 = (bf16[2,128,256]{2,1,0:T(8,128)(2,1)S(1)}, bf16[2,128,256]{2,1,0:T(8,128)(2,1)S(1)}, u32[]{:S(2)}, u32[]{:S(2)}) collective-permute-start(bf16[2,128,256]{2,1,0:T(8,128)(2,1)S(1)} %get-tuple-element.60.refs_3_), channel_id=1, source_target_pairs={{0,12},{4,0},{8,4},{12,8},{1,13},{5,1},{9,5},{13,9},{2,14},{6,2},{... | collective-permute-start | bytes 393224 | tf_op jit(solution)/shard_map/ppermute | solution.py:524
  102.2 12.4 %collective-permute-start.21 = (bf16[6,128,256]{2,1,0:T(8,128)(2,1)S(1)}, bf16[6,128,256]{2,1,0:T(8,128)(2,1)S(1)}, u32[]{:S(2)}, u32[]{:S(2)}) collective-permute-start(bf16[6,128,256]{2,1,0:T(8,128)(2,1)S(1)} %merge_chunk.10.rest_2_.rest_1_), channel_id=1, source_target_pairs={{0,2},{2,0},{1,3},{3,1},{4,6},{6,4},{5,7},{7,5},{8,10},{10,8},{9,1... | collective-permute-start | bytes 1179656 | tf_op jit(solution)/shard_map/ppermute | solution.py:463
  111.5 11.3 %collective-permute-start.26 = (bf16[6,128,256]{2,1,0:T(8,128)(2,1)S(1)}, bf16[6,128,256]{2,1,0:T(8,128)(2,1)S(1)}, u32[]{:S(2)}, u32[]{:S(2)}) collective-permute-start(bf16[6,128,256]{2,1,0:T(8,128)(2,1)S(1)} %merge_chunk.11.rest_0_.rest_4_), channel_id=1, source_target_pairs={{0,2},{2,0},{1,3},{3,1},{4,6},{6,4},{5,7},{7,5},{8,10},{10,8},{9,1... | collective-permute-start | bytes 1179656 | tf_op jit(solution)/shard_map/ppermute | solution.py:463
  128.5 7.8 %collective-permute-start.32 = (bf16[2,128,256]{2,1,0:T(8,128)(2,1)S(1)}, bf16[2,128,256]{2,1,0:T(8,128)(2,1)S(1)}, u32[]{:S(2)}, u32[]{:S(2)}) collective-permute-start(bf16[2,128,256]{2,1,0:T(8,128)(2,1)S(1)} %get-tuple-element.71), channel_id=1, source_target_pairs={{0,4},{4,8},{8,12},{12,0},{1,5},{5,9},{9,13},{13,1},{2,6},{6,10},{... | collective-permute-start | bytes 393224 | tf_op jit(solution)/shard_map/ppermute | solution.py:558
  129.5 11.1 %collective-permute-start.33 = (bf16[2,128,256]{2,1,0:T(8,128)(2,1)S(1)}, bf16[2,128,256]{2,1,0:T(8,128)(2,1)S(1)}, u32[]{:S(2)}, u32[]{:S(2)}) collective-permute-start(bf16[2,128,256]{2,1,0:T(8,128)(2,1)S(1)} %get-tuple-element.72), channel_id=1, source_target_pairs={{0,8},{4,12},{8,0},{12,4},{1,9},{5,13},{9,1},{13,5},{2,10},{6,14},... | collective-permute-start | bytes 393224 | tf_op jit(solution)/shard_map/ppermute | solution.py:558
  132.4 34.2 %collective-permute-start.35 = (bf16[2,224,256]{2,1,0:T(8,128)(2,1)S(1)}, bf16[2,224,256]{2,1,0:T(8,128)(2,1)S(1)}, u32[]{:S(2)}, u32[]{:S(2)}) collective-permute-start(bf16[2,224,256]{2,1,0:T(8,128)(2,1)S(1)} %get-tuple-element.75), channel_id=1, source_target_pairs={{0,4},{4,8},{8,12},{12,0},{1,5},{5,9},{9,13},{13,1},{2,6},{6,10},{... | collective-permute-start | bytes 688136 | tf_op jit(solution)/shard_map/ppermute | solution.py:558
  134.1 32.5 %collective-permute-start.36 = (bf16[2,224,256]{2,1,0:T(8,128)(2,1)S(1)}, bf16[2,224,256]{2,1,0:T(8,128)(2,1)S(1)}, u32[]{:S(2)}, u32[]{:S(2)}) collective-permute-start(bf16[2,224,256]{2,1,0:T(8,128)(2,1)S(1)} %get-tuple-element.76), channel_id=1, source_target_pairs={{0,8},{4,12},{8,0},{12,4},{1,9},{5,13},{9,1},{13,5},{2,10},{6,14},... | collective-permute-start | bytes 688136 | tf_op jit(solution)/shard_map/ppermute | solution.py:558
  135.8 30.8 %collective-permute-start.37 = (bf16[2,224,256]{2,1,0:T(8,128)(2,1)S(1)}, bf16[2,224,256]{2,1,0:T(8,128)(2,1)S(1)}, u32[]{:S(2)}, u32[]{:S(2)}) collective-permute-start(bf16[2,224,256]{2,1,0:T(8,128)(2,1)S(1)} %get-tuple-element.77), channel_id=1, source_target_pairs={{0,12},{4,0},{8,4},{12,8},{1,13},{5,1},{9,5},{13,9},{2,14},{6,2},{... | collective-permute-start | bytes 688136 | tf_op jit(solution)/shard_map/ppermute | solution.py:558
  136.3 4.5 %copy-start.3 = (s32[1,2]{1,0:T(1,128)S(1)}, s32[1,2]{1,0:T(1,128)}, u32[]{:S(2)}) copy-start(s32[1,2]{1,0:T(1,128)} %copy-done.2) | copy-start | bytes 28
  136.3 30.3 %collective-permute-start.34 = (bf16[2,128,256]{2,1,0:T(8,128)(2,1)S(1)}, bf16[2,128,256]{2,1,0:T(8,128)(2,1)S(1)}, u32[]{:S(2)}, u32[]{:S(2)}) collective-permute-start(bf16[2,128,256]{2,1,0:T(8,128)(2,1)S(1)} %get-tuple-element.73), channel_id=1, source_target_pairs={{0,12},{4,0},{8,4},{12,8},{1,13},{5,1},{9,5},{13,9},{2,14},{6,2},{... | collective-permute-start | bytes 393224 | tf_op jit(solution)/shard_map/ppermute | solution.py:558
  140.7 35.6 %collective-permute-start.38 = (bf16[2,224,256]{2,1,0:T(8,128)(2,1)S(1)}, bf16[2,224,256]{2,1,0:T(8,128)(2,1)S(1)}, u32[]{:S(2)}, u32[]{:S(2)}) collective-permute-start(bf16[2,224,256]{2,1,0:T(8,128)(2,1)S(1)} %get-tuple-element.79), channel_id=1, source_target_pairs={{0,4},{4,8},{8,12},{12,0},{1,5},{5,9},{9,13},{13,1},{2,6},{6,10},{... | collective-permute-start | bytes 688136 | tf_op jit(solution)/shard_map/ppermute | solution.py:558
  166.6 11.0 %collective-permute-start.39 = (bf16[2,224,256]{2,1,0:T(8,128)(2,1)S(1)}, bf16[2,224,256]{2,1,0:T(8,128)(2,1)S(1)}, u32[]{:S(2)}, u32[]{:S(2)}) collective-permute-start(bf16[2,224,256]{2,1,0:T(8,128)(2,1)S(1)} %get-tuple-element.80), channel_id=1, source_target_pairs={{0,8},{4,12},{8,0},{12,4},{1,9},{5,13},{9,1},{13,5},{2,10},{6,14},... | collective-permute-start | bytes 688136 | tf_op jit(solution)/shard_map/ppermute | solution.py:558
  167.8 57.7 %collective-permute-start.44 = (bf16[8,352,256]{2,1,0:T(8,128)(2,1)S(1)}, bf16[8,352,256]{2,1,0:T(8,128)(2,1)S(1)}, u32[]{:S(2)}, u32[]{:S(2)}) collective-permute-start(bf16[8,352,256]{2,1,0:T(8,128)(2,1)S(1)} %settle_chunks.5.rest_4_.refs_0_), channel_id=1, source_target_pairs={{0,1},{1,0},{2,3},{3,2},{4,5},{5,4},{6,7},{7,6},{8,9},{9,8},{10,11... | collective-permute-start | bytes 4325384 | tf_op jit(solution)/shard_map/ppermute | solution.py:568
  173.4 24.0 %collective-permute-start.28 = (bf16[2,240,256]{2,1,0:T(8,128)(2,1)S(1)}, bf16[2,240,256]{2,1,0:T(8,128)(2,1)S(1)}, u32[]{:S(2)}, u32[]{:S(2)}) collective-permute-start(bf16[2,240,256]{2,1,0:T(8,128)(2,1)S(1)} %get-tuple-element.67), channel_id=1, source_target_pairs={{0,4},{4,8},{8,12},{12,0},{1,5},{5,9},{9,13},{13,1},{2,6},{6,10},{... | collective-permute-start | bytes 737288 | tf_op jit(solution)/shard_map/ppermute | solution.py:558
  173.5 29.2 %collective-permute-start.29 = (bf16[2,240,256]{2,1,0:T(8,128)(2,1)S(1)}, bf16[2,240,256]{2,1,0:T(8,128)(2,1)S(1)}, u32[]{:S(2)}, u32[]{:S(2)}) collective-permute-start(bf16[2,240,256]{2,1,0:T(8,128)(2,1)S(1)} %get-tuple-element.68), channel_id=1, source_target_pairs={{0,8},{4,12},{8,0},{12,4},{1,9},{5,13},{9,1},{13,5},{2,10},{6,14},... | collective-permute-start | bytes 737288 | tf_op jit(solution)/shard_map/ppermute | solution.py:558
  176.3 30.0 %collective-permute-start.30 = (bf16[2,240,256]{2,1,0:T(8,128)(2,1)S(1)}, bf16[2,240,256]{2,1,0:T(8,128)(2,1)S(1)}, u32[]{:S(2)}, u32[]{:S(2)}) collective-permute-start(bf16[2,240,256]{2,1,0:T(8,128)(2,1)S(1)} %get-tuple-element.69), channel_id=1, source_target_pairs={{0,12},{4,0},{8,4},{12,8},{1,13},{5,1},{9,5},{13,9},{2,14},{6,2},{... | collective-permute-start | bytes 737288 | tf_op jit(solution)/shard_map/ppermute | solution.py:558
  177.5 34.2 %collective-permute-start.40 = (bf16[2,224,256]{2,1,0:T(8,128)(2,1)S(1)}, bf16[2,224,256]{2,1,0:T(8,128)(2,1)S(1)}, u32[]{:S(2)}, u32[]{:S(2)}) collective-permute-start(bf16[2,224,256]{2,1,0:T(8,128)(2,1)S(1)} %get-tuple-element.81), channel_id=1, source_target_pairs={{0,12},{4,0},{8,4},{12,8},{1,13},{5,1},{9,5},{13,9},{2,14},{6,2},{... | collective-permute-start | bytes 688136 | tf_op jit(solution)/shard_map/ppermute | solution.py:558
  197.4 19.0 %collective-permute-start.41 = (bf16[2,208,256]{2,1,0:T(8,128)(2,1)S(1)}, bf16[2,208,256]{2,1,0:T(8,128)(2,1)S(1)}, u32[]{:S(2)}, u32[]{:S(2)}) collective-permute-start(bf16[2,208,256]{2,1,0:T(8,128)(2,1)S(1)} %get-tuple-element.83), channel_id=1, source_target_pairs={{0,4},{4,8},{8,12},{12,0},{1,5},{5,9},{9,13},{13,1},{2,6},{6,10},{... | collective-permute-start | bytes 638984 | tf_op jit(solution)/shard_map/ppermute | solution.py:558
  202.7 18.2 %collective-permute-start.42 = (bf16[2,208,256]{2,1,0:T(8,128)(2,1)S(1)}, bf16[2,208,256]{2,1,0:T(8,128)(2,1)S(1)}, u32[]{:S(2)}, u32[]{:S(2)}) collective-permute-start(bf16[2,208,256]{2,1,0:T(8,128)(2,1)S(1)} %get-tuple-element.84), channel_id=1, source_target_pairs={{0,8},{4,12},{8,0},{12,4},{1,9},{5,13},{9,1},{13,5},{2,10},{6,14},... | collective-permute-start | bytes 638984 | tf_op jit(solution)/shard_map/ppermute | solution.py:558
  206.3 15.7 %collective-permute-start.43 = (bf16[2,208,256]{2,1,0:T(8,128)(2,1)S(1)}, bf16[2,208,256]{2,1,0:T(8,128)(2,1)S(1)}, u32[]{:S(2)}, u32[]{:S(2)}) collective-permute-start(bf16[2,208,256]{2,1,0:T(8,128)(2,1)S(1)} %get-tuple-element.85), channel_id=1, source_target_pairs={{0,12},{4,0},{8,4},{12,8},{1,13},{5,1},{9,5},{13,9},{2,14},{6,2},{... | collective-permute-start | bytes 638984 | tf_op jit(solution)/shard_map/ppermute | solution.py:558
  211.8 16.7 %collective-permute-start.31 = (bf16[8,240,256]{2,1,0:T(8,128)(2,1)S(1)}, bf16[8,240,256]{2,1,0:T(8,128)(2,1)S(1)}, u32[]{:S(2)}, u32[]{:S(2)}) collective-permute-start(bf16[8,240,256]{2,1,0:T(8,128)(2,1)S(1)} %settle_chunks.4.refs_0_), channel_id=1, source_target_pairs={{0,1},{1,0},{2,3},{3,2},{4,5},{5,4},{6,7},{7,6},{8,9},{9,8},{10,11... | collective-permute-start | bytes 2949128 | tf_op jit(solution)/shard_map/ppermute | solution.py:568
  216.4 9.1 %collective-permute-start.45 = (bf16[8,224,256]{2,1,0:T(8,128)(2,1)S(1)}, bf16[8,224,256]{2,1,0:T(8,128)(2,1)S(1)}, u32[]{:S(2)}, u32[]{:S(2)}) collective-permute-start(bf16[8,224,256]{2,1,0:T(8,128)(2,1)S(1)} %settle_chunks.6.rest_4_.refs_1_), channel_id=1, source_target_pairs={{0,1},{1,0},{2,3},{3,2},{4,5},{5,4},{6,7},{7,6},{8,9},{9,8},{10,11... | collective-permute-start | bytes 2752520 | tf_op jit(solution)/shard_map/ppermute | solution.py:568
  222.9 2.6 %collective-permute-start.46 = (bf16[8,208,256]{2,1,0:T(8,128)(2,1)S(1)}, bf16[8,208,256]{2,1,0:T(8,128)(2,1)S(1)}, u32[]{:S(2)}, u32[]{:S(2)}) collective-permute-start(bf16[8,208,256]{2,1,0:T(8,128)(2,1)S(1)} %settle_chunks.7.refs_2_), channel_id=1, source_target_pairs={{0,1},{1,0},{2,3},{3,2},{4,5},{5,4},{6,7},{7,6},{8,9},{9,8},{10,11... | collective-permute-start | bytes 2555912 | tf_op jit(solution)/shard_map/ppermute | solution.py:568

commit v6 on v5

--- a/solution.py
+++ b/solution.py
@@ -471,7 +471,7 @@
     total_orbs = local_orbs * n
     me = lax.axis_index("orb")
 
-    blocks = pltpu.with_memory_space_constraint(blocks, pltpu.HBM)
+    far_blocks = pltpu.with_memory_space_constraint(blocks, pltpu.HBM)
     endpoints = pair_list.reshape(-1)
     relative = (endpoints - me * local_orbs) % total_orbs
     named = jnp.any(
@@ -501,7 +501,7 @@
 
     chunks = cut_rows(fit_rows, FORWARD_ROWS)
     fit = lax.axis_index("fit").astype(jnp.int32).reshape(1)
-    mine = around_fit(pick_blocks(wanted[:1], blocks, 0, fit_rows)[0], n_fit)
+    mine = around_fit(pick_blocks(wanted[:1], far_blocks, 0, fit_rows)[0], n_fit)
     inverse, off = prepare_pairs(energies, relative, pno_sizes, fock_virt)
     merged, arrived = [], []
     ints = None
@@ -519,7 +519,8 @@
         if place < count:
             c = chunks[place]
             after = [mine[0]] if place < 2 else [merged[place - 2][0]]
-            picked = pick_blocks(asked[1:], blocks, c.start, c.count, after)
+            source = far_blocks if place == 0 else blocks
+            picked = pick_blocks(asked[1:], source, c.start, c.count, after)
             arrived.append(
                 [lax.ppermute(picked[d - 1], "orb", shifted(n, n - d)) for d in range(1, n)]
             )

time: 230 us -> 234 us (1.017)
  starting transfers between devices: 48.7 us -> 79.7 us
  Pallas kernels: 84.1 us -> 54.5 us
  local copies, waits for them, and re-layouts: 4.66 us -> 9.21 us
  waiting for transfers between devices: 88.8 us -> 85.2 us
    pallas_call x7, Pallas kernels: 39.8 us -> 10.1 us  [pick_blocks(): pl.pallas_call(functools.partial(pick_kernel, start, rows, len(after)), o...]
    ppermute x15, waiting for transfers between devices: 57.7 us -> 37.5 us  [per_device(): lax.ppermute(sums[d], 'orb', shifted(n, d))]
    ppermute x15, starting transfers between devices: 16.4 us -> 34 us  [per_device(): lax.ppermute(sums[d], 'orb', shifted(n, d))]
    ppermute x18, waiting for transfers between devices: 20.9 us -> 33.5 us  [per_device(): lax.ppermute(picked[d - 1], 'orb', shifted(n, n - d))]
    ppermute x7, starting transfers between devices: 4.72 us -> 10.8 us  [around_fit(): lax.ppermute(x, 'fit', shifted(n_fit, d))]
    ppermute x18, starting transfers between devices: 18.7 us -> 24 us  [per_device(): lax.ppermute(picked[d - 1], 'orb', shifted(n, n - d))]
    unnamed x19 -> x31, local copies, waits for them, and re-layouts: 2.24 us -> 6.66 us
    ppermute x7, waiting for transfers between devices: 8.14 us -> 12.2 us  [around_fit(): lax.ppermute(x, 'fit', shifted(n_fit, d))]
  transfers between devices with their start and end apart: 47 -> 47, of which waited for: 16 -> 13; matrix products, arithmetic and copies ran while one was open for 1% -> 1% of each run, Pallas kernels for 33% -> 20%
where the time goes in v6:
time: 234 us; the launch traced here: 232 us
  waiting for transfers between devices  85.2 us (36%)
  starting transfers between devices  79.7 us (34%)
  Pallas kernels  54.5 us (23%)
  local copies, waits for them, and re-layouts  9.21 us (4%)
  other arithmetic  2.41 us (1%)
    ppermute x15, waiting for transfers between devices, per_device(): lax.ppermute(sums[d], 'orb', shifted(n, d))  37.5 us
    ppermute x15, starting transfers between devices, per_device(): lax.ppermute(sums[d], 'orb', shifted(n, d))  34 us
    ppermute x18, waiting for transfers between devices, per_device(): lax.ppermute(picked[d - 1], 'orb', shifted(n, n - d))  33.5 us
    ppermute x18, starting transfers between devices, per_device(): lax.ppermute(picked[d - 1], 'orb', shifted(n, n - d))  24 us
    pallas_call x4, Pallas kernels, exchange_chunks(): pl.pallas_call(functools.partial(exchange_kernel, chunks, n_fit, first, l...  13.3 us
    ppermute x7, waiting for transfers between devices, around_fit(): lax.ppermute(x, 'fit', shifted(n_fit, d))  12.2 us
    pallas_call x4, Pallas kernels, gradient_chunk(): pl.pallas_call(functools.partial(gradient_kernel, parts, n), out_shape=[j...  11.7 us
    ppermute x7, starting transfers between devices, around_fit(): lax.ppermute(x, 'fit', shifted(n_fit, d))  10.8 us
  transfers between devices with their start and end apart: 47, of which 13 were waited for; matrix products, arithmetic and copies ran while one was open for 1% of the time, Pallas kernels for 20%

profile of v6, /device:TPU:9, one launch (start us, length us, event | category | flops | bytes accessed | tf_op | source)
XLA Modules:
  0.0 232.3 jit_solution(6265712554660464606)
XLA Ops:
  3.0 1.3 collective-permute-start.1
  5.4 1.4 collective-permute-start.3
  6.9 1.8 pick_blocks.7.rest_0_.rest_1_.mine_ref
  9.3 2.1 pick_blocks.8
  11.4 1.1 collective-permute-start.4
  12.6 1.1 collective-permute-start.5
  13.7 2.3 collective-permute-start.6
  16.0 1.2 collective-permute-start
  17.2 1.4 pick_blocks.9
  18.6 21.6 %collective-permute-done.7.refs_4_.refs_2_ = bf16[2,208,256]{2,1,0:T(8,128)(2,1)S(1)} collective-permute-done((bf16[2,208,256]{2,1,0:T(8,128)(2,1)S(1)}, bf16[2,208,256]{2,1,0:T(8,128)(2,1)S(1)}, u32[]{:S(2)}, u32[]{:S(2)}) %collective-permute-start.7) | collective-permute-done | bytes 213024 | tf_op jit(solution)/shard_map/ppermute | solution.py:525
  40.4 1.3 collective-permute-start.19
  41.7 3.4 %collective-permute-start.11 = (bf16[2,208,256]{2,1,0:T(8,128)(2,1)}, bf16[2,208,256]{2,1,0:T(8,128)(2,1)S(1)}, u32[]{:S(2)}, u32[]{:S(2)}) collective-permute-start(bf16[2,208,256]{2,1,0:T(8,128)(2,1)} %get-tuple-element.47.refs_3_), channel_id=1, source_target_pairs={{0,12},{4,0},{8,4},{12,8},{1,13},{5,1},{9,5},{13,9},{2,14},{6,2},{... | collective-permute-start | bytes 638984 | tf_op jit(solution)/shard_map/ppermute | solution.py:525
  45.3 2.2 copy-done.1
  47.5 1.4 pick_blocks.10
  49.0 5.4 %collective-permute-start.10 = (bf16[2,160,256]{2,1,0:T(8,128)(2,1)}, bf16[2,160,256]{2,1,0:T(8,128)(2,1)}, u32[]{:S(2)}, u32[]{:S(2)}) collective-permute-start(bf16[2,160,256]{2,1,0:T(8,128)(2,1)} %get-tuple-element.51), channel_id=1, source_target_pairs={{0,4},{4,8},{8,12},{12,0},{1,5},{5,9},{9,13},{13,1},{2,6},{6,10},{... | collective-permute-start | bytes 491528 | tf_op jit(solution)/shard_map/ppermute | solution.py:525
  54.4 9.6 %collective-permute-done.11.refs_0_ = bf16[2,208,256]{2,1,0:T(8,128)(2,1)S(1)} collective-permute-done((bf16[2,208,256]{2,1,0:T(8,128)(2,1)}, bf16[2,208,256]{2,1,0:T(8,128)(2,1)S(1)}, u32[]{:S(2)}, u32[]{:S(2)}) %collective-permute-start.11) | collective-permute-done | bytes 213024 | tf_op jit(solution)/shard_map/ppermute | solution.py:525
  66.4 1.6 copy-done.4
  68.0 1.7 prepare_pairs.1
  70.6 2.2 copy-done.2
  72.8 1.2 pick_blocks.11
  74.9 2.1 collective-permute-start.16
  78.1 1.1 pick_blocks.12
  79.3 1.3 collective-permute-start.25
  80.6 4.1 %exchange_chunks.4.refs_4_.rest_4_ = f32[8,256,256]{2,1,0:T(8,128)S(1)} custom-call(s32[16]{0:T(128)S(1)} %multiply_add_fusion.slot_ref, s32[1]{0:T(128)} %bitcast.fit_ref, bf16[2,1024,256]{2,1,0:T(8,128)(2,1)S(1)} %pick_blocks.7.rest_0_.rest_1_.mine_ref, bf16[2,1024,256]{2,1,0:T(8,128)(2,1)S(1)} %collective-permute-done.rest_1_.rest_2_, ...), custom_call_target="tpu_custom_call" | custom-call | flops 26843545600 | bytes 314572800 | tf_op jit(solution)/shard_map/exchange_chunks/pallas_call | solution.py:187
  84.7 2.9 %collective-permute-start.14 = (bf16[2,128,256]{2,1,0:T(8,128)(2,1)S(1)}, bf16[2,128,256]{2,1,0:T(8,128)(2,1)S(1)}, u32[]{:S(2)}, u32[]{:S(2)}) collective-permute-start(bf16[2,128,256]{2,1,0:T(8,128)(2,1)S(1)} %get-tuple-element.56), channel_id=1, source_target_pairs={{0,8},{4,12},{8,0},{12,4},{1,9},{5,13},{9,1},{13,5},{2,10},{6,14},... | collective-permute-start | bytes 393224 | tf_op jit(solution)/shard_map/ppermute | solution.py:525
  87.6 1.5 collective-permute-start.15
  89.7 1.1 pick_blocks.13
  90.9 2.2 collective-permute-start.27
  93.1 3.2 %exchange_chunks.5.refs_4_.rest_4_ = f32[8,256,256]{2,1,0:T(8,128)S(1)} custom-call(s32[16]{0:T(128)S(1)} %multiply_add_fusion.slot_ref, s32[1]{0:T(128)} %bitcast.fit_ref, bf16[2,1024,256]{2,1,0:T(8,128)(2,1)S(1)} %pick_blocks.7.rest_0_.rest_1_.mine_ref, bf16[2,1024,256]{2,1,0:T(8,128)(2,1)S(1)} %collective-permute-done.rest_1_.rest_2_, ...), custom_call_target="tpu_custom_call" | custom-call | flops 21810380800 | bytes 294912000 | tf_op jit(solution)/shard_map/exchange_chunks/pallas_call | solution.py:187
  96.3 1.2 collective-permute-start.23
  98.1 2.2 collective-permute-start.24
  100.9 1.5 collective-permute-start.21
  102.3 3.1 %exchange_chunks.6.refs_3_.rest_5_ = f32[8,256,256]{2,1,0:T(8,128)S(1)} custom-call(s32[16]{0:T(128)S(1)} %multiply_add_fusion.slot_ref, s32[1]{0:T(128)} %bitcast.fit_ref, bf16[2,1024,256]{2,1,0:T(8,128)(2,1)S(1)} %pick_blocks.7.rest_0_.rest_1_.mine_ref, bf16[2,1024,256]{2,1,0:T(8,128)(2,1)S(1)} %collective-permute-done.rest_1_.rest_2_, ...), custom_call_target="tpu_custom_call" | custom-call | flops 16777216000 | bytes 275251200 | tf_op jit(solution)/shard_map/exchange_chunks/pallas_call | solution.py:187
  105.4 1.6 collective-permute-done.22.refs_0_
  107.5 3.1 %collective-permute-start.26 = (bf16[6,128,256]{2,1,0:T(8,128)(2,1)S(1)}, bf16[6,128,256]{2,1,0:T(8,128)(2,1)S(1)}, u32[]{:S(2)}, u32[]{:S(2)}) collective-permute-start(bf16[6,128,256]{2,1,0:T(8,128)(2,1)S(1)} %merge_chunk.11.rest_0_.rest_4_), channel_id=1, source_target_pairs={{0,2},{2,0},{1,3},{3,1},{4,6},{6,4},{5,7},{7,5},{8,10},{10,8},{9,1... | collective-permute-start | bytes 1179656 | tf_op jit(solution)/shard_map/ppermute | solution.py:463
  110.6 3.0 %exchange_chunks.7.rest_6_ = f32[8,256,256]{2,1,0:T(8,128)S(1)} custom-call(s32[16]{0:T(128)S(1)} %multiply_add_fusion.slot_ref, s32[1]{0:T(128)} %bitcast.fit_ref, bf16[6,128,256]{2,1,0:T(8,128)(2,1)S(1)} %merge_chunk.11.rest_0_.rest_4_, bf16[2,1024,256]{2,1,0:T(8,128)(2,1)S(1)} %pick_blocks.7.rest_0_.rest_1_.mine_ref, ...), custom_call_target="tpu_custom_call" | custom-call | flops 15099494400 | bytes 268697600 | tf_op jit(solution)/shard_map/exchange_chunks/pallas_call | solution.py:187
  113.6 3.7 %collective-permute-done.21.rest_3_ = bf16[6,128,256]{2,1,0:T(8,128)(2,1)S(1)} collective-permute-done((bf16[6,128,256]{2,1,0:T(8,128)(2,1)S(1)}, bf16[6,128,256]{2,1,0:T(8,128)(2,1)S(1)}, u32[]{:S(2)}, u32[]{:S(2)}) %collective-permute-start.21) | collective-permute-done | bytes 393248 | tf_op jit(solution)/shard_map/ppermute | solution.py:463
  117.4 8.4 %collective-permute-done.26.rest_5_ = bf16[6,128,256]{2,1,0:T(8,128)(2,1)S(1)} collective-permute-done((bf16[6,128,256]{2,1,0:T(8,128)(2,1)S(1)}, bf16[6,128,256]{2,1,0:T(8,128)(2,1)S(1)}, u32[]{:S(2)}, u32[]{:S(2)}) %collective-permute-start.26) | collective-permute-done | bytes 393248 | tf_op jit(solution)/shard_map/ppermute | solution.py:463
  125.8 5.7 %middle_step.1 = (bf16[8,256,256]{2,1,0:T(8,128)(2,1)}, bf16[16,256,256]{2,1,0:T(8,128)(2,1)S(1)}, bf16[2,128,256]{2,1,0:T(8,128)(2,1)S(1)}, bf16[2,128,256]{2,1...) custom-call(s32[16]{0:T(128)S(1)} %multiply_add_fusion.slot_ref, ...), custom_call_target="tpu_custom_call" | custom-call | flops 2147483648 | bytes 8388608 | tf_op jit(solution)/shard_map/middle_step/pallas_call | solution.py:295
  131.5 1.3 collective-permute-start.32
  132.8 2.9 %gradient_chunk.5 = (bf16[2,224,256]{2,1,0:T(8,128)(2,1)S(1)}, bf16[2,224,256]{2,1,0:T(8,128)(2,1)S(1)}, bf16[2,224,256]{2,1,0:T(8,128)(2,1)S(1)}, bf16[2,224,256]{2,1,0:T(8,128)(2,1)S(1)}) custom-call(s32[16]{0:T(128)S(1)} %multiply_add_fusion.slot_ref, bf16[16,256,256]{2,1,0:T(8,128)(2,1)S(1)} %get-tuple-element.65.weight_ref, ...), custom_call_target="tpu_custom_call" | custom-call | flops 469762048 | bytes 3932160 | tf_op jit(solution)/shard_map/gradient_chunk/pallas_call | solution.py:353
  135.7 1.5 collective-permute-start.35
  137.2 1.9 collective-permute-start.36
  139.6 1.1 collective-permute-start.34
  140.7 3.0 %gradient_chunk.6 = (bf16[2,224,256]{2,1,0:T(8,128)(2,1)S(1)}, bf16[2,224,256]{2,1,0:T(8,128)(2,1)S(1)}, bf16[2,224,256]{2,1,0:T(8,128)(2,1)S(1)}, bf16[2,224,256]{2,1,0:T(8,128)(2,1)S(1)}) custom-call(s32[16]{0:T(128)S(1)} %multiply_add_fusion.slot_ref, bf16[16,256,256]{2,1,0:T(8,128)(2,1)S(1)} %get-tuple-element.65.weight_ref, ...), custom_call_target="tpu_custom_call" | custom-call | flops 469762048 | bytes 3932160 | tf_op jit(solution)/shard_map/gradient_chunk/pallas_call | solution.py:353
  143.7 6.4 %collective-permute-start.38 = (bf16[2,224,256]{2,1,0:T(8,128)(2,1)S(1)}, bf16[2,224,256]{2,1,0:T(8,128)(2,1)S(1)}, u32[]{:S(2)}, u32[]{:S(2)}) collective-permute-start(bf16[2,224,256]{2,1,0:T(8,128)(2,1)S(1)} %get-tuple-element.79), channel_id=1, source_target_pairs={{0,4},{4,8},{8,12},{12,0},{1,5},{5,9},{9,13},{13,1},{2,6},{6,10},{... | collective-permute-start | bytes 688136 | tf_op jit(solution)/shard_map/ppermute | solution.py:559
  150.1 19.7 %collective-permute-done.34.rest_3_ = bf16[2,128,256]{2,1,0:T(8,128)(2,1)S(1)} collective-permute-done((bf16[2,128,256]{2,1,0:T(8,128)(2,1)S(1)}, bf16[2,128,256]{2,1,0:T(8,128)(2,1)S(1)}, u32[]{:S(2)}, u32[]{:S(2)}) %collective-permute-start.34) | collective-permute-done | bytes 131104 | tf_op jit(solution)/shard_map/ppermute | solution.py:559
  169.8 1.1 settle_chunks.5.rest_4_.refs_0_
  171.6 3.0 %gradient_chunk.4 = (bf16[2,240,256]{2,1,0:T(8,128)(2,1)S(1)}, bf16[2,240,256]{2,1,0:T(8,128)(2,1)S(1)}, bf16[2,240,256]{2,1,0:T(8,128)(2,1)S(1)}, bf16[2,240,256]{2,1,0:T(8,128)(2,1)S(1)}) custom-call(s32[16]{0:T(128)S(1)} %multiply_add_fusion.slot_ref, bf16[16,256,256]{2,1,0:T(8,128)(2,1)S(1)} %get-tuple-element.65.weight_ref, ...), custom_call_target="tpu_custom_call" | custom-call | flops 503316480 | bytes 4063232 | tf_op jit(solution)/shard_map/gradient_chunk/pallas_call | solution.py:353
  174.6 2.8 %collective-permute-start.29 = (bf16[2,240,256]{2,1,0:T(8,128)(2,1)S(1)}, bf16[2,240,256]{2,1,0:T(8,128)(2,1)S(1)}, u32[]{:S(2)}, u32[]{:S(2)}) collective-permute-start(bf16[2,240,256]{2,1,0:T(8,128)(2,1)S(1)} %get-tuple-element.68), channel_id=1, source_target_pairs={{0,8},{4,12},{8,0},{12,4},{1,9},{5,13},{9,1},{13,5},{2,10},{6,14},... | collective-permute-start | bytes 737288 | tf_op jit(solution)/shard_map/ppermute | solution.py:559
  177.4 1.3 collective-permute-start.30
  178.7 1.2 collective-permute-done.39.rest_2_
  179.9 11.3 %collective-permute-start.40 = (bf16[2,224,256]{2,1,0:T(8,128)(2,1)S(1)}, bf16[2,224,256]{2,1,0:T(8,128)(2,1)S(1)}, u32[]{:S(2)}, u32[]{:S(2)}) collective-permute-start(bf16[2,224,256]{2,1,0:T(8,128)(2,1)S(1)} %get-tuple-element.81), channel_id=1, source_target_pairs={{0,12},{4,0},{8,4},{12,8},{1,13},{5,1},{9,5},{13,9},{2,14},{6,2},{... | collective-permute-start | bytes 688136 | tf_op jit(solution)/shard_map/ppermute | solution.py:559
  191.2 2.8 %gradient_chunk.7 = (bf16[2,208,256]{2,1,0:T(8,128)(2,1)S(1)}, bf16[2,208,256]{2,1,0:T(8,128)(2,1)S(1)}, bf16[2,208,256]{2,1,0:T(8,128)(2,1)S(1)}, bf16[2,208,256]{2,1,0:T(8,128)(2,1)S(1)}) custom-call(s32[16]{0:T(128)S(1)} %multiply_add_fusion.slot_ref, bf16[16,256,256]{2,1,0:T(8,128)(2,1)S(1)} %get-tuple-element.65.weight_ref, ...), custom_call_target="tpu_custom_call" | custom-call | flops 436207616 | bytes 3801088 | tf_op jit(solution)/shard_map/gradient_chunk/pallas_call | solution.py:353
  194.1 6.5 %collective-permute-done.28.rest_1_ = bf16[2,240,256]{2,1,0:T(8,128)(2,1)S(1)} collective-permute-done((bf16[2,240,256]{2,1,0:T(8,128)(2,1)S(1)}, bf16[2,240,256]{2,1,0:T(8,128)(2,1)S(1)}, u32[]{:S(2)}, u32[]{:S(2)}) %collective-permute-start.28) | collective-permute-done | bytes 245792 | tf_op jit(solution)/shard_map/ppermute | solution.py:559
  200.6 2.2 collective-permute-start.41
  202.8 3.1 %collective-permute-done.29.rest_2_ = bf16[2,240,256]{2,1,0:T(8,128)(2,1)S(1)} collective-permute-done((bf16[2,240,256]{2,1,0:T(8,128)(2,1)S(1)}, bf16[2,240,256]{2,1,0:T(8,128)(2,1)S(1)}, u32[]{:S(2)}, u32[]{:S(2)}) %collective-permute-start.29) | collective-permute-done | bytes 245792 | tf_op jit(solution)/shard_map/ppermute | solution.py:559
  205.9 3.6 %collective-permute-start.42 = (bf16[2,208,256]{2,1,0:T(8,128)(2,1)S(1)}, bf16[2,208,256]{2,1,0:T(8,128)(2,1)S(1)}, u32[]{:S(2)}, u32[]{:S(2)}) collective-permute-start(bf16[2,208,256]{2,1,0:T(8,128)(2,1)S(1)} %get-tuple-element.84), channel_id=1, source_target_pairs={{0,8},{4,12},{8,0},{12,4},{1,9},{5,13},{9,1},{13,5},{2,10},{6,14},... | collective-permute-start | bytes 638984 | tf_op jit(solution)/shard_map/ppermute | solution.py:559
  210.5 4.9 %collective-permute-start.31 = (bf16[8,240,256]{2,1,0:T(8,128)(2,1)S(1)}, bf16[8,240,256]{2,1,0:T(8,128)(2,1)S(1)}, u32[]{:S(2)}, u32[]{:S(2)}) collective-permute-start(bf16[8,240,256]{2,1,0:T(8,128)(2,1)S(1)} %settle_chunks.4.refs_0_), channel_id=1, source_target_pairs={{0,1},{1,0},{2,3},{3,2},{4,5},{5,4},{6,7},{7,6},{8,9},{9,8},{10,11... | collective-permute-start | bytes 2949128 | tf_op jit(solution)/shard_map/ppermute | solution.py:569
  216.3 3.3 %collective-permute-done.41.rest_1_ = bf16[2,208,256]{2,1,0:T(8,128)(2,1)S(1)} collective-permute-done((bf16[2,208,256]{2,1,0:T(8,128)(2,1)S(1)}, bf16[2,208,256]{2,1,0:T(8,128)(2,1)S(1)}, u32[]{:S(2)}, u32[]{:S(2)}) %collective-permute-start.41) | collective-permute-done | bytes 213024 | tf_op jit(solution)/shard_map/ppermute | solution.py:559
  220.5 3.6 %collective-permute-done.42.rest_2_ = bf16[2,208,256]{2,1,0:T(8,128)(2,1)S(1)} collective-permute-done((bf16[2,208,256]{2,1,0:T(8,128)(2,1)S(1)}, bf16[2,208,256]{2,1,0:T(8,128)(2,1)S(1)}, u32[]{:S(2)}, u32[]{:S(2)}) %collective-permute-start.42) | collective-permute-done | bytes 213024 | tf_op jit(solution)/shard_map/ppermute | solution.py:559
  225.8 2.0 collective-permute-done.46.refs_5_
  227.8 3.0 %add_chunks.2.refs_2_ = f32[8,1024,256]{2,1,0:T(8,128)} custom-call(bf16[8,352,256]{2,1,0:T(8,128)(2,1)S(1)} %settle_chunks.5.rest_4_.refs_0_, bf16[8,224,256]{2,1,0:T(8,128)(2,1)S(1)} %settle_chunks.6.rest_4_.refs_1_, bf16[8,208,256]{2,1,0:T(8,128)(2,1)S(1)} %settle_chunks.7.refs_2_, bf16[8,352,256]{2,1,0:T(8,128)(2,1)S(1)} %collective-permute-done.44.refs_3_, ...), custom_call_target="tpu_custom_call" | custom-call | bytes 12845056 | tf_op jit(solution)/shard_map/add_chunks/pallas_call | solution.py:433
  230.8 1.4 add_chunks.3
  (115 shorter events, 17.7 us)
Async XLA Ops:
  2.1 4.6 %copy-start.10 = (s32[16]{0:T(128)}, s32[16]{0:T(128)S(1)}, u32[]{:S(2)}) copy-start(s32[16]{0:T(128)S(1)} %sub.25) | copy-start | bytes 196
  3.0 5.6 %collective-permute-start.1 = (f32[10]{0:T(128)S(1)}, f32[10]{0:T(128)S(1)}, u32[]{:S(2)}, u32[]{:S(2)}) collective-permute-start(f32[10]{0:T(128)S(1)} %get-tuple-element.89), channel_id=1, source_target_pairs={{0,4},{4,8},{8,12},{12,0},{1,5},{5,9},{9,13},{13,1},{2,6},{6,10},{... | collective-permute-start | bytes 128 | tf_op jit(solution)/shard_map/ppermute | solution.py:496
  4.3 4.4 %collective-permute-start.2 = (f32[10]{0:T(128)S(1)}, f32[10]{0:T(128)S(1)}, u32[]{:S(2)}, u32[]{:S(2)}) collective-permute-start(f32[10]{0:T(128)S(1)} %get-tuple-element.90), channel_id=1, source_target_pairs={{0,8},{4,12},{8,0},{12,4},{1,9},{5,13},{9,1},{13,5},{2,10},{6,14},... | collective-permute-start | bytes 128 | tf_op jit(solution)/shard_map/ppermute | solution.py:496
  5.4 3.3 %collective-permute-start.3 = (f32[10]{0:T(128)S(1)}, f32[10]{0:T(128)S(1)}, u32[]{:S(2)}, u32[]{:S(2)}) collective-permute-start(f32[10]{0:T(128)S(1)} %get-tuple-element.91), channel_id=1, source_target_pairs={{0,12},{4,0},{8,4},{12,8},{1,13},{5,1},{9,5},{13,9},{2,14},{6,2},{... | collective-permute-start | bytes 128 | tf_op jit(solution)/shard_map/ppermute | solution.py:496
  8.6 0.6 copy-start.12
  8.7 0.6 copy-start.13
  8.7 0.6 copy-start.14
  9.3 2.1 copy-start.8
  9.3 7.9 %copy-start = (bf16[8,1024,256]{2,1,0:T(8,128)(2,1)S(1)}, bf16[8,1024,256]{2,1,0:T(8,128)(2,1)}, u32[]{:S(2)}) copy-start(bf16[8,1024,256]{2,1,0:T(8,128)(2,1)} %blocks_ref.13) | copy-start | bytes 12582916
  11.4 28.9 %collective-permute-start.4 = (bf16[2,256,256]{2,1,0:T(8,128)(2,1)S(1)}, bf16[2,256,256]{2,1,0:T(8,128)(2,1)S(1)}, u32[]{:S(2)}, u32[]{:S(2)}) collective-permute-start(bf16[2,256,256]{2,1,0:T(8,128)(2,1)S(1)} %get-tuple-element.44), channel_id=1, source_target_pairs={{0,12},{4,0},{8,4},{12,8},{1,13},{5,1},{9,5},{13,9},{2,14},{6,2},{... | collective-permute-start | bytes 786440 | tf_op jit(solution)/shard_map/ppermute | solution.py:525
  12.6 27.8 %collective-permute-start.5 = (bf16[2,256,256]{2,1,0:T(8,128)(2,1)S(1)}, bf16[2,256,256]{2,1,0:T(8,128)(2,1)S(1)}, u32[]{:S(2)}, u32[]{:S(2)}) collective-permute-start(bf16[2,256,256]{2,1,0:T(8,128)(2,1)S(1)} %get-tuple-element.45), channel_id=1, source_target_pairs={{0,8},{4,12},{8,0},{12,4},{1,9},{5,13},{9,1},{13,5},{2,10},{6,14},... | collective-permute-start | bytes 786440 | tf_op jit(solution)/shard_map/ppermute | solution.py:525
  13.7 26.6 %collective-permute-start.6 = (bf16[2,256,256]{2,1,0:T(8,128)(2,1)S(1)}, bf16[2,256,256]{2,1,0:T(8,128)(2,1)S(1)}, u32[]{:S(2)}, u32[]{:S(2)}) collective-permute-start(bf16[2,256,256]{2,1,0:T(8,128)(2,1)S(1)} %get-tuple-element.46), channel_id=1, source_target_pairs={{0,4},{4,8},{8,12},{12,0},{1,5},{5,9},{9,13},{13,1},{2,6},{6,10},{... | collective-permute-start | bytes 786440 | tf_op jit(solution)/shard_map/ppermute | solution.py:525
  16.0 63.3 %collective-permute-start = (bf16[2,1024,256]{2,1,0:T(8,128)(2,1)S(1)}, bf16[2,1024,256]{2,1,0:T(8,128)(2,1)S(1)}, u32[]{:S(2)}, u32[]{:S(2)}) collective-permute-start(bf16[2,1024,256]{2,1,0:T(8,128)(2,1)S(1)} %pick_blocks.7.rest_0_.rest_1_.mine_ref), channel_id=1, source_target_pairs={{0,2},{2,0},{1,3},{3,1},{4,6},{6,4},{5,7},{7,5},{8,10},{10,8},{9,1... | collective-permute-start | bytes 3145736 | tf_op jit(solution)/shard_map/ppermute | solution.py:463
  18.6 21.7 %collective-permute-start.7 = (bf16[2,208,256]{2,1,0:T(8,128)(2,1)S(1)}, bf16[2,208,256]{2,1,0:T(8,128)(2,1)S(1)}, u32[]{:S(2)}, u32[]{:S(2)}) collective-permute-start(bf16[2,208,256]{2,1,0:T(8,128)(2,1)S(1)} %get-tuple-element.48), channel_id=1, source_target_pairs={{0,4},{4,8},{8,12},{12,0},{1,5},{5,9},{9,13},{13,1},{2,6},{6,10},{... | collective-permute-start | bytes 638984 | tf_op jit(solution)/shard_map/ppermute | solution.py:525
  40.4 38.9 %collective-permute-start.19 = (bf16[6,256,256]{2,1,0:T(8,128)(2,1)S(1)}, bf16[6,256,256]{2,1,0:T(8,128)(2,1)}, u32[]{:S(2)}, u32[]{:S(2)}) collective-permute-start(bf16[6,256,256]{2,1,0:T(8,128)(2,1)S(1)} %merge_chunk.6.rest_0_.rest_2_), channel_id=1, source_target_pairs={{0,2},{2,0},{1,3},{3,1},{4,6},{6,4},{5,7},{7,5},{8,10},{10,8},{9,1... | collective-permute-start | bytes 2359304 | tf_op jit(solution)/shard_map/ppermute | solution.py:463
  41.7 7.3 %collective-permute-start.12 = (bf16[2,208,256]{2,1,0:T(8,128)(2,1)}, bf16[2,208,256]{2,1,0:T(8,128)(2,1)S(1)}, u32[]{:S(2)}, u32[]{:S(2)}) collective-permute-start(bf16[2,208,256]{2,1,0:T(8,128)(2,1)} %get-tuple-element.52), channel_id=1, source_target_pairs={{0,8},{4,12},{8,0},{12,4},{1,9},{5,13},{9,1},{13,5},{2,10},{6,14},... | collective-permute-start | bytes 638984 | tf_op jit(solution)/shard_map/ppermute | solution.py:525
  41.7 22.4 %collective-permute-start.11 = (bf16[2,208,256]{2,1,0:T(8,128)(2,1)}, bf16[2,208,256]{2,1,0:T(8,128)(2,1)S(1)}, u32[]{:S(2)}, u32[]{:S(2)}) collective-permute-start(bf16[2,208,256]{2,1,0:T(8,128)(2,1)} %get-tuple-element.47.refs_3_), channel_id=1, source_target_pairs={{0,12},{4,0},{8,4},{12,8},{1,13},{5,1},{9,5},{13,9},{2,14},{6,2},{... | collective-permute-start | bytes 638984 | tf_op jit(solution)/shard_map/ppermute | solution.py:525
  45.3 2.2 copy-start.1
  47.5 16.5 %copy-start.11 = (s32[16]{0:T(128)S(1)}, s32[16]{0:T(128)}, u32[]{:S(2)}) copy-start(s32[16]{0:T(128)} %copy-done.10) | copy-start | bytes 196
  47.5 18.8 %copy-start.7 = (s32[8]{0:T(128)S(1)}, s32[8]{0:T(128)}, u32[]{:S(2)}) copy-start(s32[8]{0:T(128)} %size_ref.1) | copy-start | bytes 100
  48.9 25.1 %collective-permute-start.9 = (bf16[2,160,256]{2,1,0:T(8,128)(2,1)}, bf16[2,160,256]{2,1,0:T(8,128)(2,1)}, u32[]{:S(2)}, u32[]{:S(2)}) collective-permute-start(bf16[2,160,256]{2,1,0:T(8,128)(2,1)} %get-tuple-element.50), channel_id=1, source_target_pairs={{0,8},{4,12},{8,0},{12,4},{1,9},{5,13},{9,1},{13,5},{2,10},{6,14},... | collective-permute-start | bytes 491528 | tf_op jit(solution)/shard_map/ppermute | solution.py:525
  49.0 25.3 %collective-permute-start.10 = (bf16[2,160,256]{2,1,0:T(8,128)(2,1)}, bf16[2,160,256]{2,1,0:T(8,128)(2,1)}, u32[]{:S(2)}, u32[]{:S(2)}) collective-permute-start(bf16[2,160,256]{2,1,0:T(8,128)(2,1)} %get-tuple-element.51), channel_id=1, source_target_pairs={{0,4},{4,8},{8,12},{12,0},{1,5},{5,9},{9,13},{13,1},{2,6},{6,10},{... | collective-permute-start | bytes 491528 | tf_op jit(solution)/shard_map/ppermute | solution.py:525
  64.0 10.8 %collective-permute-start.8 = (bf16[2,160,256]{2,1,0:T(8,128)(2,1)}, bf16[2,160,256]{2,1,0:T(8,128)(2,1)}, u32[]{:S(2)}, u32[]{:S(2)}) collective-permute-start(bf16[2,160,256]{2,1,0:T(8,128)(2,1)} %get-tuple-element.49.refs_3_), channel_id=1, source_target_pairs={{0,12},{4,0},{8,4},{12,8},{1,13},{5,1},{9,5},{13,9},{2,14},{6,2},{... | collective-permute-start | bytes 491528 | tf_op jit(solution)/shard_map/ppermute | solution.py:525
  66.4 1.6 copy-start.4
  69.7 4.3 %copy-start.5 = (bf16[8,256,256]{2,1,0:T(8,128)(2,1)}, bf16[8,256,256]{2,1,0:T(8,128)(2,1)S(1)}, u32[]{:S(2)}) copy-start(bf16[8,256,256]{2,1,0:T(8,128)(2,1)S(1)} %get-tuple-element.63.rest_8_) | copy-start | bytes 3145732
  70.6 2.2 copy-start.2
  72.8 5.3 %copy-start.3 = (bf16[8,1024,256]{2,1,0:T(8,128)(2,1)S(1)}, bf16[8,1024,256]{2,1,0:T(8,128)(2,1)}, u32[]{:S(2)}) copy-start(bf16[8,1024,256]{2,1,0:T(8,128)(2,1)} %blocks_ref.13) | copy-start | bytes 12582916
  74.0 16.9 %collective-permute-start.20 = (bf16[6,208,256]{2,1,0:T(8,128)(2,1)S(1)}, bf16[6,208,256]{2,1,0:T(8,128)(2,1)S(1)}, u32[]{:S(2)}, u32[]{:S(2)}) collective-permute-start(bf16[6,208,256]{2,1,0:T(8,128)(2,1)S(1)} %merge_chunk.7.rest_0_.rest_2_.rest_1_), channel_id=1, source_target_pairs={{0,2},{2,0},{1,3},{3,1},{4,6},{6,4},{5,7},{7,5},{8,10},{10,8},{9,1... | collective-permute-start | bytes 1916936 | tf_op jit(solution)/shard_map/ppermute | solution.py:463
  74.3 10.3 %collective-permute-start.17 = (bf16[2,144,256]{2,1,0:T(8,128)(2,1)S(1)}, bf16[2,144,256]{2,1,0:T(8,128)(2,1)S(1)}, u32[]{:S(2)}, u32[]{:S(2)}) collective-permute-start(bf16[2,144,256]{2,1,0:T(8,128)(2,1)S(1)} %get-tuple-element.58), channel_id=1, source_target_pairs={{0,8},{4,12},{8,0},{12,4},{1,9},{5,13},{9,1},{13,5},{2,10},{6,14},... | collective-permute-start | bytes 442376 | tf_op jit(solution)/shard_map/ppermute | solution.py:525
  74.9 14.2 %collective-permute-start.16 = (bf16[2,144,256]{2,1,0:T(8,128)(2,1)S(1)}, bf16[2,144,256]{2,1,0:T(8,128)(2,1)S(1)}, u32[]{:S(2)}, u32[]{:S(2)}) collective-permute-start(bf16[2,144,256]{2,1,0:T(8,128)(2,1)S(1)} %get-tuple-element.53.refs_3_), channel_id=1, source_target_pairs={{0,12},{4,0},{8,4},{12,8},{1,13},{5,1},{9,5},{13,9},{2,14},{6,2},{... | collective-permute-start | bytes 442376 | tf_op jit(solution)/shard_map/ppermute | solution.py:525
  79.3 8.4 %collective-permute-start.18 = (bf16[2,144,256]{2,1,0:T(8,128)(2,1)S(1)}, bf16[2,144,256]{2,1,0:T(8,128)(2,1)S(1)}, u32[]{:S(2)}, u32[]{:S(2)}) collective-permute-start(bf16[2,144,256]{2,1,0:T(8,128)(2,1)S(1)} %get-tuple-element.59), channel_id=1, source_target_pairs={{0,4},{4,8},{8,12},{12,0},{1,5},{5,9},{9,13},{13,1},{2,6},{6,10},{... | collective-permute-start | bytes 442376 | tf_op jit(solution)/shard_map/ppermute | solution.py:525
  79.3 21.5 %collective-permute-start.25 = (bf16[6,160,256]{2,1,0:T(8,128)(2,1)S(1)}, bf16[6,160,256]{2,1,0:T(8,128)(2,1)S(1)}, u32[]{:S(2)}, u32[]{:S(2)}) collective-permute-start(bf16[6,160,256]{2,1,0:T(8,128)(2,1)S(1)} %merge_chunk.8.rest_0_.rest_2_.rest_1_), channel_id=1, source_target_pairs={{0,2},{2,0},{1,3},{3,1},{4,6},{6,4},{5,7},{7,5},{8,10},{10,8},{9,1... | collective-permute-start | bytes 1474568 | tf_op jit(solution)/shard_map/ppermute | solution.py:463
  84.7 11.6 %collective-permute-start.14 = (bf16[2,128,256]{2,1,0:T(8,128)(2,1)S(1)}, bf16[2,128,256]{2,1,0:T(8,128)(2,1)S(1)}, u32[]{:S(2)}, u32[]{:S(2)}) collective-permute-start(bf16[2,128,256]{2,1,0:T(8,128)(2,1)S(1)} %get-tuple-element.56), channel_id=1, source_target_pairs={{0,8},{4,12},{8,0},{12,4},{1,9},{5,13},{9,1},{13,5},{2,10},{6,14},... | collective-permute-start | bytes 393224 | tf_op jit(solution)/shard_map/ppermute | solution.py:525
  87.6 10.5 %collective-permute-start.15 = (bf16[2,128,256]{2,1,0:T(8,128)(2,1)S(1)}, bf16[2,128,256]{2,1,0:T(8,128)(2,1)S(1)}, u32[]{:S(2)}, u32[]{:S(2)}) collective-permute-start(bf16[2,128,256]{2,1,0:T(8,128)(2,1)S(1)} %get-tuple-element.57), channel_id=1, source_target_pairs={{0,4},{4,8},{8,12},{12,0},{1,5},{5,9},{9,13},{13,1},{2,6},{6,10},{... | collective-permute-start | bytes 393224 | tf_op jit(solution)/shard_map/ppermute | solution.py:525
  89.1 11.2 %collective-permute-start.13 = (bf16[2,128,256]{2,1,0:T(8,128)(2,1)S(1)}, bf16[2,128,256]{2,1,0:T(8,128)(2,1)S(1)}, u32[]{:S(2)}, u32[]{:S(2)}) collective-permute-start(bf16[2,128,256]{2,1,0:T(8,128)(2,1)S(1)} %get-tuple-element.55.refs_3_), channel_id=1, source_target_pairs={{0,12},{4,0},{8,4},{12,8},{1,13},{5,1},{9,5},{13,9},{2,14},{6,2},{... | collective-permute-start | bytes 393224 | tf_op jit(solution)/shard_map/ppermute | solution.py:525
  90.9 19.7 %collective-permute-start.27 = (bf16[6,144,256]{2,1,0:T(8,128)(2,1)S(1)}, bf16[6,144,256]{2,1,0:T(8,128)(2,1)S(1)}, u32[]{:S(2)}, u32[]{:S(2)}) collective-permute-start(bf16[6,144,256]{2,1,0:T(8,128)(2,1)S(1)} %merge_chunk.9.rest_0_.rest_3_.rest_2_), channel_id=1, source_target_pairs={{0,2},{2,0},{1,3},{3,1},{4,6},{6,4},{5,7},{7,5},{8,10},{10,8},{9,1... | collective-permute-start | bytes 1327112 | tf_op jit(solution)/shard_map/ppermute | solution.py:463
  96.3 9.1 %collective-permute-start.23 = (bf16[2,128,256]{2,1,0:T(8,128)(2,1)S(1)}, bf16[2,128,256]{2,1,0:T(8,128)(2,1)S(1)}, u32[]{:S(2)}, u32[]{:S(2)}) collective-permute-start(bf16[2,128,256]{2,1,0:T(8,128)(2,1)S(1)} %get-tuple-element.61), channel_id=1, source_target_pairs={{0,8},{4,12},{8,0},{12,4},{1,9},{5,13},{9,1},{13,5},{2,10},{6,14},... | collective-permute-start | bytes 393224 | tf_op jit(solution)/shard_map/ppermute | solution.py:525
  98.1 7.3 %collective-permute-start.24 = (bf16[2,128,256]{2,1,0:T(8,128)(2,1)S(1)}, bf16[2,128,256]{2,1,0:T(8,128)(2,1)S(1)}, u32[]{:S(2)}, u32[]{:S(2)}) collective-permute-start(bf16[2,128,256]{2,1,0:T(8,128)(2,1)S(1)} %get-tuple-element.62), channel_id=1, source_target_pairs={{0,4},{4,8},{8,12},{12,0},{1,5},{5,9},{9,13},{13,1},{2,6},{6,10},{... | collective-permute-start | bytes 393224 | tf_op jit(solution)/shard_map/ppermute | solution.py:525
  100.3 6.7 %collective-permute-start.22 = (bf16[2,128,256]{2,1,0:T(8,128)(2,1)S(1)}, bf16[2,128,256]{2,1,0:T(8,128)(2,1)S(1)}, u32[]{:S(2)}, u32[]{:S(2)}) collective-permute-start(bf16[2,128,256]{2,1,0:T(8,128)(2,1)S(1)} %get-tuple-element.60.refs_3_), channel_id=1, source_target_pairs={{0,12},{4,0},{8,4},{12,8},{1,13},{5,1},{9,5},{13,9},{2,14},{6,2},{... | collective-permute-start | bytes 393224 | tf_op jit(solution)/shard_map/ppermute | solution.py:525
  100.9 16.5 %collective-permute-start.21 = (bf16[6,128,256]{2,1,0:T(8,128)(2,1)S(1)}, bf16[6,128,256]{2,1,0:T(8,128)(2,1)S(1)}, u32[]{:S(2)}, u32[]{:S(2)}) collective-permute-start(bf16[6,128,256]{2,1,0:T(8,128)(2,1)S(1)} %merge_chunk.10.rest_2_.rest_1_), channel_id=1, source_target_pairs={{0,2},{2,0},{1,3},{3,1},{4,6},{6,4},{5,7},{7,5},{8,10},{10,8},{9,1... | collective-permute-start | bytes 1179656 | tf_op jit(solution)/shard_map/ppermute | solution.py:463
  107.5 18.3 %copy-start.6 = (bf16[8,256,256]{2,1,0:T(8,128)(2,1)S(1)}, bf16[8,256,256]{2,1,0:T(8,128)(2,1)}, u32[]{:S(2)}) copy-start(bf16[8,256,256]{2,1,0:T(8,128)(2,1)} %copy-done.5) | copy-start | bytes 3145732
  107.5 18.3 %collective-permute-start.26 = (bf16[6,128,256]{2,1,0:T(8,128)(2,1)S(1)}, bf16[6,128,256]{2,1,0:T(8,128)(2,1)S(1)}, u32[]{:S(2)}, u32[]{:S(2)}) collective-permute-start(bf16[6,128,256]{2,1,0:T(8,128)(2,1)S(1)} %merge_chunk.11.rest_0_.rest_4_), channel_id=1, source_target_pairs={{0,2},{2,0},{1,3},{3,1},{4,6},{6,4},{5,7},{7,5},{8,10},{10,8},{9,1... | collective-permute-start | bytes 1179656 | tf_op jit(solution)/shard_map/ppermute | solution.py:463
  131.5 8.1 %collective-permute-start.32 = (bf16[2,128,256]{2,1,0:T(8,128)(2,1)S(1)}, bf16[2,128,256]{2,1,0:T(8,128)(2,1)S(1)}, u32[]{:S(2)}, u32[]{:S(2)}) collective-permute-start(bf16[2,128,256]{2,1,0:T(8,128)(2,1)S(1)} %get-tuple-element.71), channel_id=1, source_target_pairs={{0,4},{4,8},{8,12},{12,0},{1,5},{5,9},{9,13},{13,1},{2,6},{6,10},{... | collective-permute-start | bytes 393224 | tf_op jit(solution)/shard_map/ppermute | solution.py:559
  132.8 10.9 %collective-permute-start.33 = (bf16[2,128,256]{2,1,0:T(8,128)(2,1)S(1)}, bf16[2,128,256]{2,1,0:T(8,128)(2,1)S(1)}, u32[]{:S(2)}, u32[]{:S(2)}) collective-permute-start(bf16[2,128,256]{2,1,0:T(8,128)(2,1)S(1)} %get-tuple-element.72), channel_id=1, source_target_pairs={{0,8},{4,12},{8,0},{12,4},{1,9},{5,13},{9,1},{13,5},{2,10},{6,14},... | collective-permute-start | bytes 393224 | tf_op jit(solution)/shard_map/ppermute | solution.py:559
  135.7 34.1 %collective-permute-start.35 = (bf16[2,224,256]{2,1,0:T(8,128)(2,1)S(1)}, bf16[2,224,256]{2,1,0:T(8,128)(2,1)S(1)}, u32[]{:S(2)}, u32[]{:S(2)}) collective-permute-start(bf16[2,224,256]{2,1,0:T(8,128)(2,1)S(1)} %get-tuple-element.75), channel_id=1, source_target_pairs={{0,4},{4,8},{8,12},{12,0},{1,5},{5,9},{9,13},{13,1},{2,6},{6,10},{... | collective-permute-start | bytes 688136 | tf_op jit(solution)/shard_map/ppermute | solution.py:559
  137.2 32.6 %collective-permute-start.36 = (bf16[2,224,256]{2,1,0:T(8,128)(2,1)S(1)}, bf16[2,224,256]{2,1,0:T(8,128)(2,1)S(1)}, u32[]{:S(2)}, u32[]{:S(2)}) collective-permute-start(bf16[2,224,256]{2,1,0:T(8,128)(2,1)S(1)} %get-tuple-element.76), channel_id=1, source_target_pairs={{0,8},{4,12},{8,0},{12,4},{1,9},{5,13},{9,1},{13,5},{2,10},{6,14},... | collective-permute-start | bytes 688136 | tf_op jit(solution)/shard_map/ppermute | solution.py:559
  139.1 30.7 %collective-permute-start.37 = (bf16[2,224,256]{2,1,0:T(8,128)(2,1)S(1)}, bf16[2,224,256]{2,1,0:T(8,128)(2,1)S(1)}, u32[]{:S(2)}, u32[]{:S(2)}) collective-permute-start(bf16[2,224,256]{2,1,0:T(8,128)(2,1)S(1)} %get-tuple-element.77), channel_id=1, source_target_pairs={{0,12},{4,0},{8,4},{12,8},{1,13},{5,1},{9,5},{13,9},{2,14},{6,2},{... | collective-permute-start | bytes 688136 | tf_op jit(solution)/shard_map/ppermute | solution.py:559
  139.6 10.5 %copy-start.9 = (s32[1,2]{1,0:T(1,128)S(1)}, s32[1,2]{1,0:T(1,128)}, u32[]{:S(2)}) copy-start(s32[1,2]{1,0:T(1,128)} %copy-done.8) | copy-start | bytes 28
  139.6 30.2 %collective-permute-start.34 = (bf16[2,128,256]{2,1,0:T(8,128)(2,1)S(1)}, bf16[2,128,256]{2,1,0:T(8,128)(2,1)S(1)}, u32[]{:S(2)}, u32[]{:S(2)}) collective-permute-start(bf16[2,128,256]{2,1,0:T(8,128)(2,1)S(1)} %get-tuple-element.73), channel_id=1, source_target_pairs={{0,12},{4,0},{8,4},{12,8},{1,13},{5,1},{9,5},{13,9},{2,14},{6,2},{... | collective-permute-start | bytes 393224 | tf_op jit(solution)/shard_map/ppermute | solution.py:559
  143.7 33.7 %collective-permute-start.38 = (bf16[2,224,256]{2,1,0:T(8,128)(2,1)S(1)}, bf16[2,224,256]{2,1,0:T(8,128)(2,1)S(1)}, u32[]{:S(2)}, u32[]{:S(2)}) collective-permute-start(bf16[2,224,256]{2,1,0:T(8,128)(2,1)S(1)} %get-tuple-element.79), channel_id=1, source_target_pairs={{0,4},{4,8},{8,12},{12,0},{1,5},{5,9},{9,13},{13,1},{2,6},{6,10},{... | collective-permute-start | bytes 688136 | tf_op jit(solution)/shard_map/ppermute | solution.py:559
  169.8 10.1 %collective-permute-start.39 = (bf16[2,224,256]{2,1,0:T(8,128)(2,1)S(1)}, bf16[2,224,256]{2,1,0:T(8,128)(2,1)S(1)}, u32[]{:S(2)}, u32[]{:S(2)}) collective-permute-start(bf16[2,224,256]{2,1,0:T(8,128)(2,1)S(1)} %get-tuple-element.80), channel_id=1, source_target_pairs={{0,8},{4,12},{8,0},{12,4},{1,9},{5,13},{9,1},{13,5},{2,10},{6,14},... | collective-permute-start | bytes 688136 | tf_op jit(solution)/shard_map/ppermute | solution.py:559
  171.0 56.9 %collective-permute-start.44 = (bf16[8,352,256]{2,1,0:T(8,128)(2,1)S(1)}, bf16[8,352,256]{2,1,0:T(8,128)(2,1)S(1)}, u32[]{:S(2)}, u32[]{:S(2)}) collective-permute-start(bf16[8,352,256]{2,1,0:T(8,128)(2,1)S(1)} %settle_chunks.5.rest_4_.refs_0_), channel_id=1, source_target_pairs={{0,1},{1,0},{2,3},{3,2},{4,5},{5,4},{6,7},{7,6},{8,9},{9,8},{10,11... | collective-permute-start | bytes 4325384 | tf_op jit(solution)/shard_map/ppermute | solution.py:569
  174.6 26.1 %collective-permute-start.28 = (bf16[2,240,256]{2,1,0:T(8,128)(2,1)S(1)}, bf16[2,240,256]{2,1,0:T(8,128)(2,1)S(1)}, u32[]{:S(2)}, u32[]{:S(2)}) collective-permute-start(bf16[2,240,256]{2,1,0:T(8,128)(2,1)S(1)} %get-tuple-element.67), channel_id=1, source_target_pairs={{0,4},{4,8},{8,12},{12,0},{1,5},{5,9},{9,13},{13,1},{2,6},{6,10},{... | collective-permute-start | bytes 737288 | tf_op jit(solution)/shard_map/ppermute | solution.py:559
  174.6 31.3 %collective-permute-start.29 = (bf16[2,240,256]{2,1,0:T(8,128)(2,1)S(1)}, bf16[2,240,256]{2,1,0:T(8,128)(2,1)S(1)}, u32[]{:S(2)}, u32[]{:S(2)}) collective-permute-start(bf16[2,240,256]{2,1,0:T(8,128)(2,1)S(1)} %get-tuple-element.68), channel_id=1, source_target_pairs={{0,8},{4,12},{8,0},{12,4},{1,9},{5,13},{9,1},{13,5},{2,10},{6,14},... | collective-permute-start | bytes 737288 | tf_op jit(solution)/shard_map/ppermute | solution.py:559
  177.4 32.1 %collective-permute-start.30 = (bf16[2,240,256]{2,1,0:T(8,128)(2,1)S(1)}, bf16[2,240,256]{2,1,0:T(8,128)(2,1)S(1)}, u32[]{:S(2)}, u32[]{:S(2)}) collective-permute-start(bf16[2,240,256]{2,1,0:T(8,128)(2,1)S(1)} %get-tuple-element.69), channel_id=1, source_target_pairs={{0,12},{4,0},{8,4},{12,8},{1,13},{5,1},{9,5},{13,9},{2,14},{6,2},{... | collective-permute-start | bytes 737288 | tf_op jit(solution)/shard_map/ppermute | solution.py:559
  179.9 30.6 %collective-permute-start.40 = (bf16[2,224,256]{2,1,0:T(8,128)(2,1)S(1)}, bf16[2,224,256]{2,1,0:T(8,128)(2,1)S(1)}, u32[]{:S(2)}, u32[]{:S(2)}) collective-permute-start(bf16[2,224,256]{2,1,0:T(8,128)(2,1)S(1)} %get-tuple-element.81), channel_id=1, source_target_pairs={{0,12},{4,0},{8,4},{12,8},{1,13},{5,1},{9,5},{13,9},{2,14},{6,2},{... | collective-permute-start | bytes 688136 | tf_op jit(solution)/shard_map/ppermute | solution.py:559
  200.6 19.0 %collective-permute-start.41 = (bf16[2,208,256]{2,1,0:T(8,128)(2,1)S(1)}, bf16[2,208,256]{2,1,0:T(8,128)(2,1)S(1)}, u32[]{:S(2)}, u32[]{:S(2)}) collective-permute-start(bf16[2,208,256]{2,1,0:T(8,128)(2,1)S(1)} %get-tuple-element.83), channel_id=1, source_target_pairs={{0,4},{4,8},{8,12},{12,0},{1,5},{5,9},{9,13},{13,1},{2,6},{6,10},{... | collective-permute-start | bytes 638984 | tf_op jit(solution)/shard_map/ppermute | solution.py:559
  205.9 18.3 %collective-permute-start.42 = (bf16[2,208,256]{2,1,0:T(8,128)(2,1)S(1)}, bf16[2,208,256]{2,1,0:T(8,128)(2,1)S(1)}, u32[]{:S(2)}, u32[]{:S(2)}) collective-permute-start(bf16[2,208,256]{2,1,0:T(8,128)(2,1)S(1)} %get-tuple-element.84), channel_id=1, source_target_pairs={{0,8},{4,12},{8,0},{12,4},{1,9},{5,13},{9,1},{13,5},{2,10},{6,14},... | collective-permute-start | bytes 638984 | tf_op jit(solution)/shard_map/ppermute | solution.py:559
  209.5 14.7 %collective-permute-start.43 = (bf16[2,208,256]{2,1,0:T(8,128)(2,1)S(1)}, bf16[2,208,256]{2,1,0:T(8,128)(2,1)S(1)}, u32[]{:S(2)}, u32[]{:S(2)}) collective-permute-start(bf16[2,208,256]{2,1,0:T(8,128)(2,1)S(1)} %get-tuple-element.85), channel_id=1, source_target_pairs={{0,12},{4,0},{8,4},{12,8},{1,13},{5,1},{9,5},{13,9},{2,14},{6,2},{... | collective-permute-start | bytes 638984 | tf_op jit(solution)/shard_map/ppermute | solution.py:559
  210.5 20.3 %collective-permute-start.31 = (bf16[8,240,256]{2,1,0:T(8,128)(2,1)S(1)}, bf16[8,240,256]{2,1,0:T(8,128)(2,1)S(1)}, u32[]{:S(2)}, u32[]{:S(2)}) collective-permute-start(bf16[8,240,256]{2,1,0:T(8,128)(2,1)S(1)} %settle_chunks.4.refs_0_), channel_id=1, source_target_pairs={{0,1},{1,0},{2,3},{3,2},{4,5},{5,4},{6,7},{7,6},{8,9},{9,8},{10,11... | collective-permute-start | bytes 2949128 | tf_op jit(solution)/shard_map/ppermute | solution.py:569
  219.6 8.2 %collective-permute-start.45 = (bf16[8,224,256]{2,1,0:T(8,128)(2,1)S(1)}, bf16[8,224,256]{2,1,0:T(8,128)(2,1)S(1)}, u32[]{:S(2)}, u32[]{:S(2)}) collective-permute-start(bf16[8,224,256]{2,1,0:T(8,128)(2,1)S(1)} %settle_chunks.6.rest_4_.refs_1_), channel_id=1, source_target_pairs={{0,1},{1,0},{2,3},{3,2},{4,5},{5,4},{6,7},{7,6},{8,9},{9,8},{10,11... | collective-permute-start | bytes 2752520 | tf_op jit(solution)/shard_map/ppermute | solution.py:569
  225.1 2.7 %collective-permute-start.46 = (bf16[8,208,256]{2,1,0:T(8,128)(2,1)S(1)}, bf16[8,208,256]{2,1,0:T(8,128)(2,1)S(1)}, u32[]{:S(2)}, u32[]{:S(2)}) collective-permute-start(bf16[8,208,256]{2,1,0:T(8,128)(2,1)S(1)} %settle_chunks.7.refs_2_), channel_id=1, source_target_pairs={{0,1},{1,0},{2,3},{3,2},{4,5},{5,4},{6,7},{7,6},{8,9},{9,8},{10,11... | collective-permute-start | bytes 2555912 | tf_op jit(solution)/shard_map/ppermute | solution.py:569

commit v7 on v6

--- a/solution.py
+++ b/solution.py
@@ -17,7 +17,7 @@
 CHAIN_GRADIENTS = False
 SETTLE_FROM = 99
 UNROLL = 4
-PREPARE_AT = 3
+PREPARE_AT = 1
 FIRST_WAITS = (2,)
 SETTLE_WEIGHT = 50
 MERGE_WEIGHT = 50

time: 234 us -> 227 us (0.970)
  starting transfers between devices: 79.7 us -> 59.1 us
  waiting for transfers between devices: 85.2 us -> 103 us
  local copies, waits for them, and re-layouts: 9.21 us -> 5.61 us
    ppermute x18, waiting for transfers between devices: 33.5 us -> 46.3 us  [per_device(): lax.ppermute(picked[d - 1], 'orb', shifted(n, n - d))]
    ppermute x15, starting transfers between devices: 34 us -> 22.6 us  [per_device(): lax.ppermute(sums[d], 'orb', shifted(n, d))]
    ppermute x15, waiting for transfers between devices: 37.5 us -> 48.1 us  [per_device(): lax.ppermute(sums[d], 'orb', shifted(n, d))]
    ppermute x7, starting transfers between devices: 10.8 us -> 3.7 us  [around_fit(): lax.ppermute(x, 'fit', shifted(n_fit, d))]
    ppermute x7, waiting for transfers between devices: 12.2 us -> 6.89 us  [around_fit(): lax.ppermute(x, 'fit', shifted(n_fit, d))]
    ppermute x18, starting transfers between devices: 24 us -> 20.2 us  [per_device(): lax.ppermute(picked[d - 1], 'orb', shifted(n, n - d))]
    unnamed x31 -> x19, local copies, waits for them, and re-layouts: 6.66 us -> 4.59 us
  transfers between devices with their start and end apart: 47 -> 47, of which waited for: 13 -> 17; matrix products, arithmetic and copies ran while one was open for 1% -> 1% of each run, Pallas kernels for 20% -> 20%
where the time goes in v7:
time: 227 us; the launch traced here: 226 us
  waiting for transfers between devices  103 us (45%)
  starting transfers between devices  59.1 us (26%)
  Pallas kernels  54.1 us (24%)
  local copies, waits for them, and re-layouts  5.61 us (2%)
  other arithmetic  2.98 us (1%)
    ppermute x15, waiting for transfers between devices, per_device(): lax.ppermute(sums[d], 'orb', shifted(n, d))  48.1 us
    ppermute x18, waiting for transfers between devices, per_device(): lax.ppermute(picked[d - 1], 'orb', shifted(n, n - d))  46.3 us
    ppermute x15, starting transfers between devices, per_device(): lax.ppermute(sums[d], 'orb', shifted(n, d))  22.6 us
    ppermute x18, starting transfers between devices, per_device(): lax.ppermute(picked[d - 1], 'orb', shifted(n, n - d))  20.2 us
    pallas_call x4, Pallas kernels, exchange_chunks(): pl.pallas_call(functools.partial(exchange_kernel, chunks, n_fit, first, l...  13.3 us
    pallas_call x4, Pallas kernels, gradient_chunk(): pl.pallas_call(functools.partial(gradient_kernel, parts, n), out_shape=[j...  11.7 us
    pallas_call x7, Pallas kernels, pick_blocks(): pl.pallas_call(functools.partial(pick_kernel, start, rows, len(after)), o...  10 us
    ppermute x4, starting transfers between devices, per_device(): waiting.append((group, here, lax.ppermute(here, 'rep', swap)))  8.82 us
  transfers between devices with their start and end apart: 47, of which 17 were waited for; matrix products, arithmetic and copies ran while one was open for 1% of the time, Pallas kernels for 20%

profile of v7, /device:TPU:9, one launch (start us, length us, event | category | flops | bytes accessed | tf_op | source)
XLA Modules:
  0.0 226.4 jit_solution(15592489173267659214)
XLA Ops:
  3.0 1.3 collective-permute-start.1
  4.3 1.1 collective-permute-start.2
  5.4 1.4 collective-permute-start.3
  6.9 1.8 pick_blocks.7.rest_0_.rest_1_.mine_ref
  8.7 2.1 pick_blocks.8
  10.8 1.1 collective-permute-start.4
  12.0 1.2 collective-permute-start.5
  13.1 2.3 %collective-permute-start.6 = (bf16[2,256,256]{2,1,0:T(8,128)(2,1)S(1)}, bf16[2,256,256]{2,1,0:T(8,128)(2,1)S(1)}, u32[]{:S(2)}, u32[]{:S(2)}) collective-permute-start(bf16[2,256,256]{2,1,0:T(8,128)(2,1)S(1)} %get-tuple-element.46), channel_id=1, source_target_pairs={{0,4},{4,8},{8,12},{12,0},{1,5},{5,9},{9,13},{13,1},{2,6},{6,10},{... | collective-permute-start | bytes 786440 | tf_op jit(solution)/shard_map/ppermute | solution.py:525
  15.4 1.2 collective-permute-start
  16.6 1.4 pick_blocks.9
  18.4 1.7 prepare_pairs.1
  20.2 1.0 copy-done.6
  21.1 18.6 %collective-permute-done.7.refs_5_.refs_2_ = bf16[2,208,256]{2,1,0:T(8,128)(2,1)S(1)} collective-permute-done((bf16[2,208,256]{2,1,0:T(8,128)(2,1)S(1)}, bf16[2,208,256]{2,1,0:T(8,128)(2,1)S(1)}, u32[]{:S(2)}, u32[]{:S(2)}) %collective-permute-start.7) | collective-permute-done | bytes 213024 | tf_op jit(solution)/shard_map/ppermute | solution.py:525
  39.8 1.3 copy-done.3
  41.1 1.2 collective-permute-start.19
  42.4 3.4 %collective-permute-start.11 = (bf16[2,208,256]{2,1,0:T(8,128)(2,1)}, bf16[2,208,256]{2,1,0:T(8,128)(2,1)S(1)}, u32[]{:S(2)}, u32[]{:S(2)}) collective-permute-start(bf16[2,208,256]{2,1,0:T(8,128)(2,1)} %get-tuple-element.47.refs_3_), channel_id=1, source_target_pairs={{0,12},{4,0},{8,4},{12,8},{1,13},{5,1},{9,5},{13,9},{2,14},{6,2},{... | collective-permute-start | bytes 638984 | tf_op jit(solution)/shard_map/ppermute | solution.py:525
  47.1 2.2 copy-done.1
  49.2 1.3 pick_blocks.10
  50.6 3.8 %collective-permute-start.10 = (bf16[2,160,256]{2,1,0:T(8,128)(2,1)S(1)}, bf16[2,160,256]{2,1,0:T(8,128)(2,1)S(1)}, u32[]{:S(2)}, u32[]{:S(2)}) collective-permute-start(bf16[2,160,256]{2,1,0:T(8,128)(2,1)S(1)} %get-tuple-element.52), channel_id=1, source_target_pairs={{0,4},{4,8},{8,12},{12,0},{1,5},{5,9},{9,13},{13,1},{2,6},{6,10},{... | collective-permute-start | bytes 491528 | tf_op jit(solution)/shard_map/ppermute | solution.py:525
  54.5 10.3 %collective-permute-done.11.refs_0_ = bf16[2,208,256]{2,1,0:T(8,128)(2,1)S(1)} collective-permute-done((bf16[2,208,256]{2,1,0:T(8,128)(2,1)}, bf16[2,208,256]{2,1,0:T(8,128)(2,1)S(1)}, u32[]{:S(2)}, u32[]{:S(2)}) %collective-permute-start.11) | collective-permute-done | bytes 213024 | tf_op jit(solution)/shard_map/ppermute | solution.py:525
  65.7 1.2 pick_blocks.11
  67.8 7.4 %collective-permute-done.8.refs_0_ = bf16[2,160,256]{2,1,0:T(8,128)(2,1)S(1)} collective-permute-done((bf16[2,160,256]{2,1,0:T(8,128)(2,1)S(1)}, bf16[2,160,256]{2,1,0:T(8,128)(2,1)S(1)}, u32[]{:S(2)}, u32[]{:S(2)}) %collective-permute-start.8) | collective-permute-done | bytes 163872 | tf_op jit(solution)/shard_map/ppermute | solution.py:525
  75.8 1.1 pick_blocks.12
  77.0 1.5 collective-permute-start.18
  78.7 4.1 %exchange_chunks.4.refs_4_.rest_4_ = f32[8,256,256]{2,1,0:T(8,128)S(1)} custom-call(s32[16]{0:T(128)S(1)} %multiply_add_fusion.slot_ref, s32[1]{0:T(128)} %bitcast.fit_ref, bf16[2,1024,256]{2,1,0:T(8,128)(2,1)S(1)} %pick_blocks.7.rest_0_.rest_1_.mine_ref, bf16[2,1024,256]{2,1,0:T(8,128)(2,1)S(1)} %collective-permute-done.rest_1_.rest_2_, ...), custom_call_target="tpu_custom_call" | custom-call | flops 26843545600 | bytes 314572800 | tf_op jit(solution)/shard_map/exchange_chunks/pallas_call | solution.py:187
  84.1 2.2 collective-permute-start.15
  87.5 3.2 %exchange_chunks.5.refs_4_.rest_4_ = f32[8,256,256]{2,1,0:T(8,128)S(1)} custom-call(s32[16]{0:T(128)S(1)} %multiply_add_fusion.slot_ref, s32[1]{0:T(128)} %bitcast.fit_ref, bf16[2,1024,256]{2,1,0:T(8,128)(2,1)S(1)} %pick_blocks.7.rest_0_.rest_1_.mine_ref, bf16[2,1024,256]{2,1,0:T(8,128)(2,1)S(1)} %collective-permute-done.rest_1_.rest_2_, ...), custom_call_target="tpu_custom_call" | custom-call | flops 21810380800 | bytes 294912000 | tf_op jit(solution)/shard_map/exchange_chunks/pallas_call | solution.py:187
  90.7 1.1 pick_blocks.13
  91.9 1.9 collective-permute-start.23
  93.8 1.1 collective-permute-done.15.refs_2_
  94.9 2.2 collective-permute-start.24
  97.1 1.2 collective-permute-done.13.refs_0_
  99.0 3.1 %exchange_chunks.6.refs_3_.rest_5_ = f32[8,256,256]{2,1,0:T(8,128)S(1)} custom-call(s32[16]{0:T(128)S(1)} %multiply_add_fusion.slot_ref, s32[1]{0:T(128)} %bitcast.fit_ref, bf16[2,1024,256]{2,1,0:T(8,128)(2,1)S(1)} %pick_blocks.7.rest_0_.rest_1_.mine_ref, bf16[2,1024,256]{2,1,0:T(8,128)(2,1)S(1)} %collective-permute-done.rest_1_.rest_2_, ...), custom_call_target="tpu_custom_call" | custom-call | flops 16777216000 | bytes 275251200 | tf_op jit(solution)/shard_map/exchange_chunks/pallas_call | solution.py:187
  102.1 3.8 %collective-permute-done.24.refs_2_ = bf16[2,128,256]{2,1,0:T(8,128)(2,1)S(1)} collective-permute-done((bf16[2,128,256]{2,1,0:T(8,128)(2,1)S(1)}, bf16[2,128,256]{2,1,0:T(8,128)(2,1)S(1)}, u32[]{:S(2)}, u32[]{:S(2)}) %collective-permute-start.24) | collective-permute-done | bytes 131104 | tf_op jit(solution)/shard_map/ppermute | solution.py:525
  105.8 2.4 %collective-permute-done.22.refs_0_ = bf16[2,128,256]{2,1,0:T(8,128)(2,1)S(1)} collective-permute-done((bf16[2,128,256]{2,1,0:T(8,128)(2,1)S(1)}, bf16[2,128,256]{2,1,0:T(8,128)(2,1)S(1)}, u32[]{:S(2)}, u32[]{:S(2)}) %collective-permute-start.22) | collective-permute-done | bytes 131104 | tf_op jit(solution)/shard_map/ppermute | solution.py:525
  108.8 3.0 %exchange_chunks.7.rest_6_ = f32[8,256,256]{2,1,0:T(8,128)S(1)} custom-call(s32[16]{0:T(128)S(1)} %multiply_add_fusion.slot_ref, s32[1]{0:T(128)} %bitcast.fit_ref, bf16[6,128,256]{2,1,0:T(8,128)(2,1)S(1)} %merge_chunk.11.rest_0_.rest_4_, bf16[2,1024,256]{2,1,0:T(8,128)(2,1)S(1)} %pick_blocks.7.rest_0_.rest_1_.mine_ref, ...), custom_call_target="tpu_custom_call" | custom-call | flops 15099494400 | bytes 268697600 | tf_op jit(solution)/shard_map/exchange_chunks/pallas_call | solution.py:187
  111.9 6.9 %collective-permute-done.26.rest_5_ = bf16[6,128,256]{2,1,0:T(8,128)(2,1)S(1)} collective-permute-done((bf16[6,128,256]{2,1,0:T(8,128)(2,1)S(1)}, bf16[6,128,256]{2,1,0:T(8,128)(2,1)S(1)}, u32[]{:S(2)}, u32[]{:S(2)}) %collective-permute-start.26) | collective-permute-done | bytes 393248 | tf_op jit(solution)/shard_map/ppermute | solution.py:463
  118.7 5.8 %middle_step.1 = (bf16[8,256,256]{2,1,0:T(8,128)(2,1)}, bf16[16,256,256]{2,1,0:T(8,128)(2,1)S(1)}, bf16[2,128,256]{2,1,0:T(8,128)(2,1)S(1)}, bf16[2,128,256]{2,1...) custom-call(s32[16]{0:T(128)S(1)} %multiply_add_fusion.slot_ref, ...), custom_call_target="tpu_custom_call" | custom-call | flops 2147483648 | bytes 8388608 | tf_op jit(solution)/shard_map/middle_step/pallas_call | solution.py:295
  124.6 1.2 collective-permute-start.32
  125.8 1.8 collective-permute-start.33
  127.6 2.9 %gradient_chunk.5 = (bf16[2,224,256]{2,1,0:T(8,128)(2,1)S(1)}, bf16[2,224,256]{2,1,0:T(8,128)(2,1)S(1)}, bf16[2,224,256]{2,1,0:T(8,128)(2,1)S(1)}, bf16[2,224,256]{2,1,0:T(8,128)(2,1)S(1)}) custom-call(s32[16]{0:T(128)S(1)} %multiply_add_fusion.slot_ref, bf16[16,256,256]{2,1,0:T(8,128)(2,1)S(1)} %get-tuple-element.65.weight_ref, ...), custom_call_target="tpu_custom_call" | custom-call | flops 469762048 | bytes 3932160 | tf_op jit(solution)/shard_map/gradient_chunk/pallas_call | solution.py:353
  130.5 1.5 collective-permute-start.36
  132.5 1.6 collective-permute-start.34
  134.1 3.0 %gradient_chunk.6 = (bf16[2,224,256]{2,1,0:T(8,128)(2,1)S(1)}, bf16[2,224,256]{2,1,0:T(8,128)(2,1)S(1)}, bf16[2,224,256]{2,1,0:T(8,128)(2,1)S(1)}, bf16[2,224,256]{2,1,0:T(8,128)(2,1)S(1)}) custom-call(s32[16]{0:T(128)S(1)} %multiply_add_fusion.slot_ref, bf16[16,256,256]{2,1,0:T(8,128)(2,1)S(1)} %get-tuple-element.65.weight_ref, ...), custom_call_target="tpu_custom_call" | custom-call | flops 469762048 | bytes 3932160 | tf_op jit(solution)/shard_map/gradient_chunk/pallas_call | solution.py:353
  137.1 5.7 %collective-permute-start.38 = (bf16[2,224,256]{2,1,0:T(8,128)(2,1)S(1)}, bf16[2,224,256]{2,1,0:T(8,128)(2,1)S(1)}, u32[]{:S(2)}, u32[]{:S(2)}) collective-permute-start(bf16[2,224,256]{2,1,0:T(8,128)(2,1)S(1)} %get-tuple-element.79), channel_id=1, source_target_pairs={{0,4},{4,8},{8,12},{12,0},{1,5},{5,9},{9,13},{13,1},{2,6},{6,10},{... | collective-permute-start | bytes 688136 | tf_op jit(solution)/shard_map/ppermute | solution.py:559
  142.8 20.7 %collective-permute-done.34.rest_3_ = bf16[2,128,256]{2,1,0:T(8,128)(2,1)S(1)} collective-permute-done((bf16[2,128,256]{2,1,0:T(8,128)(2,1)S(1)}, bf16[2,128,256]{2,1,0:T(8,128)(2,1)S(1)}, u32[]{:S(2)}, u32[]{:S(2)}) %collective-permute-start.34) | collective-permute-done | bytes 131104 | tf_op jit(solution)/shard_map/ppermute | solution.py:559
  163.6 1.2 settle_chunks.5.rest_4_.refs_0_
  164.8 1.4 collective-permute-start.44
  166.2 3.0 %gradient_chunk.4 = (bf16[2,240,256]{2,1,0:T(8,128)(2,1)S(1)}, bf16[2,240,256]{2,1,0:T(8,128)(2,1)S(1)}, bf16[2,240,256]{2,1,0:T(8,128)(2,1)S(1)}, bf16[2,240,256]{2,1,0:T(8,128)(2,1)S(1)}) custom-call(s32[16]{0:T(128)S(1)} %multiply_add_fusion.slot_ref, bf16[16,256,256]{2,1,0:T(8,128)(2,1)S(1)} %get-tuple-element.65.weight_ref, ...), custom_call_target="tpu_custom_call" | custom-call | flops 503316480 | bytes 4063232 | tf_op jit(solution)/shard_map/gradient_chunk/pallas_call | solution.py:353
  169.2 2.8 %collective-permute-start.29 = (bf16[2,240,256]{2,1,0:T(8,128)(2,1)S(1)}, bf16[2,240,256]{2,1,0:T(8,128)(2,1)S(1)}, u32[]{:S(2)}, u32[]{:S(2)}) collective-permute-start(bf16[2,240,256]{2,1,0:T(8,128)(2,1)S(1)} %get-tuple-element.68), channel_id=1, source_target_pairs={{0,8},{4,12},{8,0},{12,4},{1,9},{5,13},{9,1},{13,5},{2,10},{6,14},... | collective-permute-start | bytes 737288 | tf_op jit(solution)/shard_map/ppermute | solution.py:559
  172.0 1.3 collective-permute-start.30
  174.0 2.9 %gradient_chunk.7 = (bf16[2,208,256]{2,1,0:T(8,128)(2,1)S(1)}, bf16[2,208,256]{2,1,0:T(8,128)(2,1)S(1)}, bf16[2,208,256]{2,1,0:T(8,128)(2,1)S(1)}, bf16[2,208,256]{2,1,0:T(8,128)(2,1)S(1)}) custom-call(s32[16]{0:T(128)S(1)} %multiply_add_fusion.slot_ref, bf16[16,256,256]{2,1,0:T(8,128)(2,1)S(1)} %get-tuple-element.65.weight_ref, ...), custom_call_target="tpu_custom_call" | custom-call | flops 436207616 | bytes 3801088 | tf_op jit(solution)/shard_map/gradient_chunk/pallas_call | solution.py:353
  176.9 17.5 %collective-permute-done.28.rest_1_ = bf16[2,240,256]{2,1,0:T(8,128)(2,1)S(1)} collective-permute-done((bf16[2,240,256]{2,1,0:T(8,128)(2,1)S(1)}, bf16[2,240,256]{2,1,0:T(8,128)(2,1)S(1)}, u32[]{:S(2)}, u32[]{:S(2)}) %collective-permute-start.28) | collective-permute-done | bytes 245792 | tf_op jit(solution)/shard_map/ppermute | solution.py:559
  194.4 2.2 collective-permute-start.41
  196.6 3.1 %collective-permute-done.29.rest_2_ = bf16[2,240,256]{2,1,0:T(8,128)(2,1)S(1)} collective-permute-done((bf16[2,240,256]{2,1,0:T(8,128)(2,1)S(1)}, bf16[2,240,256]{2,1,0:T(8,128)(2,1)S(1)}, u32[]{:S(2)}, u32[]{:S(2)}) %collective-permute-start.29) | collective-permute-done | bytes 245792 | tf_op jit(solution)/shard_map/ppermute | solution.py:559
  199.7 3.6 %collective-permute-start.42 = (bf16[2,208,256]{2,1,0:T(8,128)(2,1)S(1)}, bf16[2,208,256]{2,1,0:T(8,128)(2,1)S(1)}, u32[]{:S(2)}, u32[]{:S(2)}) collective-permute-start(bf16[2,208,256]{2,1,0:T(8,128)(2,1)S(1)} %get-tuple-element.84), channel_id=1, source_target_pairs={{0,8},{4,12},{8,0},{12,4},{1,9},{5,13},{9,1},{13,5},{2,10},{6,14},... | collective-permute-start | bytes 638984 | tf_op jit(solution)/shard_map/ppermute | solution.py:559
  203.3 1.0 settle_chunks.4.refs_0_
  204.3 5.5 %collective-permute-start.31 = (bf16[8,240,256]{2,1,0:T(8,128)(2,1)S(1)}, bf16[8,240,256]{2,1,0:T(8,128)(2,1)S(1)}, u32[]{:S(2)}, u32[]{:S(2)}) collective-permute-start(bf16[8,240,256]{2,1,0:T(8,128)(2,1)S(1)} %settle_chunks.4.refs_0_), channel_id=1, source_target_pairs={{0,1},{1,0},{2,3},{3,2},{4,5},{5,4},{6,7},{7,6},{8,9},{9,8},{10,11... | collective-permute-start | bytes 2949128 | tf_op jit(solution)/shard_map/ppermute | solution.py:569
  210.8 2.7 %collective-permute-done.41.rest_1_ = bf16[2,208,256]{2,1,0:T(8,128)(2,1)S(1)} collective-permute-done((bf16[2,208,256]{2,1,0:T(8,128)(2,1)S(1)}, bf16[2,208,256]{2,1,0:T(8,128)(2,1)S(1)}, u32[]{:S(2)}, u32[]{:S(2)}) %collective-permute-start.41) | collective-permute-done | bytes 213024 | tf_op jit(solution)/shard_map/ppermute | solution.py:559
  214.3 3.6 %collective-permute-done.42.rest_2_ = bf16[2,208,256]{2,1,0:T(8,128)(2,1)S(1)} collective-permute-done((bf16[2,208,256]{2,1,0:T(8,128)(2,1)S(1)}, bf16[2,208,256]{2,1,0:T(8,128)(2,1)S(1)}, u32[]{:S(2)}, u32[]{:S(2)}) %collective-permute-start.42) | collective-permute-done | bytes 213024 | tf_op jit(solution)/shard_map/ppermute | solution.py:559
  218.9 1.0 collective-permute-start.46
  219.9 2.0 collective-permute-done.46.refs_5_
  221.9 3.0 %add_chunks.2.refs_2_ = f32[8,1024,256]{2,1,0:T(8,128)} custom-call(bf16[8,352,256]{2,1,0:T(8,128)(2,1)S(1)} %settle_chunks.5.rest_4_.refs_0_, bf16[8,224,256]{2,1,0:T(8,128)(2,1)S(1)} %settle_chunks.6.rest_4_.refs_1_, bf16[8,208,256]{2,1,0:T(8,128)(2,1)S(1)} %settle_chunks.7.refs_2_, bf16[8,352,256]{2,1,0:T(8,128)(2,1)S(1)} %collective-permute-done.44.refs_3_, ...), custom_call_target="tpu_custom_call" | custom-call | bytes 12845056 | tf_op jit(solution)/shard_map/add_chunks/pallas_call | solution.py:433
  224.9 1.4 add_chunks.3
  (103 shorter events, 14.8 us)
Async XLA Ops:
  3.0 5.6 %collective-permute-start.1 = (f32[10]{0:T(128)S(1)}, f32[10]{0:T(128)S(1)}, u32[]{:S(2)}, u32[]{:S(2)}) collective-permute-start(f32[10]{0:T(128)S(1)} %get-tuple-element.89), channel_id=1, source_target_pairs={{0,4},{4,8},{8,12},{12,0},{1,5},{5,9},{9,13},{13,1},{2,6},{6,10},{... | collective-permute-start | bytes 128 | tf_op jit(solution)/shard_map/ppermute | solution.py:496
  4.3 4.4 %collective-permute-start.2 = (f32[10]{0:T(128)S(1)}, f32[10]{0:T(128)S(1)}, u32[]{:S(2)}, u32[]{:S(2)}) collective-permute-start(f32[10]{0:T(128)S(1)} %get-tuple-element.90), channel_id=1, source_target_pairs={{0,8},{4,12},{8,0},{12,4},{1,9},{5,13},{9,1},{13,5},{2,10},{6,14},... | collective-permute-start | bytes 128 | tf_op jit(solution)/shard_map/ppermute | solution.py:496
  5.4 3.3 %collective-permute-start.3 = (f32[10]{0:T(128)S(1)}, f32[10]{0:T(128)S(1)}, u32[]{:S(2)}, u32[]{:S(2)}) collective-permute-start(f32[10]{0:T(128)S(1)} %get-tuple-element.91), channel_id=1, source_target_pairs={{0,12},{4,0},{8,4},{12,8},{1,13},{5,1},{9,5},{13,9},{2,14},{6,2},{... | collective-permute-start | bytes 128 | tf_op jit(solution)/shard_map/ppermute | solution.py:496
  8.7 7.9 %copy-start = (bf16[8,1024,256]{2,1,0:T(8,128)(2,1)S(1)}, bf16[8,1024,256]{2,1,0:T(8,128)(2,1)}, u32[]{:S(2)}) copy-start(bf16[8,1024,256]{2,1,0:T(8,128)(2,1)} %blocks_ref.13) | copy-start | bytes 12582916
  10.8 28.9 %collective-permute-start.4 = (bf16[2,256,256]{2,1,0:T(8,128)(2,1)S(1)}, bf16[2,256,256]{2,1,0:T(8,128)(2,1)S(1)}, u32[]{:S(2)}, u32[]{:S(2)}) collective-permute-start(bf16[2,256,256]{2,1,0:T(8,128)(2,1)S(1)} %get-tuple-element.44), channel_id=1, source_target_pairs={{0,12},{4,0},{8,4},{12,8},{1,13},{5,1},{9,5},{13,9},{2,14},{6,2},{... | collective-permute-start | bytes 786440 | tf_op jit(solution)/shard_map/ppermute | solution.py:525
  12.0 27.8 %collective-permute-start.5 = (bf16[2,256,256]{2,1,0:T(8,128)(2,1)S(1)}, bf16[2,256,256]{2,1,0:T(8,128)(2,1)S(1)}, u32[]{:S(2)}, u32[]{:S(2)}) collective-permute-start(bf16[2,256,256]{2,1,0:T(8,128)(2,1)S(1)} %get-tuple-element.45), channel_id=1, source_target_pairs={{0,8},{4,12},{8,0},{12,4},{1,9},{5,13},{9,1},{13,5},{2,10},{6,14},... | collective-permute-start | bytes 786440 | tf_op jit(solution)/shard_map/ppermute | solution.py:525
  13.1 5.3 %copy-start.5 = (f32[8,256,256]{2,1,0:T(8,128)S(1)}, f32[8,256,256]{2,1,0:T(8,128)}, u32[]{:S(2)}) copy-start(f32[8,256,256]{2,1,0:T(8,128)} %fock_ref.1) | copy-start | bytes 6291460
  13.1 5.3 %copy-start.8 = (s32[8]{0:T(128)S(1)}, s32[8]{0:T(128)}, u32[]{:S(2)}) copy-start(s32[8]{0:T(128)} %size_ref.1) | copy-start | bytes 100
  13.1 26.6 %collective-permute-start.6 = (bf16[2,256,256]{2,1,0:T(8,128)(2,1)S(1)}, bf16[2,256,256]{2,1,0:T(8,128)(2,1)S(1)}, u32[]{:S(2)}, u32[]{:S(2)}) collective-permute-start(bf16[2,256,256]{2,1,0:T(8,128)(2,1)S(1)} %get-tuple-element.46), channel_id=1, source_target_pairs={{0,4},{4,8},{8,12},{12,0},{1,5},{5,9},{9,13},{13,1},{2,6},{6,10},{... | collective-permute-start | bytes 786440 | tf_op jit(solution)/shard_map/ppermute | solution.py:525
  15.4 61.6 %collective-permute-start = (bf16[2,1024,256]{2,1,0:T(8,128)(2,1)S(1)}, bf16[2,1024,256]{2,1,0:T(8,128)(2,1)S(1)}, u32[]{:S(2)}, u32[]{:S(2)}) collective-permute-start(bf16[2,1024,256]{2,1,0:T(8,128)(2,1)S(1)} %pick_blocks.7.rest_0_.rest_1_.mine_ref), channel_id=1, source_target_pairs={{0,2},{2,0},{1,3},{3,1},{4,6},{6,4},{5,7},{7,5},{8,10},{10,8},{9,1... | collective-permute-start | bytes 3145736 | tf_op jit(solution)/shard_map/ppermute | solution.py:463
  18.0 21.7 %collective-permute-start.7 = (bf16[2,208,256]{2,1,0:T(8,128)(2,1)S(1)}, bf16[2,208,256]{2,1,0:T(8,128)(2,1)S(1)}, u32[]{:S(2)}, u32[]{:S(2)}) collective-permute-start(bf16[2,208,256]{2,1,0:T(8,128)(2,1)S(1)} %get-tuple-element.49), channel_id=1, source_target_pairs={{0,4},{4,8},{8,12},{12,0},{1,5},{5,9},{9,13},{13,1},{2,6},{6,10},{... | collective-permute-start | bytes 638984 | tf_op jit(solution)/shard_map/ppermute | solution.py:525
  20.1 1.0 copy-start.6
  39.8 1.3 copy-start.3
  41.1 37.3 %collective-permute-start.19 = (bf16[6,256,256]{2,1,0:T(8,128)(2,1)S(1)}, bf16[6,256,256]{2,1,0:T(8,128)(2,1)}, u32[]{:S(2)}, u32[]{:S(2)}) collective-permute-start(bf16[6,256,256]{2,1,0:T(8,128)(2,1)S(1)} %merge_chunk.6.rest_0_.rest_2_), channel_id=1, source_target_pairs={{0,2},{2,0},{1,3},{3,1},{4,6},{6,4},{5,7},{7,5},{8,10},{10,8},{9,1... | collective-permute-start | bytes 2359304 | tf_op jit(solution)/shard_map/ppermute | solution.py:463
  42.4 8.3 %collective-permute-start.12 = (bf16[2,208,256]{2,1,0:T(8,128)(2,1)}, bf16[2,208,256]{2,1,0:T(8,128)(2,1)S(1)}, u32[]{:S(2)}, u32[]{:S(2)}) collective-permute-start(bf16[2,208,256]{2,1,0:T(8,128)(2,1)} %get-tuple-element.53), channel_id=1, source_target_pairs={{0,8},{4,12},{8,0},{12,4},{1,9},{5,13},{9,1},{13,5},{2,10},{6,14},... | collective-permute-start | bytes 638984 | tf_op jit(solution)/shard_map/ppermute | solution.py:525
  42.4 22.4 %collective-permute-start.11 = (bf16[2,208,256]{2,1,0:T(8,128)(2,1)}, bf16[2,208,256]{2,1,0:T(8,128)(2,1)S(1)}, u32[]{:S(2)}, u32[]{:S(2)}) collective-permute-start(bf16[2,208,256]{2,1,0:T(8,128)(2,1)} %get-tuple-element.47.refs_3_), channel_id=1, source_target_pairs={{0,12},{4,0},{8,4},{12,8},{1,13},{5,1},{9,5},{13,9},{2,14},{6,2},{... | collective-permute-start | bytes 638984 | tf_op jit(solution)/shard_map/ppermute | solution.py:525
  47.1 2.2 copy-start.1
  49.2 16.4 %copy-start.2 = (bf16[8,1024,256]{2,1,0:T(8,128)(2,1)S(1)}, bf16[8,1024,256]{2,1,0:T(8,128)(2,1)}, u32[]{:S(2)}) copy-start(bf16[8,1024,256]{2,1,0:T(8,128)(2,1)} %blocks_ref.13) | copy-start | bytes 12582916
  50.5 16.3 %collective-permute-start.9 = (bf16[2,160,256]{2,1,0:T(8,128)(2,1)S(1)}, bf16[2,160,256]{2,1,0:T(8,128)(2,1)S(1)}, u32[]{:S(2)}, u32[]{:S(2)}) collective-permute-start(bf16[2,160,256]{2,1,0:T(8,128)(2,1)S(1)} %get-tuple-element.51), channel_id=1, source_target_pairs={{0,8},{4,12},{8,0},{12,4},{1,9},{5,13},{9,1},{13,5},{2,10},{6,14},... | collective-permute-start | bytes 491528 | tf_op jit(solution)/shard_map/ppermute | solution.py:525
  50.6 17.1 %collective-permute-start.10 = (bf16[2,160,256]{2,1,0:T(8,128)(2,1)S(1)}, bf16[2,160,256]{2,1,0:T(8,128)(2,1)S(1)}, u32[]{:S(2)}, u32[]{:S(2)}) collective-permute-start(bf16[2,160,256]{2,1,0:T(8,128)(2,1)S(1)} %get-tuple-element.52), channel_id=1, source_target_pairs={{0,4},{4,8},{8,12},{12,0},{1,5},{5,9},{9,13},{13,1},{2,6},{6,10},{... | collective-permute-start | bytes 491528 | tf_op jit(solution)/shard_map/ppermute | solution.py:525
  64.8 10.4 %collective-permute-start.8 = (bf16[2,160,256]{2,1,0:T(8,128)(2,1)S(1)}, bf16[2,160,256]{2,1,0:T(8,128)(2,1)S(1)}, u32[]{:S(2)}, u32[]{:S(2)}) collective-permute-start(bf16[2,160,256]{2,1,0:T(8,128)(2,1)S(1)} %get-tuple-element.50.refs_3_), channel_id=1, source_target_pairs={{0,12},{4,0},{8,4},{12,8},{1,13},{5,1},{9,5},{13,9},{2,14},{6,2},{... | collective-permute-start | bytes 491528 | tf_op jit(solution)/shard_map/ppermute | solution.py:525
  66.9 20.1 %collective-permute-start.20 = (bf16[6,208,256]{2,1,0:T(8,128)(2,1)S(1)}, bf16[6,208,256]{2,1,0:T(8,128)(2,1)S(1)}, u32[]{:S(2)}, u32[]{:S(2)}) collective-permute-start(bf16[6,208,256]{2,1,0:T(8,128)(2,1)S(1)} %merge_chunk.7.rest_0_.rest_2_.rest_1_), channel_id=1, source_target_pairs={{0,2},{2,0},{1,3},{3,1},{4,6},{6,4},{5,7},{7,5},{8,10},{10,8},{9,1... | collective-permute-start | bytes 1916936 | tf_op jit(solution)/shard_map/ppermute | solution.py:463
  67.8 15.0 %collective-permute-start.17 = (bf16[2,144,256]{2,1,0:T(8,128)(2,1)S(1)}, bf16[2,144,256]{2,1,0:T(8,128)(2,1)S(1)}, u32[]{:S(2)}, u32[]{:S(2)}) collective-permute-start(bf16[2,144,256]{2,1,0:T(8,128)(2,1)S(1)} %get-tuple-element.58), channel_id=1, source_target_pairs={{0,8},{4,12},{8,0},{12,4},{1,9},{5,13},{9,1},{13,5},{2,10},{6,14},... | collective-permute-start | bytes 442376 | tf_op jit(solution)/shard_map/ppermute | solution.py:525
  75.2 11.2 %collective-permute-start.16 = (bf16[2,144,256]{2,1,0:T(8,128)(2,1)S(1)}, bf16[2,144,256]{2,1,0:T(8,128)(2,1)S(1)}, u32[]{:S(2)}, u32[]{:S(2)}) collective-permute-start(bf16[2,144,256]{2,1,0:T(8,128)(2,1)S(1)} %get-tuple-element.54.refs_3_), channel_id=1, source_target_pairs={{0,12},{4,0},{8,4},{12,8},{1,13},{5,1},{9,5},{13,9},{2,14},{6,2},{... | collective-permute-start | bytes 442376 | tf_op jit(solution)/shard_map/ppermute | solution.py:525
  77.0 7.2 %collective-permute-start.18 = (bf16[2,144,256]{2,1,0:T(8,128)(2,1)S(1)}, bf16[2,144,256]{2,1,0:T(8,128)(2,1)S(1)}, u32[]{:S(2)}, u32[]{:S(2)}) collective-permute-start(bf16[2,144,256]{2,1,0:T(8,128)(2,1)S(1)} %get-tuple-element.59), channel_id=1, source_target_pairs={{0,4},{4,8},{8,12},{12,0},{1,5},{5,9},{9,13},{13,1},{2,6},{6,10},{... | collective-permute-start | bytes 442376 | tf_op jit(solution)/shard_map/ppermute | solution.py:525
  78.5 20.4 %collective-permute-start.25 = (bf16[6,160,256]{2,1,0:T(8,128)(2,1)S(1)}, bf16[6,160,256]{2,1,0:T(8,128)(2,1)S(1)}, u32[]{:S(2)}, u32[]{:S(2)}) collective-permute-start(bf16[6,160,256]{2,1,0:T(8,128)(2,1)S(1)} %merge_chunk.8.rest_0_.rest_2_.rest_1_), channel_id=1, source_target_pairs={{0,2},{2,0},{1,3},{3,1},{4,6},{6,4},{5,7},{7,5},{8,10},{10,8},{9,1... | collective-permute-start | bytes 1474568 | tf_op jit(solution)/shard_map/ppermute | solution.py:463
  82.8 9.1 %collective-permute-start.14 = (bf16[2,128,256]{2,1,0:T(8,128)(2,1)S(1)}, bf16[2,128,256]{2,1,0:T(8,128)(2,1)S(1)}, u32[]{:S(2)}, u32[]{:S(2)}) collective-permute-start(bf16[2,128,256]{2,1,0:T(8,128)(2,1)S(1)} %get-tuple-element.56), channel_id=1, source_target_pairs={{0,8},{4,12},{8,0},{12,4},{1,9},{5,13},{9,1},{13,5},{2,10},{6,14},... | collective-permute-start | bytes 393224 | tf_op jit(solution)/shard_map/ppermute | solution.py:525
  84.1 10.8 %collective-permute-start.15 = (bf16[2,128,256]{2,1,0:T(8,128)(2,1)S(1)}, bf16[2,128,256]{2,1,0:T(8,128)(2,1)S(1)}, u32[]{:S(2)}, u32[]{:S(2)}) collective-permute-start(bf16[2,128,256]{2,1,0:T(8,128)(2,1)S(1)} %get-tuple-element.57), channel_id=1, source_target_pairs={{0,4},{4,8},{8,12},{12,0},{1,5},{5,9},{9,13},{13,1},{2,6},{6,10},{... | collective-permute-start | bytes 393224 | tf_op jit(solution)/shard_map/ppermute | solution.py:525
  86.3 12.0 %collective-permute-start.13 = (bf16[2,128,256]{2,1,0:T(8,128)(2,1)S(1)}, bf16[2,128,256]{2,1,0:T(8,128)(2,1)S(1)}, u32[]{:S(2)}, u32[]{:S(2)}) collective-permute-start(bf16[2,128,256]{2,1,0:T(8,128)(2,1)S(1)} %get-tuple-element.55.refs_3_), channel_id=1, source_target_pairs={{0,12},{4,0},{8,4},{12,8},{1,13},{5,1},{9,5},{13,9},{2,14},{6,2},{... | collective-permute-start | bytes 393224 | tf_op jit(solution)/shard_map/ppermute | solution.py:525
  87.0 21.9 %collective-permute-start.27 = (bf16[6,144,256]{2,1,0:T(8,128)(2,1)S(1)}, bf16[6,144,256]{2,1,0:T(8,128)(2,1)S(1)}, u32[]{:S(2)}, u32[]{:S(2)}) collective-permute-start(bf16[6,144,256]{2,1,0:T(8,128)(2,1)S(1)} %merge_chunk.9.rest_0_.rest_3_.rest_2_), channel_id=1, source_target_pairs={{0,2},{2,0},{1,3},{3,1},{4,6},{6,4},{5,7},{7,5},{8,10},{10,8},{9,1... | collective-permute-start | bytes 1327112 | tf_op jit(solution)/shard_map/ppermute | solution.py:463
  91.9 10.2 %collective-permute-start.23 = (bf16[2,128,256]{2,1,0:T(8,128)(2,1)S(1)}, bf16[2,128,256]{2,1,0:T(8,128)(2,1)S(1)}, u32[]{:S(2)}, u32[]{:S(2)}) collective-permute-start(bf16[2,128,256]{2,1,0:T(8,128)(2,1)S(1)} %get-tuple-element.61), channel_id=1, source_target_pairs={{0,8},{4,12},{8,0},{12,4},{1,9},{5,13},{9,1},{13,5},{2,10},{6,14},... | collective-permute-start | bytes 393224 | tf_op jit(solution)/shard_map/ppermute | solution.py:525
  94.9 10.9 %collective-permute-start.24 = (bf16[2,128,256]{2,1,0:T(8,128)(2,1)S(1)}, bf16[2,128,256]{2,1,0:T(8,128)(2,1)S(1)}, u32[]{:S(2)}, u32[]{:S(2)}) collective-permute-start(bf16[2,128,256]{2,1,0:T(8,128)(2,1)S(1)} %get-tuple-element.62), channel_id=1, source_target_pairs={{0,4},{4,8},{8,12},{12,0},{1,5},{5,9},{9,13},{13,1},{2,6},{6,10},{... | collective-permute-start | bytes 393224 | tf_op jit(solution)/shard_map/ppermute | solution.py:525
  98.4 9.8 %collective-permute-start.22 = (bf16[2,128,256]{2,1,0:T(8,128)(2,1)S(1)}, bf16[2,128,256]{2,1,0:T(8,128)(2,1)S(1)}, u32[]{:S(2)}, u32[]{:S(2)}) collective-permute-start(bf16[2,128,256]{2,1,0:T(8,128)(2,1)S(1)} %get-tuple-element.60.refs_3_), channel_id=1, source_target_pairs={{0,12},{4,0},{8,4},{12,8},{1,13},{5,1},{9,5},{13,9},{2,14},{6,2},{... | collective-permute-start | bytes 393224 | tf_op jit(solution)/shard_map/ppermute | solution.py:525
  98.9 12.9 %collective-permute-start.21 = (bf16[6,128,256]{2,1,0:T(8,128)(2,1)S(1)}, bf16[6,128,256]{2,1,0:T(8,128)(2,1)S(1)}, u32[]{:S(2)}, u32[]{:S(2)}) collective-permute-start(bf16[6,128,256]{2,1,0:T(8,128)(2,1)S(1)} %merge_chunk.10.rest_2_.rest_1_), channel_id=1, source_target_pairs={{0,2},{2,0},{1,3},{3,1},{4,6},{6,4},{5,7},{7,5},{8,10},{10,8},{9,1... | collective-permute-start | bytes 1179656 | tf_op jit(solution)/shard_map/ppermute | solution.py:463
  108.7 10.0 %copy-start.4 = (f32[8,256,256]{2,1,0:T(8,128)S(1)}, f32[8,256,256]{2,1,0:T(8,128)}, u32[]{:S(2)}) copy-start(f32[8,256,256]{2,1,0:T(8,128)} %copy-done.3) | copy-start | bytes 6291460
  108.7 10.0 %copy-start.7 = (bf16[8,256,256]{2,1,0:T(8,128)(2,1)S(1)}, bf16[8,256,256]{2,1,0:T(8,128)(2,1)}, u32[]{:S(2)}) copy-start(bf16[8,256,256]{2,1,0:T(8,128)(2,1)} %copy-done.6) | copy-start | bytes 3145732
  108.7 10.0 %collective-permute-start.26 = (bf16[6,128,256]{2,1,0:T(8,128)(2,1)S(1)}, bf16[6,128,256]{2,1,0:T(8,128)(2,1)S(1)}, u32[]{:S(2)}, u32[]{:S(2)}) collective-permute-start(bf16[6,128,256]{2,1,0:T(8,128)(2,1)S(1)} %merge_chunk.11.rest_0_.rest_4_), channel_id=1, source_target_pairs={{0,2},{2,0},{1,3},{3,1},{4,6},{6,4},{5,7},{7,5},{8,10},{10,8},{9,1... | collective-permute-start | bytes 1179656 | tf_op jit(solution)/shard_map/ppermute | solution.py:463
  124.6 8.0 %collective-permute-start.32 = (bf16[2,128,256]{2,1,0:T(8,128)(2,1)S(1)}, bf16[2,128,256]{2,1,0:T(8,128)(2,1)S(1)}, u32[]{:S(2)}, u32[]{:S(2)}) collective-permute-start(bf16[2,128,256]{2,1,0:T(8,128)(2,1)S(1)} %get-tuple-element.71), channel_id=1, source_target_pairs={{0,4},{4,8},{8,12},{12,0},{1,5},{5,9},{9,13},{13,1},{2,6},{6,10},{... | collective-permute-start | bytes 393224 | tf_op jit(solution)/shard_map/ppermute | solution.py:559
  125.8 11.3 %collective-permute-start.33 = (bf16[2,128,256]{2,1,0:T(8,128)(2,1)S(1)}, bf16[2,128,256]{2,1,0:T(8,128)(2,1)S(1)}, u32[]{:S(2)}, u32[]{:S(2)}) collective-permute-start(bf16[2,128,256]{2,1,0:T(8,128)(2,1)S(1)} %get-tuple-element.72), channel_id=1, source_target_pairs={{0,8},{4,12},{8,0},{12,4},{1,9},{5,13},{9,1},{13,5},{2,10},{6,14},... | collective-permute-start | bytes 393224 | tf_op jit(solution)/shard_map/ppermute | solution.py:559
  130.5 33.1 %collective-permute-start.35 = (bf16[2,224,256]{2,1,0:T(8,128)(2,1)S(1)}, bf16[2,224,256]{2,1,0:T(8,128)(2,1)S(1)}, u32[]{:S(2)}, u32[]{:S(2)}) collective-permute-start(bf16[2,224,256]{2,1,0:T(8,128)(2,1)S(1)} %get-tuple-element.75), channel_id=1, source_target_pairs={{0,4},{4,8},{8,12},{12,0},{1,5},{5,9},{9,13},{13,1},{2,6},{6,10},{... | collective-permute-start | bytes 688136 | tf_op jit(solution)/shard_map/ppermute | solution.py:559
  130.5 33.1 %collective-permute-start.36 = (bf16[2,224,256]{2,1,0:T(8,128)(2,1)S(1)}, bf16[2,224,256]{2,1,0:T(8,128)(2,1)S(1)}, u32[]{:S(2)}, u32[]{:S(2)}) collective-permute-start(bf16[2,224,256]{2,1,0:T(8,128)(2,1)S(1)} %get-tuple-element.76), channel_id=1, source_target_pairs={{0,8},{4,12},{8,0},{12,4},{1,9},{5,13},{9,1},{13,5},{2,10},{6,14},... | collective-permute-start | bytes 688136 | tf_op jit(solution)/shard_map/ppermute | solution.py:559
  132.1 31.5 %collective-permute-start.37 = (bf16[2,224,256]{2,1,0:T(8,128)(2,1)S(1)}, bf16[2,224,256]{2,1,0:T(8,128)(2,1)S(1)}, u32[]{:S(2)}, u32[]{:S(2)}) collective-permute-start(bf16[2,224,256]{2,1,0:T(8,128)(2,1)S(1)} %get-tuple-element.77), channel_id=1, source_target_pairs={{0,12},{4,0},{8,4},{12,8},{1,13},{5,1},{9,5},{13,9},{2,14},{6,2},{... | collective-permute-start | bytes 688136 | tf_op jit(solution)/shard_map/ppermute | solution.py:559
  132.5 31.0 %collective-permute-start.34 = (bf16[2,128,256]{2,1,0:T(8,128)(2,1)S(1)}, bf16[2,128,256]{2,1,0:T(8,128)(2,1)S(1)}, u32[]{:S(2)}, u32[]{:S(2)}) collective-permute-start(bf16[2,128,256]{2,1,0:T(8,128)(2,1)S(1)} %get-tuple-element.73), channel_id=1, source_target_pairs={{0,12},{4,0},{8,4},{12,8},{1,13},{5,1},{9,5},{13,9},{2,14},{6,2},{... | collective-permute-start | bytes 393224 | tf_op jit(solution)/shard_map/ppermute | solution.py:559
  137.1 34.9 %collective-permute-start.38 = (bf16[2,224,256]{2,1,0:T(8,128)(2,1)S(1)}, bf16[2,224,256]{2,1,0:T(8,128)(2,1)S(1)}, u32[]{:S(2)}, u32[]{:S(2)}) collective-permute-start(bf16[2,224,256]{2,1,0:T(8,128)(2,1)S(1)} %get-tuple-element.79), channel_id=1, source_target_pairs={{0,4},{4,8},{8,12},{12,0},{1,5},{5,9},{9,13},{13,1},{2,6},{6,10},{... | collective-permute-start | bytes 688136 | tf_op jit(solution)/shard_map/ppermute | solution.py:559
  163.6 10.1 %collective-permute-start.39 = (bf16[2,224,256]{2,1,0:T(8,128)(2,1)S(1)}, bf16[2,224,256]{2,1,0:T(8,128)(2,1)S(1)}, u32[]{:S(2)}, u32[]{:S(2)}) collective-permute-start(bf16[2,224,256]{2,1,0:T(8,128)(2,1)S(1)} %get-tuple-element.80), channel_id=1, source_target_pairs={{0,8},{4,12},{8,0},{12,4},{1,9},{5,13},{9,1},{13,5},{2,10},{6,14},... | collective-permute-start | bytes 688136 | tf_op jit(solution)/shard_map/ppermute | solution.py:559
  164.8 57.1 %collective-permute-start.44 = (bf16[8,352,256]{2,1,0:T(8,128)(2,1)S(1)}, bf16[8,352,256]{2,1,0:T(8,128)(2,1)S(1)}, u32[]{:S(2)}, u32[]{:S(2)}) collective-permute-start(bf16[8,352,256]{2,1,0:T(8,128)(2,1)S(1)} %settle_chunks.5.rest_4_.refs_0_), channel_id=1, source_target_pairs={{0,1},{1,0},{2,3},{3,2},{4,5},{5,4},{6,7},{7,6},{8,9},{9,8},{10,11... | collective-permute-start | bytes 4325384 | tf_op jit(solution)/shard_map/ppermute | solution.py:569
  169.2 25.2 %collective-permute-start.28 = (bf16[2,240,256]{2,1,0:T(8,128)(2,1)S(1)}, bf16[2,240,256]{2,1,0:T(8,128)(2,1)S(1)}, u32[]{:S(2)}, u32[]{:S(2)}) collective-permute-start(bf16[2,240,256]{2,1,0:T(8,128)(2,1)S(1)} %get-tuple-element.67), channel_id=1, source_target_pairs={{0,4},{4,8},{8,12},{12,0},{1,5},{5,9},{9,13},{13,1},{2,6},{6,10},{... | collective-permute-start | bytes 737288 | tf_op jit(solution)/shard_map/ppermute | solution.py:559
  169.2 30.5 %collective-permute-start.29 = (bf16[2,240,256]{2,1,0:T(8,128)(2,1)S(1)}, bf16[2,240,256]{2,1,0:T(8,128)(2,1)S(1)}, u32[]{:S(2)}, u32[]{:S(2)}) collective-permute-start(bf16[2,240,256]{2,1,0:T(8,128)(2,1)S(1)} %get-tuple-element.68), channel_id=1, source_target_pairs={{0,8},{4,12},{8,0},{12,4},{1,9},{5,13},{9,1},{13,5},{2,10},{6,14},... | collective-permute-start | bytes 737288 | tf_op jit(solution)/shard_map/ppermute | solution.py:559
  172.0 31.3 %collective-permute-start.30 = (bf16[2,240,256]{2,1,0:T(8,128)(2,1)S(1)}, bf16[2,240,256]{2,1,0:T(8,128)(2,1)S(1)}, u32[]{:S(2)}, u32[]{:S(2)}) collective-permute-start(bf16[2,240,256]{2,1,0:T(8,128)(2,1)S(1)} %get-tuple-element.69), channel_id=1, source_target_pairs={{0,12},{4,0},{8,4},{12,8},{1,13},{5,1},{9,5},{13,9},{2,14},{6,2},{... | collective-permute-start | bytes 737288 | tf_op jit(solution)/shard_map/ppermute | solution.py:559
  173.7 30.6 %collective-permute-start.40 = (bf16[2,224,256]{2,1,0:T(8,128)(2,1)S(1)}, bf16[2,224,256]{2,1,0:T(8,128)(2,1)S(1)}, u32[]{:S(2)}, u32[]{:S(2)}) collective-permute-start(bf16[2,224,256]{2,1,0:T(8,128)(2,1)S(1)} %get-tuple-element.81), channel_id=1, source_target_pairs={{0,12},{4,0},{8,4},{12,8},{1,13},{5,1},{9,5},{13,9},{2,14},{6,2},{... | collective-permute-start | bytes 688136 | tf_op jit(solution)/shard_map/ppermute | solution.py:559
  194.4 19.0 %collective-permute-start.41 = (bf16[2,208,256]{2,1,0:T(8,128)(2,1)S(1)}, bf16[2,208,256]{2,1,0:T(8,128)(2,1)S(1)}, u32[]{:S(2)}, u32[]{:S(2)}) collective-permute-start(bf16[2,208,256]{2,1,0:T(8,128)(2,1)S(1)} %get-tuple-element.83), channel_id=1, source_target_pairs={{0,4},{4,8},{8,12},{12,0},{1,5},{5,9},{9,13},{13,1},{2,6},{6,10},{... | collective-permute-start | bytes 638984 | tf_op jit(solution)/shard_map/ppermute | solution.py:559
  199.7 18.3 %collective-permute-start.42 = (bf16[2,208,256]{2,1,0:T(8,128)(2,1)S(1)}, bf16[2,208,256]{2,1,0:T(8,128)(2,1)S(1)}, u32[]{:S(2)}, u32[]{:S(2)}) collective-permute-start(bf16[2,208,256]{2,1,0:T(8,128)(2,1)S(1)} %get-tuple-element.84), channel_id=1, source_target_pairs={{0,8},{4,12},{8,0},{12,4},{1,9},{5,13},{9,1},{13,5},{2,10},{6,14},... | collective-permute-start | bytes 638984 | tf_op jit(solution)/shard_map/ppermute | solution.py:559
  203.3 14.7 %collective-permute-start.43 = (bf16[2,208,256]{2,1,0:T(8,128)(2,1)S(1)}, bf16[2,208,256]{2,1,0:T(8,128)(2,1)S(1)}, u32[]{:S(2)}, u32[]{:S(2)}) collective-permute-start(bf16[2,208,256]{2,1,0:T(8,128)(2,1)S(1)} %get-tuple-element.85), channel_id=1, source_target_pairs={{0,12},{4,0},{8,4},{12,8},{1,13},{5,1},{9,5},{13,9},{2,14},{6,2},{... | collective-permute-start | bytes 638984 | tf_op jit(solution)/shard_map/ppermute | solution.py:559
  204.3 20.6 %collective-permute-start.31 = (bf16[8,240,256]{2,1,0:T(8,128)(2,1)S(1)}, bf16[8,240,256]{2,1,0:T(8,128)(2,1)S(1)}, u32[]{:S(2)}, u32[]{:S(2)}) collective-permute-start(bf16[8,240,256]{2,1,0:T(8,128)(2,1)S(1)} %settle_chunks.4.refs_0_), channel_id=1, source_target_pairs={{0,1},{1,0},{2,3},{3,2},{4,5},{5,4},{6,7},{7,6},{8,9},{9,8},{10,11... | collective-permute-start | bytes 2949128 | tf_op jit(solution)/shard_map/ppermute | solution.py:569
  213.4 8.5 %collective-permute-start.45 = (bf16[8,224,256]{2,1,0:T(8,128)(2,1)S(1)}, bf16[8,224,256]{2,1,0:T(8,128)(2,1)S(1)}, u32[]{:S(2)}, u32[]{:S(2)}) collective-permute-start(bf16[8,224,256]{2,1,0:T(8,128)(2,1)S(1)} %settle_chunks.6.rest_4_.refs_1_), channel_id=1, source_target_pairs={{0,1},{1,0},{2,3},{3,2},{4,5},{5,4},{6,7},{7,6},{8,9},{9,8},{10,11... | collective-permute-start | bytes 2752520 | tf_op jit(solution)/shard_map/ppermute | solution.py:569
  218.9 3.0 %collective-permute-start.46 = (bf16[8,208,256]{2,1,0:T(8,128)(2,1)S(1)}, bf16[8,208,256]{2,1,0:T(8,128)(2,1)S(1)}, u32[]{:S(2)}, u32[]{:S(2)}) collective-permute-start(bf16[8,208,256]{2,1,0:T(8,128)(2,1)S(1)} %settle_chunks.7.refs_2_), channel_id=1, source_target_pairs={{0,1},{1,0},{2,3},{3,2},{4,5},{5,4},{6,7},{7,6},{8,9},{9,8},{10,11... | collective-permute-start | bytes 2555912 | tf_op jit(solution)/shard_map/ppermute | solution.py:569

commit v8 on v7

--- a/solution.py
+++ b/solution.py
@@ -16,7 +16,7 @@
 BACK_GROUPS = (2, 3, 4, 5)
 CHAIN_GRADIENTS = False
 SETTLE_FROM = 99
-UNROLL = 4
+UNROLL = 8
 PREPARE_AT = 1
 FIRST_WAITS = (2,)
 SETTLE_WEIGHT = 50

time: 227 us -> 227 us (level)
  no operation moved by 1% of the time
where the time goes in v8:
time: 227 us; the launch traced here: 226 us
  waiting for transfers between devices  103 us (45%)
  starting transfers between devices  59.1 us (26%)
  Pallas kernels  53.7 us (24%)
  local copies, waits for them, and re-layouts  5.61 us (2%)
  other arithmetic  2.98 us (1%)
    ppermute x15, waiting for transfers between devices, per_device(): lax.ppermute(sums[d], 'orb', shifted(n, d))  48.1 us
    ppermute x18, waiting for transfers between devices, per_device(): lax.ppermute(picked[d - 1], 'orb', shifted(n, n - d))  46.3 us
    ppermute x15, starting transfers between devices, per_device(): lax.ppermute(sums[d], 'orb', shifted(n, d))  22.7 us
    ppermute x18, starting transfers between devices, per_device(): lax.ppermute(picked[d - 1], 'orb', shifted(n, n - d))  20.2 us
    pallas_call x4, Pallas kernels, exchange_chunks(): pl.pallas_call(functools.partial(exchange_kernel, chunks, n_fit, first, l...  13.3 us
    pallas_call x4, Pallas kernels, gradient_chunk(): pl.pallas_call(functools.partial(gradient_kernel, parts, n), out_shape=[j...  11.7 us
    pallas_call x7, Pallas kernels, pick_blocks(): pl.pallas_call(functools.partial(pick_kernel, start, rows, len(after)), o...  10 us
    ppermute x4, starting transfers between devices, per_device(): waiting.append((group, here, lax.ppermute(here, 'rep', swap)))  8.77 us
  transfers between devices with their start and end apart: 47, of which 17 were waited for; matrix products, arithmetic and copies ran while one was open for 1% of the time, Pallas kernels for 20%

profile of v8, /device:TPU:9, one launch (start us, length us, event | category | flops | bytes accessed | tf_op | source)
XLA Modules:
  0.0 226.0 jit_solution(2216945179492940885)
XLA Ops:
  3.0 1.3 collective-permute-start.1
  4.3 1.1 collective-permute-start.2
  5.4 1.4 collective-permute-start.3
  6.9 1.8 pick_blocks.7.rest_0_.rest_1_.mine_ref
  8.7 2.1 pick_blocks.8
  10.8 1.1 collective-permute-start.4
  12.0 1.2 collective-permute-start.5
  13.1 2.3 %collective-permute-start.6 = (bf16[2,256,256]{2,1,0:T(8,128)(2,1)S(1)}, bf16[2,256,256]{2,1,0:T(8,128)(2,1)S(1)}, u32[]{:S(2)}, u32[]{:S(2)}) collective-permute-start(bf16[2,256,256]{2,1,0:T(8,128)(2,1)S(1)} %get-tuple-element.46), channel_id=1, source_target_pairs={{0,4},{4,8},{8,12},{12,0},{1,5},{5,9},{9,13},{13,1},{2,6},{6,10},{... | collective-permute-start | bytes 786440 | tf_op jit(solution)/shard_map/ppermute | solution.py:525
  15.4 1.2 collective-permute-start
  16.6 1.4 pick_blocks.9
  18.4 1.7 prepare_pairs.1
  20.2 1.0 copy-done.6
  21.1 18.6 %collective-permute-done.7.refs_5_.refs_2_ = bf16[2,208,256]{2,1,0:T(8,128)(2,1)S(1)} collective-permute-done((bf16[2,208,256]{2,1,0:T(8,128)(2,1)S(1)}, bf16[2,208,256]{2,1,0:T(8,128)(2,1)S(1)}, u32[]{:S(2)}, u32[]{:S(2)}) %collective-permute-start.7) | collective-permute-done | bytes 213024 | tf_op jit(solution)/shard_map/ppermute | solution.py:525
  39.8 1.3 copy-done.3
  41.1 1.2 collective-permute-start.19
  42.4 3.4 %collective-permute-start.11 = (bf16[2,208,256]{2,1,0:T(8,128)(2,1)}, bf16[2,208,256]{2,1,0:T(8,128)(2,1)S(1)}, u32[]{:S(2)}, u32[]{:S(2)}) collective-permute-start(bf16[2,208,256]{2,1,0:T(8,128)(2,1)} %get-tuple-element.47.refs_3_), channel_id=1, source_target_pairs={{0,12},{4,0},{8,4},{12,8},{1,13},{5,1},{9,5},{13,9},{2,14},{6,2},{... | collective-permute-start | bytes 638984 | tf_op jit(solution)/shard_map/ppermute | solution.py:525
  47.1 2.2 copy-done.1
  49.2 1.3 pick_blocks.10
  50.6 3.8 %collective-permute-start.10 = (bf16[2,160,256]{2,1,0:T(8,128)(2,1)S(1)}, bf16[2,160,256]{2,1,0:T(8,128)(2,1)S(1)}, u32[]{:S(2)}, u32[]{:S(2)}) collective-permute-start(bf16[2,160,256]{2,1,0:T(8,128)(2,1)S(1)} %get-tuple-element.52), channel_id=1, source_target_pairs={{0,4},{4,8},{8,12},{12,0},{1,5},{5,9},{9,13},{13,1},{2,6},{6,10},{... | collective-permute-start | bytes 491528 | tf_op jit(solution)/shard_map/ppermute | solution.py:525
  54.5 10.3 %collective-permute-done.11.refs_0_ = bf16[2,208,256]{2,1,0:T(8,128)(2,1)S(1)} collective-permute-done((bf16[2,208,256]{2,1,0:T(8,128)(2,1)}, bf16[2,208,256]{2,1,0:T(8,128)(2,1)S(1)}, u32[]{:S(2)}, u32[]{:S(2)}) %collective-permute-start.11) | collective-permute-done | bytes 213024 | tf_op jit(solution)/shard_map/ppermute | solution.py:525
  65.7 1.2 pick_blocks.11
  67.8 7.4 %collective-permute-done.8.refs_0_ = bf16[2,160,256]{2,1,0:T(8,128)(2,1)S(1)} collective-permute-done((bf16[2,160,256]{2,1,0:T(8,128)(2,1)S(1)}, bf16[2,160,256]{2,1,0:T(8,128)(2,1)S(1)}, u32[]{:S(2)}, u32[]{:S(2)}) %collective-permute-start.8) | collective-permute-done | bytes 163872 | tf_op jit(solution)/shard_map/ppermute | solution.py:525
  75.8 1.1 pick_blocks.12
  77.0 1.5 collective-permute-start.18
  78.7 4.1 %exchange_chunks.4.refs_4_.rest_4_ = f32[8,256,256]{2,1,0:T(8,128)S(1)} custom-call(s32[16]{0:T(128)S(1)} %multiply_add_fusion.slot_ref, s32[1]{0:T(128)} %bitcast.fit_ref, bf16[2,1024,256]{2,1,0:T(8,128)(2,1)S(1)} %pick_blocks.7.rest_0_.rest_1_.mine_ref, bf16[2,1024,256]{2,1,0:T(8,128)(2,1)S(1)} %collective-permute-done.rest_1_.rest_2_, ...), custom_call_target="tpu_custom_call" | custom-call | flops 26843545600 | bytes 314572800 | tf_op jit(solution)/shard_map/exchange_chunks/pallas_call | solution.py:187
  84.1 2.2 collective-permute-start.15
  87.5 3.2 %exchange_chunks.5.refs_4_.rest_4_ = f32[8,256,256]{2,1,0:T(8,128)S(1)} custom-call(s32[16]{0:T(128)S(1)} %multiply_add_fusion.slot_ref, s32[1]{0:T(128)} %bitcast.fit_ref, bf16[2,1024,256]{2,1,0:T(8,128)(2,1)S(1)} %pick_blocks.7.rest_0_.rest_1_.mine_ref, bf16[2,1024,256]{2,1,0:T(8,128)(2,1)S(1)} %collective-permute-done.rest_1_.rest_2_, ...), custom_call_target="tpu_custom_call" | custom-call | flops 21810380800 | bytes 294912000 | tf_op jit(solution)/shard_map/exchange_chunks/pallas_call | solution.py:187
  90.7 1.1 pick_blocks.13
  91.9 1.9 collective-permute-start.23
  93.8 1.1 collective-permute-done.15.refs_2_
  94.9 2.2 collective-permute-start.24
  97.1 1.2 collective-permute-done.13.refs_0_
  99.0 3.1 %exchange_chunks.6.refs_3_.rest_5_ = f32[8,256,256]{2,1,0:T(8,128)S(1)} custom-call(s32[16]{0:T(128)S(1)} %multiply_add_fusion.slot_ref, s32[1]{0:T(128)} %bitcast.fit_ref, bf16[2,1024,256]{2,1,0:T(8,128)(2,1)S(1)} %pick_blocks.7.rest_0_.rest_1_.mine_ref, bf16[2,1024,256]{2,1,0:T(8,128)(2,1)S(1)} %collective-permute-done.rest_1_.rest_2_, ...), custom_call_target="tpu_custom_call" | custom-call | flops 16777216000 | bytes 275251200 | tf_op jit(solution)/shard_map/exchange_chunks/pallas_call | solution.py:187
  102.1 3.8 %collective-permute-done.24.refs_2_ = bf16[2,128,256]{2,1,0:T(8,128)(2,1)S(1)} collective-permute-done((bf16[2,128,256]{2,1,0:T(8,128)(2,1)S(1)}, bf16[2,128,256]{2,1,0:T(8,128)(2,1)S(1)}, u32[]{:S(2)}, u32[]{:S(2)}) %collective-permute-start.24) | collective-permute-done | bytes 131104 | tf_op jit(solution)/shard_map/ppermute | solution.py:525
  105.8 2.4 %collective-permute-done.22.refs_0_ = bf16[2,128,256]{2,1,0:T(8,128)(2,1)S(1)} collective-permute-done((bf16[2,128,256]{2,1,0:T(8,128)(2,1)S(1)}, bf16[2,128,256]{2,1,0:T(8,128)(2,1)S(1)}, u32[]{:S(2)}, u32[]{:S(2)}) %collective-permute-start.22) | collective-permute-done | bytes 131104 | tf_op jit(solution)/shard_map/ppermute | solution.py:525
  108.8 3.0 %exchange_chunks.7.rest_6_ = f32[8,256,256]{2,1,0:T(8,128)S(1)} custom-call(s32[16]{0:T(128)S(1)} %multiply_add_fusion.slot_ref, s32[1]{0:T(128)} %bitcast.fit_ref, bf16[6,128,256]{2,1,0:T(8,128)(2,1)S(1)} %merge_chunk.11.rest_0_.rest_4_, bf16[2,1024,256]{2,1,0:T(8,128)(2,1)S(1)} %pick_blocks.7.rest_0_.rest_1_.mine_ref, ...), custom_call_target="tpu_custom_call" | custom-call | flops 15099494400 | bytes 268697600 | tf_op jit(solution)/shard_map/exchange_chunks/pallas_call | solution.py:187
  111.9 6.9 %collective-permute-done.26.rest_5_ = bf16[6,128,256]{2,1,0:T(8,128)(2,1)S(1)} collective-permute-done((bf16[6,128,256]{2,1,0:T(8,128)(2,1)S(1)}, bf16[6,128,256]{2,1,0:T(8,128)(2,1)S(1)}, u32[]{:S(2)}, u32[]{:S(2)}) %collective-permute-start.26) | collective-permute-done | bytes 393248 | tf_op jit(solution)/shard_map/ppermute | solution.py:463
  118.7 5.4 %middle_step.1 = (bf16[8,256,256]{2,1,0:T(8,128)(2,1)}, bf16[16,256,256]{2,1,0:T(8,128)(2,1)S(1)}, bf16[2,128,256]{2,1,0:T(8,128)(2,1)S(1)}, bf16[2,128,256]{2,1...) custom-call(s32[16]{0:T(128)S(1)} %multiply_add_fusion.slot_ref, ...), custom_call_target="tpu_custom_call" | custom-call | flops 2147483648 | bytes 8388608 | tf_op jit(solution)/shard_map/middle_step/pallas_call | solution.py:295
  124.2 1.2 collective-permute-start.32
  125.4 1.8 collective-permute-start.33
  127.2 2.9 %gradient_chunk.5 = (bf16[2,224,256]{2,1,0:T(8,128)(2,1)S(1)}, bf16[2,224,256]{2,1,0:T(8,128)(2,1)S(1)}, bf16[2,224,256]{2,1,0:T(8,128)(2,1)S(1)}, bf16[2,224,256]{2,1,0:T(8,128)(2,1)S(1)}) custom-call(s32[16]{0:T(128)S(1)} %multiply_add_fusion.slot_ref, bf16[16,256,256]{2,1,0:T(8,128)(2,1)S(1)} %get-tuple-element.65.weight_ref, ...), custom_call_target="tpu_custom_call" | custom-call | flops 469762048 | bytes 3932160 | tf_op jit(solution)/shard_map/gradient_chunk/pallas_call | solution.py:353
  130.1 1.5 collective-permute-start.36
  132.1 1.6 collective-permute-start.34
  133.7 3.0 %gradient_chunk.6 = (bf16[2,224,256]{2,1,0:T(8,128)(2,1)S(1)}, bf16[2,224,256]{2,1,0:T(8,128)(2,1)S(1)}, bf16[2,224,256]{2,1,0:T(8,128)(2,1)S(1)}, bf16[2,224,256]{2,1,0:T(8,128)(2,1)S(1)}) custom-call(s32[16]{0:T(128)S(1)} %multiply_add_fusion.slot_ref, bf16[16,256,256]{2,1,0:T(8,128)(2,1)S(1)} %get-tuple-element.65.weight_ref, ...), custom_call_target="tpu_custom_call" | custom-call | flops 469762048 | bytes 3932160 | tf_op jit(solution)/shard_map/gradient_chunk/pallas_call | solution.py:353
  136.7 5.8 %collective-permute-start.38 = (bf16[2,224,256]{2,1,0:T(8,128)(2,1)S(1)}, bf16[2,224,256]{2,1,0:T(8,128)(2,1)S(1)}, u32[]{:S(2)}, u32[]{:S(2)}) collective-permute-start(bf16[2,224,256]{2,1,0:T(8,128)(2,1)S(1)} %get-tuple-element.79), channel_id=1, source_target_pairs={{0,4},{4,8},{8,12},{12,0},{1,5},{5,9},{9,13},{13,1},{2,6},{6,10},{... | collective-permute-start | bytes 688136 | tf_op jit(solution)/shard_map/ppermute | solution.py:559
  142.5 20.7 %collective-permute-done.34.rest_3_ = bf16[2,128,256]{2,1,0:T(8,128)(2,1)S(1)} collective-permute-done((bf16[2,128,256]{2,1,0:T(8,128)(2,1)S(1)}, bf16[2,128,256]{2,1,0:T(8,128)(2,1)S(1)}, u32[]{:S(2)}, u32[]{:S(2)}) %collective-permute-start.34) | collective-permute-done | bytes 131104 | tf_op jit(solution)/shard_map/ppermute | solution.py:559
  163.2 1.2 settle_chunks.5.rest_4_.refs_0_
  164.4 1.4 collective-permute-start.44
  165.8 3.0 %gradient_chunk.4 = (bf16[2,240,256]{2,1,0:T(8,128)(2,1)S(1)}, bf16[2,240,256]{2,1,0:T(8,128)(2,1)S(1)}, bf16[2,240,256]{2,1,0:T(8,128)(2,1)S(1)}, bf16[2,240,256]{2,1,0:T(8,128)(2,1)S(1)}) custom-call(s32[16]{0:T(128)S(1)} %multiply_add_fusion.slot_ref, bf16[16,256,256]{2,1,0:T(8,128)(2,1)S(1)} %get-tuple-element.65.weight_ref, ...), custom_call_target="tpu_custom_call" | custom-call | flops 503316480 | bytes 4063232 | tf_op jit(solution)/shard_map/gradient_chunk/pallas_call | solution.py:353
  168.8 2.8 %collective-permute-start.29 = (bf16[2,240,256]{2,1,0:T(8,128)(2,1)S(1)}, bf16[2,240,256]{2,1,0:T(8,128)(2,1)S(1)}, u32[]{:S(2)}, u32[]{:S(2)}) collective-permute-start(bf16[2,240,256]{2,1,0:T(8,128)(2,1)S(1)} %get-tuple-element.68), channel_id=1, source_target_pairs={{0,8},{4,12},{8,0},{12,4},{1,9},{5,13},{9,1},{13,5},{2,10},{6,14},... | collective-permute-start | bytes 737288 | tf_op jit(solution)/shard_map/ppermute | solution.py:559
  171.6 1.3 collective-permute-start.30
  173.6 2.9 %gradient_chunk.7 = (bf16[2,208,256]{2,1,0:T(8,128)(2,1)S(1)}, bf16[2,208,256]{2,1,0:T(8,128)(2,1)S(1)}, bf16[2,208,256]{2,1,0:T(8,128)(2,1)S(1)}, bf16[2,208,256]{2,1,0:T(8,128)(2,1)S(1)}) custom-call(s32[16]{0:T(128)S(1)} %multiply_add_fusion.slot_ref, bf16[16,256,256]{2,1,0:T(8,128)(2,1)S(1)} %get-tuple-element.65.weight_ref, ...), custom_call_target="tpu_custom_call" | custom-call | flops 436207616 | bytes 3801088 | tf_op jit(solution)/shard_map/gradient_chunk/pallas_call | solution.py:353
  176.5 17.5 %collective-permute-done.28.rest_1_ = bf16[2,240,256]{2,1,0:T(8,128)(2,1)S(1)} collective-permute-done((bf16[2,240,256]{2,1,0:T(8,128)(2,1)S(1)}, bf16[2,240,256]{2,1,0:T(8,128)(2,1)S(1)}, u32[]{:S(2)}, u32[]{:S(2)}) %collective-permute-start.28) | collective-permute-done | bytes 245792 | tf_op jit(solution)/shard_map/ppermute | solution.py:559
  194.0 2.2 collective-permute-start.41
  196.2 3.1 %collective-permute-done.29.rest_2_ = bf16[2,240,256]{2,1,0:T(8,128)(2,1)S(1)} collective-permute-done((bf16[2,240,256]{2,1,0:T(8,128)(2,1)S(1)}, bf16[2,240,256]{2,1,0:T(8,128)(2,1)S(1)}, u32[]{:S(2)}, u32[]{:S(2)}) %collective-permute-start.29) | collective-permute-done | bytes 245792 | tf_op jit(solution)/shard_map/ppermute | solution.py:559
  199.3 3.6 %collective-permute-start.42 = (bf16[2,208,256]{2,1,0:T(8,128)(2,1)S(1)}, bf16[2,208,256]{2,1,0:T(8,128)(2,1)S(1)}, u32[]{:S(2)}, u32[]{:S(2)}) collective-permute-start(bf16[2,208,256]{2,1,0:T(8,128)(2,1)S(1)} %get-tuple-element.84), channel_id=1, source_target_pairs={{0,8},{4,12},{8,0},{12,4},{1,9},{5,13},{9,1},{13,5},{2,10},{6,14},... | collective-permute-start | bytes 638984 | tf_op jit(solution)/shard_map/ppermute | solution.py:559
  202.9 1.0 settle_chunks.4.refs_0_
  203.9 5.5 %collective-permute-start.31 = (bf16[8,240,256]{2,1,0:T(8,128)(2,1)S(1)}, bf16[8,240,256]{2,1,0:T(8,128)(2,1)S(1)}, u32[]{:S(2)}, u32[]{:S(2)}) collective-permute-start(bf16[8,240,256]{2,1,0:T(8,128)(2,1)S(1)} %settle_chunks.4.refs_0_), channel_id=1, source_target_pairs={{0,1},{1,0},{2,3},{3,2},{4,5},{5,4},{6,7},{7,6},{8,9},{9,8},{10,11... | collective-permute-start | bytes 2949128 | tf_op jit(solution)/shard_map/ppermute | solution.py:569
  210.4 2.7 %collective-permute-done.41.rest_1_ = bf16[2,208,256]{2,1,0:T(8,128)(2,1)S(1)} collective-permute-done((bf16[2,208,256]{2,1,0:T(8,128)(2,1)S(1)}, bf16[2,208,256]{2,1,0:T(8,128)(2,1)S(1)}, u32[]{:S(2)}, u32[]{:S(2)}) %collective-permute-start.41) | collective-permute-done | bytes 213024 | tf_op jit(solution)/shard_map/ppermute | solution.py:559
  214.0 3.6 %collective-permute-done.42.rest_2_ = bf16[2,208,256]{2,1,0:T(8,128)(2,1)S(1)} collective-permute-done((bf16[2,208,256]{2,1,0:T(8,128)(2,1)S(1)}, bf16[2,208,256]{2,1,0:T(8,128)(2,1)S(1)}, u32[]{:S(2)}, u32[]{:S(2)}) %collective-permute-start.42) | collective-permute-done | bytes 213024 | tf_op jit(solution)/shard_map/ppermute | solution.py:559
  218.5 1.0 collective-permute-start.46
  219.5 2.0 collective-permute-done.46.refs_5_
  221.5 3.0 %add_chunks.2.refs_2_ = f32[8,1024,256]{2,1,0:T(8,128)} custom-call(bf16[8,352,256]{2,1,0:T(8,128)(2,1)S(1)} %settle_chunks.5.rest_4_.refs_0_, bf16[8,224,256]{2,1,0:T(8,128)(2,1)S(1)} %settle_chunks.6.rest_4_.refs_1_, bf16[8,208,256]{2,1,0:T(8,128)(2,1)S(1)} %settle_chunks.7.refs_2_, bf16[8,352,256]{2,1,0:T(8,128)(2,1)S(1)} %collective-permute-done.44.refs_3_, ...), custom_call_target="tpu_custom_call" | custom-call | bytes 12845056 | tf_op jit(solution)/shard_map/add_chunks/pallas_call | solution.py:433
  224.5 1.4 add_chunks.3
  (103 shorter events, 14.8 us)
Async XLA Ops:
  3.0 5.6 %collective-permute-start.1 = (f32[10]{0:T(128)S(1)}, f32[10]{0:T(128)S(1)}, u32[]{:S(2)}, u32[]{:S(2)}) collective-permute-start(f32[10]{0:T(128)S(1)} %get-tuple-element.89), channel_id=1, source_target_pairs={{0,4},{4,8},{8,12},{12,0},{1,5},{5,9},{9,13},{13,1},{2,6},{6,10},{... | collective-permute-start | bytes 128 | tf_op jit(solution)/shard_map/ppermute | solution.py:496
  4.3 4.4 %collective-permute-start.2 = (f32[10]{0:T(128)S(1)}, f32[10]{0:T(128)S(1)}, u32[]{:S(2)}, u32[]{:S(2)}) collective-permute-start(f32[10]{0:T(128)S(1)} %get-tuple-element.90), channel_id=1, source_target_pairs={{0,8},{4,12},{8,0},{12,4},{1,9},{5,13},{9,1},{13,5},{2,10},{6,14},... | collective-permute-start | bytes 128 | tf_op jit(solution)/shard_map/ppermute | solution.py:496
  5.4 3.3 %collective-permute-start.3 = (f32[10]{0:T(128)S(1)}, f32[10]{0:T(128)S(1)}, u32[]{:S(2)}, u32[]{:S(2)}) collective-permute-start(f32[10]{0:T(128)S(1)} %get-tuple-element.91), channel_id=1, source_target_pairs={{0,12},{4,0},{8,4},{12,8},{1,13},{5,1},{9,5},{13,9},{2,14},{6,2},{... | collective-permute-start | bytes 128 | tf_op jit(solution)/shard_map/ppermute | solution.py:496
  8.7 7.9 %copy-start = (bf16[8,1024,256]{2,1,0:T(8,128)(2,1)S(1)}, bf16[8,1024,256]{2,1,0:T(8,128)(2,1)}, u32[]{:S(2)}) copy-start(bf16[8,1024,256]{2,1,0:T(8,128)(2,1)} %blocks_ref.13) | copy-start | bytes 12582916
  10.8 28.9 %collective-permute-start.4 = (bf16[2,256,256]{2,1,0:T(8,128)(2,1)S(1)}, bf16[2,256,256]{2,1,0:T(8,128)(2,1)S(1)}, u32[]{:S(2)}, u32[]{:S(2)}) collective-permute-start(bf16[2,256,256]{2,1,0:T(8,128)(2,1)S(1)} %get-tuple-element.44), channel_id=1, source_target_pairs={{0,12},{4,0},{8,4},{12,8},{1,13},{5,1},{9,5},{13,9},{2,14},{6,2},{... | collective-permute-start | bytes 786440 | tf_op jit(solution)/shard_map/ppermute | solution.py:525
  12.0 27.8 %collective-permute-start.5 = (bf16[2,256,256]{2,1,0:T(8,128)(2,1)S(1)}, bf16[2,256,256]{2,1,0:T(8,128)(2,1)S(1)}, u32[]{:S(2)}, u32[]{:S(2)}) collective-permute-start(bf16[2,256,256]{2,1,0:T(8,128)(2,1)S(1)} %get-tuple-element.45), channel_id=1, source_target_pairs={{0,8},{4,12},{8,0},{12,4},{1,9},{5,13},{9,1},{13,5},{2,10},{6,14},... | collective-permute-start | bytes 786440 | tf_op jit(solution)/shard_map/ppermute | solution.py:525
  13.1 5.3 %copy-start.5 = (f32[8,256,256]{2,1,0:T(8,128)S(1)}, f32[8,256,256]{2,1,0:T(8,128)}, u32[]{:S(2)}) copy-start(f32[8,256,256]{2,1,0:T(8,128)} %fock_ref.1) | copy-start | bytes 6291460
  13.1 5.3 %copy-start.8 = (s32[8]{0:T(128)S(1)}, s32[8]{0:T(128)}, u32[]{:S(2)}) copy-start(s32[8]{0:T(128)} %size_ref.1) | copy-start | bytes 100
  13.1 26.6 %collective-permute-start.6 = (bf16[2,256,256]{2,1,0:T(8,128)(2,1)S(1)}, bf16[2,256,256]{2,1,0:T(8,128)(2,1)S(1)}, u32[]{:S(2)}, u32[]{:S(2)}) collective-permute-start(bf16[2,256,256]{2,1,0:T(8,128)(2,1)S(1)} %get-tuple-element.46), channel_id=1, source_target_pairs={{0,4},{4,8},{8,12},{12,0},{1,5},{5,9},{9,13},{13,1},{2,6},{6,10},{... | collective-permute-start | bytes 786440 | tf_op jit(solution)/shard_map/ppermute | solution.py:525
  15.4 61.6 %collective-permute-start = (bf16[2,1024,256]{2,1,0:T(8,128)(2,1)S(1)}, bf16[2,1024,256]{2,1,0:T(8,128)(2,1)S(1)}, u32[]{:S(2)}, u32[]{:S(2)}) collective-permute-start(bf16[2,1024,256]{2,1,0:T(8,128)(2,1)S(1)} %pick_blocks.7.rest_0_.rest_1_.mine_ref), channel_id=1, source_target_pairs={{0,2},{2,0},{1,3},{3,1},{4,6},{6,4},{5,7},{7,5},{8,10},{10,8},{9,1... | collective-permute-start | bytes 3145736 | tf_op jit(solution)/shard_map/ppermute | solution.py:463
  18.0 21.7 %collective-permute-start.7 = (bf16[2,208,256]{2,1,0:T(8,128)(2,1)S(1)}, bf16[2,208,256]{2,1,0:T(8,128)(2,1)S(1)}, u32[]{:S(2)}, u32[]{:S(2)}) collective-permute-start(bf16[2,208,256]{2,1,0:T(8,128)(2,1)S(1)} %get-tuple-element.49), channel_id=1, source_target_pairs={{0,4},{4,8},{8,12},{12,0},{1,5},{5,9},{9,13},{13,1},{2,6},{6,10},{... | collective-permute-start | bytes 638984 | tf_op jit(solution)/shard_map/ppermute | solution.py:525
  20.1 1.0 copy-start.6
  39.8 1.3 copy-start.3
  41.1 37.3 %collective-permute-start.19 = (bf16[6,256,256]{2,1,0:T(8,128)(2,1)S(1)}, bf16[6,256,256]{2,1,0:T(8,128)(2,1)}, u32[]{:S(2)}, u32[]{:S(2)}) collective-permute-start(bf16[6,256,256]{2,1,0:T(8,128)(2,1)S(1)} %merge_chunk.6.rest_0_.rest_2_), channel_id=1, source_target_pairs={{0,2},{2,0},{1,3},{3,1},{4,6},{6,4},{5,7},{7,5},{8,10},{10,8},{9,1... | collective-permute-start | bytes 2359304 | tf_op jit(solution)/shard_map/ppermute | solution.py:463
  42.4 8.3 %collective-permute-start.12 = (bf16[2,208,256]{2,1,0:T(8,128)(2,1)}, bf16[2,208,256]{2,1,0:T(8,128)(2,1)S(1)}, u32[]{:S(2)}, u32[]{:S(2)}) collective-permute-start(bf16[2,208,256]{2,1,0:T(8,128)(2,1)} %get-tuple-element.53), channel_id=1, source_target_pairs={{0,8},{4,12},{8,0},{12,4},{1,9},{5,13},{9,1},{13,5},{2,10},{6,14},... | collective-permute-start | bytes 638984 | tf_op jit(solution)/shard_map/ppermute | solution.py:525
  42.4 22.4 %collective-permute-start.11 = (bf16[2,208,256]{2,1,0:T(8,128)(2,1)}, bf16[2,208,256]{2,1,0:T(8,128)(2,1)S(1)}, u32[]{:S(2)}, u32[]{:S(2)}) collective-permute-start(bf16[2,208,256]{2,1,0:T(8,128)(2,1)} %get-tuple-element.47.refs_3_), channel_id=1, source_target_pairs={{0,12},{4,0},{8,4},{12,8},{1,13},{5,1},{9,5},{13,9},{2,14},{6,2},{... | collective-permute-start | bytes 638984 | tf_op jit(solution)/shard_map/ppermute | solution.py:525
  47.1 2.2 copy-start.1
  49.2 16.4 %copy-start.2 = (bf16[8,1024,256]{2,1,0:T(8,128)(2,1)S(1)}, bf16[8,1024,256]{2,1,0:T(8,128)(2,1)}, u32[]{:S(2)}) copy-start(bf16[8,1024,256]{2,1,0:T(8,128)(2,1)} %blocks_ref.13) | copy-start | bytes 12582916
  50.5 16.3 %collective-permute-start.9 = (bf16[2,160,256]{2,1,0:T(8,128)(2,1)S(1)}, bf16[2,160,256]{2,1,0:T(8,128)(2,1)S(1)}, u32[]{:S(2)}, u32[]{:S(2)}) collective-permute-start(bf16[2,160,256]{2,1,0:T(8,128)(2,1)S(1)} %get-tuple-element.51), channel_id=1, source_target_pairs={{0,8},{4,12},{8,0},{12,4},{1,9},{5,13},{9,1},{13,5},{2,10},{6,14},... | collective-permute-start | bytes 491528 | tf_op jit(solution)/shard_map/ppermute | solution.py:525
  50.6 17.1 %collective-permute-start.10 = (bf16[2,160,256]{2,1,0:T(8,128)(2,1)S(1)}, bf16[2,160,256]{2,1,0:T(8,128)(2,1)S(1)}, u32[]{:S(2)}, u32[]{:S(2)}) collective-permute-start(bf16[2,160,256]{2,1,0:T(8,128)(2,1)S(1)} %get-tuple-element.52), channel_id=1, source_target_pairs={{0,4},{4,8},{8,12},{12,0},{1,5},{5,9},{9,13},{13,1},{2,6},{6,10},{... | collective-permute-start | bytes 491528 | tf_op jit(solution)/shard_map/ppermute | solution.py:525
  64.8 10.4 %collective-permute-start.8 = (bf16[2,160,256]{2,1,0:T(8,128)(2,1)S(1)}, bf16[2,160,256]{2,1,0:T(8,128)(2,1)S(1)}, u32[]{:S(2)}, u32[]{:S(2)}) collective-permute-start(bf16[2,160,256]{2,1,0:T(8,128)(2,1)S(1)} %get-tuple-element.50.refs_3_), channel_id=1, source_target_pairs={{0,12},{4,0},{8,4},{12,8},{1,13},{5,1},{9,5},{13,9},{2,14},{6,2},{... | collective-permute-start | bytes 491528 | tf_op jit(solution)/shard_map/ppermute | solution.py:525
  66.9 20.1 %collective-permute-start.20 = (bf16[6,208,256]{2,1,0:T(8,128)(2,1)S(1)}, bf16[6,208,256]{2,1,0:T(8,128)(2,1)S(1)}, u32[]{:S(2)}, u32[]{:S(2)}) collective-permute-start(bf16[6,208,256]{2,1,0:T(8,128)(2,1)S(1)} %merge_chunk.7.rest_0_.rest_2_.rest_1_), channel_id=1, source_target_pairs={{0,2},{2,0},{1,3},{3,1},{4,6},{6,4},{5,7},{7,5},{8,10},{10,8},{9,1... | collective-permute-start | bytes 1916936 | tf_op jit(solution)/shard_map/ppermute | solution.py:463
  67.8 15.0 %collective-permute-start.17 = (bf16[2,144,256]{2,1,0:T(8,128)(2,1)S(1)}, bf16[2,144,256]{2,1,0:T(8,128)(2,1)S(1)}, u32[]{:S(2)}, u32[]{:S(2)}) collective-permute-start(bf16[2,144,256]{2,1,0:T(8,128)(2,1)S(1)} %get-tuple-element.58), channel_id=1, source_target_pairs={{0,8},{4,12},{8,0},{12,4},{1,9},{5,13},{9,1},{13,5},{2,10},{6,14},... | collective-permute-start | bytes 442376 | tf_op jit(solution)/shard_map/ppermute | solution.py:525
  75.2 11.2 %collective-permute-start.16 = (bf16[2,144,256]{2,1,0:T(8,128)(2,1)S(1)}, bf16[2,144,256]{2,1,0:T(8,128)(2,1)S(1)}, u32[]{:S(2)}, u32[]{:S(2)}) collective-permute-start(bf16[2,144,256]{2,1,0:T(8,128)(2,1)S(1)} %get-tuple-element.54.refs_3_), channel_id=1, source_target_pairs={{0,12},{4,0},{8,4},{12,8},{1,13},{5,1},{9,5},{13,9},{2,14},{6,2},{... | collective-permute-start | bytes 442376 | tf_op jit(solution)/shard_map/ppermute | solution.py:525
  77.0 7.2 %collective-permute-start.18 = (bf16[2,144,256]{2,1,0:T(8,128)(2,1)S(1)}, bf16[2,144,256]{2,1,0:T(8,128)(2,1)S(1)}, u32[]{:S(2)}, u32[]{:S(2)}) collective-permute-start(bf16[2,144,256]{2,1,0:T(8,128)(2,1)S(1)} %get-tuple-element.59), channel_id=1, source_target_pairs={{0,4},{4,8},{8,12},{12,0},{1,5},{5,9},{9,13},{13,1},{2,6},{6,10},{... | collective-permute-start | bytes 442376 | tf_op jit(solution)/shard_map/ppermute | solution.py:525
  78.5 20.4 %collective-permute-start.25 = (bf16[6,160,256]{2,1,0:T(8,128)(2,1)S(1)}, bf16[6,160,256]{2,1,0:T(8,128)(2,1)S(1)}, u32[]{:S(2)}, u32[]{:S(2)}) collective-permute-start(bf16[6,160,256]{2,1,0:T(8,128)(2,1)S(1)} %merge_chunk.8.rest_0_.rest_2_.rest_1_), channel_id=1, source_target_pairs={{0,2},{2,0},{1,3},{3,1},{4,6},{6,4},{5,7},{7,5},{8,10},{10,8},{9,1... | collective-permute-start | bytes 1474568 | tf_op jit(solution)/shard_map/ppermute | solution.py:463
  82.8 9.1 %collective-permute-start.14 = (bf16[2,128,256]{2,1,0:T(8,128)(2,1)S(1)}, bf16[2,128,256]{2,1,0:T(8,128)(2,1)S(1)}, u32[]{:S(2)}, u32[]{:S(2)}) collective-permute-start(bf16[2,128,256]{2,1,0:T(8,128)(2,1)S(1)} %get-tuple-element.56), channel_id=1, source_target_pairs={{0,8},{4,12},{8,0},{12,4},{1,9},{5,13},{9,1},{13,5},{2,10},{6,14},... | collective-permute-start | bytes 393224 | tf_op jit(solution)/shard_map/ppermute | solution.py:525
  84.1 10.8 %collective-permute-start.15 = (bf16[2,128,256]{2,1,0:T(8,128)(2,1)S(1)}, bf16[2,128,256]{2,1,0:T(8,128)(2,1)S(1)}, u32[]{:S(2)}, u32[]{:S(2)}) collective-permute-start(bf16[2,128,256]{2,1,0:T(8,128)(2,1)S(1)} %get-tuple-element.57), channel_id=1, source_target_pairs={{0,4},{4,8},{8,12},{12,0},{1,5},{5,9},{9,13},{13,1},{2,6},{6,10},{... | collective-permute-start | bytes 393224 | tf_op jit(solution)/shard_map/ppermute | solution.py:525
  86.3 12.0 %collective-permute-start.13 = (bf16[2,128,256]{2,1,0:T(8,128)(2,1)S(1)}, bf16[2,128,256]{2,1,0:T(8,128)(2,1)S(1)}, u32[]{:S(2)}, u32[]{:S(2)}) collective-permute-start(bf16[2,128,256]{2,1,0:T(8,128)(2,1)S(1)} %get-tuple-element.55.refs_3_), channel_id=1, source_target_pairs={{0,12},{4,0},{8,4},{12,8},{1,13},{5,1},{9,5},{13,9},{2,14},{6,2},{... | collective-permute-start | bytes 393224 | tf_op jit(solution)/shard_map/ppermute | solution.py:525
  87.0 21.9 %collective-permute-start.27 = (bf16[6,144,256]{2,1,0:T(8,128)(2,1)S(1)}, bf16[6,144,256]{2,1,0:T(8,128)(2,1)S(1)}, u32[]{:S(2)}, u32[]{:S(2)}) collective-permute-start(bf16[6,144,256]{2,1,0:T(8,128)(2,1)S(1)} %merge_chunk.9.rest_0_.rest_3_.rest_2_), channel_id=1, source_target_pairs={{0,2},{2,0},{1,3},{3,1},{4,6},{6,4},{5,7},{7,5},{8,10},{10,8},{9,1... | collective-permute-start | bytes 1327112 | tf_op jit(solution)/shard_map/ppermute | solution.py:463
  91.9 10.2 %collective-permute-start.23 = (bf16[2,128,256]{2,1,0:T(8,128)(2,1)S(1)}, bf16[2,128,256]{2,1,0:T(8,128)(2,1)S(1)}, u32[]{:S(2)}, u32[]{:S(2)}) collective-permute-start(bf16[2,128,256]{2,1,0:T(8,128)(2,1)S(1)} %get-tuple-element.61), channel_id=1, source_target_pairs={{0,8},{4,12},{8,0},{12,4},{1,9},{5,13},{9,1},{13,5},{2,10},{6,14},... | collective-permute-start | bytes 393224 | tf_op jit(solution)/shard_map/ppermute | solution.py:525
  94.9 10.9 %collective-permute-start.24 = (bf16[2,128,256]{2,1,0:T(8,128)(2,1)S(1)}, bf16[2,128,256]{2,1,0:T(8,128)(2,1)S(1)}, u32[]{:S(2)}, u32[]{:S(2)}) collective-permute-start(bf16[2,128,256]{2,1,0:T(8,128)(2,1)S(1)} %get-tuple-element.62), channel_id=1, source_target_pairs={{0,4},{4,8},{8,12},{12,0},{1,5},{5,9},{9,13},{13,1},{2,6},{6,10},{... | collective-permute-start | bytes 393224 | tf_op jit(solution)/shard_map/ppermute | solution.py:525
  98.4 9.8 %collective-permute-start.22 = (bf16[2,128,256]{2,1,0:T(8,128)(2,1)S(1)}, bf16[2,128,256]{2,1,0:T(8,128)(2,1)S(1)}, u32[]{:S(2)}, u32[]{:S(2)}) collective-permute-start(bf16[2,128,256]{2,1,0:T(8,128)(2,1)S(1)} %get-tuple-element.60.refs_3_), channel_id=1, source_target_pairs={{0,12},{4,0},{8,4},{12,8},{1,13},{5,1},{9,5},{13,9},{2,14},{6,2},{... | collective-permute-start | bytes 393224 | tf_op jit(solution)/shard_map/ppermute | solution.py:525
  98.9 12.9 %collective-permute-start.21 = (bf16[6,128,256]{2,1,0:T(8,128)(2,1)S(1)}, bf16[6,128,256]{2,1,0:T(8,128)(2,1)S(1)}, u32[]{:S(2)}, u32[]{:S(2)}) collective-permute-start(bf16[6,128,256]{2,1,0:T(8,128)(2,1)S(1)} %merge_chunk.10.rest_2_.rest_1_), channel_id=1, source_target_pairs={{0,2},{2,0},{1,3},{3,1},{4,6},{6,4},{5,7},{7,5},{8,10},{10,8},{9,1... | collective-permute-start | bytes 1179656 | tf_op jit(solution)/shard_map/ppermute | solution.py:463
  108.7 10.0 %copy-start.4 = (f32[8,256,256]{2,1,0:T(8,128)S(1)}, f32[8,256,256]{2,1,0:T(8,128)}, u32[]{:S(2)}) copy-start(f32[8,256,256]{2,1,0:T(8,128)} %copy-done.3) | copy-start | bytes 6291460
  108.7 10.0 %copy-start.7 = (bf16[8,256,256]{2,1,0:T(8,128)(2,1)S(1)}, bf16[8,256,256]{2,1,0:T(8,128)(2,1)}, u32[]{:S(2)}) copy-start(bf16[8,256,256]{2,1,0:T(8,128)(2,1)} %copy-done.6) | copy-start | bytes 3145732
  108.7 10.0 %collective-permute-start.26 = (bf16[6,128,256]{2,1,0:T(8,128)(2,1)S(1)}, bf16[6,128,256]{2,1,0:T(8,128)(2,1)S(1)}, u32[]{:S(2)}, u32[]{:S(2)}) collective-permute-start(bf16[6,128,256]{2,1,0:T(8,128)(2,1)S(1)} %merge_chunk.11.rest_0_.rest_4_), channel_id=1, source_target_pairs={{0,2},{2,0},{1,3},{3,1},{4,6},{6,4},{5,7},{7,5},{8,10},{10,8},{9,1... | collective-permute-start | bytes 1179656 | tf_op jit(solution)/shard_map/ppermute | solution.py:463
  124.2 8.0 %collective-permute-start.32 = (bf16[2,128,256]{2,1,0:T(8,128)(2,1)S(1)}, bf16[2,128,256]{2,1,0:T(8,128)(2,1)S(1)}, u32[]{:S(2)}, u32[]{:S(2)}) collective-permute-start(bf16[2,128,256]{2,1,0:T(8,128)(2,1)S(1)} %get-tuple-element.71), channel_id=1, source_target_pairs={{0,4},{4,8},{8,12},{12,0},{1,5},{5,9},{9,13},{13,1},{2,6},{6,10},{... | collective-permute-start | bytes 393224 | tf_op jit(solution)/shard_map/ppermute | solution.py:559
  125.4 11.3 %collective-permute-start.33 = (bf16[2,128,256]{2,1,0:T(8,128)(2,1)S(1)}, bf16[2,128,256]{2,1,0:T(8,128)(2,1)S(1)}, u32[]{:S(2)}, u32[]{:S(2)}) collective-permute-start(bf16[2,128,256]{2,1,0:T(8,128)(2,1)S(1)} %get-tuple-element.72), channel_id=1, source_target_pairs={{0,8},{4,12},{8,0},{12,4},{1,9},{5,13},{9,1},{13,5},{2,10},{6,14},... | collective-permute-start | bytes 393224 | tf_op jit(solution)/shard_map/ppermute | solution.py:559
  130.1 33.1 %collective-permute-start.35 = (bf16[2,224,256]{2,1,0:T(8,128)(2,1)S(1)}, bf16[2,224,256]{2,1,0:T(8,128)(2,1)S(1)}, u32[]{:S(2)}, u32[]{:S(2)}) collective-permute-start(bf16[2,224,256]{2,1,0:T(8,128)(2,1)S(1)} %get-tuple-element.75), channel_id=1, source_target_pairs={{0,4},{4,8},{8,12},{12,0},{1,5},{5,9},{9,13},{13,1},{2,6},{6,10},{... | collective-permute-start | bytes 688136 | tf_op jit(solution)/shard_map/ppermute | solution.py:559
  130.1 33.1 %collective-permute-start.36 = (bf16[2,224,256]{2,1,0:T(8,128)(2,1)S(1)}, bf16[2,224,256]{2,1,0:T(8,128)(2,1)S(1)}, u32[]{:S(2)}, u32[]{:S(2)}) collective-permute-start(bf16[2,224,256]{2,1,0:T(8,128)(2,1)S(1)} %get-tuple-element.76), channel_id=1, source_target_pairs={{0,8},{4,12},{8,0},{12,4},{1,9},{5,13},{9,1},{13,5},{2,10},{6,14},... | collective-permute-start | bytes 688136 | tf_op jit(solution)/shard_map/ppermute | solution.py:559
  131.7 31.6 %collective-permute-start.37 = (bf16[2,224,256]{2,1,0:T(8,128)(2,1)S(1)}, bf16[2,224,256]{2,1,0:T(8,128)(2,1)S(1)}, u32[]{:S(2)}, u32[]{:S(2)}) collective-permute-start(bf16[2,224,256]{2,1,0:T(8,128)(2,1)S(1)} %get-tuple-element.77), channel_id=1, source_target_pairs={{0,12},{4,0},{8,4},{12,8},{1,13},{5,1},{9,5},{13,9},{2,14},{6,2},{... | collective-permute-start | bytes 688136 | tf_op jit(solution)/shard_map/ppermute | solution.py:559
  132.1 31.0 %collective-permute-start.34 = (bf16[2,128,256]{2,1,0:T(8,128)(2,1)S(1)}, bf16[2,128,256]{2,1,0:T(8,128)(2,1)S(1)}, u32[]{:S(2)}, u32[]{:S(2)}) collective-permute-start(bf16[2,128,256]{2,1,0:T(8,128)(2,1)S(1)} %get-tuple-element.73), channel_id=1, source_target_pairs={{0,12},{4,0},{8,4},{12,8},{1,13},{5,1},{9,5},{13,9},{2,14},{6,2},{... | collective-permute-start | bytes 393224 | tf_op jit(solution)/shard_map/ppermute | solution.py:559
  136.7 34.9 %collective-permute-start.38 = (bf16[2,224,256]{2,1,0:T(8,128)(2,1)S(1)}, bf16[2,224,256]{2,1,0:T(8,128)(2,1)S(1)}, u32[]{:S(2)}, u32[]{:S(2)}) collective-permute-start(bf16[2,224,256]{2,1,0:T(8,128)(2,1)S(1)} %get-tuple-element.79), channel_id=1, source_target_pairs={{0,4},{4,8},{8,12},{12,0},{1,5},{5,9},{9,13},{13,1},{2,6},{6,10},{... | collective-permute-start | bytes 688136 | tf_op jit(solution)/shard_map/ppermute | solution.py:559
  163.2 10.1 %collective-permute-start.39 = (bf16[2,224,256]{2,1,0:T(8,128)(2,1)S(1)}, bf16[2,224,256]{2,1,0:T(8,128)(2,1)S(1)}, u32[]{:S(2)}, u32[]{:S(2)}) collective-permute-start(bf16[2,224,256]{2,1,0:T(8,128)(2,1)S(1)} %get-tuple-element.80), channel_id=1, source_target_pairs={{0,8},{4,12},{8,0},{12,4},{1,9},{5,13},{9,1},{13,5},{2,10},{6,14},... | collective-permute-start | bytes 688136 | tf_op jit(solution)/shard_map/ppermute | solution.py:559
  164.4 57.1 %collective-permute-start.44 = (bf16[8,352,256]{2,1,0:T(8,128)(2,1)S(1)}, bf16[8,352,256]{2,1,0:T(8,128)(2,1)S(1)}, u32[]{:S(2)}, u32[]{:S(2)}) collective-permute-start(bf16[8,352,256]{2,1,0:T(8,128)(2,1)S(1)} %settle_chunks.5.rest_4_.refs_0_), channel_id=1, source_target_pairs={{0,1},{1,0},{2,3},{3,2},{4,5},{5,4},{6,7},{7,6},{8,9},{9,8},{10,11... | collective-permute-start | bytes 4325384 | tf_op jit(solution)/shard_map/ppermute | solution.py:569
  168.8 25.3 %collective-permute-start.28 = (bf16[2,240,256]{2,1,0:T(8,128)(2,1)S(1)}, bf16[2,240,256]{2,1,0:T(8,128)(2,1)S(1)}, u32[]{:S(2)}, u32[]{:S(2)}) collective-permute-start(bf16[2,240,256]{2,1,0:T(8,128)(2,1)S(1)} %get-tuple-element.67), channel_id=1, source_target_pairs={{0,4},{4,8},{8,12},{12,0},{1,5},{5,9},{9,13},{13,1},{2,6},{6,10},{... | collective-permute-start | bytes 737288 | tf_op jit(solution)/shard_map/ppermute | solution.py:559
  168.8 30.5 %collective-permute-start.29 = (bf16[2,240,256]{2,1,0:T(8,128)(2,1)S(1)}, bf16[2,240,256]{2,1,0:T(8,128)(2,1)S(1)}, u32[]{:S(2)}, u32[]{:S(2)}) collective-permute-start(bf16[2,240,256]{2,1,0:T(8,128)(2,1)S(1)} %get-tuple-element.68), channel_id=1, source_target_pairs={{0,8},{4,12},{8,0},{12,4},{1,9},{5,13},{9,1},{13,5},{2,10},{6,14},... | collective-permute-start | bytes 737288 | tf_op jit(solution)/shard_map/ppermute | solution.py:559
  171.6 31.3 %collective-permute-start.30 = (bf16[2,240,256]{2,1,0:T(8,128)(2,1)S(1)}, bf16[2,240,256]{2,1,0:T(8,128)(2,1)S(1)}, u32[]{:S(2)}, u32[]{:S(2)}) collective-permute-start(bf16[2,240,256]{2,1,0:T(8,128)(2,1)S(1)} %get-tuple-element.69), channel_id=1, source_target_pairs={{0,12},{4,0},{8,4},{12,8},{1,13},{5,1},{9,5},{13,9},{2,14},{6,2},{... | collective-permute-start | bytes 737288 | tf_op jit(solution)/shard_map/ppermute | solution.py:559
  173.3 30.6 %collective-permute-start.40 = (bf16[2,224,256]{2,1,0:T(8,128)(2,1)S(1)}, bf16[2,224,256]{2,1,0:T(8,128)(2,1)S(1)}, u32[]{:S(2)}, u32[]{:S(2)}) collective-permute-start(bf16[2,224,256]{2,1,0:T(8,128)(2,1)S(1)} %get-tuple-element.81), channel_id=1, source_target_pairs={{0,12},{4,0},{8,4},{12,8},{1,13},{5,1},{9,5},{13,9},{2,14},{6,2},{... | collective-permute-start | bytes 688136 | tf_op jit(solution)/shard_map/ppermute | solution.py:559
  194.0 19.0 %collective-permute-start.41 = (bf16[2,208,256]{2,1,0:T(8,128)(2,1)S(1)}, bf16[2,208,256]{2,1,0:T(8,128)(2,1)S(1)}, u32[]{:S(2)}, u32[]{:S(2)}) collective-permute-start(bf16[2,208,256]{2,1,0:T(8,128)(2,1)S(1)} %get-tuple-element.83), channel_id=1, source_target_pairs={{0,4},{4,8},{8,12},{12,0},{1,5},{5,9},{9,13},{13,1},{2,6},{6,10},{... | collective-permute-start | bytes 638984 | tf_op jit(solution)/shard_map/ppermute | solution.py:559
  199.3 18.3 %collective-permute-start.42 = (bf16[2,208,256]{2,1,0:T(8,128)(2,1)S(1)}, bf16[2,208,256]{2,1,0:T(8,128)(2,1)S(1)}, u32[]{:S(2)}, u32[]{:S(2)}) collective-permute-start(bf16[2,208,256]{2,1,0:T(8,128)(2,1)S(1)} %get-tuple-element.84), channel_id=1, source_target_pairs={{0,8},{4,12},{8,0},{12,4},{1,9},{5,13},{9,1},{13,5},{2,10},{6,14},... | collective-permute-start | bytes 638984 | tf_op jit(solution)/shard_map/ppermute | solution.py:559
  202.9 14.7 %collective-permute-start.43 = (bf16[2,208,256]{2,1,0:T(8,128)(2,1)S(1)}, bf16[2,208,256]{2,1,0:T(8,128)(2,1)S(1)}, u32[]{:S(2)}, u32[]{:S(2)}) collective-permute-start(bf16[2,208,256]{2,1,0:T(8,128)(2,1)S(1)} %get-tuple-element.85), channel_id=1, source_target_pairs={{0,12},{4,0},{8,4},{12,8},{1,13},{5,1},{9,5},{13,9},{2,14},{6,2},{... | collective-permute-start | bytes 638984 | tf_op jit(solution)/shard_map/ppermute | solution.py:559
  203.9 20.6 %collective-permute-start.31 = (bf16[8,240,256]{2,1,0:T(8,128)(2,1)S(1)}, bf16[8,240,256]{2,1,0:T(8,128)(2,1)S(1)}, u32[]{:S(2)}, u32[]{:S(2)}) collective-permute-start(bf16[8,240,256]{2,1,0:T(8,128)(2,1)S(1)} %settle_chunks.4.refs_0_), channel_id=1, source_target_pairs={{0,1},{1,0},{2,3},{3,2},{4,5},{5,4},{6,7},{7,6},{8,9},{9,8},{10,11... | collective-permute-start | bytes 2949128 | tf_op jit(solution)/shard_map/ppermute | solution.py:569
  213.0 8.4 %collective-permute-start.45 = (bf16[8,224,256]{2,1,0:T(8,128)(2,1)S(1)}, bf16[8,224,256]{2,1,0:T(8,128)(2,1)S(1)}, u32[]{:S(2)}, u32[]{:S(2)}) collective-permute-start(bf16[8,224,256]{2,1,0:T(8,128)(2,1)S(1)} %settle_chunks.6.rest_4_.refs_1_), channel_id=1, source_target_pairs={{0,1},{1,0},{2,3},{3,2},{4,5},{5,4},{6,7},{7,6},{8,9},{9,8},{10,11... | collective-permute-start | bytes 2752520 | tf_op jit(solution)/shard_map/ppermute | solution.py:569
  218.5 3.0 %collective-permute-start.46 = (bf16[8,208,256]{2,1,0:T(8,128)(2,1)S(1)}, bf16[8,208,256]{2,1,0:T(8,128)(2,1)S(1)}, u32[]{:S(2)}, u32[]{:S(2)}) collective-permute-start(bf16[8,208,256]{2,1,0:T(8,128)(2,1)S(1)} %settle_chunks.7.refs_2_), channel_id=1, source_target_pairs={{0,1},{1,0},{2,3},{3,2},{4,5},{5,4},{6,7},{7,6},{8,9},{9,8},{10,11... | collective-permute-start | bytes 2555912 | tf_op jit(solution)/shard_map/ppermute | solution.py:569
